TPU v7x, 32 devices: a whole 2x2x4 slice. The times are simulated.
32 devices in a mesh: row: 8 (over y, x, core), col: 4 (over z).
Axes of the slice: x: 2, y: 2, z: 4, core: 2. Of those that a mesh axis runs over, the one named last changes fastest.
Arguments:
- inputs: bfloat16 [4096, 1792], P(('row', 'col')), may hold values from -6 to 6
- attention_norm_gain: float32 [1792], replicated, may hold values from 0.5 to 1.5
- query_key_value_weight: bfloat16 [1792, 3, 1792], P('row', None, 'col'), may hold values from -0.125 to 0.125
- filter_taps: float32 [3, 2, 1792], P(None, None, 'col'), may hold values from -3 to 3
- output_projection: bfloat16 [1792, 1792], P('col', 'row'), may hold values from -0.125 to 0.125
- window_key_value: bfloat16 [64, 2, 16, 7168], P('row', None, 'col'), may hold values from -300 to 300
- cache_valid_length: int32 [64], P('row'), may hold values from 0 to 64
- lengths: int32 [8, 8], P('row'), may hold values from 1 to 128, 512 in all within a row
- token_adapter_index: int32 [4096, 1], P('row'), may hold values from 0 to 15; in each aligned block of 128 rows (0 to 127, 128 to 255, ...) at most 16 rows name the same one
- adapter_down_map: bfloat16 [16, 1792, 16], P('row'), may hold values from -0.125 to 0.125
- adapter_up_map: bfloat16 [16, 16, 1792], P('row'), may hold values from -1.5 to 1.5
- feed_forward_gain: float32 [1792], replicated, may hold values from 0.5 to 1.5
- gate_projection: bfloat16 [1792, 4096], P('row', 'col'), may hold values from -0.125 to 0.125
- up_projection: bfloat16 [1792, 4096], P('row', 'col'), may hold values from -0.125 to 0.125
- down_projection: bfloat16 [4096, 1792], P('col', 'row'), may hold values from -0.09375 to 0.09375
Outputs:
- layer_out: bfloat16 [4096, 1792], P(('row', 'col'))
Inputs may be any that keep to these rules, and one draw needn't show every extreme that they name: Each row of lengths sums to 512, and its largest entry is exactly 128. `cache_valid_length`: A request with 0 is a new prompt without cached positions. `token_adapter_index`: in each aligned block of 128 tokens no adapter serves more than 16 tokens, and some adapter serves exactly 16.
All inputs are finite; a program needn't handle non-finite values.
Results may differ from a plain program's by a relative error of at most 0.019.
Values may be sent and summed in bfloat16 or wider, within the bound.
No kernel may reach another device: no remote copies, remote signals or barrier semaphores. Data moves between devices by JAX's collectives and lax.ppermute only.
A program may use at most 64 MiB of HBM per device.

v0:
```python
import jax
import jax.numpy as jnp
from jax import lax
from jax.sharding import PartitionSpec as P

HD = 112


epsilon = 1e-05


def rms_scaled(values, gain_row):
    mean_square = jnp.mean(values * values, axis=-1, keepdims=True)
    return values * lax.rsqrt(mean_square + epsilon) * gain_row


def layout(lengths_row, tok_count):
    finish = jnp.cumsum(lengths_row)
    begins = finish - lengths_row
    places = jnp.arange(tok_count, dtype=jnp.int32)
    segment = jnp.sum((places[:, None] >= finish[None, :]).astype(jnp.int32), axis=1)
    member = segment[:, None] == jnp.arange(lengths_row.shape[0], dtype=jnp.int32)[None, :]
    inside = places - jnp.sum(jnp.where(member, begins[None, :], 0), axis=1)
    return (segment, inside)


def shifted(values, offset, inside):
    moved_rows = jnp.pad(values[: values.shape[0] - offset], ((offset, 0), (0, 0)))
    return jnp.where((inside >= offset)[:, None], moved_rows, jnp.zeros_like(moved_rows))


def convolve(values, taps, inside):
    running = jnp.zeros_like(values)
    for offset in range(taps.shape[0]):
        running = running + taps[offset][None, :] * shifted(values, offset, inside)
    return running


def make_qkv(qkv_mixed, filter_taps, inside):
    queries = qkv_mixed[:, 0].astype(jnp.bfloat16)
    keys_used = convolve(qkv_mixed[:, 1], filter_taps[:, 0], inside).astype(jnp.bfloat16)
    raw_values = qkv_mixed[:, 2]
    gates = jax.nn.sigmoid(convolve(raw_values, filter_taps[:, 1], inside))
    values_used = (raw_values * gates).astype(jnp.bfloat16)
    return (queries, keys_used, values_used)


def split_cache(window_key_value, head_size):
    requests_here, head_count = (window_key_value.shape[0], window_key_value.shape[2])
    window = window_key_value.shape[3] // head_size
    split_kv = window_key_value.reshape(requests_here, 2, head_count, window, head_size)
    cached_key_rows = jnp.transpose(split_kv[:, 0], (0, 2, 1, 3)).reshape(
        requests_here * window, head_count, head_size
    )
    cached_value_rows = jnp.transpose(split_kv[:, 1], (0, 2, 1, 3)).reshape(
        requests_here * window, head_count, head_size
    )
    return (cached_key_rows, cached_value_rows, window)


def attend(
    queries,
    keys_used,
    values_used,
    window_key_value,
    segment,
    inside,
    cache_valid_length,
    head_size,
):
    tok_count = queries.shape[0]
    head_count = queries.shape[1] // head_size
    requests_here = window_key_value.shape[0]
    cached_key_rows, cached_value_rows, window = split_cache(window_key_value, head_size)
    query_per_head = queries.reshape(tok_count, head_count, head_size)
    key_h = keys_used.reshape(tok_count, head_count, head_size)
    value_per_head = values_used.reshape(tok_count, head_count, head_size)
    attention_score_scale = head_size ** (-0.5)
    places = jnp.arange(tok_count, dtype=jnp.int32)
    local_mask = (
        (segment[:, None] == segment[None, :])
        & (places[None, :] <= places[:, None])
        & (places[None, :] > places[:, None] - window)
    )
    slot_ids = jnp.arange(requests_here * window, dtype=jnp.int32)
    owner_req = slot_ids // window
    within = slot_ids % window
    slot_ages = jnp.repeat(cache_valid_length, window)
    cache_mask = (
        (segment[:, None] == owner_req[None, :])
        & (within[None, :] >= window - slot_ages[None, :])
        & (within[None, :] > inside[:, None])
    )
    local_scores = (
        jnp.einsum("thd,jhd->htj", query_per_head, key_h, preferred_element_type=jnp.float32)
        * attention_score_scale
    )
    cached_score_rows = (
        jnp.einsum(
            "sek,yek->esy", query_per_head, cached_key_rows, preferred_element_type=jnp.float32
        )
        * attention_score_scale
    )
    local_scores = jnp.where(local_mask[None], local_scores, -jnp.inf)
    cached_score_rows = jnp.where(cache_mask[None], cached_score_rows, -jnp.inf)
    row_max = jnp.maximum(
        jnp.max(local_scores, axis=-1, keepdims=True),
        jnp.max(cached_score_rows, axis=-1, keepdims=True),
    )
    local_exp = jnp.exp(local_scores - row_max)
    cache_exp = jnp.exp(cached_score_rows - row_max)
    denominator = jnp.sum(local_exp, axis=-1, keepdims=True) + jnp.sum(
        cache_exp, axis=-1, keepdims=True
    )
    window_attention_weight = (local_exp / denominator).astype(jnp.bfloat16)
    cached_attention_weight = (cache_exp / denominator).astype(jnp.bfloat16)
    joined_output = jnp.einsum(
        "zkc,czu->kzu", window_attention_weight, value_per_head, preferred_element_type=jnp.float32
    )
    joined_output = joined_output + jnp.einsum(
        "lar,rlx->alx",
        cached_attention_weight,
        cached_value_rows,
        preferred_element_type=jnp.float32,
    )
    return joined_output.reshape(tok_count, head_count * head_size).astype(jnp.bfloat16)


def on_device(
    inputs,
    attention_norm_gain,
    query_key_value_weight,
    filter_taps,
    output_projection,
    window_key_value,
    cache_valid_length,
    lengths,
    token_adapter_index,
    adapter_down_map,
    adapter_up_map,
    feed_forward_gain,
    gate_projection,
    up_projection,
    down_projection,
):
    own_count = inputs.shape[0]
    column = lax.axis_index("col")
    row_count = lax.axis_size("row")
    gathered = lax.all_gather(inputs, "col", axis=0, tiled=True)
    tok_count = gathered.shape[0]
    normalized_input = rms_scaled(gathered.astype(jnp.float32), attention_norm_gain).astype(
        jnp.bfloat16
    )
    qkv_mixed = jnp.einsum(
        "td,dka->tka",
        normalized_input,
        lax.all_gather(query_key_value_weight, "row", axis=0, tiled=True),
        preferred_element_type=jnp.float32,
    )
    segment, inside = layout(lengths[0], tok_count)
    queries, keys_used, values_used = make_qkv(qkv_mixed, filter_taps, inside)
    attended = attend(
        queries, keys_used, values_used, window_key_value, segment, inside, cache_valid_length, HD
    )
    kept_count = adapter_down_map.shape[0]
    every_adapter = kept_count * row_count
    capacity = max(2, 2 * own_count // every_adapter)
    first_row = column * own_count
    own_rows = lax.dynamic_slice_in_dim(normalized_input, first_row, own_count, 0)
    own_ids = lax.dynamic_slice_in_dim(token_adapter_index[:, 0], first_row, own_count, 0)
    member = (own_ids[:, None] == jnp.arange(every_adapter, dtype=jnp.int32)[None, :]).astype(
        jnp.int32
    )
    before = jnp.cumsum(member, axis=0) - member
    slot_rank = jnp.sum(before * member, axis=1)
    target = own_ids * capacity + slot_rank
    placer = (
        target[None, :] == jnp.arange(every_adapter * capacity, dtype=jnp.int32)[:, None]
    ).astype(jnp.bfloat16)
    outgoing = jnp.dot(placer, own_rows, preferred_element_type=jnp.float32).astype(jnp.bfloat16)
    outgoing = outgoing.reshape(row_count, kept_count, capacity, normalized_input.shape[1])
    reduced_rank_input = jnp.einsum(
        "sakd,adr->sakr",
        lax.all_to_all(outgoing, "row", split_axis=0, concat_axis=0, tiled=True),
        adapter_down_map,
        preferred_element_type=jnp.float32,
    ).astype(jnp.bfloat16)
    answered = jnp.einsum(
        "zjbf,jfm->zjbm", reduced_rank_input, adapter_up_map, preferred_element_type=jnp.float32
    ).astype(jnp.bfloat16)
    returned = lax.all_to_all(answered, "row", split_axis=0, concat_axis=0, tiled=True).reshape(
        every_adapter * capacity, normalized_input.shape[1]
    )
    delta_rows = jnp.dot(jnp.transpose(placer), returned, preferred_element_type=jnp.float32)
    out_term = jnp.dot(
        attended,
        lax.all_gather(output_projection, "row", axis=1, tiled=True),
        preferred_element_type=jnp.float32,
    )
    own_term = lax.dynamic_slice_in_dim(out_term, first_row, own_count, 0) + delta_rows
    out_term = lax.dynamic_update_slice_in_dim(out_term, own_term, first_row, 0)
    attn_share = lax.psum_scatter(
        out_term.astype(jnp.bfloat16), "col", scatter_dimension=0, tiled=True
    ).astype(jnp.float32)
    residual = (inputs.astype(jnp.float32) + attn_share).astype(jnp.bfloat16)
    whole_mixed = lax.all_gather(residual, "col", axis=0, tiled=True)
    normed_mlp = rms_scaled(whole_mixed.astype(jnp.float32), feed_forward_gain).astype(jnp.bfloat16)

    def add_rows(piece):
        return jnp.dot(normed_mlp, piece, preferred_element_type=jnp.float32)

    gate = add_rows(lax.all_gather(gate_projection, "row", axis=0, tiled=True))
    up_part = add_rows(lax.all_gather(up_projection, "row", axis=0, tiled=True))
    hidden = (jax.nn.silu(gate) * up_part).astype(jnp.bfloat16)
    down_term = jnp.dot(
        hidden,
        lax.all_gather(down_projection, "row", axis=1, tiled=True),
        preferred_element_type=jnp.float32,
    )
    mlp_added = lax.psum_scatter(
        down_term.astype(jnp.bfloat16), "col", scatter_dimension=0, tiled=True
    ).astype(jnp.float32)
    return (residual.astype(jnp.float32) + mlp_added).astype(jnp.bfloat16)


def solution(mesh):
    placed = (
        P(("row", "col"), None),
        P(),
        P("row", None, "col"),
        P(None, None, "col"),
        P("col", "row"),
        P("row", None, "col", None),
        P("row"),
        P("row", None),
        P("row", None),
        P("row", None, None),
        P("row", None, None),
        P(),
        P("row", "col"),
        P("row", "col"),
        P("col", "row"),
    )
    return jax.shard_map(
        on_device, mesh=mesh, in_specs=placed, out_specs=P(("row", "col"), None), check_vma=False
    )
```

profile of v0, /device:TPU:0, one launch (start us, length us, event | category | flops | bytes accessed | tf_op | source)
XLA Modules:
  0.0 409.9 jit_solution(8645656561165145441)
XLA Ops:
  7.3 2.6 copy.51
  10.0 1.8 copy.59
  12.9 1.5 reshape.283
  15.1 37.9 %all-gather.8.cloned.1.call-done = bf16[512,1792]{1,0:T(8,128)(2,1)} async-done(((bf16[128,1792]{1,0:T(8,128)(2,1)}), bf16[512,1792]{1,0:T(8,128)(2,1)}) %all-gather.8.cloned.1.call-update) | async-done | bytes 1835024 | tf_op jit(solution)/shard_map/all_gather | solution.py:149
  53.1 1.9 fusion.4
  55.0 2.0 fusion.6
  58.2 1.4 convolution_convert_fusion.1
  59.6 3.7 all-to-all-start
  64.1 20.7 %all-to-all-done = bf16[8,2,16,1792]{3,2,1,0:T(8,128)(2,1)S(1)} async-done(((bf16[8,2,16,1792]{3,2,1,0:T(8,128)(2,1)}), bf16[8,2,16,1792]{3,2,1,0:T(8,128)(2,1)S(1)}, u32[]{:S(2)}, u32[]{:S(2)}) %all-to-all-start) | async-done | bytes 917536 | tf_op jit(solution)/shard_map/all_to_all | solution.py:184
  84.8 1.6 fusion.13
  87.4 3.6 all-to-all-start.1
  91.3 31.9 %all-gather.10.cloned.1.call-done = bf16[1792,3,448]{2,1,0:T(4,128)(2,1)} async-done(((bf16[224,3,448]{2,1,0:T(4,128)(2,1)}), bf16[1792,3,448]{2,1,0:T(4,128)(2,1)}) %all-gather.10.cloned.1.call-update) | async-done | bytes 4816912 | tf_op jit(solution)/shard_map/all_gather | solution.py:157
  123.2 6.5 %fusion = f32[512,3,448]{0,2,1:T(8,128)S(1)} fusion(bf16[1792,3,448]{2,1,0:T(4,128)(2,1)} %all-gather.10.cloned.1.call-done, bf16[512,1792]{1,0:T(8,128)(2,1)} %copy-done.3), kind=kOutput, calls=%fused_computation | convolution fusion | flops 2466250752 | bytes 9404416 | tf_op jit(solution)/shard_map/td,dka->tka/dot_general | solution.py:154
  130.5 1.7 fusion.28
  133.9 1.8 fusion.11
  135.8 1.5 fusion.17
  137.3 1.4 fusion.20
  138.7 13.3 %all-gather.12.cloned.1.call-done = bf16[448,1792]{0,1:T(8,128)(2,1)} async-done(((bf16[448,224]{0,1:T(8,128)(2,1)}), bf16[448,1792]{0,1:T(8,128)(2,1)}) %all-gather.12.cloned.1.call-update) | async-done | bytes 1605648 | tf_op jit(solution)/shard_map/all_gather | solution.py:197
  151.9 4.5 %fusion.60 = f32[512,1792]{1,0:T(8,128)} fusion(bf16[512,448]{0,1:T(8,128)(2,1)S(1)} %bitcast.103, bf16[448,1792]{0,1:T(8,128)(2,1)} %all-gather.12.cloned.1.call-done), kind=kOutput, calls=%fused_computation.106 | convolution fusion | flops 822083584 | bytes 5734400 | tf_op jit(solution)/shard_map/dot_general | solution.py:195
  156.4 2.4 fusion.12
  158.9 3.5 convert_element_type.107
  162.5 39.5 %reduce-scatter.3.cloned.1.call-done = bf16[128,1792]{1,0:T(8,128)(2,1)} async-done(((bf16[512,1792]{1,0:T(8,128)(2,1)}), bf16[128,1792]{1,0:T(8,128)(2,1)}) %reduce-scatter.3.cloned.1.call-update) | async-done | bytes 458768 | tf_op jit(solution)/shard_map/reduce_scatter | solution.py:202
  202.0 1.9 add_convert_fusion.1
  206.3 38.3 %all-gather.14.cloned.1.call-done = bf16[512,1792]{1,0:T(8,128)(2,1)} async-done(((bf16[128,1792]{1,0:T(8,128)(2,1)}), bf16[512,1792]{1,0:T(8,128)(2,1)}) %all-gather.14.cloned.1.call-update) | async-done | bytes 1835024 | tf_op jit(solution)/shard_map/all_gather | solution.py:206
  244.6 1.9 fusion.7
  246.6 33.2 %all-gather.16.cloned.1.call-done = bf16[1792,1024]{1,0:T(8,128)(2,1)} async-done(((bf16[224,1024]{1,0:T(8,128)(2,1)}), bf16[1792,1024]{1,0:T(8,128)(2,1)}) %all-gather.16.cloned.1.call-update) | async-done | bytes 3670032 | tf_op jit(solution)/shard_map/all_gather | solution.py:212
  279.8 6.1 %fusion.33 = f32[512,1024]{1,0:T(8,128)} fusion(bf16[1792,1024]{1,0:T(8,128)(2,1)} %all-gather.16.cloned.1.call-done, bf16[512,1792]{1,0:T(8,128)(2,1)} %all-gather.14.cloned.1.call-done, f32[1792]{0:T(1024)S(1)} %copy-done.12, f32[512]{0:T(512)S(1)} %add_rsqrt_fusion), kind=kOutput, calls=%fused_computation.59 | convolution fusion | flops 1882718208 | bytes 7611392 | tf_op jit(solution)/shard_map/dot_general | solution.py:210
  285.9 30.3 %all-gather.18.cloned.1.call-done = bf16[1792,1024]{1,0:T(8,128)(2,1)} async-done(((bf16[224,1024]{1,0:T(8,128)(2,1)}), bf16[1792,1024]{1,0:T(8,128)(2,1)}) %all-gather.18.cloned.1.call-update) | async-done | bytes 3670032 | tf_op jit(solution)/shard_map/all_gather | solution.py:213
  316.2 36.4 %all-gather.20.cloned.1.call-done = bf16[1024,1792]{0,1:T(8,128)(2,1)} async-done(((bf16[1024,224]{0,1:T(8,128)(2,1)}), bf16[1024,1792]{0,1:T(8,128)(2,1)}) %all-gather.20.cloned.1.call-update) | async-done | bytes 3670032 | tf_op jit(solution)/shard_map/all_gather | solution.py:217
  352.6 9.2 %convolution_convert_fusion = bf16[512,1792]{1,0:T(8,128)(2,1)} fusion(bf16[1024,1792]{0,1:T(8,128)(2,1)} %all-gather.20.cloned.1.call-done, f32[512,1024]{1,0:T(8,128)} %fusion.33, bf16[1792,1024]{1,0:T(8,128)(2,1)} %all-gather.18.cloned.1.call-done, bf16[512,1792]{1,0:T(8,128)(2,1)S(1)} %copy-done.4, f32[1792]{0:T(1024)S(1)} %copy-done.12, ...), kind=kOutput, calls=%fused_computation.22 | convolution fusion | flops 3765829632 | bytes 13116416 | tf_op jit(solution)/shard_map/dot_general | solution.py:215
  361.9 39.6 %reduce-scatter.5.cloned.1.call-done = bf16[128,1792]{1,0:T(8,128)(2,1)} async-done(((bf16[512,1792]{1,0:T(8,128)(2,1)}), bf16[128,1792]{1,0:T(8,128)(2,1)}) %reduce-scatter.5.cloned.1.call-update) | async-done | bytes 458768 | tf_op jit(solution)/shard_map/reduce_scatter | solution.py:220
  401.5 1.9 add_convert_fusion
  (80 shorter events, 10.7 us)
Async XLA Ops:
  6.5 78.3 %copy-start = (bf16[2,16,1792]{2,1,0:T(8,128)(2,1)S(1)}, bf16[2,16,1792]{2,1,0:T(8,128)(2,1)}, u32[]{:S(2)}) copy-start(bf16[2,16,1792]{2,1,0:T(8,128)(2,1)} %param.25) | copy-start | bytes 344068
  6.5 5.3 %copy-start.13 = (s32[1,8]{1,0:T(1,128)S(1)}, s32[1,8]{1,0:T(1,128)}, u32[]{:S(2)}) copy-start(s32[1,8]{1,0:T(1,128)} %param.22) | copy-start | bytes 100
  6.5 6.2 %copy-start.14 = (s32[8]{0:T(128)S(1)}, s32[8]{0:T(128)}, u32[]{:S(2)}) copy-start(s32[8]{0:T(128)} %param.21) | copy-start | bytes 100
  6.5 6.4 %copy-start.6 = (bf16[8,2,4,7168]{3,2,1,0:T(4,128)(2,1)S(1)}, bf16[8,2,4,7168]{3,2,1,0:T(4,128)(2,1)}, u32[]{:S(2)}) copy-start(bf16[8,2,4,7168]{3,2,1,0:T(4,128)(2,1)} %param.20) | copy-start | bytes 2752516
  6.5 46.5 %all-gather.8.cloned.1.call-start = ((), (), s32[]{:S(2)}) async-start(), calls=%async_computation.4 | async-start | bytes 2293760 | tf_op jit(solution)/shard_map/all_gather | solution.py:149
  7.3 116.0 %all-gather.10.cloned.1.call-start = ((), (), s32[]{:S(2)}) async-start(), calls=%async_computation.5 | async-start | bytes 8257536 | tf_op jit(solution)/shard_map/all_gather | solution.py:157
  10.0 4.7 %copy-start.11 = (s32[512,1]{0,1:T(1,128)S(1)}, s32[512,1]{0,1:T(1,128)}, u32[]{:S(2)}) copy-start(s32[512,1]{0,1:T(1,128)} %param.23) | copy-start | bytes 6148
  10.0 142.0 %all-gather.12.cloned.1.call-start = ((), (), s32[]{:S(2)}) async-start(), calls=%async_computation.6 | async-start | bytes 2064384 | tf_op jit(solution)/shard_map/all_gather | solution.py:197
  12.9 42.1 %copy-start.8 = (f32[1792]{0:T(1024)S(1)}, f32[1792]{0:T(1024)}, u32[]{:S(2)}) copy-start(f32[1792]{0:T(1024)} %param.16) | copy-start | bytes 21508
  55.0 8.3 %copy-start.7 = (f32[3,2,448]{2,1,0:T(2,128)S(1)}, f32[3,2,448]{2,1,0:T(2,128)}, u32[]{:S(2)}) copy-start(f32[3,2,448]{2,1,0:T(2,128)} %param.18) | copy-start | bytes 32260
  57.0 1.2 copy-start.3
  59.6 25.2 %all-to-all-start = ((bf16[8,2,16,1792]{3,2,1,0:T(8,128)(2,1)}), bf16[8,2,16,1792]{3,2,1,0:T(8,128)(2,1)S(1)}, u32[]{:S(2)}, u32[]{:S(2)}) async-start(bf16[8,2,16,1792]{3,2,1,0:T(8,128)(2,1)} %bitcast.30), calls=%async_computation | async-start | bytes 1835008 | tf_op jit(solution)/shard_map/all_to_all | solution.py:184
  87.4 69.0 %all-to-all-start.1 = ((bf16[8,2,16,1792]{3,2,1,0:T(8,128)(2,1)}), bf16[8,2,16,1792]{3,2,1,0:T(8,128)(2,1)S(1)}, u32[]{:S(2)}, u32[]{:S(2)}) async-start(bf16[8,2,16,1792]{3,2,1,0:T(8,128)(2,1)} %copy.61), calls=%async_computation.1 | async-start | bytes 1835008 | tf_op jit(solution)/shard_map/all_to_all | solution.py:191
  91.1 110.9 %reduce-scatter.3.cloned.1.call-start = ((), (), s32[]{:S(2)}) async-start(), calls=%async_computation.7 | async-start | bytes 2293760 | tf_op jit(solution)/shard_map/reduce_scatter | solution.py:202
  129.8 0.7 copy-start.9
  129.8 0.7 copy-start.10
  158.9 43.1 %copy-start.5 = (bf16[128,1792]{1,0:T(8,128)(2,1)S(1)}, bf16[128,1792]{1,0:T(8,128)(2,1)}, u32[]{:S(2)}) copy-start(bf16[128,1792]{1,0:T(8,128)(2,1)} %param.15) | copy-start | bytes 1376260
  162.4 117.4 %copy-start.12 = (f32[1792]{0:T(1024)S(1)}, f32[1792]{0:T(1024)}, u32[]{:S(2)}) copy-start(f32[1792]{0:T(1024)} %param.26) | copy-start | bytes 21508
  162.4 82.2 %all-gather.14.cloned.1.call-start = ((), (), s32[]{:S(2)}) async-start(), calls=%async_computation.8 | async-start | bytes 2293760 | tf_op jit(solution)/shard_map/all_gather | solution.py:206
  203.9 75.8 %all-gather.16.cloned.1.call-start = ((), (), s32[]{:S(2)}) async-start(), calls=%async_computation.9 | async-start | bytes 4128768 | tf_op jit(solution)/shard_map/all_gather | solution.py:212
  204.5 111.7 %all-gather.18.cloned.1.call-start = ((), (), s32[]{:S(2)}) async-start(), calls=%async_computation.10 | async-start | bytes 4128768 | tf_op jit(solution)/shard_map/all_gather | solution.py:213
  205.3 147.4 %all-gather.20.cloned.1.call-start = ((), (), s32[]{:S(2)}) async-start(), calls=%async_computation.11 | async-start | bytes 4128768 | tf_op jit(solution)/shard_map/all_gather | solution.py:217
  206.0 195.5 %reduce-scatter.5.cloned.1.call-start = ((), (), s32[]{:S(2)}) async-start(), calls=%async_computation.12 | async-start | bytes 2293760 | tf_op jit(solution)/shard_map/reduce_scatter | solution.py:220
  246.5 106.1 %copy-start.4 = (bf16[512,1792]{1,0:T(8,128)(2,1)S(1)}, bf16[512,1792]{1,0:T(8,128)(2,1)}, u32[]{:S(2)}) copy-start(bf16[512,1792]{1,0:T(8,128)(2,1)} %all-gather.14.cloned.1.call-done) | copy-start | bytes 5505028
  285.9 115.6 %copy-start.2 = (bf16[128,1792]{1,0:T(8,128)(2,1)S(1)}, bf16[128,1792]{1,0:T(8,128)(2,1)}, u32[]{:S(2)}) copy-start(bf16[128,1792]{1,0:T(8,128)(2,1)} %add_convert_fusion.1) | copy-start | bytes 1376260
  352.6 50.7 %copy-start.1 = (bf16[2,16,1792]{2,1,0:T(8,128)(2,1)S(1)}, bf16[2,16,1792]{2,1,0:T(8,128)(2,1)}, u32[]{:S(2)}) copy-start(bf16[2,16,1792]{2,1,0:T(8,128)(2,1)} %param.25) | copy-start | bytes 344068
Sparse Core Ops, SparseCore 0:
  8.9 44.0 all-gather.7
  55.0 68.2 all-gather.9
  125.1 26.7 all-gather.11
  162.6 39.4 reduce-scatter.2
  204.0 40.5 all-gather.13
  246.3 33.3 all-gather.15
  281.6 34.5 all-gather.17
  318.1 34.5 all-gather.19
  362.0 39.4 reduce-scatter.4
where the time goes:
time: 410 us
  waiting for transfers between devices  324 us (79%)
  matrix products  36.4 us (9%)
  other arithmetic  18.9 us (5%)
  between operations  13.5 us (3%)
  local copies, waits for them, and re-layouts  9.15 us (2%)
  starting transfers between devices  8.02 us (2%)
    reduce_scatter x1, waiting for transfers between devices, on_device(): lax.psum_scatter(down_term.astype(jnp.bfloat16), 'col', scatter_dimension...  39.6 us
    reduce_scatter x1, waiting for transfers between devices, on_device(): lax.psum_scatter(out_term.astype(jnp.bfloat16), 'col', scatter_dimension=...  39.5 us
    all_gather x1, waiting for transfers between devices, on_device(): whole_mixed = lax.all_gather(residual, 'col', axis=0, tiled=True)  38.3 us
    all_gather x1, waiting for transfers between devices, on_device(): gathered = lax.all_gather(inputs, 'col', axis=0, tiled=True)  37.9 us
    all_gather x1, waiting for transfers between devices, on_device(): lax.all_gather(down_projection, 'row', axis=1, tiled=True)  36.4 us
    all_gather x1, waiting for transfers between devices, on_device(): gate = add_rows(lax.all_gather(gate_projection, 'row', axis=0, tiled=True))  33.2 us
    all_gather x1, waiting for transfers between devices, on_device(): lax.all_gather(query_key_value_weight, 'row', axis=0, tiled=True)  31.9 us
    all_gather x1, waiting for transfers between devices, on_device(): up_part = add_rows(lax.all_gather(up_projection, 'row', axis=0, tiled=True))  30.3 us
  transfers between devices with their start and end apart: 11, of which 10 were waited for; matrix products, arithmetic and copies ran while one was open for 11% of the time, Pallas kernels for 0%

commit v1 on v0

--- a/solution.py
+++ b/solution.py
@@ -1,6 +1,10 @@
+import functools
+
 import jax
 import jax.numpy as jnp
 from jax import lax
+from jax.experimental import pallas as pl
+from jax.experimental.pallas import tpu as pltpu
 from jax.sharding import PartitionSpec as P
 
 HD = 112
@@ -126,7 +130,7 @@
     return joined_output.reshape(tok_count, head_count * head_size).astype(jnp.bfloat16)
 
 
-def on_device(
+def plain(
     inputs,
     attention_norm_gain,
     query_key_value_weight,
@@ -223,6 +227,378 @@
     return (residual.astype(jnp.float32) + mlp_added).astype(jnp.bfloat16)
 
 
+LANES = 128
+MIB = 1 << 20
+
+
+def params(mib):
+    return pltpu.CompilerParams(vmem_limit_bytes=mib * MIB)
+
+
+HBM = pl.BlockSpec(memory_space=pl.ANY)
+VMEM = pl.BlockSpec(memory_space=pltpu.VMEM)
+NT = (((1,), (1,)), ((), ()))
+
+
+def rms_kernel(x_ref, gain_ref, out_ref):
+    values = x_ref[...].astype(jnp.float32)
+    mean_square = jnp.mean(values * values, axis=-1, keepdims=True)
+    out_ref[...] = (values * lax.rsqrt(mean_square + epsilon) * gain_ref[...]).astype(out_ref.dtype)
+
+
+def normed_rows(rows, gain):
+    return pl.pallas_call(
+        rms_kernel,
+        out_shape=jax.ShapeDtypeStruct(rows.shape, jnp.bfloat16),
+        in_specs=[VMEM, VMEM],
+        out_specs=VMEM,
+        compiler_params=params(16),
+    )(rows, gain[None, :])
+
+
+def xor_pairs(count, mask):
+    return [(i, i ^ mask) for i in range(count)]
+
+
+def swap(value, axis, mask):
+    return lax.ppermute(value, axis, xor_pairs(lax.axis_size(axis), mask))
+
+
+def spread_weights(own):
+    half = own.shape[1] // 2
+    low, high = own[:, :half], own[:, half:]
+    x_low, y_high = swap(low, "row", 2), swap(high, "row", 4)
+    y_low, x_high = swap(low, "row", 4), swap(high, "row", 2)
+    xy_low, xy_high = swap(x_low, "row", 4), swap(y_high, "row", 2)
+    pieces = [
+        (own, 0, 0),
+        (x_low, 2, 0),
+        (y_high, 4, half),
+        (y_low, 4, 0),
+        (x_high, 2, half),
+        (xy_low, 6, 0),
+        (xy_high, 6, half),
+    ]
+    return pieces + [(swap(piece, "row", 1), mask ^ 1, first) for piece, mask, first in pieces]
+
+
+def qkv_kernel(places, x_refs, w_refs, taps_ref, inside_ref, q_ref, k_ref, v_ref, x_all, w_all, padded, sems):
+    row, col = lax.axis_index("row"), lax.axis_index("col")
+    count = x_refs[0].shape[0]
+    shard = x_all.shape[1] // lax.axis_size("row")
+    copies = []
+    for i, (ref, (mask, first)) in enumerate(zip(w_refs, places)):
+        start = pl.multiple_of((row ^ mask) * shard + first, 16)
+        copies.append(
+            pltpu.make_async_copy(
+                ref.at[pl.ds(0, 3)], w_all.at[:, pl.ds(start, ref.shape[1])], sems.at[i]
+            )
+        )
+    for i, ref in enumerate(x_refs):
+        start = pl.multiple_of((col ^ i) * count, 16)
+        copies.append(
+            pltpu.make_async_copy(ref, x_all.at[pl.ds(start, count)], sems.at[len(w_refs) + i])
+        )
+    for copy in copies:
+        copy.start()
+    padded[0:8, :] = jnp.zeros((8, padded.shape[1]), jnp.float32)
+    for copy in copies:
+        copy.wait()
+    tokens = x_all.shape[0]
+    inside = inside_ref[...]
+
+    def mixed(which):
+        return jnp.dot(x_all[...], w_all[which], preferred_element_type=jnp.float32)
+
+    def convolved(raw, which):
+        padded[8:, :] = raw
+        running = taps_ref[which : which + 1, :] * raw
+        for offset in range(1, taps_ref.shape[0] // 2):
+            moved = padded[8 - offset : 8 - offset + tokens, :]
+            tap = taps_ref[2 * offset + which : 2 * offset + which + 1, :]
+            running = running + jnp.where(inside >= offset, tap * moved, 0.0)
+        return running
+
+    q_ref[...] = mixed(0).astype(jnp.bfloat16)
+    k_ref[...] = convolved(mixed(1), 0).astype(jnp.bfloat16)
+    raw_values = mixed(2)
+    gates = jax.nn.sigmoid(convolved(raw_values, 1))
+    v_ref[...] = (raw_values * gates).astype(jnp.bfloat16)
+
+
+def qkv_call(blocks, pieces, taps, inside_col):
+    tokens, width = blocks[0].shape[0] * len(blocks), blocks[0].shape[1]
+    lanes = pieces[0][0].shape[2]
+    places = [(mask, first) for _, mask, first in pieces]
+    n_x, n_w = len(blocks), len(pieces)
+
+    def body(*refs):
+        x_refs, w_refs = refs[:n_x], refs[n_x : n_x + n_w]
+        qkv_kernel(places, x_refs, w_refs, *refs[n_x + n_w :])
+
+    one = jax.ShapeDtypeStruct((tokens, lanes), jnp.bfloat16)
+    return pl.pallas_call(
+        body,
+        out_shape=[one, one, one],
+        in_specs=[HBM] * (n_x + n_w) + [VMEM, VMEM],
+        out_specs=[VMEM] * 3,
+        scratch_shapes=[
+            pltpu.VMEM((tokens, width), jnp.bfloat16),
+            pltpu.VMEM((3, width, lanes), jnp.bfloat16),
+            pltpu.VMEM((tokens + 8, lanes), jnp.float32),
+            pltpu.SemaphoreType.DMA((n_x + n_w,)),
+        ],
+        compiler_params=params(40),
+        cost_estimate=pl.CostEstimate(
+            flops=2 * tokens * width * 3 * lanes, bytes_accessed=2 * width * 3 * lanes, transcendentals=0
+        ),
+    )(*blocks, *(piece for piece, _, _ in pieces), taps, inside_col)
+
+
+def attend_kernel(
+    places, masks, w_refs, q_ref, k_ref, v_ref, ck_ref, cv_ref, inside_ref, segment_ref, slot_ref, out_refs, w_all, sems
+):
+    row, col = lax.axis_index("row"), lax.axis_index("col")
+    shard = w_all.shape[0] // lax.axis_size("row")
+    copies = []
+    for i, (ref, (mask, first)) in enumerate(zip(w_refs, places)):
+        start = pl.multiple_of((row ^ mask) * shard + first, 16)
+        copies.append(
+            pltpu.make_async_copy(ref.at[3], w_all.at[pl.ds(start, ref.shape[1])], sems.at[i])
+        )
+    for copy in copies:
+        copy.start()
+    heads, slots, lanes = ck_ref.shape
+    window = slots // 8
+    scale = HD ** (-0.5)
+    attended = []
+    for mask, out_ref in zip(masks, out_refs):
+        count = out_ref.shape[0]
+        begin = pl.multiple_of((col ^ mask) * count, count)
+        key_begin = pl.multiple_of(jnp.maximum(begin - window, 0), window)
+        key_count = count + window
+        inside = inside_ref[pl.ds(begin, count), :]
+        segment = segment_ref[pl.ds(begin, count), :]
+        place = begin + lax.broadcasted_iota(jnp.int32, (count, 1), 0)
+        first_key = jnp.maximum(place - inside, place - window + 1)
+        keys = key_begin + lax.broadcasted_iota(jnp.int32, (count, key_count), 1)
+        local_mask = (keys >= first_key) & (keys <= place)
+        owner = lax.broadcasted_iota(jnp.int32, (count, slots), 1) // window
+        cache_mask = (owner == segment) & (slot_ref[...] > inside)
+        outs = []
+        for h in range(heads):
+            cols = slice(h * lanes, (h + 1) * lanes)
+            q = q_ref[pl.ds(begin, count), cols]
+            k = k_ref[pl.ds(key_begin, key_count), cols]
+            v = v_ref[pl.ds(key_begin, key_count), cols]
+            local = lax.dot_general(q, k, NT, preferred_element_type=jnp.float32)
+            cached = lax.dot_general(q, ck_ref[h], NT, preferred_element_type=jnp.float32)
+            local = jnp.where(local_mask, local * scale, -jnp.inf)
+            cached = jnp.where(cache_mask, cached * scale, -jnp.inf)
+            top = jnp.maximum(
+                jnp.max(local, axis=-1, keepdims=True), jnp.max(cached, axis=-1, keepdims=True)
+            )
+            local = jnp.exp(local - top)
+            cached = jnp.exp(cached - top)
+            total = jnp.sum(local, axis=-1, keepdims=True) + jnp.sum(cached, axis=-1, keepdims=True)
+            summed = jnp.dot(local.astype(jnp.bfloat16), v, preferred_element_type=jnp.float32)
+            summed = summed + jnp.dot(
+                cached.astype(jnp.bfloat16), cv_ref[h], preferred_element_type=jnp.float32
+            )
+            outs.append((summed / total).astype(jnp.bfloat16))
+        attended.append(jnp.concatenate(outs, axis=1))
+    for copy in copies:
+        copy.wait()
+    for block, out_ref in zip(attended, out_refs):
+        out_ref[...] = lax.dot_general(
+            block, w_all[...], NT, preferred_element_type=jnp.float32
+        ).astype(out_ref.dtype)
+
+
+def attend_call(masks, out_types, count, pieces, q, k, v, ck, cv, inside_col, segment_col, slot_row):
+    places = [(mask, first) for _, mask, first in pieces]
+    n_w, lanes = len(pieces), pieces[0][0].shape[2]
+    width = pieces[0][0].shape[1] * lax.axis_size("row")
+    n_out = len(masks)
+
+    def body(*refs):
+        w_refs = refs[:n_w]
+        out_refs = refs[n_w + 8 : n_w + 8 + n_out]
+        attend_kernel(places, masks, w_refs, *refs[n_w : n_w + 8], out_refs, *refs[n_w + 8 + n_out :])
+
+    return pl.pallas_call(
+        body,
+        out_shape=[jax.ShapeDtypeStruct((count, width), t) for t in out_types],
+        in_specs=[HBM] * n_w + [VMEM] * 8,
+        out_specs=[VMEM] * n_out,
+        scratch_shapes=[pltpu.VMEM((width, lanes), jnp.bfloat16), pltpu.SemaphoreType.DMA((n_w,))],
+        compiler_params=params(40),
+        cost_estimate=pl.CostEstimate(
+            flops=n_out * 2 * count * width * lanes * 2, bytes_accessed=2 * width * lanes, transcendentals=0
+        ),
+    )(*(piece for piece, _, _ in pieces), q, k, v, ck, cv, inside_col, segment_col, slot_row)
+
+
+def feed_kernel(n_x, hidden, x_refs, w_ref, out_refs, gate_w, up_w, down_w, sems):
+    copies = [
+        pltpu.make_async_copy(w_ref.at[:, pl.ds(i * hidden, hidden)], dst, sems.at[i])
+        for i, dst in enumerate((gate_w, up_w, down_w))
+    ]
+    for copy in copies:
+        copy.start()
+    x = jnp.concatenate([ref[...] for ref in x_refs], axis=0) if n_x > 1 else x_refs[0][...]
+    copies[0].wait()
+    gate = jnp.dot(x, gate_w[...], preferred_element_type=jnp.float32)
+    copies[1].wait()
+    up = jnp.dot(x, up_w[...], preferred_element_type=jnp.float32)
+    act = (jax.nn.silu(gate) * up).astype(jnp.bfloat16)
+    copies[2].wait()
+    down = lax.dot_general(act, down_w[...], NT, preferred_element_type=jnp.float32)
+    count = x_refs[0].shape[0]
+    for i, ref in enumerate(out_refs):
+        ref[...] = down[i * count : (i + 1) * count].astype(ref.dtype)
+
+
+def feed_call(blocks, weights, out_types):
+    n_x, (count, width) = len(blocks), blocks[0].shape
+    hidden = weights.shape[1] // 3
+
+    def body(*refs):
+        feed_kernel(n_x, hidden, refs[:n_x], refs[n_x], refs[n_x + 1 : 2 * n_x + 1], *refs[2 * n_x + 1 :])
+
+    return pl.pallas_call(
+        body,
+        out_shape=[jax.ShapeDtypeStruct((count, width), t) for t in out_types],
+        in_specs=[VMEM] * n_x + [HBM],
+        out_specs=[VMEM] * n_x,
+        scratch_shapes=[pltpu.VMEM((width, hidden), jnp.bfloat16)] * 3 + [pltpu.SemaphoreType.DMA((3,))],
+        compiler_params=params(48),
+        cost_estimate=pl.CostEstimate(
+            flops=6 * n_x * count * width * hidden, bytes_accessed=6 * width * hidden, transcendentals=0
+        ),
+    )(*blocks, weights)
+
+
+def pad_heads(value, heads):
+    lead = value.shape[:-1]
+    value = value.reshape(lead + (heads, HD))
+    value = jnp.pad(value, [(0, 0)] * (len(lead) + 1) + [(0, LANES - HD)])
+    return value.reshape(lead + (heads * LANES,))
+
+
+def spread_tokens(block):
+    two = swap(block, "col", 2)
+    one = swap(block, "col", 1)
+    three = swap(two, "col", 1)
+    return [block, one, two, three]
+
+
+def tuned(
+    inputs,
+    attention_norm_gain,
+    query_key_value_weight,
+    filter_taps,
+    output_projection,
+    window_key_value,
+    cache_valid_length,
+    lengths,
+    token_adapter_index,
+    adapter_down_map,
+    adapter_up_map,
+    feed_forward_gain,
+    gate_projection,
+    up_projection,
+    down_projection,
+):
+    bf16, f32 = jnp.bfloat16, jnp.float32
+    row, col = lax.axis_index("row"), lax.axis_index("col")
+    count, width = inputs.shape
+    tokens = count * lax.axis_size("col")
+    heads = window_key_value.shape[2]
+
+    normed = normed_rows(inputs, attention_norm_gain)
+    blocks = spread_tokens(normed)
+
+    packed = jnp.concatenate(
+        [
+            pad_heads(jnp.transpose(query_key_value_weight, (1, 0, 2)), heads),
+            pad_heads(jnp.transpose(output_projection), heads)[None],
+        ],
+        axis=0,
+    )
+    pieces = spread_weights(packed)
+
+    feed = jnp.concatenate([gate_projection, up_projection, jnp.transpose(down_projection)], axis=1)
+    feed = lax.all_gather(feed, "row", axis=0, tiled=True)
+
+    rank = adapter_down_map.shape[2]
+    kept = adapter_down_map.shape[0]
+    maps = jnp.concatenate(
+        [
+            jnp.transpose(adapter_down_map, (0, 2, 1)).reshape(1, kept * rank, width),
+            adapter_up_map.reshape(1, kept * rank, width),
+        ],
+        axis=1,
+    )
+    for mask in (2, 4, 1):
+        maps = jnp.concatenate([maps, swap(maps, "row", mask)], axis=0)
+    order = jnp.array([0, 2, 4, 6, 1, 3, 5, 7], jnp.int32)
+    holder = jnp.bitwise_xor(order, row)
+    slots = holder[:, None] * kept + jnp.arange(kept, dtype=jnp.int32)[None, :]
+    slots = jnp.repeat(slots.reshape(-1), rank)
+    own_ids = lax.dynamic_slice_in_dim(token_adapter_index, col * count, count, 0)
+    low = lax.dot_general(
+        normed, maps[:, : kept * rank].reshape(-1, width), NT, preferred_element_type=f32
+    )
+    low = jnp.where(own_ids == slots[None, :], low, 0.0).astype(bf16)
+    adapter_term = jnp.dot(low, maps[:, kept * rank :].reshape(-1, width), preferred_element_type=f32)
+    adapter_term = adapter_term.astype(bf16)
+
+    taps = pad_heads(filter_taps, heads).reshape(-1, heads * LANES)
+    segment, inside = layout(lengths[0], tokens)
+    inside_col, segment_col = inside[:, None], segment[:, None]
+    requests = window_key_value.shape[0]
+    window = window_key_value.shape[3] // HD
+    within = jnp.arange(window, dtype=jnp.int32)[None, :]
+    slot_row = jnp.where(within >= window - cache_valid_length[:, None], within, -1).reshape(1, -1)
+    cache = window_key_value.reshape(requests, 2, heads, window, HD)
+    cache = jnp.transpose(cache, (1, 2, 0, 3, 4)).reshape(2, heads, requests * window, HD)
+    cache = jnp.pad(cache, ((0, 0), (0, 0), (0, 0), (0, LANES - HD)))
+
+    q, k, v = qkv_call(blocks, pieces, taps, inside_col)
+    rest = (count, pieces, q, k, v, cache[0], cache[1], inside_col, segment_col, slot_row)
+    (part_three,) = attend_call([3], [bf16], *rest)
+    passed = swap(part_three, "col", 1)
+    part_two, part_one, part_own = attend_call([2, 1, 0], [bf16, bf16, f32], *rest)
+
+    def summed_up(passed, part_two, part_one):
+        part_two = (part_two.astype(f32) + passed.astype(f32)).astype(bf16)
+        part_two, part_one = lax.optimization_barrier((part_two, part_one))
+        return swap(part_two, "col", 2), swap(part_one, "col", 1)
+
+    got_two, got_one = summed_up(passed, part_two, part_one)
+    attn_sum = part_own + adapter_term.astype(f32) + got_one.astype(f32) + got_two.astype(f32)
+    residual = (inputs.astype(f32) + attn_sum).astype(bf16)
+
+    normed_mlp = normed_rows(residual, feed_forward_gain)
+    blocks = spread_tokens(normed_mlp)
+    part_two, part_one, part_own = feed_call(
+        [blocks[2], blocks[1], blocks[0]], feed, [bf16, bf16, f32]
+    )
+    (part_three,) = feed_call([blocks[3]], feed, [bf16])
+    passed = swap(part_three, "col", 1)
+    got_two, got_one = summed_up(passed, part_two, part_one)
+    added = part_own + got_one.astype(f32) + got_two.astype(f32)
+    return (residual.astype(f32) + added).astype(bf16)
+
+
+def on_device(*args):
+    rows, cols = lax.axis_size("row"), lax.axis_size("col")
+    if (rows, cols) == (8, 4):
+        return tuned(*args)
+    return plain(*args)
+
+
 def solution(mesh):
     placed = (
         P(("row", "col"), None),

time: 410 us -> 243 us (0.59)
  waiting for transfers between devices: 324 us -> 128 us
  matrix products: 36.4 us -> 2.39 us
  Pallas kernels: 0 us -> 32.3 us
  starting transfers between devices: 8.02 us -> 31.4 us
  local copies, waits for them, and re-layouts: 9.15 us -> 20 us
  other arithmetic: 18.9 us -> 12 us
    all_gather x7 -> x1, waiting for transfers between devices: 221 us -> 0.01 us  [tuned(): feed = lax.all_gather(feed, 'row', axis=0, tiled=True)]
    ppermute x0 -> x28, waiting for transfers between devices: none -> 128 us  [swap(): return lax.ppermute(value, axis, xor_pairs(lax.axis_size(axis), mask))]
    reduce_scatter x2 -> x0, waiting for transfers between devices: 79.1 us -> none  [the longest x1 39.6 us: on_device(): lax.psum_scatter(down_term.astype(jnp.bfloat16), 'col', scatter_dimension...]
    dot_general x11 -> x1, matrix products: 36.4 us -> 2.39 us  [tuned(): jnp.dot(low, maps[:, kept * rank:].reshape(-1, width), preferred_element_...]
    pallas_call x0 -> x7, Pallas kernels: none -> 32.3 us  [the longest x2 12.9 us: attend_call(): pl.pallas_call(body, out_shape=[jax.ShapeDtypeStruct((count, width), t) f...]
    ppermute x0 -> x28, starting transfers between devices: none -> 31.4 us  [swap(): return lax.ppermute(value, axis, xor_pairs(lax.axis_size(axis), mask))]
    all_to_all x2 -> x0, waiting for transfers between devices: 20.7 us -> none  [the longest x1 20.7 us: on_device(): lax.all_to_all(outgoing, 'row', split_axis=0, concat_axis=0, tiled=True)]
    all_to_all x2 -> x0, starting transfers between devices: 7.26 us -> none  [the longest x1 3.66 us: on_device(): lax.all_to_all(outgoing, 'row', split_axis=0, concat_axis=0, tiled=True)]
  transfers between devices with their start and end apart: 11 -> 29, of which waited for: 10 -> 10; matrix products, arithmetic and copies ran while one was open for 11% -> 9% of each run, Pallas kernels for 0% -> 13%
where the time goes in v1:
time: 243 us; the launch traced here: 240 us
  waiting for transfers between devices  128 us (53%)
  Pallas kernels  32.3 us (13%)
  starting transfers between devices  31.4 us (13%)
  local copies, waits for them, and re-layouts  20 us (8%)
  between operations  14 us (6%)
  other arithmetic  12 us (5%)
    ppermute x28, waiting for transfers between devices, swap(): return lax.ppermute(value, axis, xor_pairs(lax.axis_size(axis), mask))  128 us
    ppermute x28, starting transfers between devices, swap(): return lax.ppermute(value, axis, xor_pairs(lax.axis_size(axis), mask))  31.4 us
    pallas_call x2, Pallas kernels, attend_call(): pl.pallas_call(body, out_shape=[jax.ShapeDtypeStruct((count, width), t) f...  12.9 us
    pallas_call x2, Pallas kernels, feed_call(): pl.pallas_call(body, out_shape=[jax.ShapeDtypeStruct((count, width), t) f...  12.8 us
    unnamed x88, local copies, waits for them, and re-layouts  8.83 us
    pallas_call x1, Pallas kernels, qkv_call(): pl.pallas_call(body, out_shape=[one, one, one], in_specs=[HBM] * (n_x + n...  6.15 us
    reshape x2, local copies, waits for them, and re-layouts, tuned(): cache = window_key_value.reshape(requests, 2, heads, window, HD)  5.55 us
  transfers between devices with their start and end apart: 29, of which 10 were waited for; matrix products, arithmetic and copies ran while one was open for 9% of the time, Pallas kernels for 13%

profile of v1, /device:TPU:0, one launch (start us, length us, event | category | flops | bytes accessed | tf_op | source)
XLA Modules:
  0.0 239.8 jit_solution(17889543735079513000)
XLA Ops:
  6.6 2.6 %pad_maximum_fusion.1 = bf16[224,3072]{1,0:T(8,128)(2,1)} fusion(bf16[224,1024]{1,0:T(8,128)(2,1)} %bitcast.51, bf16[224,1024]{1,0:T(8,128)(2,1)} %param.29, bf16[224,1024]{1,0:T(8,128)(2,1)} %param.28), kind=kLoop, calls=%fused_computation.3 | loop fusion | flops 4128768 | bytes 2752512 | tf_op jit(solution)/shard_map/concatenate | solution.py:531
  9.2 3.0 %collective-permute-start.16 = (bf16[1,64,1792]{2,1,0:T(8,128)(2,1)S(1)}, bf16[1,64,1792]{2,1,0:T(8,128)(2,1)S(1)}, u32[]{:S(2)}, u32[]{:S(2)}) collective-permute-start(bf16[1,64,1792]{2,1,0:T(8,128)(2,1)S(1)} %pad_maximum_fusion.4), channel_id=1, source_target_pairs={{0,8},{4,12},{8,0},{12,4},{16,24},{20,28},{24,16},{28,20},{1,9},{5... | collective-permute-start | bytes 688136 | tf_op jit(solution)/shard_map/ppermute | solution.py:264
  14.9 2.0 collective-permute-start.1
  19.2 2.7 %collective-permute-start.14 = (bf16[128,1792]{1,0:T(8,128)(2,1)S(1)}, bf16[128,1792]{1,0:T(8,128)(2,1)}, u32[]{:S(2)}, u32[]{:S(2)}) collective-permute-start(bf16[128,1792]{1,0:T(8,128)(2,1)S(1)} %shard_map.154.refs_0_), channel_id=1, source_target_pairs={{0,2},{1,3},{2,0},{3,1},{4,6},{5,7},{6,4},{7,5},{8,10},{9,11},{10,... | collective-permute-start | bytes 1376264 | tf_op jit(solution)/shard_map/ppermute | solution.py:264
  22.6 12.7 %collective-permute-done.refs_5_.refs_1_ = bf16[4,112,512]{2,1,0:T(8,128)(2,1)S(1)} collective-permute-done((bf16[4,112,512]{2,1,0:T(8,128)(2,1)}, bf16[4,112,512]{2,1,0:T(8,128)(2,1)S(1)}, u32[]{:S(2)}, u32[]{:S(2)}) %collective-permute-start) | collective-permute-done | bytes 458784 | tf_op jit(solution)/shard_map/ppermute | solution.py:264
  38.8 13.5 %collective-permute-done.3.refs_8_.refs_4_ = bf16[4,112,512]{2,1,0:T(8,128)(2,1)} collective-permute-done((bf16[4,112,512]{2,1,0:T(8,128)(2,1)}, bf16[4,112,512]{2,1,0:T(8,128)(2,1)}, u32[]{:S(2)}, u32[]{:S(2)}) %collective-permute-start.3) | collective-permute-done | bytes 458784 | tf_op jit(solution)/shard_map/ppermute | solution.py:264
  52.4 1.8 collective-permute-start.4
  56.9 9.6 %collective-permute-done.17 = bf16[2,64,1792]{2,1,0:T(8,128)(2,1)S(1)} collective-permute-done((bf16[2,64,1792]{2,1,0:T(8,128)(2,1)}, bf16[2,64,1792]{2,1,0:T(8,128)(2,1)S(1)}, u32[]{:S(2)}, u32[]{:S(2)}) %collective-permute-start.17) | collective-permute-done | bytes 458784 | tf_op jit(solution)/shard_map/ppermute | solution.py:264
  67.3 17.0 %collective-permute-done.4.refs_9_.refs_5_ = bf16[4,112,512]{2,1,0:T(8,128)(2,1)} collective-permute-done((bf16[4,112,512]{2,1,0:T(8,128)(2,1)S(1)}, bf16[4,112,512]{2,1,0:T(8,128)(2,1)}, u32[]{:S(2)}, u32[]{:S(2)}) %collective-permute-start.4) | collective-permute-done | bytes 458784 | tf_op jit(solution)/shard_map/ppermute | solution.py:264
  85.5 3.3 %reshape.101 = bf16[8,2,4,64,112]{4,3,2,1,0:T(8,128)(2,1)} reshape(bf16[8,2,4,7168]{3,2,1,0:T(4,128)(2,1)} %param.21) | data formatting | bytes 1835008 | tf_op jit(solution)/shard_map/reshape | solution.py:564
  88.8 2.3 copy.26
  91.8 1.6 collective-permute-start.15
  93.9 2.2 pad_maximum_fusion.2
  96.4 8.1 %collective-permute-done.15.refs_3_ = bf16[128,1792]{1,0:T(8,128)(2,1)S(1)} collective-permute-done((bf16[128,1792]{1,0:T(8,128)(2,1)}, bf16[128,1792]{1,0:T(8,128)(2,1)S(1)}, u32[]{:S(2)}, u32[]{:S(2)}) %collective-permute-start.15) | collective-permute-done | bytes 458784 | tf_op jit(solution)/shard_map/ppermute | solution.py:264
  104.5 6.2 %shard_map.155 = (bf16[512,512]{1,0:T(8,128)(2,1)S(1)}, bf16[512,512]{1,0:T(8,128)(2,1)S(1)}, bf16[512,512]{1,0:T(8,128)(2,1)S(1)}) custom-call(bf16[128,1792]{1,0:T(8,128)(2,1)S(1)} %copy-done.10, bf16[128,1792]{1,0:T(8,128)(2,1)S(1)} %copy-done.24, bf16[128,1792]{1,0:T(8,128)(2,1)} %collective-permute-done.14.refs_2_, ...), custom_call_target="tpu_custom_call" | custom-call | flops 2818572288 | bytes 5505024 | tf_op jit(solution)/shard_map/pallas_call | solution.py:340
  110.7 4.7 %shard_map.157 = bf16[128,1792]{1,0:T(8,128)(2,1)} custom-call(bf16[4,224,512]{2,1,0:T(8,128)(2,1)S(1)} %constant_dynamic-update-slice_fusion.refs_4_.refs_0_, bf16[4,112,512]{2,1,0:T(8,128)(2,1)S(1)} %copy-done.13, bf16[4,112,512]{2,1,0:T(8,128)(2,1)} %collective-permute-done.1.refs_6_.refs_2_, bf16[4,112,512]{2,1,0:T(8,128)(2,1)} %collective-permute-done.2.refs_7_.refs_3_, ...), custom_call_target="tpu_custom_call" | custom-call | flops 469762048 | bytes 1835008 | tf_op jit(solution)/shard_map/pallas_call | solution.py:429
  115.5 1.6 collective-permute-start.19
  124.5 8.3 %shard_map.156 = (bf16[128,1792]{1,0:T(8,128)(2,1)S(1)}, bf16[128,1792]{1,0:T(8,128)(2,1)}, f32[128,1792]{1,0:T(8,128)S(1)}) custom-call(bf16[4,224,512]{2,1,0:T(8,128)(2,1)S(1)} %constant_dynamic-update-slice_fusion.refs_4_.refs_0_, bf16[4,112,512]{2,1,0:T(8,128)(2,1)S(1)} %copy-done.14, bf16[4,112,512]{2,1,0:T(8,128)(2,1)} %collective-permute-done.1.refs_6_.refs_2_, ...), custom_call_target="tpu_custom_call" | custom-call | flops 1409286144 | bytes 1835008 | tf_op jit(solution)/shard_map/pallas_call | solution.py:429
  132.9 1.6 pad_maximum_fusion
  134.5 1.9 add_convert_fusion.3
  136.9 2.6 %collective-permute-start.21 = (bf16[128,1792]{1,0:T(8,128)(2,1)}, bf16[128,1792]{1,0:T(8,128)(2,1)}, u32[]{:S(2)}, u32[]{:S(2)}) collective-permute-start(bf16[128,1792]{1,0:T(8,128)(2,1)} %add_convert_fusion.3), channel_id=1, source_target_pairs={{0,2},{1,3},{2,0},{3,1},{4,6},{5,7},{6,4},{7,5},{8,10},{9,11},{10,... | collective-permute-start | bytes 1376264 | tf_op jit(solution)/shard_map/ppermute | solution.py:264
  140.9 2.4 fusion
  143.3 14.5 %collective-permute-done.20 = bf16[128,1792]{1,0:T(8,128)(2,1)S(1)} collective-permute-done((bf16[128,1792]{1,0:T(8,128)(2,1)}, bf16[128,1792]{1,0:T(8,128)(2,1)S(1)}, u32[]{:S(2)}, u32[]{:S(2)}) %collective-permute-start.20) | collective-permute-done | bytes 458784 | tf_op jit(solution)/shard_map/ppermute | solution.py:264
  159.3 1.7 collective-permute-start.22
  161.0 20.4 %collective-permute-done.22.refs_0_ = bf16[128,1792]{1,0:T(8,128)(2,1)S(1)} collective-permute-done((bf16[128,1792]{1,0:T(8,128)(2,1)S(1)}, bf16[128,1792]{1,0:T(8,128)(2,1)S(1)}, u32[]{:S(2)}, u32[]{:S(2)}) %collective-permute-start.22) | collective-permute-done | bytes 458784 | tf_op jit(solution)/shard_map/ppermute | solution.py:264
  181.3 2.0 collective-permute-start.23
  183.4 11.4 %collective-permute-done.24.refs_0_ = bf16[128,1792]{1,0:T(8,128)(2,1)S(1)} collective-permute-done((bf16[128,1792]{1,0:T(8,128)(2,1)S(1)}, bf16[128,1792]{1,0:T(8,128)(2,1)S(1)}, u32[]{:S(2)}, u32[]{:S(2)}) %collective-permute-start.24) | collective-permute-done | bytes 458784 | tf_op jit(solution)/shard_map/ppermute | solution.py:264
  194.8 5.6 %shard_map.160 = bf16[128,1792]{1,0:T(8,128)(2,1)S(1)} custom-call(bf16[128,1792]{1,0:T(8,128)(2,1)S(1)} %collective-permute-done.24.refs_0_, bf16[1792,3072]{1,0:T(8,128)(2,1)} %all-gather.2.cloned.1.call-done.refs_3_.refs_1_), custom_call_target="tpu_custom_call" | custom-call | flops 1409286144 | bytes 11010048 | tf_op jit(solution)/shard_map/pallas_call | solution.py:469
  200.5 4.2 %collective-permute-done.23.refs_1_ = bf16[128,1792]{1,0:T(8,128)(2,1)S(1)} collective-permute-done((bf16[128,1792]{1,0:T(8,128)(2,1)S(1)}, bf16[128,1792]{1,0:T(8,128)(2,1)S(1)}, u32[]{:S(2)}, u32[]{:S(2)}) %collective-permute-start.23) | collective-permute-done | bytes 458784 | tf_op jit(solution)/shard_map/ppermute | solution.py:264
  204.6 7.3 %shard_map.159 = (bf16[128,1792]{1,0:T(8,128)(2,1)S(1)}, bf16[128,1792]{1,0:T(8,128)(2,1)S(1)}, f32[128,1792]{1,0:T(8,128)S(1)}) custom-call(bf16[128,1792]{1,0:T(8,128)(2,1)S(1)} %collective-permute-done.22.refs_0_, bf16[128,1792]{1,0:T(8,128)(2,1)S(1)} %collective-permute-done.23.refs_1_, bf16[128,1792]{1,0:T(8,128)(2,1)S(1)} %shard_map.158.refs_2_, ...), custom_call_target="tpu_custom_call" | custom-call | flops 4227858432 | bytes 11010048 | tf_op jit(solution)/shard_map/pallas_call | solution.py:469
  212.4 3.4 %collective-permute-start.27 = (bf16[128,1792]{1,0:T(8,128)(2,1)S(1)}, bf16[128,1792]{1,0:T(8,128)(2,1)S(1)}, u32[]{:S(2)}, u32[]{:S(2)}) collective-permute-start(bf16[128,1792]{1,0:T(8,128)(2,1)S(1)} %add_convert_fusion.1), channel_id=1, source_target_pairs={{0,2},{1,3},{2,0},{3,1},{4,6},{5,7},{6,4},{7,5},{8,10},{9,11},{10,... | collective-permute-start | bytes 1376264 | tf_op jit(solution)/shard_map/ppermute | solution.py:264
  215.8 16.2 %collective-permute-done.26 = bf16[128,1792]{1,0:T(8,128)(2,1)S(1)} collective-permute-done((bf16[128,1792]{1,0:T(8,128)(2,1)S(1)}, bf16[128,1792]{1,0:T(8,128)(2,1)S(1)}, u32[]{:S(2)}, u32[]{:S(2)}) %collective-permute-start.26) | collective-permute-done | bytes 458784 | tf_op jit(solution)/shard_map/ppermute | solution.py:264
  (167 shorter events, 27.7 us)
Async XLA Ops:
  6.5 110.5 %copy-start = (s32[512,1]{0,1:T(1,128)S(1)}, s32[512,1]{0,1:T(1,128)}, u32[]{:S(2)}) copy-start(s32[512,1]{0,1:T(1,128)} %param.24) | copy-start | bytes 6148
  6.5 188.3 %all-gather.2.cloned.1.call-start = ((), (), s32[]{:S(2)}) async-start(), calls=%async_computation | async-start | bytes 12386304 | tf_op jit(solution)/shard_map/all_gather | solution.py:532
  9.2 9.9 %collective-permute-start.16 = (bf16[1,64,1792]{2,1,0:T(8,128)(2,1)S(1)}, bf16[1,64,1792]{2,1,0:T(8,128)(2,1)S(1)}, u32[]{:S(2)}, u32[]{:S(2)}) collective-permute-start(bf16[1,64,1792]{2,1,0:T(8,128)(2,1)S(1)} %pad_maximum_fusion.4), channel_id=1, source_target_pairs={{0,8},{4,12},{8,0},{12,4},{16,24},{20,28},{24,16},{28,20},{1,9},{5... | collective-permute-start | bytes 688136 | tf_op jit(solution)/shard_map/ppermute | solution.py:264
  14.9 20.5 %collective-permute-start = (bf16[4,112,512]{2,1,0:T(8,128)(2,1)}, bf16[4,112,512]{2,1,0:T(8,128)(2,1)S(1)}, u32[]{:S(2)}, u32[]{:S(2)}) collective-permute-start(bf16[4,112,512]{2,1,0:T(8,128)(2,1)} %get-tuple-element.36), channel_id=1, source_target_pairs={{0,8},{4,12},{8,0},{12,4},{16,24},{20,28},{24,16},{28,20},{1,9},{5... | collective-permute-start | bytes 1376264 | tf_op jit(solution)/shard_map/ppermute | solution.py:264
  14.9 21.9 %collective-permute-start.1 = (bf16[4,112,512]{2,1,0:T(8,128)(2,1)}, bf16[4,112,512]{2,1,0:T(8,128)(2,1)}, u32[]{:S(2)}, u32[]{:S(2)}) collective-permute-start(bf16[4,112,512]{2,1,0:T(8,128)(2,1)} %get-tuple-element.35), channel_id=1, source_target_pairs={{0,16},{4,20},{8,24},{12,28},{16,0},{20,4},{24,8},{28,12},{1,17},{... | collective-permute-start | bytes 1376264 | tf_op jit(solution)/shard_map/ppermute | solution.py:264
  16.9 35.4 %collective-permute-start.3 = (bf16[4,112,512]{2,1,0:T(8,128)(2,1)}, bf16[4,112,512]{2,1,0:T(8,128)(2,1)}, u32[]{:S(2)}, u32[]{:S(2)}) collective-permute-start(bf16[4,112,512]{2,1,0:T(8,128)(2,1)} %get-tuple-element.35), channel_id=1, source_target_pairs={{0,8},{4,12},{8,0},{12,4},{16,24},{20,28},{24,16},{28,20},{1,9},{5... | collective-permute-start | bytes 1376264 | tf_op jit(solution)/shard_map/ppermute | solution.py:264
  18.4 35.7 %collective-permute-start.2 = (bf16[4,112,512]{2,1,0:T(8,128)(2,1)}, bf16[4,112,512]{2,1,0:T(8,128)(2,1)}, u32[]{:S(2)}, u32[]{:S(2)}) collective-permute-start(bf16[4,112,512]{2,1,0:T(8,128)(2,1)} %get-tuple-element.36), channel_id=1, source_target_pairs={{0,16},{4,20},{8,24},{12,28},{16,0},{20,4},{24,8},{28,12},{1,17},{... | collective-permute-start | bytes 1376264 | tf_op jit(solution)/shard_map/ppermute | solution.py:264
  19.2 71.9 %copy-start.9 = (bf16[128,1792]{1,0:T(8,128)(2,1)}, bf16[128,1792]{1,0:T(8,128)(2,1)S(1)}, u32[]{:S(2)}) copy-start(bf16[128,1792]{1,0:T(8,128)(2,1)S(1)} %shard_map.154.refs_0_) | copy-start | bytes 1376260
  19.2 74.7 %copy-start.26 = (bf16[1,64,1792]{2,1,0:T(8,128)(2,1)}, bf16[1,64,1792]{2,1,0:T(8,128)(2,1)S(1)}, u32[]{:S(2)}) copy-start(bf16[1,64,1792]{2,1,0:T(8,128)(2,1)S(1)} %collective-permute-done.16) | copy-start | bytes 688132
  19.2 36.4 %collective-permute-start.14 = (bf16[128,1792]{1,0:T(8,128)(2,1)S(1)}, bf16[128,1792]{1,0:T(8,128)(2,1)}, u32[]{:S(2)}, u32[]{:S(2)}) collective-permute-start(bf16[128,1792]{1,0:T(8,128)(2,1)S(1)} %shard_map.154.refs_0_), channel_id=1, source_target_pairs={{0,2},{1,3},{2,0},{3,1},{4,6},{5,7},{6,4},{7,5},{8,10},{9,11},{10,... | collective-permute-start | bytes 1376264 | tf_op jit(solution)/shard_map/ppermute | solution.py:264
  35.4 20.3 %collective-permute-start.13 = (bf16[128,1792]{1,0:T(8,128)(2,1)S(1)}, bf16[128,1792]{1,0:T(8,128)(2,1)S(1)}, u32[]{:S(2)}, u32[]{:S(2)}) collective-permute-start(bf16[128,1792]{1,0:T(8,128)(2,1)S(1)} %shard_map.154.refs_0_), channel_id=1, source_target_pairs={{0,1},{1,0},{2,3},{3,2},{4,5},{5,4},{6,7},{7,6},{8,9},{9,8},{10,11... | collective-permute-start | bytes 1376264 | tf_op jit(solution)/shard_map/ppermute | solution.py:264
  36.8 29.7 %collective-permute-start.17 = (bf16[2,64,1792]{2,1,0:T(8,128)(2,1)}, bf16[2,64,1792]{2,1,0:T(8,128)(2,1)S(1)}, u32[]{:S(2)}, u32[]{:S(2)}) collective-permute-start(bf16[2,64,1792]{2,1,0:T(8,128)(2,1)} %pad_maximum_fusion.3), channel_id=1, source_target_pairs={{0,16},{4,20},{8,24},{12,28},{16,0},{20,4},{24,8},{28,12},{1,17},{... | collective-permute-start | bytes 1376264 | tf_op jit(solution)/shard_map/ppermute | solution.py:264
  52.4 31.9 %collective-permute-start.4 = (bf16[4,112,512]{2,1,0:T(8,128)(2,1)S(1)}, bf16[4,112,512]{2,1,0:T(8,128)(2,1)}, u32[]{:S(2)}, u32[]{:S(2)}) collective-permute-start(bf16[4,112,512]{2,1,0:T(8,128)(2,1)S(1)} %collective-permute-done.refs_5_.refs_1_), channel_id=1, source_target_pairs={{0,16},{4,20},{8,24},{12,28},{16,0},{20,4},{24,8},{28,12},{1,17},{... | collective-permute-start | bytes 1376264 | tf_op jit(solution)/shard_map/ppermute | solution.py:264
  54.1 37.0 %collective-permute-start.5 = (bf16[4,112,512]{2,1,0:T(8,128)(2,1)}, bf16[4,112,512]{2,1,0:T(8,128)(2,1)}, u32[]{:S(2)}, u32[]{:S(2)}) collective-permute-start(bf16[4,112,512]{2,1,0:T(8,128)(2,1)} %collective-permute-done.1.refs_6_.refs_2_), channel_id=1, source_target_pairs={{0,8},{4,12},{8,0},{12,4},{16,24},{20,28},{24,16},{28,20},{1,9},{5... | collective-permute-start | bytes 1376264 | tf_op jit(solution)/shard_map/ppermute | solution.py:264
  55.6 36.1 %collective-permute-start.7 = (bf16[4,112,512]{2,1,0:T(8,128)(2,1)S(1)}, bf16[4,112,512]{2,1,0:T(8,128)(2,1)}, u32[]{:S(2)}, u32[]{:S(2)}) collective-permute-start(bf16[4,112,512]{2,1,0:T(8,128)(2,1)S(1)} %collective-permute-done.refs_5_.refs_1_), channel_id=1, source_target_pairs={{0,4},{4,0},{8,12},{12,8},{16,20},{20,16},{24,28},{28,24},{1,5},{5... | collective-permute-start | bytes 1376264 | tf_op jit(solution)/shard_map/ppermute | solution.py:264
  56.4 36.9 %collective-permute-start.8 = (bf16[4,112,512]{2,1,0:T(8,128)(2,1)}, bf16[4,112,512]{2,1,0:T(8,128)(2,1)}, u32[]{:S(2)}, u32[]{:S(2)}) collective-permute-start(bf16[4,112,512]{2,1,0:T(8,128)(2,1)} %collective-permute-done.1.refs_6_.refs_2_), channel_id=1, source_target_pairs={{0,4},{4,0},{8,12},{12,8},{16,20},{20,16},{24,28},{28,24},{1,5},{5... | collective-permute-start | bytes 1376264 | tf_op jit(solution)/shard_map/ppermute | solution.py:264
  66.5 26.9 %collective-permute-start.10 = (bf16[4,112,512]{2,1,0:T(8,128)(2,1)}, bf16[4,112,512]{2,1,0:T(8,128)(2,1)}, u32[]{:S(2)}, u32[]{:S(2)}) collective-permute-start(bf16[4,112,512]{2,1,0:T(8,128)(2,1)} %collective-permute-done.3.refs_8_.refs_4_), channel_id=1, source_target_pairs={{0,4},{4,0},{8,12},{12,8},{16,20},{20,16},{24,28},{28,24},{1,5},{5... | collective-permute-start | bytes 1376264 | tf_op jit(solution)/shard_map/ppermute | solution.py:264
  84.3 12.1 %collective-permute-start.6 = (bf16[4,224,512]{2,1,0:T(8,128)(2,1)S(1)}, bf16[4,224,512]{2,1,0:T(8,128)(2,1)S(1)}, u32[]{:S(2)}, u32[]{:S(2)}) collective-permute-start(bf16[4,224,512]{2,1,0:T(8,128)(2,1)S(1)} %constant_dynamic-update-slice_fusion.refs_4_.refs_0_), channel_id=1, source_target_pairs={{0,4},{4,0},{8,12},{12,8},{16,20},{20,16},{24,28},{28,24},{1,5},{5... | collective-permute-start | bytes 2752520 | tf_op jit(solution)/shard_map/ppermute | solution.py:264
  91.1 5.0 %collective-permute-start.9 = (bf16[4,112,512]{2,1,0:T(8,128)(2,1)}, bf16[4,112,512]{2,1,0:T(8,128)(2,1)S(1)}, u32[]{:S(2)}, u32[]{:S(2)}) collective-permute-start(bf16[4,112,512]{2,1,0:T(8,128)(2,1)} %collective-permute-done.2.refs_7_.refs_3_), channel_id=1, source_target_pairs={{0,4},{4,0},{8,12},{12,8},{16,20},{20,16},{24,28},{28,24},{1,5},{5... | collective-permute-start | bytes 1376264 | tf_op jit(solution)/shard_map/ppermute | solution.py:264
  91.8 12.7 %collective-permute-start.15 = (bf16[128,1792]{1,0:T(8,128)(2,1)}, bf16[128,1792]{1,0:T(8,128)(2,1)S(1)}, u32[]{:S(2)}, u32[]{:S(2)}) collective-permute-start(bf16[128,1792]{1,0:T(8,128)(2,1)} %collective-permute-done.14.refs_2_), channel_id=1, source_target_pairs={{0,1},{1,0},{2,3},{3,2},{4,5},{5,4},{6,7},{7,6},{8,9},{9,8},{10,11... | collective-permute-start | bytes 1376264 | tf_op jit(solution)/shard_map/ppermute | solution.py:264
  93.4 11.1 %collective-permute-start.11 = (bf16[4,112,512]{2,1,0:T(8,128)(2,1)}, bf16[4,112,512]{2,1,0:T(8,128)(2,1)S(1)}, u32[]{:S(2)}, u32[]{:S(2)}) collective-permute-start(bf16[4,112,512]{2,1,0:T(8,128)(2,1)} %collective-permute-done.4.refs_9_.refs_5_), channel_id=1, source_target_pairs={{0,4},{4,0},{8,12},{12,8},{16,20},{20,16},{24,28},{28,24},{1,5},{5... | collective-permute-start | bytes 1376264 | tf_op jit(solution)/shard_map/ppermute | solution.py:264
  93.4 11.1 %collective-permute-start.12 = (bf16[4,112,512]{2,1,0:T(8,128)(2,1)}, bf16[4,112,512]{2,1,0:T(8,128)(2,1)S(1)}, u32[]{:S(2)}, u32[]{:S(2)}) collective-permute-start(bf16[4,112,512]{2,1,0:T(8,128)(2,1)} %collective-permute-done.5.refs_10_.refs_6_), channel_id=1, source_target_pairs={{0,4},{4,0},{8,12},{12,8},{16,20},{20,16},{24,28},{28,24},{1,5},{5... | collective-permute-start | bytes 1376264 | tf_op jit(solution)/shard_map/ppermute | solution.py:264
  96.0 36.8 %collective-permute-start.18 = (bf16[4,64,1792]{2,1,0:T(8,128)(2,1)}, bf16[4,64,1792]{2,1,0:T(8,128)(2,1)}, u32[]{:S(2)}, u32[]{:S(2)}) collective-permute-start(bf16[4,64,1792]{2,1,0:T(8,128)(2,1)} %pad_maximum_fusion.2), channel_id=1, source_target_pairs={{0,4},{4,0},{8,12},{12,8},{16,20},{20,16},{24,28},{28,24},{1,5},{5... | collective-permute-start | bytes 2752520 | tf_op jit(solution)/shard_map/ppermute | solution.py:264
  115.5 19.0 %collective-permute-start.19 = (bf16[128,1792]{1,0:T(8,128)(2,1)}, bf16[128,1792]{1,0:T(8,128)(2,1)}, u32[]{:S(2)}, u32[]{:S(2)}) collective-permute-start(bf16[128,1792]{1,0:T(8,128)(2,1)} %shard_map.157), channel_id=1, source_target_pairs={{0,1},{1,0},{2,3},{3,2},{4,5},{5,4},{6,7},{7,6},{8,9},{9,8},{10,11... | collective-permute-start | bytes 1376264 | tf_op jit(solution)/shard_map/ppermute | solution.py:264
  136.4 21.4 %collective-permute-start.20 = (bf16[128,1792]{1,0:T(8,128)(2,1)}, bf16[128,1792]{1,0:T(8,128)(2,1)S(1)}, u32[]{:S(2)}, u32[]{:S(2)}) collective-permute-start(bf16[128,1792]{1,0:T(8,128)(2,1)} %get-tuple-element.24), channel_id=1, source_target_pairs={{0,1},{1,0},{2,3},{3,2},{4,5},{5,4},{6,7},{7,6},{8,9},{9,8},{10,11... | collective-permute-start | bytes 1376264 | tf_op jit(solution)/shard_map/ppermute | solution.py:264
  136.9 20.9 %collective-permute-start.21 = (bf16[128,1792]{1,0:T(8,128)(2,1)}, bf16[128,1792]{1,0:T(8,128)(2,1)}, u32[]{:S(2)}, u32[]{:S(2)}) collective-permute-start(bf16[128,1792]{1,0:T(8,128)(2,1)} %add_convert_fusion.3), channel_id=1, source_target_pairs={{0,2},{1,3},{2,0},{3,1},{4,6},{5,7},{6,4},{7,5},{8,10},{9,11},{10,... | collective-permute-start | bytes 1376264 | tf_op jit(solution)/shard_map/ppermute | solution.py:264
  159.3 22.0 %collective-permute-start.22 = (bf16[128,1792]{1,0:T(8,128)(2,1)S(1)}, bf16[128,1792]{1,0:T(8,128)(2,1)S(1)}, u32[]{:S(2)}, u32[]{:S(2)}) collective-permute-start(bf16[128,1792]{1,0:T(8,128)(2,1)S(1)} %shard_map.158.refs_2_), channel_id=1, source_target_pairs={{0,2},{1,3},{2,0},{3,1},{4,6},{5,7},{6,4},{7,5},{8,10},{9,11},{10,... | collective-permute-start | bytes 1376264 | tf_op jit(solution)/shard_map/ppermute | solution.py:264
  181.3 13.5 %collective-permute-start.24 = (bf16[128,1792]{1,0:T(8,128)(2,1)S(1)}, bf16[128,1792]{1,0:T(8,128)(2,1)S(1)}, u32[]{:S(2)}, u32[]{:S(2)}) collective-permute-start(bf16[128,1792]{1,0:T(8,128)(2,1)S(1)} %collective-permute-done.22.refs_0_), channel_id=1, source_target_pairs={{0,1},{1,0},{2,3},{3,2},{4,5},{5,4},{6,7},{7,6},{8,9},{9,8},{10,11... | collective-permute-start | bytes 1376264 | tf_op jit(solution)/shard_map/ppermute | solution.py:264
  181.3 23.3 %collective-permute-start.23 = (bf16[128,1792]{1,0:T(8,128)(2,1)S(1)}, bf16[128,1792]{1,0:T(8,128)(2,1)S(1)}, u32[]{:S(2)}, u32[]{:S(2)}) collective-permute-start(bf16[128,1792]{1,0:T(8,128)(2,1)S(1)} %shard_map.158.refs_2_), channel_id=1, source_target_pairs={{0,1},{1,0},{2,3},{3,2},{4,5},{5,4},{6,7},{7,6},{8,9},{9,8},{10,11... | collective-permute-start | bytes 1376264 | tf_op jit(solution)/shard_map/ppermute | solution.py:264
  200.4 11.6 %collective-permute-start.25 = (bf16[128,1792]{1,0:T(8,128)(2,1)S(1)}, bf16[128,1792]{1,0:T(8,128)(2,1)S(1)}, u32[]{:S(2)}, u32[]{:S(2)}) collective-permute-start(bf16[128,1792]{1,0:T(8,128)(2,1)S(1)} %shard_map.160), channel_id=1, source_target_pairs={{0,1},{1,0},{2,3},{3,2},{4,5},{5,4},{6,7},{7,6},{8,9},{9,8},{10,11... | collective-permute-start | bytes 1376264 | tf_op jit(solution)/shard_map/ppermute | solution.py:264
  212.1 19.9 %collective-permute-start.26 = (bf16[128,1792]{1,0:T(8,128)(2,1)S(1)}, bf16[128,1792]{1,0:T(8,128)(2,1)S(1)}, u32[]{:S(2)}, u32[]{:S(2)}) collective-permute-start(bf16[128,1792]{1,0:T(8,128)(2,1)S(1)} %get-tuple-element.29), channel_id=1, source_target_pairs={{0,1},{1,0},{2,3},{3,2},{4,5},{5,4},{6,7},{7,6},{8,9},{9,8},{10,11... | collective-permute-start | bytes 1376264 | tf_op jit(solution)/shard_map/ppermute | solution.py:264
  212.4 19.6 %collective-permute-start.27 = (bf16[128,1792]{1,0:T(8,128)(2,1)S(1)}, bf16[128,1792]{1,0:T(8,128)(2,1)S(1)}, u32[]{:S(2)}, u32[]{:S(2)}) collective-permute-start(bf16[128,1792]{1,0:T(8,128)(2,1)S(1)} %add_convert_fusion.1), channel_id=1, source_target_pairs={{0,2},{1,3},{2,0},{3,1},{4,6},{5,7},{6,4},{7,5},{8,10},{9,11},{10,... | collective-permute-start | bytes 1376264 | tf_op jit(solution)/shard_map/ppermute | solution.py:264
  (40 other events, 429.4 us)
Sparse Core Ops, SparseCore 0:
  9.3 93.6 all-gather.1

commit v2 on v0

--- a/solution.py
+++ b/solution.py
@@ -1,6 +1,10 @@
+import functools
+
 import jax
 import jax.numpy as jnp
 from jax import lax
+from jax.experimental import pallas as pl
+from jax.experimental.pallas import tpu as pltpu
 from jax.sharding import PartitionSpec as P
 
 HD = 112
@@ -126,7 +130,7 @@
     return joined_output.reshape(tok_count, head_count * head_size).astype(jnp.bfloat16)
 
 
-def on_device(
+def plain(
     inputs,
     attention_norm_gain,
     query_key_value_weight,
@@ -223,6 +227,471 @@
     return (residual.astype(jnp.float32) + mlp_added).astype(jnp.bfloat16)
 
 
+LANES = 128
+MIB = 1 << 20
+
+
+def params(mib):
+    return pltpu.CompilerParams(vmem_limit_bytes=mib * MIB)
+
+
+HBM = pl.BlockSpec(memory_space=pl.ANY)
+VMEM = pl.BlockSpec(memory_space=pltpu.VMEM)
+SMEM = pl.BlockSpec(memory_space=pltpu.SMEM)
+NT = (((1,), (1,)), ((), ()))
+
+
+def normed(values, gain_ref):
+    mean_square = jnp.mean(values * values, axis=-1, keepdims=True)
+    return (values * lax.rsqrt(mean_square + epsilon) * gain_ref[...]).astype(jnp.bfloat16)
+
+
+def pack_maps(down_ref, up_ref, packed_ref):
+    ranks, width = down_ref.shape
+    lanes = packed_ref.shape[1]
+    for c in range(width // lanes):
+        cols = slice(c * lanes, (c + 1) * lanes)
+        packed_ref[2 * c * ranks : (2 * c + 1) * ranks, :] = down_ref[:, cols]
+        packed_ref[(2 * c + 1) * ranks : (2 * c + 2) * ranks, :] = up_ref[:, cols]
+    whole = width // lanes * lanes
+    packed_ref[2 * whole // lanes * ranks :, : lanes // 2] = down_ref[:, whole:]
+    packed_ref[2 * whole // lanes * ranks :, lanes // 2 :] = up_ref[:, whole:]
+
+
+def unpack_maps(places, w_refs, down_ref, up_ref):
+    row = lax.axis_index("row")
+    ranks, width = down_ref.shape[0] // lax.axis_size("row"), down_ref.shape[1]
+    lanes, step = w_refs[0].shape[2], 16
+    whole = width // lanes
+    for ref, (mask, first) in zip(w_refs, places):
+        start = (row ^ mask) * ranks
+        for at in range(0, ref.shape[1], step):
+            chunk, inner = divmod(first + at, 2 * ranks)
+            rows = pl.ds(pl.multiple_of(start + inner % ranks, step), step)
+            cols = slice(chunk * lanes, min((chunk + 1) * lanes, width))
+            if chunk < whole:
+                target = down_ref if inner < ranks else up_ref
+                target[rows, cols] = ref[0, at : at + step, :]
+            else:
+                down_ref[rows, cols] = ref[0, at : at + step, : lanes // 2]
+                up_ref[rows, cols] = ref[0, at : at + step, lanes // 2 :]
+
+
+def entry_kernel(
+    x_hbm, gain_ref, qkv_hbm, out_hbm, taps_ref, down_ref, up_ref, normed_ref, packed_ref, padded_taps_ref, x_ref, qkv_ref, out_ref, sems
+):
+    loads = [
+        pltpu.make_async_copy(source, target, sems.at[i])
+        for i, (source, target) in enumerate(
+            ((x_hbm, x_ref), (qkv_hbm, qkv_ref), (out_hbm, out_ref))
+        )
+    ]
+    for load in loads:
+        load.start()
+    heads = qkv_ref.shape[2] // HD
+    blank = jnp.zeros((packed_ref.shape[1], LANES - HD), jnp.bfloat16)
+    pack_maps(down_ref, up_ref, packed_ref.at[4])
+    for h in range(heads):
+        middle = h * LANES + HD
+        padded_taps_ref[:, :, h * LANES : middle] = taps_ref[:, :, h * HD : (h + 1) * HD]
+        padded_taps_ref[:, :, middle : (h + 1) * LANES] = jnp.zeros(
+            taps_ref.shape[:2] + (LANES - HD,), jnp.float32
+        )
+        for i in range(4):
+            packed_ref[i, :, middle : (h + 1) * LANES] = blank
+    loads[0].wait()
+    normed_ref[...] = normed(x_ref[...].astype(jnp.float32), gain_ref)
+    loads[1].wait()
+    for h in range(heads):
+        for i in range(3):
+            packed_ref[i, :, h * LANES : h * LANES + HD] = qkv_ref[i, :, h * HD : (h + 1) * HD]
+    loads[2].wait()
+    out_rows = jnp.transpose(out_ref[...].astype(jnp.float32)).astype(jnp.bfloat16)
+    for h in range(heads):
+        packed_ref[3, :, h * LANES : h * LANES + HD] = out_rows[:, h * HD : (h + 1) * HD]
+
+
+def entry_call(rows, gain, qkv, out, taps, down, up):
+    lanes = qkv.shape[2] // HD * LANES
+    return pl.pallas_call(
+        entry_kernel,
+        out_shape=[
+            jax.ShapeDtypeStruct(rows.shape, jnp.bfloat16),
+            jax.ShapeDtypeStruct((5, qkv.shape[1], lanes), jnp.bfloat16),
+            jax.ShapeDtypeStruct(taps.shape[:2] + (lanes,), jnp.float32),
+        ],
+        in_specs=[HBM, VMEM, HBM, HBM, VMEM, VMEM, VMEM],
+        out_specs=[VMEM] * 3,
+        scratch_shapes=[
+            pltpu.VMEM(rows.shape, rows.dtype),
+            pltpu.VMEM(qkv.shape, qkv.dtype),
+            pltpu.VMEM(out.shape, out.dtype),
+            pltpu.SemaphoreType.DMA((3,)),
+        ],
+        compiler_params=params(40),
+    )(rows, gain[None, :], qkv, out, taps, down, up)
+
+
+def residual_kernel(x_ref, own_ref, one_ref, two_ref, gain_ref, residual_ref, normed_ref):
+    total = own_ref[...] + one_ref[...].astype(jnp.float32) + two_ref[...].astype(jnp.float32)
+    residual = (x_ref[...].astype(jnp.float32) + total).astype(jnp.bfloat16)
+    residual_ref[...] = residual
+    normed_ref[...] = normed(residual.astype(jnp.float32), gain_ref)
+
+
+def residual_call(rows, own, one, two, gain):
+    block = jax.ShapeDtypeStruct(rows.shape, jnp.bfloat16)
+    return pl.pallas_call(
+        residual_kernel,
+        out_shape=[block, block],
+        in_specs=[VMEM] * 5,
+        out_specs=[VMEM] * 2,
+        compiler_params=params(12),
+    )(rows, own, one, two, gain[None, :])
+
+
+def adapter_term(x_ref, ids_ref, down_ref, up_ref, rank):
+    low = lax.dot_general(x_ref[...], down_ref[...], NT, preferred_element_type=jnp.float32)
+    adapter = lax.broadcasted_iota(jnp.int32, low.shape, 1) // rank
+    low = jnp.where(ids_ref[...] == adapter, low, 0.0).astype(jnp.bfloat16)
+    return jnp.dot(low, up_ref[...], preferred_element_type=jnp.float32).astype(jnp.bfloat16)
+
+
+def xor_pairs(count, mask):
+    return [(i, i ^ mask) for i in range(count)]
+
+
+def swap(value, axis, mask):
+    return lax.ppermute(value, axis, xor_pairs(lax.axis_size(axis), mask))
+
+
+def first_hops(own):
+    return swap(own, "row", 2), swap(own, "row", 4)
+
+
+def second_hops(own, from_x, from_y):
+    half = own.shape[1] // 2
+    diagonal = swap(from_x[:, :half], "row", 4), swap(from_y[:, half:], "row", 2)
+    return diagonal + tuple(swap(piece, "row", 1) for piece in (own, from_x, from_y))
+
+
+def named_pieces(own, firsts, seconds, thirds):
+    half = own.shape[1] // 2
+    masks = [(0, 0), (2, 0), (4, 0), (6, 0), (6, half), (1, 0), (3, 0), (5, 0), (7, 0), (7, half)]
+    return [(piece, *at) for piece, at in zip((own,) + firsts + seconds + thirds, masks)]
+
+
+def assemble(places, w_refs, all_w):
+    row = lax.axis_index("row")
+    shard = all_w.shape[1] // lax.axis_size("row")
+    for ref, (mask, first) in zip(w_refs, places):
+        start = pl.multiple_of((row ^ mask) * shard + first, 16)
+        for part in range(ref.shape[0]):
+            all_w[part, pl.ds(start, ref.shape[1]), :] = ref[part]
+
+
+def request_columns(lengths_ref, begin, count):
+    place = begin + lax.broadcasted_iota(jnp.int32, (count, 1), 0)
+    segment, first = jnp.zeros_like(place), jnp.zeros_like(place)
+    finish = jnp.int32(0)
+    for s in range(lengths_ref.shape[1]):
+        finish = finish + lengths_ref[0, s]
+        later = place >= finish
+        segment = segment + later.astype(jnp.int32)
+        first = jnp.where(later, finish, first)
+    return place, segment, first
+
+
+def attend_block(mask, count, lengths_ref, valid_ref, q_ref, k_ref, v_ref, cache_ref):
+    col = lax.axis_index("col")
+    _, heads, slots, lanes = cache_ref.shape
+    requests = valid_ref.shape[0]
+    window = slots // requests
+    scale = HD ** (-0.5)
+    begin = pl.multiple_of((col ^ mask) * count, count)
+    key_begin = pl.multiple_of(jnp.maximum(begin - window, 0), window)
+    key_count = count + window
+    place, segment, first = request_columns(lengths_ref, begin, count)
+    first_key = jnp.maximum(first, place - window + 1)
+    keys = key_begin + lax.broadcasted_iota(jnp.int32, (count, key_count), 1)
+    local_mask = (keys >= first_key) & (keys <= place)
+    slot = lax.broadcasted_iota(jnp.int32, (1, slots), 1)
+    owner, within = slot // window, slot % window
+    oldest = jnp.full_like(slot, window)
+    for s in range(requests):
+        oldest = jnp.where(owner == s, window - valid_ref[s], oldest)
+    within = jnp.where(within >= oldest, within, -1)
+    cache_mask = (owner == segment) & (within > place - first)
+    outs = []
+    for h in range(heads):
+        cols = slice(h * lanes, (h + 1) * lanes)
+        q = q_ref[pl.ds(begin, count), cols]
+        k = k_ref[pl.ds(key_begin, key_count), cols]
+        v = v_ref[pl.ds(key_begin, key_count), cols]
+        local = lax.dot_general(q, k, NT, preferred_element_type=jnp.float32)
+        cached = lax.dot_general(q, cache_ref[0, h], NT, preferred_element_type=jnp.float32)
+        local = jnp.where(local_mask, local * scale, -jnp.inf)
+        cached = jnp.where(cache_mask, cached * scale, -jnp.inf)
+        top = jnp.maximum(
+            jnp.max(local, axis=-1, keepdims=True), jnp.max(cached, axis=-1, keepdims=True)
+        )
+        local = jnp.exp(local - top)
+        cached = jnp.exp(cached - top)
+        total = jnp.sum(local, axis=-1, keepdims=True) + jnp.sum(cached, axis=-1, keepdims=True)
+        summed = jnp.dot(local.astype(jnp.bfloat16), v, preferred_element_type=jnp.float32)
+        summed = summed + jnp.dot(
+            cached.astype(jnp.bfloat16), cache_ref[1, h], preferred_element_type=jnp.float32
+        )
+        outs.append((summed / total).astype(jnp.bfloat16))
+    return jnp.concatenate(outs, axis=1)
+
+
+def first_kernel(places, n_x, n_w, *refs):
+    x_refs, w_refs = refs[:n_x], refs[n_x : n_x + n_w]
+    taps_ref, lengths_ref, valid_ref, cache_ref = refs[n_x + n_w : n_x + n_w + 4]
+    q_ref, k_ref, v_ref, out_w, down_ref, up_ref, part_ref = refs[n_x + n_w + 4 : n_x + n_w + 11]
+    x_all, w_all, padded = refs[n_x + n_w + 11 :]
+    col = lax.axis_index("col")
+    count, tokens = x_refs[0].shape[0], x_all.shape[0]
+    for i, ref in enumerate(x_refs):
+        x_all[pl.ds(pl.multiple_of((col ^ i) * count, 16), count), :] = ref[...]
+    assemble(places, [ref.at[pl.ds(0, 3)] for ref in w_refs], w_all)
+    assemble(places, [ref.at[pl.ds(3, 1)] for ref in w_refs], out_w)
+    unpack_maps(places, [ref.at[pl.ds(4, 1)] for ref in w_refs], down_ref, up_ref)
+    padded[0:8, :] = jnp.zeros((8, padded.shape[1]), jnp.float32)
+    place, _, first = request_columns(lengths_ref, 0, tokens)
+    inside = place - first
+
+    def mixed(which):
+        return jnp.dot(x_all[...], w_all[which], preferred_element_type=jnp.float32)
+
+    def convolved(raw, which):
+        padded[8:, :] = raw
+        running = taps_ref[0, which : which + 1, :] * raw
+        for offset in range(1, taps_ref.shape[0]):
+            moved = padded[8 - offset : 8 - offset + tokens, :]
+            tap = taps_ref[offset, which : which + 1, :]
+            running = running + jnp.where(inside >= offset, tap * moved, 0.0)
+        return running
+
+    q_ref[...] = mixed(0).astype(jnp.bfloat16)
+    k_ref[...] = convolved(mixed(1), 0).astype(jnp.bfloat16)
+    raw_values = mixed(2)
+    v_ref[...] = (raw_values * jax.nn.sigmoid(convolved(raw_values, 1))).astype(jnp.bfloat16)
+    attended = attend_block(n_x - 1, count, lengths_ref, valid_ref, q_ref, k_ref, v_ref, cache_ref)
+    part_ref[...] = lax.dot_general(
+        attended, out_w[0], NT, preferred_element_type=jnp.float32
+    ).astype(jnp.bfloat16)
+
+
+def first_call(blocks, pieces, ranks, taps, lengths, valid, cache):
+    (count, width), n_x, n_w = blocks[0].shape, len(blocks), len(pieces)
+    tokens, lanes = count * n_x, pieces[0][0].shape[2]
+    places = [(mask, first) for _, mask, first in pieces]
+    one = jax.ShapeDtypeStruct((tokens, lanes), jnp.bfloat16)
+    return pl.pallas_call(
+        functools.partial(first_kernel, places, n_x, n_w),
+        out_shape=[
+            one,
+            one,
+            one,
+            jax.ShapeDtypeStruct((1, width, lanes), jnp.bfloat16),
+            jax.ShapeDtypeStruct((ranks, width), jnp.bfloat16),
+            jax.ShapeDtypeStruct((ranks, width), jnp.bfloat16),
+            jax.ShapeDtypeStruct((count, width), jnp.bfloat16),
+        ],
+        in_specs=[VMEM] * (n_x + n_w + 1) + [SMEM, SMEM, VMEM],
+        out_specs=[VMEM] * 7,
+        scratch_shapes=[
+            pltpu.VMEM((tokens, width), jnp.bfloat16),
+            pltpu.VMEM((3, width, lanes), jnp.bfloat16),
+            pltpu.VMEM((tokens + 8, lanes), jnp.float32),
+        ],
+        compiler_params=params(36),
+        cost_estimate=pl.CostEstimate(
+            flops=2 * tokens * width * 4 * lanes, bytes_accessed=2 * width * 4 * lanes, transcendentals=0
+        ),
+    )(*blocks, *(piece for piece, _, _ in pieces), taps, lengths, valid, cache)
+
+
+def attend_kernel(rank, masks, q_ref, k_ref, v_ref, out_w, x_ref, ids_ref, down_ref, up_ref, *refs):
+    lengths_ref, valid_ref, cache_ref = refs[:3]
+    for mask, out_ref in zip(masks, refs[3:]):
+        attended = attend_block(
+            mask, out_ref.shape[0], lengths_ref, valid_ref, q_ref, k_ref, v_ref, cache_ref
+        )
+        part = lax.dot_general(attended, out_w[0], NT, preferred_element_type=jnp.float32)
+        if mask == 0:
+            part = part + adapter_term(x_ref, ids_ref, down_ref, up_ref, rank).astype(jnp.float32)
+        out_ref[...] = part.astype(out_ref.dtype)
+
+
+def attend_call(rank, masks, out_types, q, k, v, out_w, x, ids, down, up, lengths, valid, cache):
+    _, width, lanes = out_w.shape
+    count = x.shape[0]
+    return pl.pallas_call(
+        functools.partial(attend_kernel, rank, masks),
+        out_shape=[jax.ShapeDtypeStruct((count, width), t) for t in out_types],
+        in_specs=[VMEM] * 8 + [SMEM, SMEM, VMEM],
+        out_specs=[VMEM] * len(masks),
+        compiler_params=params(20),
+        cost_estimate=pl.CostEstimate(
+            flops=len(masks) * 16 * count * width * lanes, bytes_accessed=2 * width * lanes, transcendentals=0
+        ),
+    )(q, k, v, out_w, x, ids, down, up, lengths, valid, cache)
+
+
+def feed(x, all_w):
+    gate = jnp.dot(x, all_w[0], preferred_element_type=jnp.float32)
+    up = jnp.dot(x, all_w[1], preferred_element_type=jnp.float32)
+    act = (jax.nn.silu(gate) * up).astype(jnp.bfloat16)
+    return lax.dot_general(act, all_w[2], NT, preferred_element_type=jnp.float32)
+
+
+def feed_first_kernel(places, n_x, n_w, *refs):
+    x_refs, w_refs = refs[:n_x], refs[n_x : n_x + n_w]
+    all_w, out_refs = refs[n_x + n_w], refs[n_x + n_w + 1 :]
+    assemble(places, w_refs, all_w)
+    down = feed(jnp.concatenate([ref[...] for ref in x_refs], axis=0), all_w)
+    count = x_refs[0].shape[0]
+    for i, ref in enumerate(out_refs):
+        ref[...] = down[i * count : (i + 1) * count].astype(ref.dtype)
+
+
+def feed_first_call(blocks, pieces, out_types):
+    n_x, n_w, (count, width) = len(blocks), len(pieces), blocks[0].shape
+    places = [(mask, first) for _, mask, first in pieces]
+    hidden = pieces[0][0].shape[2]
+    return pl.pallas_call(
+        functools.partial(feed_first_kernel, places, n_x, n_w),
+        out_shape=[pltpu.VMEM((3, width, hidden), jnp.bfloat16)]
+        + [jax.ShapeDtypeStruct((count, width), t) for t in out_types],
+        in_specs=[VMEM] * (n_x + n_w),
+        out_specs=[VMEM] * (n_x + 1),
+        compiler_params=params(40),
+        cost_estimate=pl.CostEstimate(
+            flops=6 * n_x * count * width * hidden, bytes_accessed=12 * width * hidden, transcendentals=0
+        ),
+    )(*blocks, *(piece for piece, _, _ in pieces))
+
+
+def feed_last_kernel(x_ref, all_w, out_ref):
+    out_ref[...] = feed(x_ref[...], all_w).astype(out_ref.dtype)
+
+
+def feed_last_call(block, all_w):
+    count, (_, width, hidden) = block.shape[0], all_w.shape
+    return pl.pallas_call(
+        feed_last_kernel,
+        out_shape=jax.ShapeDtypeStruct((count, width), jnp.bfloat16),
+        in_specs=[VMEM] * 2,
+        out_specs=VMEM,
+        compiler_params=params(20),
+        cost_estimate=pl.CostEstimate(
+            flops=6 * count * width * hidden, bytes_accessed=6 * width * hidden, transcendentals=0
+        ),
+    )(block, all_w)
+
+
+def tuned(
+    inputs,
+    attention_norm_gain,
+    query_key_value_weight,
+    filter_taps,
+    output_projection,
+    window_key_value,
+    cache_valid_length,
+    lengths,
+    token_adapter_index,
+    adapter_down_map,
+    adapter_up_map,
+    feed_forward_gain,
+    gate_projection,
+    up_projection,
+    down_projection,
+):
+    bf16, f32 = jnp.bfloat16, jnp.float32
+    col = lax.axis_index("col")
+    count, width = inputs.shape
+    heads = window_key_value.shape[2]
+
+    rank, kept = adapter_down_map.shape[2], adapter_down_map.shape[0]
+    ranks = kept * lax.axis_size("row") * rank
+    normed_attention, packed, taps = entry_call(
+        inputs,
+        attention_norm_gain,
+        jnp.transpose(query_key_value_weight, (1, 0, 2)),
+        output_projection,
+        filter_taps,
+        jnp.transpose(adapter_down_map, (0, 2, 1)).reshape(kept * rank, width),
+        adapter_up_map.reshape(kept * rank, width),
+    )
+    token_two, token_one = swap(normed_attention, "col", 2), swap(normed_attention, "col", 1)
+    firsts = first_hops(packed)
+    requests = window_key_value.shape[0]
+    window = window_key_value.shape[3] // HD
+    cache = window_key_value.reshape(requests, 2, heads, window, HD)
+    cache = jnp.transpose(cache, (1, 2, 0, 3, 4)).reshape(2, heads, requests * window, HD)
+    cache = jnp.pad(cache, ((0, 0), (0, 0), (0, 0), (0, LANES - HD)))
+    own_ids = lax.dynamic_slice_in_dim(token_adapter_index, col * count, count, 0)
+    feed_own = jnp.concatenate(
+        [gate_projection[None], up_projection[None], jnp.transpose(down_projection)[None]], axis=0
+    )
+    token_two, token_one, firsts, packed, cache, own_ids, feed_own = lax.optimization_barrier(
+        (token_two, token_one, firsts, packed, cache, own_ids, feed_own)
+    )
+    token_three = swap(token_two, "col", 1)
+    seconds = second_hops(packed, *firsts)
+    token_three, diagonal, feed_own = lax.optimization_barrier((token_three, seconds[:2], feed_own))
+    thirds = tuple(swap(piece, "row", 1) for piece in diagonal)
+    feed_firsts = first_hops(feed_own)
+
+    pieces = named_pieces(packed, firsts, diagonal + seconds[2:], thirds)
+    blocks = [normed_attention, token_one, token_two, token_three]
+    requests_here = (lengths, cache_valid_length, cache)
+    q, k, v, out_w, down_maps, up_maps, part_three = first_call(
+        blocks, pieces, ranks, taps, *requests_here
+    )
+    passed = swap(part_three, "col", 1)
+    part_two, part_one, part_own = attend_call(
+        rank, [2, 1, 0], [bf16, bf16, f32], q, k, v, out_w, normed_attention, own_ids, down_maps, up_maps, *requests_here
+    )
+
+    def summed_up(passed, part_two, part_one):
+        part_two = (part_two.astype(f32) + passed.astype(f32)).astype(bf16)
+        part_two, part_one = lax.optimization_barrier((part_two, part_one))
+        return swap(part_two, "col", 2), swap(part_one, "col", 1)
+
+    passed, part_two, part_one = lax.optimization_barrier((passed, part_two, part_one))
+    got_two, got_one = summed_up(passed, part_two, part_one)
+    got_one, feed_own, feed_firsts = lax.optimization_barrier((got_one, feed_own, feed_firsts))
+    feed_seconds = second_hops(feed_own, *feed_firsts)
+    residual, normed_mlp = residual_call(inputs, part_own, got_one, got_two, feed_forward_gain)
+    token_two, token_one = swap(normed_mlp, "col", 2), swap(normed_mlp, "col", 1)
+    feed_diagonal = feed_seconds[:2]
+    feed_thirds = tuple(swap(piece, "row", 1) for piece in feed_diagonal)
+    token_two, token_one, feed_thirds, feed_seconds = lax.optimization_barrier(
+        (token_two, token_one, feed_thirds, feed_seconds[2:])
+    )
+    token_three = swap(token_two, "col", 1)
+    feed_pieces = named_pieces(feed_own, feed_firsts, feed_diagonal + feed_seconds, feed_thirds)
+    feed_w, part_two, part_one, part_own = feed_first_call(
+        [token_two, token_one, normed_mlp], feed_pieces, [bf16, bf16, f32]
+    )
+    part_three = feed_last_call(token_three, feed_w)
+    passed = swap(part_three, "col", 1)
+    got_two, got_one = summed_up(passed, part_two, part_one)
+    added = part_own + got_one.astype(f32) + got_two.astype(f32)
+    return (residual.astype(f32) + added).astype(bf16)
+
+
+def on_device(*args):
+    rows, cols = lax.axis_size("row"), lax.axis_size("col")
+    if (rows, cols) == (8, 4):
+        return tuned(*args)
+    return plain(*args)
+
+
 def solution(mesh):
     placed = (
         P(("row", "col"), None),

time: 410 us -> 185 us (0.45)
  waiting for transfers between devices: 324 us -> 103 us
  matrix products: 36.4 us -> 0 us
  Pallas kernels: 0 us -> 30.8 us
  starting transfers between devices: 8.02 us -> 35.1 us
  other arithmetic: 18.9 us -> 1.36 us
  between operations: 13.5 us -> 0.26 us
  local copies, waits for them, and re-layouts: 9.15 us -> 14.6 us
    all_gather x7 -> x0, waiting for transfers between devices: 221 us -> none  [the longest x1 38.3 us: on_device(): whole_mixed = lax.all_gather(residual, 'col', axis=0, tiled=True)]
    ppermute x0 -> x30, waiting for transfers between devices: none -> 103 us  [swap(): return lax.ppermute(value, axis, xor_pairs(lax.axis_size(axis), mask))]
    reduce_scatter x2 -> x0, waiting for transfers between devices: 79.1 us -> none  [the longest x1 39.6 us: on_device(): lax.psum_scatter(down_term.astype(jnp.bfloat16), 'col', scatter_dimension...]
    dot_general x11 -> x0, matrix products: 36.4 us -> none  [the longest x1 9.24 us: on_device(): jnp.dot(hidden, lax.all_gather(down_projection, 'row', axis=1, tiled=True...]
    ppermute x0 -> x30, starting transfers between devices: none -> 35.1 us  [swap(): return lax.ppermute(value, axis, xor_pairs(lax.axis_size(axis), mask))]
    pallas_call x0 -> x6, Pallas kernels: none -> 30.8 us  [the longest x1 10.2 us: feed_first_call(): pl.pallas_call(functools.partial(feed_first_kernel, places, n_x, n_w), ou...]
    all_to_all x2 -> x0, waiting for transfers between devices: 20.7 us -> none  [the longest x1 20.7 us: on_device(): lax.all_to_all(outgoing, 'row', split_axis=0, concat_axis=0, tiled=True)]
    convert_element_type x6 -> x3, other arithmetic: 11.1 us -> 1.21 us  [the longest x1 1 us: tuned(): return (residual.astype(f32) + added).astype(bf16)]
  transfers between devices with their start and end apart: 11 -> 30, of which waited for: 10 -> 23; matrix products, arithmetic and copies ran while one was open for 11% -> 3% of each run, Pallas kernels for 0% -> 14%
where the time goes in v2:
time: 185 us
  waiting for transfers between devices  103 us (56%)
  starting transfers between devices  35.1 us (19%)
  Pallas kernels  30.8 us (17%)
  local copies, waits for them, and re-layouts  14.6 us (8%)
    ppermute x30, waiting for transfers between devices, swap(): return lax.ppermute(value, axis, xor_pairs(lax.axis_size(axis), mask))  103 us
    ppermute x30, starting transfers between devices, swap(): return lax.ppermute(value, axis, xor_pairs(lax.axis_size(axis), mask))  35.1 us
    pallas_call x1, Pallas kernels, feed_first_call(): pl.pallas_call(functools.partial(feed_first_kernel, places, n_x, n_w), ou...  10.2 us
    unnamed x48, local copies, waits for them, and re-layouts  8.8 us
    pallas_call x1, Pallas kernels, attend_call(): pl.pallas_call(functools.partial(attend_kernel, rank, masks), out_shape=[...  7.73 us
    pallas_call x1, Pallas kernels, first_call(): pl.pallas_call(functools.partial(first_kernel, places, n_x, n_w), out_sha...  7.65 us
    reshape x2, local copies, waits for them, and re-layouts, tuned(): cache = window_key_value.reshape(requests, 2, heads, window, HD)  4.54 us
  transfers between devices with their start and end apart: 30, of which 23 were waited for; matrix products, arithmetic and copies ran while one was open for 3% of the time, Pallas kernels for 14%

profile of v2, /device:TPU:0, one launch (start us, length us, event | category | flops | bytes accessed | tf_op | source)
XLA Modules:
  0.0 184.9 jit_solution(17577980405580535359)
XLA Ops:
  6.3 2.5 %shard_map.145 = (bf16[128,1792]{1,0:T(8,128)(2,1)}, bf16[5,224,512]{2,1,0:T(8,128)(2,1)S(1)}, f32[3,2,512]{2,1,0:T(2,128)S(1)}) custom-call(bf16[128,1792]{1,0:T(8,128)(2,1)S(1)} %copy-done.1, f32[1,1792]{1,0:T(1,128)S(1)} %broadcast_in_dim.15.gain_ref, bf16[3,224,448]{2,1,0:T(8,128)(2,1)S(1)} %bitcast.13, bf16[448,224]{1,0:T(8,128)(2,1)S(1)} %copy-done.4, ...), custom_call_target="tpu_custom_call" | custom-call | tf_op jit(solution)/shard_map/pallas_call | solution.py:316
  8.8 3.0 %collective-permute-start.2 = (bf16[5,224,512]{2,1,0:T(8,128)(2,1)S(1)}, bf16[5,224,512]{2,1,0:T(8,128)(2,1)S(1)}, u32[]{:S(2)}, u32[]{:S(2)}) collective-permute-start(bf16[5,224,512]{2,1,0:T(8,128)(2,1)S(1)} %get-tuple-element.62.refs_4_), channel_id=1, source_target_pairs={{0,8},{4,12},{8,0},{12,4},{16,24},{20,28},{24,16},{28,20},{1,9},{5... | collective-permute-start | bytes 3440648 | tf_op jit(solution)/shard_map/ppermute | solution.py:365
  11.8 1.5 collective-permute-start.3
  13.4 2.6 %collective-permute-start = (bf16[128,1792]{1,0:T(8,128)(2,1)}, bf16[128,1792]{1,0:T(8,128)(2,1)}, u32[]{:S(2)}, u32[]{:S(2)}) collective-permute-start(bf16[128,1792]{1,0:T(8,128)(2,1)} %get-tuple-element.54.refs_0_.x_ref), channel_id=1, source_target_pairs={{0,2},{1,3},{2,0},{3,1},{4,6},{5,7},{6,4},{7,5},{8,10},{9,11},{10,... | collective-permute-start | bytes 1376264 | tf_op jit(solution)/shard_map/ppermute | solution.py:365
  16.0 1.6 collective-permute-start.1
  17.7 3.2 %reshape.14 = bf16[8,2,4,64,112]{4,3,2,1,0:T(8,128)(2,1)} reshape(bf16[8,2,4,7168]{3,2,1,0:T(4,128)(2,1)} %param.20) | data formatting | bytes 1835008 | tf_op jit(solution)/shard_map/reshape | solution.py:633
  23.7 12.5 %collective-permute-done.refs_2_ = bf16[128,1792]{1,0:T(8,128)(2,1)} collective-permute-done((bf16[128,1792]{1,0:T(8,128)(2,1)}, bf16[128,1792]{1,0:T(8,128)(2,1)}, u32[]{:S(2)}, u32[]{:S(2)}) %collective-permute-start) | collective-permute-done | bytes 458784 | tf_op jit(solution)/shard_map/ppermute | solution.py:365
  37.1 1.5 collective-permute-done.3.refs_6_
  38.6 1.6 collective-permute-start.4
  40.2 1.6 collective-permute-start.5
  42.9 6.9 %collective-permute-done.4.refs_3_ = bf16[128,1792]{1,0:T(8,128)(2,1)S(1)} collective-permute-done((bf16[128,1792]{1,0:T(8,128)(2,1)}, bf16[128,1792]{1,0:T(8,128)(2,1)S(1)}, u32[]{:S(2)}, u32[]{:S(2)}) %collective-permute-start.4) | collective-permute-done | bytes 458784 | tf_op jit(solution)/shard_map/ppermute | solution.py:365
  49.9 3.6 %collective-permute-done.5.refs_7_ = bf16[5,112,512]{2,1,0:T(8,128)(2,1)S(1)} collective-permute-done((bf16[5,112,512]{2,1,0:T(8,128)(2,1)S(1)}, bf16[5,112,512]{2,1,0:T(8,128)(2,1)S(1)}, u32[]{:S(2)}, u32[]{:S(2)}) %collective-permute-start.5) | collective-permute-done | bytes 573472 | tf_op jit(solution)/shard_map/ppermute | solution.py:365
  53.5 1.3 collective-permute-done.6.refs_8_
  55.4 1.5 collective-permute-done.10.refs_12_
  58.2 7.6 %shard_map.146 = (bf16[512,512]{1,0:T(8,128)(2,1)S(1)}, bf16[512,512]{1,0:T(8,128)(2,1)S(1)}, bf16[512,512]{1,0:T(8,128)(2,1)S(1)}, bf16[1,1792,512]{2,1,0:T(8,1...) custom-call(bf16[128,1792]{1,0:T(8,128)(2,1)} %get-tuple-element.54.refs_0, ...), custom_call_target="tpu_custom_call" | custom-call | flops 3758096384 | bytes 7340032 | tf_op jit(solution)/shard_map/pallas_call | solution.py:492
  66.4 7.7 %shard_map.147 = (bf16[128,1792]{1,0:T(8,128)(2,1)S(1)}, bf16[128,1792]{1,0:T(8,128)(2,1)S(1)}, f32[128,1792]{1,0:T(8,128)S(1)}) custom-call(bf16[512,512]{1,0:T(8,128)(2,1)S(1)} %get-tuple-element.67.q_ref, bf16[512,512]{1,0:T(8,128)(2,1)S(1)} %get-tuple-element.68.k_ref, bf16[512,512]{1,0:T(8,128)(2,1)S(1)} %get-tuple-element.69.v_ref, ...), custom_call_target="tpu_custom_call" | custom-call | flops 5637144576 | bytes 1835008 | tf_op jit(solution)/shard_map/pallas_call | solution.py:532
  74.1 4.1 %collective-permute-done.12 = bf16[128,1792]{1,0:T(8,128)(2,1)S(1)} collective-permute-done((bf16[128,1792]{1,0:T(8,128)(2,1)S(1)}, bf16[128,1792]{1,0:T(8,128)(2,1)S(1)}, u32[]{:S(2)}, u32[]{:S(2)}) %collective-permute-start.12) | collective-permute-done | bytes 458784 | tf_op jit(solution)/shard_map/ppermute | solution.py:365
  78.8 2.6 %collective-permute-start.16 = (bf16[128,1792]{1,0:T(8,128)(2,1)S(1)}, bf16[128,1792]{1,0:T(8,128)(2,1)S(1)}, u32[]{:S(2)}, u32[]{:S(2)}) collective-permute-start(bf16[128,1792]{1,0:T(8,128)(2,1)S(1)} %add_convert_fusion.2), channel_id=1, source_target_pairs={{0,2},{1,3},{2,0},{3,1},{4,6},{5,7},{6,4},{7,5},{8,10},{9,11},{10,... | collective-permute-start | bytes 1376264 | tf_op jit(solution)/shard_map/ppermute | solution.py:365
  81.4 7.6 %collective-permute-done.14.refs_4_ = bf16[3,224,1024]{2,1,0:T(8,128)(2,1)S(1)} collective-permute-done((bf16[3,224,1024]{2,1,0:T(8,128)(2,1)S(1)}, bf16[3,224,1024]{2,1,0:T(8,128)(2,1)S(1)}, u32[]{:S(2)}, u32[]{:S(2)}) %collective-permute-start.14) | collective-permute-done | bytes 1376288 | tf_op jit(solution)/shard_map/ppermute | solution.py:365
  89.9 9.7 %collective-permute-done.13.one_ref = bf16[128,1792]{1,0:T(8,128)(2,1)S(1)} collective-permute-done((bf16[128,1792]{1,0:T(8,128)(2,1)S(1)}, bf16[128,1792]{1,0:T(8,128)(2,1)S(1)}, u32[]{:S(2)}, u32[]{:S(2)}) %collective-permute-start.13) | collective-permute-done | bytes 458784 | tf_op jit(solution)/shard_map/ppermute | solution.py:365
  100.2 1.5 collective-permute-start.17
  101.7 10.9 %collective-permute-start.18 = (bf16[128,1792]{1,0:T(8,128)(2,1)S(1)}, bf16[128,1792]{1,0:T(8,128)(2,1)S(1)}, u32[]{:S(2)}, u32[]{:S(2)}) collective-permute-start(bf16[128,1792]{1,0:T(8,128)(2,1)S(1)} %get-tuple-element.86.refs_2_), channel_id=1, source_target_pairs={{0,1},{1,0},{2,3},{3,2},{4,5},{5,4},{6,7},{7,6},{8,9},{9,8},{10,11... | collective-permute-start | bytes 1376264 | tf_op jit(solution)/shard_map/ppermute | solution.py:365
  112.8 1.6 collective-permute-start.19
  114.4 1.5 collective-permute-start.21
  115.9 6.6 %collective-permute-done.17.refs_0_ = bf16[128,1792]{1,0:T(8,128)(2,1)S(1)} collective-permute-done((bf16[128,1792]{1,0:T(8,128)(2,1)S(1)}, bf16[128,1792]{1,0:T(8,128)(2,1)S(1)}, u32[]{:S(2)}, u32[]{:S(2)}) %collective-permute-start.17) | collective-permute-done | bytes 458784 | tf_op jit(solution)/shard_map/ppermute | solution.py:365
  123.0 7.7 %collective-permute-done.19.refs_6_ = bf16[3,112,1024]{2,1,0:T(8,128)(2,1)S(1)} collective-permute-done((bf16[3,112,1024]{2,1,0:T(8,128)(2,1)S(1)}, bf16[3,112,1024]{2,1,0:T(8,128)(2,1)S(1)}, u32[]{:S(2)}, u32[]{:S(2)}) %collective-permute-start.19) | collective-permute-done | bytes 688160 | tf_op jit(solution)/shard_map/ppermute | solution.py:365
  132.8 1.3 collective-permute-done.22.refs_12_
  136.3 10.2 %shard_map.149 = (bf16[3,1792,1024]{2,1,0:T(8,128)(2,1)S(1)}, bf16[128,1792]{1,0:T(8,128)(2,1)S(1)}, bf16[128,1792]{1,0:T(8,128)(2,1)S(1)}, f32[128,1792]{1,0:T(8,128)}) custom-call(bf16[128,1792]{1,0:T(8,128)(2,1)S(1)} %collective-permute-done.17.refs_0_, bf16[128,1792]{1,0:T(8,128)(2,1)S(1)} %collective-permute-done.18.refs_1_, ...), custom_call_target="tpu_custom_call" | custom-call | flops 4227858432 | bytes 22020096 | tf_op jit(solution)/shard_map/pallas_call | solution.py:565
  147.5 2.1 %shard_map.150 = bf16[128,1792]{1,0:T(8,128)(2,1)S(1)} custom-call(bf16[128,1792]{1,0:T(8,128)(2,1)S(1)} %collective-permute-done.26.x_ref, bf16[3,1792,1024]{2,1,0:T(8,128)(2,1)S(1)} %get-tuple-element.99.all_w), custom_call_target="tpu_custom_call" | custom-call | flops 1409286144 | bytes 11010048 | tf_op jit(solution)/shard_map/pallas_call | solution.py:584
  150.0 11.4 %collective-permute-done.27 = bf16[128,1792]{1,0:T(8,128)(2,1)S(1)} collective-permute-done((bf16[128,1792]{1,0:T(8,128)(2,1)S(1)}, bf16[128,1792]{1,0:T(8,128)(2,1)S(1)}, u32[]{:S(2)}, u32[]{:S(2)}) %collective-permute-start.27) | collective-permute-done | bytes 458784 | tf_op jit(solution)/shard_map/ppermute | solution.py:365
  162.3 18.0 %collective-permute-done.28 = bf16[128,1792]{1,0:T(8,128)(2,1)S(1)} collective-permute-done((bf16[128,1792]{1,0:T(8,128)(2,1)S(1)}, bf16[128,1792]{1,0:T(8,128)(2,1)S(1)}, u32[]{:S(2)}, u32[]{:S(2)}) %collective-permute-start.28) | collective-permute-done | bytes 458784 | tf_op jit(solution)/shard_map/ppermute | solution.py:365
  180.3 3.6 %collective-permute-done.29 = bf16[128,1792]{1,0:T(8,128)(2,1)S(1)} collective-permute-done((bf16[128,1792]{1,0:T(8,128)(2,1)S(1)}, bf16[128,1792]{1,0:T(8,128)(2,1)S(1)}, u32[]{:S(2)}, u32[]{:S(2)}) %collective-permute-start.29) | collective-permute-done | bytes 458784 | tf_op jit(solution)/shard_map/ppermute | solution.py:365
  (97 shorter events, 23.8 us)
Async XLA Ops:
  8.8 28.3 %collective-permute-start.2 = (bf16[5,224,512]{2,1,0:T(8,128)(2,1)S(1)}, bf16[5,224,512]{2,1,0:T(8,128)(2,1)S(1)}, u32[]{:S(2)}, u32[]{:S(2)}) collective-permute-start(bf16[5,224,512]{2,1,0:T(8,128)(2,1)S(1)} %get-tuple-element.62.refs_4_), channel_id=1, source_target_pairs={{0,8},{4,12},{8,0},{12,4},{16,24},{20,28},{24,16},{28,20},{1,9},{5... | collective-permute-start | bytes 3440648 | tf_op jit(solution)/shard_map/ppermute | solution.py:365
  11.8 26.7 %collective-permute-start.3 = (bf16[5,224,512]{2,1,0:T(8,128)(2,1)S(1)}, bf16[5,224,512]{2,1,0:T(8,128)(2,1)S(1)}, u32[]{:S(2)}, u32[]{:S(2)}) collective-permute-start(bf16[5,224,512]{2,1,0:T(8,128)(2,1)S(1)} %get-tuple-element.62.refs_4_), channel_id=1, source_target_pairs={{0,16},{4,20},{8,24},{12,28},{16,0},{20,4},{24,8},{28,12},{1,17},{... | collective-permute-start | bytes 3440648 | tf_op jit(solution)/shard_map/ppermute | solution.py:365
  13.4 22.8 %collective-permute-start = (bf16[128,1792]{1,0:T(8,128)(2,1)}, bf16[128,1792]{1,0:T(8,128)(2,1)}, u32[]{:S(2)}, u32[]{:S(2)}) collective-permute-start(bf16[128,1792]{1,0:T(8,128)(2,1)} %get-tuple-element.54.refs_0_.x_ref), channel_id=1, source_target_pairs={{0,2},{1,3},{2,0},{3,1},{4,6},{5,7},{6,4},{7,5},{8,10},{9,11},{10,... | collective-permute-start | bytes 1376264 | tf_op jit(solution)/shard_map/ppermute | solution.py:365
  16.0 20.5 %collective-permute-start.1 = (bf16[128,1792]{1,0:T(8,128)(2,1)}, bf16[128,1792]{1,0:T(8,128)(2,1)}, u32[]{:S(2)}, u32[]{:S(2)}) collective-permute-start(bf16[128,1792]{1,0:T(8,128)(2,1)} %get-tuple-element.54.refs_0_.x_ref), channel_id=1, source_target_pairs={{0,1},{1,0},{2,3},{3,2},{4,5},{5,4},{6,7},{7,6},{8,9},{9,8},{10,11... | collective-permute-start | bytes 1376264 | tf_op jit(solution)/shard_map/ppermute | solution.py:365
  23.7 98.8 %copy-start.10 = (bf16[3,224,1024]{2,1,0:T(8,128)(2,1)}, bf16[3,224,1024]{2,1,0:T(8,128)(2,1)S(1)}, u32[]{:S(2)}) copy-start(bf16[3,224,1024]{2,1,0:T(8,128)(2,1)S(1)} %pad_maximum_fusion.refs_3_) | copy-start | bytes 4128772
  23.7 34.5 %copy-start.8 = (s32[1,8]{1,0:T(1,128)S(1)}, s32[1,8]{1,0:T(1,128)}, u32[]{:S(2)}) copy-start(s32[1,8]{1,0:T(1,128)} %refs_0_.1) | copy-start | bytes 100
  38.6 11.3 %collective-permute-start.4 = (bf16[128,1792]{1,0:T(8,128)(2,1)}, bf16[128,1792]{1,0:T(8,128)(2,1)S(1)}, u32[]{:S(2)}, u32[]{:S(2)}) collective-permute-start(bf16[128,1792]{1,0:T(8,128)(2,1)} %collective-permute-done.refs_2_), channel_id=1, source_target_pairs={{0,1},{1,0},{2,3},{3,2},{4,5},{5,4},{6,7},{7,6},{8,9},{9,8},{10,11... | collective-permute-start | bytes 1376264 | tf_op jit(solution)/shard_map/ppermute | solution.py:365
  40.2 13.3 %collective-permute-start.5 = (bf16[5,112,512]{2,1,0:T(8,128)(2,1)S(1)}, bf16[5,112,512]{2,1,0:T(8,128)(2,1)S(1)}, u32[]{:S(2)}, u32[]{:S(2)}) collective-permute-start(bf16[5,112,512]{2,1,0:T(8,128)(2,1)S(1)} %slice.12), channel_id=1, source_target_pairs={{0,16},{4,20},{8,24},{12,28},{16,0},{20,4},{24,8},{28,12},{1,17},{... | collective-permute-start | bytes 1720328 | tf_op jit(solution)/shard_map/ppermute | solution.py:365
  41.8 13.0 %collective-permute-start.6 = (bf16[5,112,512]{2,1,0:T(8,128)(2,1)S(1)}, bf16[5,112,512]{2,1,0:T(8,128)(2,1)S(1)}, u32[]{:S(2)}, u32[]{:S(2)}) collective-permute-start(bf16[5,112,512]{2,1,0:T(8,128)(2,1)S(1)} %slice.13), channel_id=1, source_target_pairs={{0,8},{4,12},{8,0},{12,4},{16,24},{20,28},{24,16},{28,20},{1,9},{5... | collective-permute-start | bytes 1720328 | tf_op jit(solution)/shard_map/ppermute | solution.py:365
  42.4 15.7 %collective-permute-start.8 = (bf16[5,224,512]{2,1,0:T(8,128)(2,1)S(1)}, bf16[5,224,512]{2,1,0:T(8,128)(2,1)S(1)}, u32[]{:S(2)}, u32[]{:S(2)}) collective-permute-start(bf16[5,224,512]{2,1,0:T(8,128)(2,1)S(1)} %collective-permute-done.2.refs_5_), channel_id=1, source_target_pairs={{0,4},{4,0},{8,12},{12,8},{16,20},{20,16},{24,28},{28,24},{1,5},{5... | collective-permute-start | bytes 3440648 | tf_op jit(solution)/shard_map/ppermute | solution.py:365
  42.4 15.7 %collective-permute-start.9 = (bf16[5,224,512]{2,1,0:T(8,128)(2,1)S(1)}, bf16[5,224,512]{2,1,0:T(8,128)(2,1)S(1)}, u32[]{:S(2)}, u32[]{:S(2)}) collective-permute-start(bf16[5,224,512]{2,1,0:T(8,128)(2,1)S(1)} %collective-permute-done.3.refs_6_), channel_id=1, source_target_pairs={{0,4},{4,0},{8,12},{12,8},{16,20},{20,16},{24,28},{28,24},{1,5},{5... | collective-permute-start | bytes 3440648 | tf_op jit(solution)/shard_map/ppermute | solution.py:365
  49.9 8.3 %collective-permute-start.7 = (bf16[5,224,512]{2,1,0:T(8,128)(2,1)S(1)}, bf16[5,224,512]{2,1,0:T(8,128)(2,1)S(1)}, u32[]{:S(2)}, u32[]{:S(2)}) collective-permute-start(bf16[5,224,512]{2,1,0:T(8,128)(2,1)S(1)} %get-tuple-element.62.refs_4_), channel_id=1, source_target_pairs={{0,4},{4,0},{8,12},{12,8},{16,20},{20,16},{24,28},{28,24},{1,5},{5... | collective-permute-start | bytes 3440648 | tf_op jit(solution)/shard_map/ppermute | solution.py:365
  54.8 2.0 %collective-permute-start.10 = (bf16[5,112,512]{2,1,0:T(8,128)(2,1)S(1)}, bf16[5,112,512]{2,1,0:T(8,128)(2,1)S(1)}, u32[]{:S(2)}, u32[]{:S(2)}) collective-permute-start(bf16[5,112,512]{2,1,0:T(8,128)(2,1)S(1)} %collective-permute-done.5.refs_7_), channel_id=1, source_target_pairs={{0,4},{4,0},{8,12},{12,8},{16,20},{20,16},{24,28},{28,24},{1,5},{5... | collective-permute-start | bytes 1720328 | tf_op jit(solution)/shard_map/ppermute | solution.py:365
  54.9 2.8 %collective-permute-start.11 = (bf16[5,112,512]{2,1,0:T(8,128)(2,1)S(1)}, bf16[5,112,512]{2,1,0:T(8,128)(2,1)S(1)}, u32[]{:S(2)}, u32[]{:S(2)}) collective-permute-start(bf16[5,112,512]{2,1,0:T(8,128)(2,1)S(1)} %collective-permute-done.6.refs_8_), channel_id=1, source_target_pairs={{0,4},{4,0},{8,12},{12,8},{16,20},{20,16},{24,28},{28,24},{1,5},{5... | collective-permute-start | bytes 1720328 | tf_op jit(solution)/shard_map/ppermute | solution.py:365
  56.8 32.2 %collective-permute-start.14 = (bf16[3,224,1024]{2,1,0:T(8,128)(2,1)S(1)}, bf16[3,224,1024]{2,1,0:T(8,128)(2,1)S(1)}, u32[]{:S(2)}, u32[]{:S(2)}) collective-permute-start(bf16[3,224,1024]{2,1,0:T(8,128)(2,1)S(1)} %pad_maximum_fusion.refs_3_), channel_id=1, source_target_pairs={{0,8},{4,12},{8,0},{12,4},{16,24},{20,28},{24,16},{28,20},{1,9},{5... | collective-permute-start | bytes 4128776 | tf_op jit(solution)/shard_map/ppermute | solution.py:365
  57.6 32.2 %collective-permute-start.15 = (bf16[3,224,1024]{2,1,0:T(8,128)(2,1)S(1)}, bf16[3,224,1024]{2,1,0:T(8,128)(2,1)S(1)}, u32[]{:S(2)}, u32[]{:S(2)}) collective-permute-start(bf16[3,224,1024]{2,1,0:T(8,128)(2,1)S(1)} %pad_maximum_fusion.refs_3_), channel_id=1, source_target_pairs={{0,16},{4,20},{8,24},{12,28},{16,0},{20,4},{24,8},{28,12},{1,17},{... | collective-permute-start | bytes 4128776 | tf_op jit(solution)/shard_map/ppermute | solution.py:365
  65.8 12.4 %collective-permute-start.12 = (bf16[128,1792]{1,0:T(8,128)(2,1)S(1)}, bf16[128,1792]{1,0:T(8,128)(2,1)S(1)}, u32[]{:S(2)}, u32[]{:S(2)}) collective-permute-start(bf16[128,1792]{1,0:T(8,128)(2,1)S(1)} %get-tuple-element.75), channel_id=1, source_target_pairs={{0,1},{1,0},{2,3},{3,2},{4,5},{5,4},{6,7},{7,6},{8,9},{9,8},{10,11... | collective-permute-start | bytes 1376264 | tf_op jit(solution)/shard_map/ppermute | solution.py:365
  78.3 21.3 %collective-permute-start.13 = (bf16[128,1792]{1,0:T(8,128)(2,1)S(1)}, bf16[128,1792]{1,0:T(8,128)(2,1)S(1)}, u32[]{:S(2)}, u32[]{:S(2)}) collective-permute-start(bf16[128,1792]{1,0:T(8,128)(2,1)S(1)} %get-tuple-element.81), channel_id=1, source_target_pairs={{0,1},{1,0},{2,3},{3,2},{4,5},{5,4},{6,7},{7,6},{8,9},{9,8},{10,11... | collective-permute-start | bytes 1376264 | tf_op jit(solution)/shard_map/ppermute | solution.py:365
  78.8 20.8 %collective-permute-start.16 = (bf16[128,1792]{1,0:T(8,128)(2,1)S(1)}, bf16[128,1792]{1,0:T(8,128)(2,1)S(1)}, u32[]{:S(2)}, u32[]{:S(2)}) collective-permute-start(bf16[128,1792]{1,0:T(8,128)(2,1)S(1)} %add_convert_fusion.2), channel_id=1, source_target_pairs={{0,2},{1,3},{2,0},{3,1},{4,6},{5,7},{6,4},{7,5},{8,10},{9,11},{10,... | collective-permute-start | bytes 1376264 | tf_op jit(solution)/shard_map/ppermute | solution.py:365
  100.2 22.2 %collective-permute-start.17 = (bf16[128,1792]{1,0:T(8,128)(2,1)S(1)}, bf16[128,1792]{1,0:T(8,128)(2,1)S(1)}, u32[]{:S(2)}, u32[]{:S(2)}) collective-permute-start(bf16[128,1792]{1,0:T(8,128)(2,1)S(1)} %get-tuple-element.86.refs_2_), channel_id=1, source_target_pairs={{0,2},{1,3},{2,0},{3,1},{4,6},{5,7},{6,4},{7,5},{8,10},{9,11},{10,... | collective-permute-start | bytes 1376264 | tf_op jit(solution)/shard_map/ppermute | solution.py:365
  101.7 21.0 %collective-permute-start.18 = (bf16[128,1792]{1,0:T(8,128)(2,1)S(1)}, bf16[128,1792]{1,0:T(8,128)(2,1)S(1)}, u32[]{:S(2)}, u32[]{:S(2)}) collective-permute-start(bf16[128,1792]{1,0:T(8,128)(2,1)S(1)} %get-tuple-element.86.refs_2_), channel_id=1, source_target_pairs={{0,1},{1,0},{2,3},{3,2},{4,5},{5,4},{6,7},{7,6},{8,9},{9,8},{10,11... | collective-permute-start | bytes 1376264 | tf_op jit(solution)/shard_map/ppermute | solution.py:365
  112.7 21.4 %collective-permute-start.24 = (bf16[3,224,1024]{2,1,0:T(8,128)(2,1)S(1)}, bf16[3,224,1024]{2,1,0:T(8,128)(2,1)S(1)}, u32[]{:S(2)}, u32[]{:S(2)}) collective-permute-start(bf16[3,224,1024]{2,1,0:T(8,128)(2,1)S(1)} %collective-permute-done.14.refs_4_), channel_id=1, source_target_pairs={{0,4},{4,0},{8,12},{12,8},{16,20},{20,16},{24,28},{28,24},{1,5},{5... | collective-permute-start | bytes 4128776 | tf_op jit(solution)/shard_map/ppermute | solution.py:365
  112.8 17.9 %collective-permute-start.19 = (bf16[3,112,1024]{2,1,0:T(8,128)(2,1)S(1)}, bf16[3,112,1024]{2,1,0:T(8,128)(2,1)S(1)}, u32[]{:S(2)}, u32[]{:S(2)}) collective-permute-start(bf16[3,112,1024]{2,1,0:T(8,128)(2,1)S(1)} %slice.14), channel_id=1, source_target_pairs={{0,16},{4,20},{8,24},{12,28},{16,0},{20,4},{24,8},{28,12},{1,17},{... | collective-permute-start | bytes 2064392 | tf_op jit(solution)/shard_map/ppermute | solution.py:365
  114.4 17.6 %collective-permute-start.21 = (bf16[3,112,1024]{2,1,0:T(8,128)(2,1)S(1)}, bf16[3,112,1024]{2,1,0:T(8,128)(2,1)S(1)}, u32[]{:S(2)}, u32[]{:S(2)}) collective-permute-start(bf16[3,112,1024]{2,1,0:T(8,128)(2,1)S(1)} %slice.15), channel_id=1, source_target_pairs={{0,8},{4,12},{8,0},{12,4},{16,24},{20,28},{24,16},{28,20},{1,9},{5... | collective-permute-start | bytes 2064392 | tf_op jit(solution)/shard_map/ppermute | solution.py:365
  122.4 11.7 %collective-permute-start.23 = (bf16[3,224,1024]{2,1,0:T(8,128)(2,1)S(1)}, bf16[3,224,1024]{2,1,0:T(8,128)(2,1)S(1)}, u32[]{:S(2)}, u32[]{:S(2)}) collective-permute-start(bf16[3,224,1024]{2,1,0:T(8,128)(2,1)S(1)} %pad_maximum_fusion.refs_3_), channel_id=1, source_target_pairs={{0,4},{4,0},{8,12},{12,8},{16,20},{20,16},{24,28},{28,24},{1,5},{5... | collective-permute-start | bytes 4128776 | tf_op jit(solution)/shard_map/ppermute | solution.py:365
  122.7 11.5 %collective-permute-start.25 = (bf16[3,224,1024]{2,1,0:T(8,128)(2,1)S(1)}, bf16[3,224,1024]{2,1,0:T(8,128)(2,1)S(1)}, u32[]{:S(2)}, u32[]{:S(2)}) collective-permute-start(bf16[3,224,1024]{2,1,0:T(8,128)(2,1)S(1)} %collective-permute-done.15.refs_5_), channel_id=1, source_target_pairs={{0,4},{4,0},{8,12},{12,8},{16,20},{20,16},{24,28},{28,24},{1,5},{5... | collective-permute-start | bytes 4128776 | tf_op jit(solution)/shard_map/ppermute | solution.py:365
  130.6 2.1 %collective-permute-start.20 = (bf16[3,112,1024]{2,1,0:T(8,128)(2,1)S(1)}, bf16[3,112,1024]{2,1,0:T(8,128)(2,1)S(1)}, u32[]{:S(2)}, u32[]{:S(2)}) collective-permute-start(bf16[3,112,1024]{2,1,0:T(8,128)(2,1)S(1)} %collective-permute-done.19.refs_6_), channel_id=1, source_target_pairs={{0,4},{4,0},{8,12},{12,8},{16,20},{20,16},{24,28},{28,24},{1,5},{5... | collective-permute-start | bytes 2064392 | tf_op jit(solution)/shard_map/ppermute | solution.py:365
  132.0 2.1 %collective-permute-start.22 = (bf16[3,112,1024]{2,1,0:T(8,128)(2,1)S(1)}, bf16[3,112,1024]{2,1,0:T(8,128)(2,1)S(1)}, u32[]{:S(2)}, u32[]{:S(2)}) collective-permute-start(bf16[3,112,1024]{2,1,0:T(8,128)(2,1)S(1)} %collective-permute-done.21.refs_7_), channel_id=1, source_target_pairs={{0,4},{4,0},{8,12},{12,8},{16,20},{20,16},{24,28},{28,24},{1,5},{5... | collective-permute-start | bytes 2064392 | tf_op jit(solution)/shard_map/ppermute | solution.py:365
  135.0 12.6 %collective-permute-start.26 = (bf16[128,1792]{1,0:T(8,128)(2,1)S(1)}, bf16[128,1792]{1,0:T(8,128)(2,1)S(1)}, u32[]{:S(2)}, u32[]{:S(2)}) collective-permute-start(bf16[128,1792]{1,0:T(8,128)(2,1)S(1)} %collective-permute-done.17.refs_0_), channel_id=1, source_target_pairs={{0,1},{1,0},{2,3},{3,2},{4,5},{5,4},{6,7},{7,6},{8,9},{9,8},{10,11... | collective-permute-start | bytes 1376264 | tf_op jit(solution)/shard_map/ppermute | solution.py:365
  149.7 11.8 %collective-permute-start.27 = (bf16[128,1792]{1,0:T(8,128)(2,1)S(1)}, bf16[128,1792]{1,0:T(8,128)(2,1)S(1)}, u32[]{:S(2)}, u32[]{:S(2)}) collective-permute-start(bf16[128,1792]{1,0:T(8,128)(2,1)S(1)} %shard_map.150), channel_id=1, source_target_pairs={{0,1},{1,0},{2,3},{3,2},{4,5},{5,4},{6,7},{7,6},{8,9},{9,8},{10,11... | collective-permute-start | bytes 1376264 | tf_op jit(solution)/shard_map/ppermute | solution.py:365
  161.6 18.7 %collective-permute-start.28 = (bf16[128,1792]{1,0:T(8,128)(2,1)S(1)}, bf16[128,1792]{1,0:T(8,128)(2,1)S(1)}, u32[]{:S(2)}, u32[]{:S(2)}) collective-permute-start(bf16[128,1792]{1,0:T(8,128)(2,1)S(1)} %get-tuple-element.101), channel_id=1, source_target_pairs={{0,1},{1,0},{2,3},{3,2},{4,5},{5,4},{6,7},{7,6},{8,9},{9,8},{10,11... | collective-permute-start | bytes 1376264 | tf_op jit(solution)/shard_map/ppermute | solution.py:365
  162.3 21.6 %collective-permute-start.29 = (bf16[128,1792]{1,0:T(8,128)(2,1)S(1)}, bf16[128,1792]{1,0:T(8,128)(2,1)S(1)}, u32[]{:S(2)}, u32[]{:S(2)}) collective-permute-start(bf16[128,1792]{1,0:T(8,128)(2,1)S(1)} %add_convert_fusion.1), channel_id=1, source_target_pairs={{0,2},{1,3},{2,0},{3,1},{4,6},{5,7},{6,4},{7,5},{8,10},{9,11},{10,... | collective-permute-start | bytes 1376264 | tf_op jit(solution)/shard_map/ppermute | solution.py:365
  (22 other events, 195.0 us)

commit v3 on v2

--- a/solution.py
+++ b/solution.py
@@ -231,6 +231,9 @@
 MIB = 1 << 20
 
 
+LIGHT = pl.CostEstimate(flops=1, bytes_accessed=1, transcendentals=0)
+
+
 def params(mib):
     return pltpu.CompilerParams(vmem_limit_bytes=mib * MIB)
 
@@ -246,100 +249,53 @@
     return (values * lax.rsqrt(mean_square + epsilon) * gain_ref[...]).astype(jnp.bfloat16)
 
 
-def pack_maps(down_ref, up_ref, packed_ref):
-    ranks, width = down_ref.shape
-    lanes = packed_ref.shape[1]
-    for c in range(width // lanes):
-        cols = slice(c * lanes, (c + 1) * lanes)
-        packed_ref[2 * c * ranks : (2 * c + 1) * ranks, :] = down_ref[:, cols]
-        packed_ref[(2 * c + 1) * ranks : (2 * c + 2) * ranks, :] = up_ref[:, cols]
-    whole = width // lanes * lanes
-    packed_ref[2 * whole // lanes * ranks :, : lanes // 2] = down_ref[:, whole:]
-    packed_ref[2 * whole // lanes * ranks :, lanes // 2 :] = up_ref[:, whole:]
-
-
-def unpack_maps(places, w_refs, down_ref, up_ref):
-    row = lax.axis_index("row")
-    ranks, width = down_ref.shape[0] // lax.axis_size("row"), down_ref.shape[1]
-    lanes, step = w_refs[0].shape[2], 16
-    whole = width // lanes
-    for ref, (mask, first) in zip(w_refs, places):
-        start = (row ^ mask) * ranks
-        for at in range(0, ref.shape[1], step):
-            chunk, inner = divmod(first + at, 2 * ranks)
-            rows = pl.ds(pl.multiple_of(start + inner % ranks, step), step)
-            cols = slice(chunk * lanes, min((chunk + 1) * lanes, width))
-            if chunk < whole:
-                target = down_ref if inner < ranks else up_ref
-                target[rows, cols] = ref[0, at : at + step, :]
-            else:
-                down_ref[rows, cols] = ref[0, at : at + step, : lanes // 2]
-                up_ref[rows, cols] = ref[0, at : at + step, lanes // 2 :]
-
-
-def entry_kernel(
-    x_hbm, gain_ref, qkv_hbm, out_hbm, taps_ref, down_ref, up_ref, normed_ref, packed_ref, padded_taps_ref, x_ref, qkv_ref, out_ref, sems
-):
+def entry_kernel(*refs):
+    sources, (normed_ref, packed_ref) = refs[:6], refs[6:8]
+    targets, sems = refs[8:14], refs[14]
     loads = [
         pltpu.make_async_copy(source, target, sems.at[i])
-        for i, (source, target) in enumerate(
-            ((x_hbm, x_ref), (qkv_hbm, qkv_ref), (out_hbm, out_ref))
-        )
+        for i, (source, target) in enumerate(zip(sources, targets))
     ]
     for load in loads:
         load.start()
-    heads = qkv_ref.shape[2] // HD
-    blank = jnp.zeros((packed_ref.shape[1], LANES - HD), jnp.bfloat16)
-    pack_maps(down_ref, up_ref, packed_ref.at[4])
-    for h in range(heads):
-        middle = h * LANES + HD
-        padded_taps_ref[:, :, h * LANES : middle] = taps_ref[:, :, h * HD : (h + 1) * HD]
-        padded_taps_ref[:, :, middle : (h + 1) * LANES] = jnp.zeros(
-            taps_ref.shape[:2] + (LANES - HD,), jnp.float32
-        )
-        for i in range(4):
-            packed_ref[i, :, middle : (h + 1) * LANES] = blank
-    loads[0].wait()
+    x_ref, qkv_ref, out_ref, gain_ref, down_ref, up_ref = targets
+    rows, part, ranks = qkv_ref.shape[1], qkv_ref.shape[2], down_ref.shape[0]
+    for load in loads:
+        load.wait()
     normed_ref[...] = normed(x_ref[...].astype(jnp.float32), gain_ref)
-    loads[1].wait()
-    for h in range(heads):
-        for i in range(3):
-            packed_ref[i, :, h * LANES : h * LANES + HD] = qkv_ref[i, :, h * HD : (h + 1) * HD]
-    loads[2].wait()
+    for place, which in enumerate((1, 0, 2)):
+        packed_ref[:rows, place * part : (place + 1) * part] = qkv_ref[which]
     out_rows = jnp.transpose(out_ref[...].astype(jnp.float32)).astype(jnp.bfloat16)
-    for h in range(heads):
-        packed_ref[3, :, h * LANES : h * LANES + HD] = out_rows[:, h * HD : (h + 1) * HD]
-
-
-def entry_call(rows, gain, qkv, out, taps, down, up):
-    lanes = qkv.shape[2] // HD * LANES
+    packed_ref[:rows, 3 * part :] = out_rows
+    packed_ref[rows : rows + ranks, :] = down_ref[...]
+    packed_ref[rows + ranks :, :] = up_ref[...]
+
+
+def entry_call(rows, qkv, out, gain, down, up):
+    sources = (rows, qkv, out, gain[None, :], down, up)
     return pl.pallas_call(
         entry_kernel,
         out_shape=[
             jax.ShapeDtypeStruct(rows.shape, jnp.bfloat16),
-            jax.ShapeDtypeStruct((5, qkv.shape[1], lanes), jnp.bfloat16),
-            jax.ShapeDtypeStruct(taps.shape[:2] + (lanes,), jnp.float32),
+            jax.ShapeDtypeStruct((qkv.shape[1] + 2 * down.shape[0], 4 * qkv.shape[2]), jnp.bfloat16),
         ],
-        in_specs=[HBM, VMEM, HBM, HBM, VMEM, VMEM, VMEM],
-        out_specs=[VMEM] * 3,
-        scratch_shapes=[
-            pltpu.VMEM(rows.shape, rows.dtype),
-            pltpu.VMEM(qkv.shape, qkv.dtype),
-            pltpu.VMEM(out.shape, out.dtype),
-            pltpu.SemaphoreType.DMA((3,)),
-        ],
-        compiler_params=params(40),
-    )(rows, gain[None, :], qkv, out, taps, down, up)
-
-
-def residual_kernel(x_ref, own_ref, one_ref, two_ref, gain_ref, residual_ref, normed_ref):
+        in_specs=[HBM] * len(sources),
+        out_specs=[VMEM] * 2,
+        scratch_shapes=[pltpu.VMEM(source.shape, source.dtype) for source in sources]
+        + [pltpu.SemaphoreType.DMA((len(sources),))],
+        compiler_params=params(60),
+        cost_estimate=LIGHT,
+    )(*sources)
+
+
+def residual_kernel(x_ref, own_ref, two_ref, one_ref, gain_ref, residual_ref, normed_ref):
     total = own_ref[...] + one_ref[...].astype(jnp.float32) + two_ref[...].astype(jnp.float32)
     residual = (x_ref[...].astype(jnp.float32) + total).astype(jnp.bfloat16)
     residual_ref[...] = residual
     normed_ref[...] = normed(residual.astype(jnp.float32), gain_ref)
 
 
-def residual_call(rows, own, one, two, gain):
+def residual_call(rows, own, two, one, gain):
     block = jax.ShapeDtypeStruct(rows.shape, jnp.bfloat16)
     return pl.pallas_call(
         residual_kernel,
@@ -347,7 +303,8 @@
         in_specs=[VMEM] * 5,
         out_specs=[VMEM] * 2,
         compiler_params=params(12),
-    )(rows, own, one, two, gain[None, :])
+        cost_estimate=LIGHT,
+    )(rows, own, two, one, gain[None, :])
 
 
 def adapter_term(x_ref, ids_ref, down_ref, up_ref, rank):
@@ -370,24 +327,20 @@
 
 
 def second_hops(own, from_x, from_y):
-    half = own.shape[1] // 2
-    diagonal = swap(from_x[:, :half], "row", 4), swap(from_y[:, half:], "row", 2)
+    half = own.shape[-2] // 2
+    diagonal = swap(from_x[..., :half, :], "row", 4), swap(from_y[..., half:, :], "row", 2)
     return diagonal + tuple(swap(piece, "row", 1) for piece in (own, from_x, from_y))
 
 
 def named_pieces(own, firsts, seconds, thirds):
-    half = own.shape[1] // 2
+    half = own.shape[-2] // 2
     masks = [(0, 0), (2, 0), (4, 0), (6, 0), (6, half), (1, 0), (3, 0), (5, 0), (7, 0), (7, half)]
     return [(piece, *at) for piece, at in zip((own,) + firsts + seconds + thirds, masks)]
 
 
-def assemble(places, w_refs, all_w):
+def shard_starts(places, shard):
     row = lax.axis_index("row")
-    shard = all_w.shape[1] // lax.axis_size("row")
-    for ref, (mask, first) in zip(w_refs, places):
-        start = pl.multiple_of((row ^ mask) * shard + first, 16)
-        for part in range(ref.shape[0]):
-            all_w[part, pl.ds(start, ref.shape[1]), :] = ref[part]
+    return [pl.multiple_of((row ^ mask) * shard + first, 16) for mask, first in places]
 
 
 def request_columns(lengths_ref, begin, count):
@@ -442,8 +395,9 @@
         summed = summed + jnp.dot(
             cached.astype(jnp.bfloat16), cache_ref[1, h], preferred_element_type=jnp.float32
         )
-        outs.append((summed / total).astype(jnp.bfloat16))
-    return jnp.concatenate(outs, axis=1)
+        outs.append((summed / total).astype(jnp.bfloat16)[:, :HD])
+    blank = jnp.zeros((count, heads * (lanes - HD)), jnp.bfloat16)
+    return jnp.concatenate([blank] + outs, axis=1)
 
 
 def first_kernel(places, n_x, n_w, *refs):
@@ -452,18 +406,26 @@
     q_ref, k_ref, v_ref, out_w, down_ref, up_ref, part_ref = refs[n_x + n_w + 4 : n_x + n_w + 11]
     x_all, w_all, padded = refs[n_x + n_w + 11 :]
     col = lax.axis_index("col")
-    count, tokens = x_refs[0].shape[0], x_all.shape[0]
+    count, (tokens, width) = x_refs[0].shape[0], x_all.shape
+    part, lanes = taps_ref.shape[2], q_ref.shape[1]
+    mixed_lanes = w_all.shape[1]
     for i, ref in enumerate(x_refs):
         x_all[pl.ds(pl.multiple_of((col ^ i) * count, 16), count), :] = ref[...]
-    assemble(places, [ref.at[pl.ds(0, 3)] for ref in w_refs], w_all)
-    assemble(places, [ref.at[pl.ds(3, 1)] for ref in w_refs], out_w)
-    unpack_maps(places, [ref.at[pl.ds(4, 1)] for ref in w_refs], down_ref, up_ref)
-    padded[0:8, :] = jnp.zeros((8, padded.shape[1]), jnp.float32)
+    shard = width // lax.axis_size("row")
+    ranks = down_ref.shape[0] // lax.axis_size("row")
+    starts = shard_starts(places, shard)
+    for ref, start, (mask, first) in zip(w_refs, starts, places):
+        rows = min(ref.shape[0], shard - first)
+        w_all[pl.ds(start, rows), :] = ref[:rows, :mixed_lanes]
+        out_w[pl.ds(start, rows), :] = ref[:rows, ref.shape[1] - lanes :]
+        if rows < ref.shape[0]:
+            at = pl.multiple_of((lax.axis_index("row") ^ mask) * ranks, 16)
+            down_ref[pl.ds(at, ranks), :] = ref[rows : rows + ranks, :]
+            up_ref[pl.ds(at, ranks), :] = ref[rows + ranks :, :]
+    padded[0:8, :] = jnp.zeros((8, part), jnp.float32)
     place, _, first = request_columns(lengths_ref, 0, tokens)
     inside = place - first
-
-    def mixed(which):
-        return jnp.dot(x_all[...], w_all[which], preferred_element_type=jnp.float32)
+    mixed = jnp.dot(x_all[...], w_all[...], preferred_element_type=jnp.float32)
 
     def convolved(raw, which):
         padded[8:, :] = raw
@@ -474,19 +436,27 @@
             running = running + jnp.where(inside >= offset, tap * moved, 0.0)
         return running
 
-    q_ref[...] = mixed(0).astype(jnp.bfloat16)
-    k_ref[...] = convolved(mixed(1), 0).astype(jnp.bfloat16)
-    raw_values = mixed(2)
-    v_ref[...] = (raw_values * jax.nn.sigmoid(convolved(raw_values, 1))).astype(jnp.bfloat16)
+    def store_heads(ref, value):
+        blank = jnp.zeros((tokens, LANES - HD), jnp.bfloat16)
+        for h in range(part // HD):
+            ref[:, h * LANES : h * LANES + HD] = value[:, h * HD : (h + 1) * HD].astype(jnp.bfloat16)
+            ref[:, h * LANES + HD : (h + 1) * LANES] = blank
+
+    store_heads(k_ref, convolved(mixed[:, :part], 0))
+    store_heads(q_ref, mixed[:, part : 2 * part])
+    raw_values = mixed[:, 2 * part : 3 * part]
+    store_heads(v_ref, raw_values * jax.nn.sigmoid(convolved(raw_values, 1)))
     attended = attend_block(n_x - 1, count, lengths_ref, valid_ref, q_ref, k_ref, v_ref, cache_ref)
     part_ref[...] = lax.dot_general(
-        attended, out_w[0], NT, preferred_element_type=jnp.float32
+        attended, out_w[...], NT, preferred_element_type=jnp.float32
     ).astype(jnp.bfloat16)
 
 
 def first_call(blocks, pieces, ranks, taps, lengths, valid, cache):
     (count, width), n_x, n_w = blocks[0].shape, len(blocks), len(pieces)
-    tokens, lanes = count * n_x, pieces[0][0].shape[2]
+    tokens, part = count * n_x, taps.shape[2]
+    lanes = part // HD * LANES
+    mixed_lanes = -(-3 * part // LANES) * LANES
     places = [(mask, first) for _, mask, first in pieces]
     one = jax.ShapeDtypeStruct((tokens, lanes), jnp.bfloat16)
     return pl.pallas_call(
@@ -495,7 +465,7 @@
             one,
             one,
             one,
-            jax.ShapeDtypeStruct((1, width, lanes), jnp.bfloat16),
+            jax.ShapeDtypeStruct((width, lanes), jnp.bfloat16),
             jax.ShapeDtypeStruct((ranks, width), jnp.bfloat16),
             jax.ShapeDtypeStruct((ranks, width), jnp.bfloat16),
             jax.ShapeDtypeStruct((count, width), jnp.bfloat16),
@@ -504,13 +474,11 @@
         out_specs=[VMEM] * 7,
         scratch_shapes=[
             pltpu.VMEM((tokens, width), jnp.bfloat16),
-            pltpu.VMEM((3, width, lanes), jnp.bfloat16),
-            pltpu.VMEM((tokens + 8, lanes), jnp.float32),
+            pltpu.VMEM((width, mixed_lanes), jnp.bfloat16),
+            pltpu.VMEM((tokens + 8, part), jnp.float32),
         ],
         compiler_params=params(36),
-        cost_estimate=pl.CostEstimate(
-            flops=2 * tokens * width * 4 * lanes, bytes_accessed=2 * width * 4 * lanes, transcendentals=0
-        ),
+        cost_estimate=LIGHT,
     )(*blocks, *(piece for piece, _, _ in pieces), taps, lengths, valid, cache)
 
 
@@ -520,24 +488,21 @@
         attended = attend_block(
             mask, out_ref.shape[0], lengths_ref, valid_ref, q_ref, k_ref, v_ref, cache_ref
         )
-        part = lax.dot_general(attended, out_w[0], NT, preferred_element_type=jnp.float32)
+        part = lax.dot_general(attended, out_w[...], NT, preferred_element_type=jnp.float32)
         if mask == 0:
             part = part + adapter_term(x_ref, ids_ref, down_ref, up_ref, rank).astype(jnp.float32)
         out_ref[...] = part.astype(out_ref.dtype)
 
 
 def attend_call(rank, masks, out_types, q, k, v, out_w, x, ids, down, up, lengths, valid, cache):
-    _, width, lanes = out_w.shape
-    count = x.shape[0]
+    count, width = x.shape
     return pl.pallas_call(
         functools.partial(attend_kernel, rank, masks),
         out_shape=[jax.ShapeDtypeStruct((count, width), t) for t in out_types],
         in_specs=[VMEM] * 8 + [SMEM, SMEM, VMEM],
         out_specs=[VMEM] * len(masks),
         compiler_params=params(20),
-        cost_estimate=pl.CostEstimate(
-            flops=len(masks) * 16 * count * width * lanes, bytes_accessed=2 * width * lanes, transcendentals=0
-        ),
+        cost_estimate=LIGHT,
     )(q, k, v, out_w, x, ids, down, up, lengths, valid, cache)
 
 
@@ -551,7 +516,10 @@
 def feed_first_kernel(places, n_x, n_w, *refs):
     x_refs, w_refs = refs[:n_x], refs[n_x : n_x + n_w]
     all_w, out_refs = refs[n_x + n_w], refs[n_x + n_w + 1 :]
-    assemble(places, w_refs, all_w)
+    starts = shard_starts(places, all_w.shape[1] // lax.axis_size("row"))
+    for part in range(3):
+        for ref, start in zip(w_refs, starts):
+            all_w[part, pl.ds(start, ref.shape[1]), :] = ref[part]
     down = feed(jnp.concatenate([ref[...] for ref in x_refs], axis=0), all_w)
     count = x_refs[0].shape[0]
     for i, ref in enumerate(out_refs):
@@ -568,10 +536,8 @@
         + [jax.ShapeDtypeStruct((count, width), t) for t in out_types],
         in_specs=[VMEM] * (n_x + n_w),
         out_specs=[VMEM] * (n_x + 1),
-        compiler_params=params(40),
-        cost_estimate=pl.CostEstimate(
-            flops=6 * n_x * count * width * hidden, bytes_accessed=12 * width * hidden, transcendentals=0
-        ),
+        compiler_params=params(28),
+        cost_estimate=LIGHT,
     )(*blocks, *(piece for piece, _, _ in pieces))
 
 
@@ -587,9 +553,7 @@
         in_specs=[VMEM] * 2,
         out_specs=VMEM,
         compiler_params=params(20),
-        cost_estimate=pl.CostEstimate(
-            flops=6 * count * width * hidden, bytes_accessed=6 * width * hidden, transcendentals=0
-        ),
+        cost_estimate=LIGHT,
     )(block, all_w)
 
 
@@ -616,13 +580,11 @@
     heads = window_key_value.shape[2]
 
     rank, kept = adapter_down_map.shape[2], adapter_down_map.shape[0]
-    ranks = kept * lax.axis_size("row") * rank
-    normed_attention, packed, taps = entry_call(
+    normed_attention, packed = entry_call(
         inputs,
-        attention_norm_gain,
         jnp.transpose(query_key_value_weight, (1, 0, 2)),
         output_projection,
-        filter_taps,
+        attention_norm_gain,
         jnp.transpose(adapter_down_map, (0, 2, 1)).reshape(kept * rank, width),
         adapter_up_map.reshape(kept * rank, width),
     )
@@ -649,38 +611,33 @@
     pieces = named_pieces(packed, firsts, diagonal + seconds[2:], thirds)
     blocks = [normed_attention, token_one, token_two, token_three]
     requests_here = (lengths, cache_valid_length, cache)
+    ranks = kept * rank * lax.axis_size("row")
     q, k, v, out_w, down_maps, up_maps, part_three = first_call(
-        blocks, pieces, ranks, taps, *requests_here
+        blocks, pieces, ranks, filter_taps, *requests_here
     )
     passed = swap(part_three, "col", 1)
     part_two, part_one, part_own = attend_call(
         rank, [2, 1, 0], [bf16, bf16, f32], q, k, v, out_w, normed_attention, own_ids, down_maps, up_maps, *requests_here
     )
-
-    def summed_up(passed, part_two, part_one):
-        part_two = (part_two.astype(f32) + passed.astype(f32)).astype(bf16)
-        part_two, part_one = lax.optimization_barrier((part_two, part_one))
-        return swap(part_two, "col", 2), swap(part_one, "col", 1)
-
-    passed, part_two, part_one = lax.optimization_barrier((passed, part_two, part_one))
-    got_two, got_one = summed_up(passed, part_two, part_one)
-    got_one, feed_own, feed_firsts = lax.optimization_barrier((got_one, feed_own, feed_firsts))
+    part_two = (part_two.astype(f32) + passed.astype(f32)).astype(bf16)
+    part_two, part_one = lax.optimization_barrier((part_two, part_one))
+    got_two, got_one = swap(part_two, "col", 2), swap(part_one, "col", 1)
     feed_seconds = second_hops(feed_own, *feed_firsts)
-    residual, normed_mlp = residual_call(inputs, part_own, got_one, got_two, feed_forward_gain)
+    residual, normed_mlp = residual_call(inputs, part_own, got_two, got_one, feed_forward_gain)
     token_two, token_one = swap(normed_mlp, "col", 2), swap(normed_mlp, "col", 1)
     feed_diagonal = feed_seconds[:2]
     feed_thirds = tuple(swap(piece, "row", 1) for piece in feed_diagonal)
-    token_two, token_one, feed_thirds, feed_seconds = lax.optimization_barrier(
-        (token_two, token_one, feed_thirds, feed_seconds[2:])
-    )
+    token_two, token_one = lax.optimization_barrier((token_two, token_one))
     token_three = swap(token_two, "col", 1)
-    feed_pieces = named_pieces(feed_own, feed_firsts, feed_diagonal + feed_seconds, feed_thirds)
+    feed_pieces = named_pieces(feed_own, feed_firsts, feed_seconds, feed_thirds)
     feed_w, part_two, part_one, part_own = feed_first_call(
         [token_two, token_one, normed_mlp], feed_pieces, [bf16, bf16, f32]
     )
     part_three = feed_last_call(token_three, feed_w)
     passed = swap(part_three, "col", 1)
-    got_two, got_one = summed_up(passed, part_two, part_one)
+    part_two = (part_two.astype(f32) + passed.astype(f32)).astype(bf16)
+    part_two, part_one = lax.optimization_barrier((part_two, part_one))
+    got_two, got_one = swap(part_two, "col", 2), swap(part_one, "col", 1)
     added = part_own + got_one.astype(f32) + got_two.astype(f32)
     return (residual.astype(f32) + added).astype(bf16)
 

time: 185 us -> 166 us (0.90)
  starting transfers between devices: 35.1 us -> 26.3 us
  local copies, waits for them, and re-layouts: 14.6 us -> 7.46 us
  Pallas kernels: 30.8 us -> 25.5 us
  waiting for transfers between devices: 103 us -> 105 us
    ppermute x30, starting transfers between devices: 35.1 us -> 26.3 us  [swap(): return lax.ppermute(value, axis, xor_pairs(lax.axis_size(axis), mask))]
    unnamed x48 -> x22, local copies, waits for them, and re-layouts: 8.8 us -> 1.08 us
    pallas_call x1, Pallas kernels: 10.2 us -> 5.29 us  [feed_first_call(): pl.pallas_call(functools.partial(feed_first_kernel, places, n_x, n_w), ou...]
    ppermute x30, waiting for transfers between devices: 103 us -> 105 us  [swap(): return lax.ppermute(value, axis, xor_pairs(lax.axis_size(axis), mask))]
  transfers between devices with their start and end apart: 30 -> 30, of which waited for: 23 -> 17; matrix products, arithmetic and copies ran while one was open for 3% -> 3% of each run, Pallas kernels for 14% -> 8%
where the time goes in v3:
time: 166 us
  waiting for transfers between devices  105 us (63%)
  starting transfers between devices  26.3 us (16%)
  Pallas kernels  25.5 us (15%)
  local copies, waits for them, and re-layouts  7.46 us (4%)
    ppermute x30, waiting for transfers between devices, swap(): return lax.ppermute(value, axis, xor_pairs(lax.axis_size(axis), mask))  105 us
    ppermute x30, starting transfers between devices, swap(): return lax.ppermute(value, axis, xor_pairs(lax.axis_size(axis), mask))  26.3 us
    pallas_call x1, Pallas kernels, attend_call(): pl.pallas_call(functools.partial(attend_kernel, rank, masks), out_shape=[...  7.57 us
    pallas_call x1, Pallas kernels, first_call(): pl.pallas_call(functools.partial(first_kernel, places, n_x, n_w), out_sha...  7.25 us
    pallas_call x1, Pallas kernels, feed_first_call(): pl.pallas_call(functools.partial(feed_first_kernel, places, n_x, n_w), ou...  5.29 us
    reshape x2, local copies, waits for them, and re-layouts, tuned(): cache = window_key_value.reshape(requests, 2, heads, window, HD)  4.56 us
  transfers between devices with their start and end apart: 30, of which 17 were waited for; matrix products, arithmetic and copies ran while one was open for 3% of the time, Pallas kernels for 8%

profile of v3, /device:TPU:0, one launch (start us, length us, event | category | flops | bytes accessed | tf_op | source)
XLA Modules:
  0.0 166.0 jit_solution(8182376418208065628)
XLA Ops:
  0.0 1.3 broadcast_in_dim.15.refs_3_
  1.3 2.9 %shard_map.145 = (bf16[128,1792]{1,0:T(8,128)(2,1)}, bf16[288,1792]{1,0:T(8,128)(2,1)}) custom-call(bf16[128,1792]{1,0:T(8,128)(2,1)} %x_ref.1, bf16[3,224,448]{2,1,0:T(8,128)(2,1)} %bitcast.14, bf16[448,224]{1,0:T(8,128)(2,1)} %refs_2_.1, f32[1,1792]{1,0:T(1,128)} %broadcast_in_dim.15.refs_3_, bf16[32,1792]{1,0:T(8,128)(2,1)} %bitcast.18, ...), custom_call_target="tpu_custom_call" | custom-call | flops 1 | bytes 1 | tf_op jit(solution)/shard_map/pallas_call | solution.py:276
  4.2 3.0 %collective-permute-start.2 = (bf16[288,1792]{1,0:T(8,128)(2,1)}, bf16[288,1792]{1,0:T(8,128)(2,1)S(1)}, u32[]{:S(2)}, u32[]{:S(2)}) collective-permute-start(bf16[288,1792]{1,0:T(8,128)(2,1)} %get-tuple-element.49.refs_4_), channel_id=1, source_target_pairs={{0,8},{4,12},{8,0},{12,4},{16,24},{20,28},{24,16},{28,20},{1,9},{5... | collective-permute-start | bytes 3096584 | tf_op jit(solution)/shard_map/ppermute | solution.py:322
  7.2 1.5 collective-permute-start.3
  8.7 2.6 %collective-permute-start = (bf16[128,1792]{1,0:T(8,128)(2,1)}, bf16[128,1792]{1,0:T(8,128)(2,1)S(1)}, u32[]{:S(2)}, u32[]{:S(2)}) collective-permute-start(bf16[128,1792]{1,0:T(8,128)(2,1)} %get-tuple-element.41.refs_0_.x_ref), channel_id=1, source_target_pairs={{0,2},{1,3},{2,0},{3,1},{4,6},{5,7},{6,4},{7,5},{8,10},{9,11},{10,... | collective-permute-start | bytes 1376264 | tf_op jit(solution)/shard_map/ppermute | solution.py:322
  11.3 1.6 collective-permute-start.1
  13.0 3.3 %reshape.14 = bf16[8,2,4,64,112]{4,3,2,1,0:T(8,128)(2,1)} reshape(bf16[8,2,4,7168]{3,2,1,0:T(4,128)(2,1)} %param.20) | data formatting | bytes 1835008 | tf_op jit(solution)/shard_map/reshape | solution.py:595
  16.3 1.3 copy.16
  19.1 12.4 %collective-permute-done.refs_2_ = bf16[128,1792]{1,0:T(8,128)(2,1)S(1)} collective-permute-done((bf16[128,1792]{1,0:T(8,128)(2,1)}, bf16[128,1792]{1,0:T(8,128)(2,1)S(1)}, u32[]{:S(2)}, u32[]{:S(2)}) %collective-permute-start) | collective-permute-done | bytes 458784 | tf_op jit(solution)/shard_map/ppermute | solution.py:322
  31.7 1.6 collective-permute-start.4
  33.3 1.6 collective-permute-start.5
  36.0 6.9 %collective-permute-done.4.refs_3_ = bf16[128,1792]{1,0:T(8,128)(2,1)S(1)} collective-permute-done((bf16[128,1792]{1,0:T(8,128)(2,1)S(1)}, bf16[128,1792]{1,0:T(8,128)(2,1)S(1)}, u32[]{:S(2)}, u32[]{:S(2)}) %collective-permute-start.4) | collective-permute-done | bytes 458784 | tf_op jit(solution)/shard_map/ppermute | solution.py:322
  42.9 2.8 %collective-permute-done.5.refs_7_ = bf16[144,1792]{1,0:T(8,128)(2,1)S(1)} collective-permute-done((bf16[144,1792]{1,0:T(8,128)(2,1)S(1)}, bf16[144,1792]{1,0:T(8,128)(2,1)S(1)}, u32[]{:S(2)}, u32[]{:S(2)}) %collective-permute-start.5) | collective-permute-done | bytes 516128 | tf_op jit(solution)/shard_map/ppermute | solution.py:322
  45.7 1.0 collective-permute-done.6.refs_8_
  47.2 1.4 collective-permute-done.10.refs_12_
  49.4 7.2 %shard_map.146 = (bf16[512,512]{1,0:T(8,128)(2,1)S(1)}, bf16[512,512]{1,0:T(8,128)(2,1)S(1)}, bf16[512,512]{1,0:T(8,128)(2,1)S(1)}, bf16[1792,512]{1,0:T(8,128)(...) custom-call(bf16[128,1792]{1,0:T(8,128)(2,1)S(1)} %copy-done.1, ...), custom_call_target="tpu_custom_call" | custom-call | flops 1 | bytes 1 | tf_op jit(solution)/shard_map/pallas_call | solution.py:462
  58.4 7.6 %shard_map.147 = (bf16[128,1792]{1,0:T(8,128)(2,1)S(1)}, bf16[128,1792]{1,0:T(8,128)(2,1)S(1)}, f32[128,1792]{1,0:T(8,128)S(1)}) custom-call(bf16[512,512]{1,0:T(8,128)(2,1)S(1)} %get-tuple-element.53.q_ref, bf16[512,512]{1,0:T(8,128)(2,1)S(1)} %get-tuple-element.54.k_ref, bf16[512,512]{1,0:T(8,128)(2,1)S(1)} %get-tuple-element.55.v_ref, ...), custom_call_target="tpu_custom_call" | custom-call | flops 1 | bytes 1 | tf_op jit(solution)/shard_map/pallas_call | solution.py:499
  66.0 3.3 %collective-permute-done.12 = bf16[128,1792]{1,0:T(8,128)(2,1)S(1)} collective-permute-done((bf16[128,1792]{1,0:T(8,128)(2,1)S(1)}, bf16[128,1792]{1,0:T(8,128)(2,1)S(1)}, u32[]{:S(2)}, u32[]{:S(2)}) %collective-permute-start.12) | collective-permute-done | bytes 458784 | tf_op jit(solution)/shard_map/ppermute | solution.py:322
  69.4 2.8 %collective-permute-start.13 = (bf16[128,1792]{1,0:T(8,128)(2,1)S(1)}, bf16[128,1792]{1,0:T(8,128)(2,1)S(1)}, u32[]{:S(2)}, u32[]{:S(2)}) collective-permute-start(bf16[128,1792]{1,0:T(8,128)(2,1)S(1)} %add_convert_fusion.2), channel_id=1, source_target_pairs={{0,2},{1,3},{2,0},{3,1},{4,6},{5,7},{6,4},{7,5},{8,10},{9,11},{10,... | collective-permute-start | bytes 1376264 | tf_op jit(solution)/shard_map/ppermute | solution.py:322
  72.7 19.4 %collective-permute-done.13.two_ref = bf16[128,1792]{1,0:T(8,128)(2,1)S(1)} collective-permute-done((bf16[128,1792]{1,0:T(8,128)(2,1)S(1)}, bf16[128,1792]{1,0:T(8,128)(2,1)S(1)}, u32[]{:S(2)}, u32[]{:S(2)}) %collective-permute-start.13) | collective-permute-done | bytes 458784 | tf_op jit(solution)/shard_map/ppermute | solution.py:322
  92.1 1.3 collective-permute-done.14.one_ref
  93.9 1.8 %collective-permute-start.16 = (bf16[128,1792]{1,0:T(8,128)(2,1)S(1)}, bf16[128,1792]{1,0:T(8,128)(2,1)S(1)}, u32[]{:S(2)}, u32[]{:S(2)}) collective-permute-start(bf16[128,1792]{1,0:T(8,128)(2,1)S(1)} %get-tuple-element.67.refs_2_), channel_id=1, source_target_pairs={{0,1},{1,0},{2,3},{3,2},{4,5},{5,4},{6,7},{7,6},{8,9},{9,8},{10,11... | collective-permute-start | bytes 1376264 | tf_op jit(solution)/shard_map/ppermute | solution.py:322
  95.7 1.4 collective-permute-start.19
  97.8 17.5 %collective-permute-done.15.refs_0_ = bf16[128,1792]{1,0:T(8,128)(2,1)S(1)} collective-permute-done((bf16[128,1792]{1,0:T(8,128)(2,1)S(1)}, bf16[128,1792]{1,0:T(8,128)(2,1)S(1)}, u32[]{:S(2)}, u32[]{:S(2)}) %collective-permute-start.15) | collective-permute-done | bytes 458784 | tf_op jit(solution)/shard_map/ppermute | solution.py:322
  116.4 5.0 %collective-permute-done.24.refs_11_ = bf16[3,112,1024]{2,1,0:T(8,128)(2,1)S(1)} collective-permute-done((bf16[3,112,1024]{2,1,0:T(8,128)(2,1)S(1)}, bf16[3,112,1024]{2,1,0:T(8,128)(2,1)S(1)}, u32[]{:S(2)}, u32[]{:S(2)}) %collective-permute-start.24) | collective-permute-done | bytes 688160 | tf_op jit(solution)/shard_map/ppermute | solution.py:322
  122.4 5.3 %shard_map.149 = (bf16[3,1792,1024]{2,1,0:T(8,128)(2,1)S(1)}, bf16[128,1792]{1,0:T(8,128)(2,1)S(1)}, bf16[128,1792]{1,0:T(8,128)(2,1)S(1)}, f32[128,1792]{1,0:T(8,128)S(1)}) custom-call(bf16[128,1792]{1,0:T(8,128)(2,1)S(1)} %collective-permute-done.15.refs_0_, bf16[128,1792]{1,0:T(8,128)(2,1)S(1)} %collective-permute-done.16.refs_1_, ...), custom_call_target="tpu_custom_call" | custom-call | flops 1 | bytes 1 | tf_op jit(solution)/shard_map/pallas_call | solution.py:533
  127.7 1.2 collective-permute-done.26.x_ref
  128.9 2.1 %shard_map.150 = bf16[128,1792]{1,0:T(8,128)(2,1)S(1)} custom-call(bf16[128,1792]{1,0:T(8,128)(2,1)S(1)} %collective-permute-done.26.x_ref, bf16[3,1792,1024]{2,1,0:T(8,128)(2,1)S(1)} %get-tuple-element.73.all_w), custom_call_target="tpu_custom_call" | custom-call | flops 1 | bytes 1 | tf_op jit(solution)/shard_map/pallas_call | solution.py:550
  131.3 11.4 %collective-permute-done.27 = bf16[128,1792]{1,0:T(8,128)(2,1)S(1)} collective-permute-done((bf16[128,1792]{1,0:T(8,128)(2,1)S(1)}, bf16[128,1792]{1,0:T(8,128)(2,1)S(1)}, u32[]{:S(2)}, u32[]{:S(2)}) %collective-permute-start.27) | collective-permute-done | bytes 458784 | tf_op jit(solution)/shard_map/ppermute | solution.py:322
  143.5 1.8 %collective-permute-start.29 = (bf16[128,1792]{1,0:T(8,128)(2,1)S(1)}, bf16[128,1792]{1,0:T(8,128)(2,1)S(1)}, u32[]{:S(2)}, u32[]{:S(2)}) collective-permute-start(bf16[128,1792]{1,0:T(8,128)(2,1)S(1)} %add_convert_fusion.1), channel_id=1, source_target_pairs={{0,2},{1,3},{2,0},{3,1},{4,6},{5,7},{6,4},{7,5},{8,10},{9,11},{10,... | collective-permute-start | bytes 1376264 | tf_op jit(solution)/shard_map/ppermute | solution.py:322
  145.3 17.7 %collective-permute-done.28 = bf16[128,1792]{1,0:T(8,128)(2,1)S(1)} collective-permute-done((bf16[128,1792]{1,0:T(8,128)(2,1)S(1)}, bf16[128,1792]{1,0:T(8,128)(2,1)S(1)}, u32[]{:S(2)}, u32[]{:S(2)}) %collective-permute-start.28) | collective-permute-done | bytes 458784 | tf_op jit(solution)/shard_map/ppermute | solution.py:322
  163.0 2.1 %collective-permute-done.29 = bf16[128,1792]{1,0:T(8,128)(2,1)S(1)} collective-permute-done((bf16[128,1792]{1,0:T(8,128)(2,1)S(1)}, bf16[128,1792]{1,0:T(8,128)(2,1)S(1)}, u32[]{:S(2)}, u32[]{:S(2)}) %collective-permute-start.29) | collective-permute-done | bytes 458784 | tf_op jit(solution)/shard_map/ppermute | solution.py:322
  (71 shorter events, 11.8 us)
Async XLA Ops:
  4.2 27.5 %collective-permute-start.2 = (bf16[288,1792]{1,0:T(8,128)(2,1)}, bf16[288,1792]{1,0:T(8,128)(2,1)S(1)}, u32[]{:S(2)}, u32[]{:S(2)}) collective-permute-start(bf16[288,1792]{1,0:T(8,128)(2,1)} %get-tuple-element.49.refs_4_), channel_id=1, source_target_pairs={{0,8},{4,12},{8,0},{12,4},{16,24},{20,28},{24,16},{28,20},{1,9},{5... | collective-permute-start | bytes 3096584 | tf_op jit(solution)/shard_map/ppermute | solution.py:322
  7.2 24.5 %collective-permute-start.3 = (bf16[288,1792]{1,0:T(8,128)(2,1)}, bf16[288,1792]{1,0:T(8,128)(2,1)S(1)}, u32[]{:S(2)}, u32[]{:S(2)}) collective-permute-start(bf16[288,1792]{1,0:T(8,128)(2,1)} %get-tuple-element.49.refs_4_), channel_id=1, source_target_pairs={{0,16},{4,20},{8,24},{12,28},{16,0},{20,4},{24,8},{28,12},{1,17},{... | collective-permute-start | bytes 3096584 | tf_op jit(solution)/shard_map/ppermute | solution.py:322
  8.7 22.7 %collective-permute-start = (bf16[128,1792]{1,0:T(8,128)(2,1)}, bf16[128,1792]{1,0:T(8,128)(2,1)S(1)}, u32[]{:S(2)}, u32[]{:S(2)}) collective-permute-start(bf16[128,1792]{1,0:T(8,128)(2,1)} %get-tuple-element.41.refs_0_.x_ref), channel_id=1, source_target_pairs={{0,2},{1,3},{2,0},{3,1},{4,6},{5,7},{6,4},{7,5},{8,10},{9,11},{10,... | collective-permute-start | bytes 1376264 | tf_op jit(solution)/shard_map/ppermute | solution.py:322
  11.3 20.3 %collective-permute-start.1 = (bf16[128,1792]{1,0:T(8,128)(2,1)}, bf16[128,1792]{1,0:T(8,128)(2,1)S(1)}, u32[]{:S(2)}, u32[]{:S(2)}) collective-permute-start(bf16[128,1792]{1,0:T(8,128)(2,1)} %get-tuple-element.41.refs_0_.x_ref), channel_id=1, source_target_pairs={{0,1},{1,0},{2,3},{3,2},{4,5},{5,4},{6,7},{7,6},{8,9},{9,8},{10,11... | collective-permute-start | bytes 1376264 | tf_op jit(solution)/shard_map/ppermute | solution.py:322
  19.0 30.3 %copy-start.1 = (bf16[128,1792]{1,0:T(8,128)(2,1)S(1)}, bf16[128,1792]{1,0:T(8,128)(2,1)}, u32[]{:S(2)}) copy-start(bf16[128,1792]{1,0:T(8,128)(2,1)} %get-tuple-element.41.refs_0_.x_ref) | copy-start | bytes 1376260
  19.0 30.3 %copy-start.4 = (f32[3,2,448]{2,1,0:T(2,128)S(1)}, f32[3,2,448]{2,1,0:T(2,128)}, u32[]{:S(2)}) copy-start(f32[3,2,448]{2,1,0:T(2,128)} %refs_14_.1) | copy-start | bytes 32260
  31.7 11.2 %collective-permute-start.4 = (bf16[128,1792]{1,0:T(8,128)(2,1)S(1)}, bf16[128,1792]{1,0:T(8,128)(2,1)S(1)}, u32[]{:S(2)}, u32[]{:S(2)}) collective-permute-start(bf16[128,1792]{1,0:T(8,128)(2,1)S(1)} %collective-permute-done.refs_2_), channel_id=1, source_target_pairs={{0,1},{1,0},{2,3},{3,2},{4,5},{5,4},{6,7},{7,6},{8,9},{9,8},{10,11... | collective-permute-start | bytes 1376264 | tf_op jit(solution)/shard_map/ppermute | solution.py:322
  33.3 12.4 %collective-permute-start.5 = (bf16[144,1792]{1,0:T(8,128)(2,1)S(1)}, bf16[144,1792]{1,0:T(8,128)(2,1)S(1)}, u32[]{:S(2)}, u32[]{:S(2)}) collective-permute-start(bf16[144,1792]{1,0:T(8,128)(2,1)S(1)} %slice.12), channel_id=1, source_target_pairs={{0,16},{4,20},{8,24},{12,28},{16,0},{20,4},{24,8},{28,12},{1,17},{... | collective-permute-start | bytes 1548296 | tf_op jit(solution)/shard_map/ppermute | solution.py:322
  34.9 11.8 %collective-permute-start.6 = (bf16[144,1792]{1,0:T(8,128)(2,1)S(1)}, bf16[144,1792]{1,0:T(8,128)(2,1)S(1)}, u32[]{:S(2)}, u32[]{:S(2)}) collective-permute-start(bf16[144,1792]{1,0:T(8,128)(2,1)S(1)} %slice.13), channel_id=1, source_target_pairs={{0,8},{4,12},{8,0},{12,4},{16,24},{20,28},{24,16},{28,20},{1,9},{5... | collective-permute-start | bytes 1548296 | tf_op jit(solution)/shard_map/ppermute | solution.py:322
  35.5 13.8 %collective-permute-start.8 = (bf16[288,1792]{1,0:T(8,128)(2,1)S(1)}, bf16[288,1792]{1,0:T(8,128)(2,1)S(1)}, u32[]{:S(2)}, u32[]{:S(2)}) collective-permute-start(bf16[288,1792]{1,0:T(8,128)(2,1)S(1)} %collective-permute-done.2.refs_5_), channel_id=1, source_target_pairs={{0,4},{4,0},{8,12},{12,8},{16,20},{20,16},{24,28},{28,24},{1,5},{5... | collective-permute-start | bytes 3096584 | tf_op jit(solution)/shard_map/ppermute | solution.py:322
  35.5 13.8 %collective-permute-start.9 = (bf16[288,1792]{1,0:T(8,128)(2,1)S(1)}, bf16[288,1792]{1,0:T(8,128)(2,1)S(1)}, u32[]{:S(2)}, u32[]{:S(2)}) collective-permute-start(bf16[288,1792]{1,0:T(8,128)(2,1)S(1)} %collective-permute-done.3.refs_6_), channel_id=1, source_target_pairs={{0,4},{4,0},{8,12},{12,8},{16,20},{20,16},{24,28},{28,24},{1,5},{5... | collective-permute-start | bytes 3096584 | tf_op jit(solution)/shard_map/ppermute | solution.py:322
  42.9 6.4 %collective-permute-start.7 = (bf16[288,1792]{1,0:T(8,128)(2,1)S(1)}, bf16[288,1792]{1,0:T(8,128)(2,1)S(1)}, u32[]{:S(2)}, u32[]{:S(2)}) collective-permute-start(bf16[288,1792]{1,0:T(8,128)(2,1)S(1)} %copy-done.3), channel_id=1, source_target_pairs={{0,4},{4,0},{8,12},{12,8},{16,20},{20,16},{24,28},{28,24},{1,5},{5... | collective-permute-start | bytes 3096584 | tf_op jit(solution)/shard_map/ppermute | solution.py:322
  46.7 1.9 %collective-permute-start.10 = (bf16[144,1792]{1,0:T(8,128)(2,1)S(1)}, bf16[144,1792]{1,0:T(8,128)(2,1)S(1)}, u32[]{:S(2)}, u32[]{:S(2)}) collective-permute-start(bf16[144,1792]{1,0:T(8,128)(2,1)S(1)} %collective-permute-done.5.refs_7_), channel_id=1, source_target_pairs={{0,4},{4,0},{8,12},{12,8},{16,20},{20,16},{24,28},{28,24},{1,5},{5... | collective-permute-start | bytes 1548296 | tf_op jit(solution)/shard_map/ppermute | solution.py:322
  46.7 2.6 %collective-permute-start.11 = (bf16[144,1792]{1,0:T(8,128)(2,1)S(1)}, bf16[144,1792]{1,0:T(8,128)(2,1)S(1)}, u32[]{:S(2)}, u32[]{:S(2)}) collective-permute-start(bf16[144,1792]{1,0:T(8,128)(2,1)S(1)} %collective-permute-done.6.refs_8_), channel_id=1, source_target_pairs={{0,4},{4,0},{8,12},{12,8},{16,20},{20,16},{24,28},{28,24},{1,5},{5... | collective-permute-start | bytes 1548296 | tf_op jit(solution)/shard_map/ppermute | solution.py:322
  56.7 12.6 %collective-permute-start.12 = (bf16[128,1792]{1,0:T(8,128)(2,1)S(1)}, bf16[128,1792]{1,0:T(8,128)(2,1)S(1)}, u32[]{:S(2)}, u32[]{:S(2)}) collective-permute-start(bf16[128,1792]{1,0:T(8,128)(2,1)S(1)} %get-tuple-element.62), channel_id=1, source_target_pairs={{0,1},{1,0},{2,3},{3,2},{4,5},{5,4},{6,7},{7,6},{8,9},{9,8},{10,11... | collective-permute-start | bytes 1376264 | tf_op jit(solution)/shard_map/ppermute | solution.py:322
  57.2 38.5 %collective-permute-start.17 = (bf16[3,224,1024]{2,1,0:T(8,128)(2,1)S(1)}, bf16[3,224,1024]{2,1,0:T(8,128)(2,1)S(1)}, u32[]{:S(2)}, u32[]{:S(2)}) collective-permute-start(bf16[3,224,1024]{2,1,0:T(8,128)(2,1)S(1)} %pad_maximum_fusion.refs_3_), channel_id=1, source_target_pairs={{0,8},{4,12},{8,0},{12,4},{16,24},{20,28},{24,16},{28,20},{1,9},{5... | collective-permute-start | bytes 4128776 | tf_op jit(solution)/shard_map/ppermute | solution.py:322
  57.8 39.4 %collective-permute-start.18 = (bf16[3,224,1024]{2,1,0:T(8,128)(2,1)S(1)}, bf16[3,224,1024]{2,1,0:T(8,128)(2,1)S(1)}, u32[]{:S(2)}, u32[]{:S(2)}) collective-permute-start(bf16[3,224,1024]{2,1,0:T(8,128)(2,1)S(1)} %pad_maximum_fusion.refs_3_), channel_id=1, source_target_pairs={{0,16},{4,20},{8,24},{12,28},{16,0},{20,4},{24,8},{28,12},{1,17},{... | collective-permute-start | bytes 4128776 | tf_op jit(solution)/shard_map/ppermute | solution.py:322
  69.4 22.7 %collective-permute-start.13 = (bf16[128,1792]{1,0:T(8,128)(2,1)S(1)}, bf16[128,1792]{1,0:T(8,128)(2,1)S(1)}, u32[]{:S(2)}, u32[]{:S(2)}) collective-permute-start(bf16[128,1792]{1,0:T(8,128)(2,1)S(1)} %add_convert_fusion.2), channel_id=1, source_target_pairs={{0,2},{1,3},{2,0},{3,1},{4,6},{5,7},{6,4},{7,5},{8,10},{9,11},{10,... | collective-permute-start | bytes 1376264 | tf_op jit(solution)/shard_map/ppermute | solution.py:322
  72.2 21.2 %collective-permute-start.14 = (bf16[128,1792]{1,0:T(8,128)(2,1)S(1)}, bf16[128,1792]{1,0:T(8,128)(2,1)S(1)}, u32[]{:S(2)}, u32[]{:S(2)}) collective-permute-start(bf16[128,1792]{1,0:T(8,128)(2,1)S(1)} %get-tuple-element.65), channel_id=1, source_target_pairs={{0,1},{1,0},{2,3},{3,2},{4,5},{5,4},{6,7},{7,6},{8,9},{9,8},{10,11... | collective-permute-start | bytes 1376264 | tf_op jit(solution)/shard_map/ppermute | solution.py:322
  93.8 21.5 %collective-permute-start.15 = (bf16[128,1792]{1,0:T(8,128)(2,1)S(1)}, bf16[128,1792]{1,0:T(8,128)(2,1)S(1)}, u32[]{:S(2)}, u32[]{:S(2)}) collective-permute-start(bf16[128,1792]{1,0:T(8,128)(2,1)S(1)} %get-tuple-element.67.refs_2_), channel_id=1, source_target_pairs={{0,2},{1,3},{2,0},{3,1},{4,6},{5,7},{6,4},{7,5},{8,10},{9,11},{10,... | collective-permute-start | bytes 1376264 | tf_op jit(solution)/shard_map/ppermute | solution.py:322
  93.9 21.4 %collective-permute-start.16 = (bf16[128,1792]{1,0:T(8,128)(2,1)S(1)}, bf16[128,1792]{1,0:T(8,128)(2,1)S(1)}, u32[]{:S(2)}, u32[]{:S(2)}) collective-permute-start(bf16[128,1792]{1,0:T(8,128)(2,1)S(1)} %get-tuple-element.67.refs_2_), channel_id=1, source_target_pairs={{0,1},{1,0},{2,3},{3,2},{4,5},{5,4},{6,7},{7,6},{8,9},{9,8},{10,11... | collective-permute-start | bytes 1376264 | tf_op jit(solution)/shard_map/ppermute | solution.py:322
  95.7 20.7 %collective-permute-start.21 = (bf16[3,224,1024]{2,1,0:T(8,128)(2,1)S(1)}, bf16[3,224,1024]{2,1,0:T(8,128)(2,1)S(1)}, u32[]{:S(2)}, u32[]{:S(2)}) collective-permute-start(bf16[3,224,1024]{2,1,0:T(8,128)(2,1)S(1)} %pad_maximum_fusion.refs_3_), channel_id=1, source_target_pairs={{0,4},{4,0},{8,12},{12,8},{16,20},{20,16},{24,28},{28,24},{1,5},{5... | collective-permute-start | bytes 4128776 | tf_op jit(solution)/shard_map/ppermute | solution.py:322
  95.7 20.1 %collective-permute-start.19 = (bf16[3,112,1024]{2,1,0:T(8,128)(2,1)S(1)}, bf16[3,112,1024]{2,1,0:T(8,128)(2,1)S(1)}, u32[]{:S(2)}, u32[]{:S(2)}) collective-permute-start(bf16[3,112,1024]{2,1,0:T(8,128)(2,1)S(1)} %slice.16), channel_id=1, source_target_pairs={{0,16},{4,20},{8,24},{12,28},{16,0},{20,4},{24,8},{28,12},{1,17},{... | collective-permute-start | bytes 2064392 | tf_op jit(solution)/shard_map/ppermute | solution.py:322
  97.2 18.7 %collective-permute-start.20 = (bf16[3,112,1024]{2,1,0:T(8,128)(2,1)S(1)}, bf16[3,112,1024]{2,1,0:T(8,128)(2,1)S(1)}, u32[]{:S(2)}, u32[]{:S(2)}) collective-permute-start(bf16[3,112,1024]{2,1,0:T(8,128)(2,1)S(1)} %slice.17), channel_id=1, source_target_pairs={{0,8},{4,12},{8,0},{12,4},{16,24},{20,28},{24,16},{28,20},{1,9},{5... | collective-permute-start | bytes 2064392 | tf_op jit(solution)/shard_map/ppermute | solution.py:322
  115.3 7.1 %collective-permute-start.22 = (bf16[3,224,1024]{2,1,0:T(8,128)(2,1)S(1)}, bf16[3,224,1024]{2,1,0:T(8,128)(2,1)S(1)}, u32[]{:S(2)}, u32[]{:S(2)}) collective-permute-start(bf16[3,224,1024]{2,1,0:T(8,128)(2,1)S(1)} %collective-permute-done.17.refs_4_), channel_id=1, source_target_pairs={{0,4},{4,0},{8,12},{12,8},{16,20},{20,16},{24,28},{28,24},{1,5},{5... | collective-permute-start | bytes 4128776 | tf_op jit(solution)/shard_map/ppermute | solution.py:322
  115.3 7.1 %collective-permute-start.23 = (bf16[3,224,1024]{2,1,0:T(8,128)(2,1)S(1)}, bf16[3,224,1024]{2,1,0:T(8,128)(2,1)S(1)}, u32[]{:S(2)}, u32[]{:S(2)}) collective-permute-start(bf16[3,224,1024]{2,1,0:T(8,128)(2,1)S(1)} %collective-permute-done.18.refs_5_), channel_id=1, source_target_pairs={{0,4},{4,0},{8,12},{12,8},{16,20},{20,16},{24,28},{28,24},{1,5},{5... | collective-permute-start | bytes 4128776 | tf_op jit(solution)/shard_map/ppermute | solution.py:322
  115.8 5.6 %collective-permute-start.24 = (bf16[3,112,1024]{2,1,0:T(8,128)(2,1)S(1)}, bf16[3,112,1024]{2,1,0:T(8,128)(2,1)S(1)}, u32[]{:S(2)}, u32[]{:S(2)}) collective-permute-start(bf16[3,112,1024]{2,1,0:T(8,128)(2,1)S(1)} %collective-permute-done.19.refs_6_), channel_id=1, source_target_pairs={{0,4},{4,0},{8,12},{12,8},{16,20},{20,16},{24,28},{28,24},{1,5},{5... | collective-permute-start | bytes 2064392 | tf_op jit(solution)/shard_map/ppermute | solution.py:322
  115.9 6.5 %collective-permute-start.25 = (bf16[3,112,1024]{2,1,0:T(8,128)(2,1)S(1)}, bf16[3,112,1024]{2,1,0:T(8,128)(2,1)S(1)}, u32[]{:S(2)}, u32[]{:S(2)}) collective-permute-start(bf16[3,112,1024]{2,1,0:T(8,128)(2,1)S(1)} %collective-permute-done.20.refs_7_), channel_id=1, source_target_pairs={{0,4},{4,0},{8,12},{12,8},{16,20},{20,16},{24,28},{28,24},{1,5},{5... | collective-permute-start | bytes 2064392 | tf_op jit(solution)/shard_map/ppermute | solution.py:322
  116.4 12.5 %collective-permute-start.26 = (bf16[128,1792]{1,0:T(8,128)(2,1)S(1)}, bf16[128,1792]{1,0:T(8,128)(2,1)S(1)}, u32[]{:S(2)}, u32[]{:S(2)}) collective-permute-start(bf16[128,1792]{1,0:T(8,128)(2,1)S(1)} %collective-permute-done.15.refs_0_), channel_id=1, source_target_pairs={{0,1},{1,0},{2,3},{3,2},{4,5},{5,4},{6,7},{7,6},{8,9},{9,8},{10,11... | collective-permute-start | bytes 1376264 | tf_op jit(solution)/shard_map/ppermute | solution.py:322
  131.0 11.7 %collective-permute-start.27 = (bf16[128,1792]{1,0:T(8,128)(2,1)S(1)}, bf16[128,1792]{1,0:T(8,128)(2,1)S(1)}, u32[]{:S(2)}, u32[]{:S(2)}) collective-permute-start(bf16[128,1792]{1,0:T(8,128)(2,1)S(1)} %shard_map.150), channel_id=1, source_target_pairs={{0,1},{1,0},{2,3},{3,2},{4,5},{5,4},{6,7},{7,6},{8,9},{9,8},{10,11... | collective-permute-start | bytes 1376264 | tf_op jit(solution)/shard_map/ppermute | solution.py:322
  142.8 20.2 %collective-permute-start.28 = (bf16[128,1792]{1,0:T(8,128)(2,1)S(1)}, bf16[128,1792]{1,0:T(8,128)(2,1)S(1)}, u32[]{:S(2)}, u32[]{:S(2)}) collective-permute-start(bf16[128,1792]{1,0:T(8,128)(2,1)S(1)} %get-tuple-element.75), channel_id=1, source_target_pairs={{0,1},{1,0},{2,3},{3,2},{4,5},{5,4},{6,7},{7,6},{8,9},{9,8},{10,11... | collective-permute-start | bytes 1376264 | tf_op jit(solution)/shard_map/ppermute | solution.py:322
  143.5 21.6 %collective-permute-start.29 = (bf16[128,1792]{1,0:T(8,128)(2,1)S(1)}, bf16[128,1792]{1,0:T(8,128)(2,1)S(1)}, u32[]{:S(2)}, u32[]{:S(2)}) collective-permute-start(bf16[128,1792]{1,0:T(8,128)(2,1)S(1)} %add_convert_fusion.1), channel_id=1, source_target_pairs={{0,2},{1,3},{2,0},{3,1},{4,6},{5,7},{6,4},{7,5},{8,10},{9,11},{10,... | collective-permute-start | bytes 1376264 | tf_op jit(solution)/shard_map/ppermute | solution.py:322
  (9 other events, 135.0 us)

commit v4 on v3

--- a/solution.py
+++ b/solution.py
@@ -244,9 +244,9 @@
 NT = (((1,), (1,)), ((), ()))
 
 
-def normed(values, gain_ref):
+def normed(values, gain):
     mean_square = jnp.mean(values * values, axis=-1, keepdims=True)
-    return (values * lax.rsqrt(mean_square + epsilon) * gain_ref[...]).astype(jnp.bfloat16)
+    return (values * lax.rsqrt(mean_square + epsilon) * gain).astype(jnp.bfloat16)
 
 
 def entry_kernel(*refs):
@@ -262,7 +262,7 @@
     rows, part, ranks = qkv_ref.shape[1], qkv_ref.shape[2], down_ref.shape[0]
     for load in loads:
         load.wait()
-    normed_ref[...] = normed(x_ref[...].astype(jnp.float32), gain_ref)
+    normed_ref[...] = normed(x_ref[...].astype(jnp.float32), gain_ref[...][None, :])
     for place, which in enumerate((1, 0, 2)):
         packed_ref[:rows, place * part : (place + 1) * part] = qkv_ref[which]
     out_rows = jnp.transpose(out_ref[...].astype(jnp.float32)).astype(jnp.bfloat16)
@@ -272,7 +272,7 @@
 
 
 def entry_call(rows, qkv, out, gain, down, up):
-    sources = (rows, qkv, out, gain[None, :], down, up)
+    sources = (rows, qkv, out, gain, down, up)
     return pl.pallas_call(
         entry_kernel,
         out_shape=[
@@ -292,7 +292,7 @@
     total = own_ref[...] + one_ref[...].astype(jnp.float32) + two_ref[...].astype(jnp.float32)
     residual = (x_ref[...].astype(jnp.float32) + total).astype(jnp.bfloat16)
     residual_ref[...] = residual
-    normed_ref[...] = normed(residual.astype(jnp.float32), gain_ref)
+    normed_ref[...] = normed(residual.astype(jnp.float32), gain_ref[...])
 
 
 def residual_call(rows, own, two, one, gain):
@@ -355,7 +355,7 @@
     return place, segment, first
 
 
-def attend_block(mask, count, lengths_ref, valid_ref, q_ref, k_ref, v_ref, cache_ref):
+def attend_block(mask, count, base, lengths_ref, valid_ref, q_ref, k_ref, v_ref, cache_ref):
     col = lax.axis_index("col")
     _, heads, slots, lanes = cache_ref.shape
     requests = valid_ref.shape[0]
@@ -376,11 +376,11 @@
     within = jnp.where(within >= oldest, within, -1)
     cache_mask = (owner == segment) & (within > place - first)
     outs = []
+    own_rows = pl.ds(pl.multiple_of(begin - base, count), count)
+    key_rows = pl.ds(pl.multiple_of(key_begin - base, window), key_count)
     for h in range(heads):
         cols = slice(h * lanes, (h + 1) * lanes)
-        q = q_ref[pl.ds(begin, count), cols]
-        k = k_ref[pl.ds(key_begin, key_count), cols]
-        v = v_ref[pl.ds(key_begin, key_count), cols]
+        q, k, v = q_ref[own_rows, cols], k_ref[key_rows, cols], v_ref[key_rows, cols]
         local = lax.dot_general(q, k, NT, preferred_element_type=jnp.float32)
         cached = lax.dot_general(q, cache_ref[0, h], NT, preferred_element_type=jnp.float32)
         local = jnp.where(local_mask, local * scale, -jnp.inf)
@@ -400,15 +400,41 @@
     return jnp.concatenate([blank] + outs, axis=1)
 
 
+def mix_rows(x, base, w_ref, taps_ref, lengths_ref, q_ref, k_ref, v_ref, padded):
+    rows, part = x.shape[0], taps_ref.shape[2]
+    padded[0:8, :] = jnp.zeros((8, part), jnp.float32)
+    place, _, first = request_columns(lengths_ref, base, rows)
+    inside = place - first
+    mixed = jnp.dot(x, w_ref[...], preferred_element_type=jnp.float32)
+
+    def convolved(raw, which):
+        padded[8:, :] = raw
+        running = taps_ref[0, which : which + 1, :] * raw
+        for offset in range(1, taps_ref.shape[0]):
+            moved = padded[8 - offset : 8 - offset + rows, :]
+            tap = taps_ref[offset, which : which + 1, :]
+            running = running + jnp.where(inside >= offset, tap * moved, 0.0)
+        return running
+
+    def store_heads(ref, value):
+        blank = jnp.zeros((rows, LANES - HD), jnp.bfloat16)
+        for h in range(part // HD):
+            ref[:, h * LANES : h * LANES + HD] = value[:, h * HD : (h + 1) * HD].astype(jnp.bfloat16)
+            ref[:, h * LANES + HD : (h + 1) * LANES] = blank
+
+    store_heads(k_ref, convolved(mixed[:, :part], 0))
+    store_heads(q_ref, mixed[:, part : 2 * part])
+    raw_values = mixed[:, 2 * part : 3 * part]
+    store_heads(v_ref, raw_values * jax.nn.sigmoid(convolved(raw_values, 1)))
+
+
 def first_kernel(places, n_x, n_w, *refs):
     x_refs, w_refs = refs[:n_x], refs[n_x : n_x + n_w]
     taps_ref, lengths_ref, valid_ref, cache_ref = refs[n_x + n_w : n_x + n_w + 4]
-    q_ref, k_ref, v_ref, out_w, down_ref, up_ref, part_ref = refs[n_x + n_w + 4 : n_x + n_w + 11]
-    x_all, w_all, padded = refs[n_x + n_w + 11 :]
+    x_all, w_all, out_w, down_ref, up_ref, part_ref, q_ref, k_ref, v_ref, padded = refs[n_x + n_w + 4 :]
     col = lax.axis_index("col")
-    count, (tokens, width) = x_refs[0].shape[0], x_all.shape
-    part, lanes = taps_ref.shape[2], q_ref.shape[1]
-    mixed_lanes = w_all.shape[1]
+    count, width = x_refs[0].shape
+    lanes, mixed_lanes = out_w.shape[1], w_all.shape[1]
     for i, ref in enumerate(x_refs):
         x_all[pl.ds(pl.multiple_of((col ^ i) * count, 16), count), :] = ref[...]
     shard = width // lax.axis_size("row")
@@ -422,31 +448,12 @@
             at = pl.multiple_of((lax.axis_index("row") ^ mask) * ranks, 16)
             down_ref[pl.ds(at, ranks), :] = ref[rows : rows + ranks, :]
             up_ref[pl.ds(at, ranks), :] = ref[rows + ranks :, :]
-    padded[0:8, :] = jnp.zeros((8, part), jnp.float32)
-    place, _, first = request_columns(lengths_ref, 0, tokens)
-    inside = place - first
-    mixed = jnp.dot(x_all[...], w_all[...], preferred_element_type=jnp.float32)
-
-    def convolved(raw, which):
-        padded[8:, :] = raw
-        running = taps_ref[0, which : which + 1, :] * raw
-        for offset in range(1, taps_ref.shape[0]):
-            moved = padded[8 - offset : 8 - offset + tokens, :]
-            tap = taps_ref[offset, which : which + 1, :]
-            running = running + jnp.where(inside >= offset, tap * moved, 0.0)
-        return running
-
-    def store_heads(ref, value):
-        blank = jnp.zeros((tokens, LANES - HD), jnp.bfloat16)
-        for h in range(part // HD):
-            ref[:, h * LANES : h * LANES + HD] = value[:, h * HD : (h + 1) * HD].astype(jnp.bfloat16)
-            ref[:, h * LANES + HD : (h + 1) * LANES] = blank
-
-    store_heads(k_ref, convolved(mixed[:, :part], 0))
-    store_heads(q_ref, mixed[:, part : 2 * part])
-    raw_values = mixed[:, 2 * part : 3 * part]
-    store_heads(v_ref, raw_values * jax.nn.sigmoid(convolved(raw_values, 1)))
-    attended = attend_block(n_x - 1, count, lengths_ref, valid_ref, q_ref, k_ref, v_ref, cache_ref)
+    base = pl.multiple_of(jnp.maximum((col ^ (n_x - 1)) * count - count, 0), count)
+    x = x_all[pl.ds(base, 2 * count), :]
+    mix_rows(x, base, w_all, taps_ref, lengths_ref, q_ref, k_ref, v_ref, padded)
+    attended = attend_block(
+        n_x - 1, count, base, lengths_ref, valid_ref, q_ref, k_ref, v_ref, cache_ref
+    )
     part_ref[...] = lax.dot_general(
         attended, out_w[...], NT, preferred_element_type=jnp.float32
     ).astype(jnp.bfloat16)
@@ -458,49 +465,62 @@
     lanes = part // HD * LANES
     mixed_lanes = -(-3 * part // LANES) * LANES
     places = [(mask, first) for _, mask, first in pieces]
-    one = jax.ShapeDtypeStruct((tokens, lanes), jnp.bfloat16)
+    shapes = [(tokens, width), (width, mixed_lanes), (width, lanes), (ranks, width), (ranks, width), (count, width)]
     return pl.pallas_call(
         functools.partial(first_kernel, places, n_x, n_w),
-        out_shape=[
-            one,
-            one,
-            one,
-            jax.ShapeDtypeStruct((width, lanes), jnp.bfloat16),
-            jax.ShapeDtypeStruct((ranks, width), jnp.bfloat16),
-            jax.ShapeDtypeStruct((ranks, width), jnp.bfloat16),
-            jax.ShapeDtypeStruct((count, width), jnp.bfloat16),
-        ],
+        out_shape=[pltpu.VMEM(shape, jnp.bfloat16) for shape in shapes[:3]]
+        + [jax.ShapeDtypeStruct(shape, jnp.bfloat16) for shape in shapes[3:]],
         in_specs=[VMEM] * (n_x + n_w + 1) + [SMEM, SMEM, VMEM],
-        out_specs=[VMEM] * 7,
-        scratch_shapes=[
-            pltpu.VMEM((tokens, width), jnp.bfloat16),
-            pltpu.VMEM((width, mixed_lanes), jnp.bfloat16),
-            pltpu.VMEM((tokens + 8, part), jnp.float32),
-        ],
-        compiler_params=params(36),
+        out_specs=[VMEM] * len(shapes),
+        scratch_shapes=[pltpu.VMEM((2 * count, lanes), jnp.bfloat16)] * 3
+        + [pltpu.VMEM((2 * count + 8, part), jnp.float32)],
+        compiler_params=params(28),
         cost_estimate=LIGHT,
     )(*blocks, *(piece for piece, _, _ in pieces), taps, lengths, valid, cache)
 
 
-def attend_kernel(rank, masks, q_ref, k_ref, v_ref, out_w, x_ref, ids_ref, down_ref, up_ref, *refs):
-    lengths_ref, valid_ref, cache_ref = refs[:3]
-    for mask, out_ref in zip(masks, refs[3:]):
+def rest_kernel(masks, x_all, w_all, out_w, taps_ref, lengths_ref, valid_ref, cache_ref, *refs):
+    q_ref, k_ref, v_ref = refs[:3]
+    out_refs, padded = refs[3:-1], refs[-1]
+    mix_rows(x_all[...], 0, w_all, taps_ref, lengths_ref, q_ref, k_ref, v_ref, padded)
+    for mask, out_ref in zip(masks, out_refs):
         attended = attend_block(
-            mask, out_ref.shape[0], lengths_ref, valid_ref, q_ref, k_ref, v_ref, cache_ref
+            mask, out_ref.shape[0], 0, lengths_ref, valid_ref, q_ref, k_ref, v_ref, cache_ref
         )
-        part = lax.dot_general(attended, out_w[...], NT, preferred_element_type=jnp.float32)
-        if mask == 0:
-            part = part + adapter_term(x_ref, ids_ref, down_ref, up_ref, rank).astype(jnp.float32)
-        out_ref[...] = part.astype(out_ref.dtype)
-
-
-def attend_call(rank, masks, out_types, q, k, v, out_w, x, ids, down, up, lengths, valid, cache):
-    count, width = x.shape
+        out_ref[...] = lax.dot_general(
+            attended, out_w[...], NT, preferred_element_type=jnp.float32
+        ).astype(out_ref.dtype)
+
+
+def rest_call(masks, count, x_all, w_all, out_w, taps, lengths, valid, cache):
+    (tokens, width), lanes = x_all.shape, out_w.shape[1]
+    shapes = [(tokens, lanes)] * 3 + [(count, width)] * len(masks)
     return pl.pallas_call(
-        functools.partial(attend_kernel, rank, masks),
-        out_shape=[jax.ShapeDtypeStruct((count, width), t) for t in out_types],
+        functools.partial(rest_kernel, masks),
+        out_shape=[jax.ShapeDtypeStruct(shape, jnp.bfloat16) for shape in shapes],
+        in_specs=[VMEM] * 4 + [SMEM, SMEM, VMEM],
+        out_specs=[VMEM] * len(shapes),
+        scratch_shapes=[pltpu.VMEM((tokens + 8, taps.shape[2]), jnp.float32)],
+        compiler_params=params(32),
+        cost_estimate=LIGHT,
+    )(x_all, w_all, out_w, taps, lengths, valid, cache)
+
+
+def own_kernel(rank, q_ref, k_ref, v_ref, out_w, x_ref, ids_ref, down_ref, up_ref, *refs):
+    lengths_ref, valid_ref, cache_ref, out_ref = refs
+    attended = attend_block(
+        0, out_ref.shape[0], 0, lengths_ref, valid_ref, q_ref, k_ref, v_ref, cache_ref
+    )
+    part = lax.dot_general(attended, out_w[...], NT, preferred_element_type=jnp.float32)
+    out_ref[...] = part + adapter_term(x_ref, ids_ref, down_ref, up_ref, rank).astype(jnp.float32)
+
+
+def own_call(rank, q, k, v, out_w, x, ids, down, up, lengths, valid, cache):
+    return pl.pallas_call(
+        functools.partial(own_kernel, rank),
+        out_shape=jax.ShapeDtypeStruct(x.shape, jnp.float32),
         in_specs=[VMEM] * 8 + [SMEM, SMEM, VMEM],
-        out_specs=[VMEM] * len(masks),
+        out_specs=VMEM,
         compiler_params=params(20),
         cost_estimate=LIGHT,
     )(q, k, v, out_w, x, ids, down, up, lengths, valid, cache)
@@ -599,34 +619,36 @@
     feed_own = jnp.concatenate(
         [gate_projection[None], up_projection[None], jnp.transpose(down_projection)[None]], axis=0
     )
-    token_two, token_one, firsts, packed, cache, own_ids, feed_own = lax.optimization_barrier(
-        (token_two, token_one, firsts, packed, cache, own_ids, feed_own)
-    )
+    firsts, cache, own_ids, feed_own = lax.optimization_barrier((firsts, cache, own_ids, feed_own))
+    token_two, token_one, cache = lax.optimization_barrier((token_two, token_one, cache))
     token_three = swap(token_two, "col", 1)
     seconds = second_hops(packed, *firsts)
     token_three, diagonal, feed_own = lax.optimization_barrier((token_three, seconds[:2], feed_own))
+    seconds = diagonal + seconds[2:]
     thirds = tuple(swap(piece, "row", 1) for piece in diagonal)
     feed_firsts = first_hops(feed_own)
 
-    pieces = named_pieces(packed, firsts, diagonal + seconds[2:], thirds)
+    pieces = named_pieces(packed, firsts, seconds, thirds)
     blocks = [normed_attention, token_one, token_two, token_three]
     requests_here = (lengths, cache_valid_length, cache)
     ranks = kept * rank * lax.axis_size("row")
-    q, k, v, out_w, down_maps, up_maps, part_three = first_call(
+    x_all, w_all, out_w, down_maps, up_maps, part_three = first_call(
         blocks, pieces, ranks, filter_taps, *requests_here
     )
     passed = swap(part_three, "col", 1)
-    part_two, part_one, part_own = attend_call(
-        rank, [2, 1, 0], [bf16, bf16, f32], q, k, v, out_w, normed_attention, own_ids, down_maps, up_maps, *requests_here
-    )
-    part_two = (part_two.astype(f32) + passed.astype(f32)).astype(bf16)
-    part_two, part_one = lax.optimization_barrier((part_two, part_one))
-    got_two, got_one = swap(part_two, "col", 2), swap(part_one, "col", 1)
-    feed_seconds = second_hops(feed_own, *feed_firsts)
+    q, k, v, part_two, part_one = rest_call(
+        [2, 1], count, x_all, w_all, out_w, filter_taps, *requests_here
+    )
+    part_own = own_call(
+        rank, q, k, v, out_w, normed_attention, own_ids, down_maps, up_maps, *requests_here
+    )
+    got_one = swap(part_one, "col", 1)
+    got_two = swap((part_two.astype(f32) + passed.astype(f32)).astype(bf16), "col", 2)
+    got_one, *hops = lax.optimization_barrier((got_one, *feed_firsts))
+    feed_seconds = second_hops(feed_own, *hops)
     residual, normed_mlp = residual_call(inputs, part_own, got_two, got_one, feed_forward_gain)
     token_two, token_one = swap(normed_mlp, "col", 2), swap(normed_mlp, "col", 1)
-    feed_diagonal = feed_seconds[:2]
-    feed_thirds = tuple(swap(piece, "row", 1) for piece in feed_diagonal)
+    feed_thirds = tuple(swap(piece, "row", 1) for piece in feed_seconds[:2])
     token_two, token_one = lax.optimization_barrier((token_two, token_one))
     token_three = swap(token_two, "col", 1)
     feed_pieces = named_pieces(feed_own, feed_firsts, feed_seconds, feed_thirds)

time: 166 us -> 162 us (0.976)
  waiting for transfers between devices: 105 us -> 98.6 us
  Pallas kernels: 25.5 us -> 28.4 us
    ppermute x30, waiting for transfers between devices: 105 us -> 98.6 us  [swap(): return lax.ppermute(value, axis, xor_pairs(lax.axis_size(axis), mask))]
    pallas_call x1 -> x2, Pallas kernels: 7.57 us -> 12.4 us  [the longest x1 8.68 us: rest_call(): pl.pallas_call(functools.partial(rest_kernel, masks), out_shape=[jax.Shap...]
    pallas_call x1, Pallas kernels: 7.25 us -> 5.34 us  [first_call(): pl.pallas_call(functools.partial(first_kernel, places, n_x, n_w), out_sha...]
  transfers between devices with their start and end apart: 30 -> 30, of which waited for: 17 -> 22; matrix products, arithmetic and copies ran while one was open for 3% -> 3% of each run, Pallas kernels for 8% -> 11%
where the time goes in v4:
time: 162 us
  waiting for transfers between devices  98.6 us (61%)
  Pallas kernels  28.4 us (18%)
  starting transfers between devices  27.5 us (17%)
  local copies, waits for them, and re-layouts  6.16 us (4%)
    ppermute x30, waiting for transfers between devices, swap(): return lax.ppermute(value, axis, xor_pairs(lax.axis_size(axis), mask))  98.6 us
    ppermute x30, starting transfers between devices, swap(): return lax.ppermute(value, axis, xor_pairs(lax.axis_size(axis), mask))  27.5 us
    pallas_call x1, Pallas kernels, rest_call(): pl.pallas_call(functools.partial(rest_kernel, masks), out_shape=[jax.Shap...  8.68 us
    pallas_call x1, Pallas kernels, first_call(): pl.pallas_call(functools.partial(first_kernel, places, n_x, n_w), out_sha...  5.34 us
    pallas_call x1, Pallas kernels, feed_first_call(): pl.pallas_call(functools.partial(feed_first_kernel, places, n_x, n_w), ou...  5.29 us
    reshape x2, local copies, waits for them, and re-layouts, tuned(): cache = window_key_value.reshape(requests, 2, heads, window, HD)  4.56 us
    pallas_call x1, Pallas kernels, own_call(): pl.pallas_call(functools.partial(own_kernel, rank), out_shape=jax.ShapeDt...  3.71 us
  transfers between devices with their start and end apart: 30, of which 22 were waited for; matrix products, arithmetic and copies ran while one was open for 3% of the time, Pallas kernels for 11%

profile of v4, /device:TPU:0, one launch (start us, length us, event | category | flops | bytes accessed | tf_op | source)
XLA Modules:
  0.0 162.3 jit_solution(16540045301519135510)
XLA Ops:
  0.0 2.9 %shard_map.145 = (bf16[128,1792]{1,0:T(8,128)(2,1)}, bf16[288,1792]{1,0:T(8,128)(2,1)}) custom-call(bf16[128,1792]{1,0:T(8,128)(2,1)} %x_ref.1, bf16[3,224,448]{2,1,0:T(8,128)(2,1)} %bitcast.14, bf16[448,224]{1,0:T(8,128)(2,1)} %refs_2_.1, f32[1792]{0:T(1024)} %refs_3_.1, bf16[32,1792]{1,0:T(8,128)(2,1)} %bitcast.18, bf16[32,1792]{1,0:T(8,128)(2,1)} %bitcast.19), custom_call_target="tpu_custom_call" | custom-call | flops 1 | bytes 1 | tf_op jit(solution)/shard_map/pallas_call | solution.py:276
  2.9 3.0 %collective-permute-start.2 = (bf16[288,1792]{1,0:T(8,128)(2,1)}, bf16[288,1792]{1,0:T(8,128)(2,1)S(1)}, u32[]{:S(2)}, u32[]{:S(2)}) collective-permute-start(bf16[288,1792]{1,0:T(8,128)(2,1)} %get-tuple-element.44.refs_4_), channel_id=1, source_target_pairs={{0,8},{4,12},{8,0},{12,4},{16,24},{20,28},{24,16},{28,20},{1,9},{5... | collective-permute-start | bytes 3096584 | tf_op jit(solution)/shard_map/ppermute | solution.py:322
  5.9 1.5 collective-permute-start.3
  7.4 2.6 %collective-permute-start = (bf16[128,1792]{1,0:T(8,128)(2,1)}, bf16[128,1792]{1,0:T(8,128)(2,1)S(1)}, u32[]{:S(2)}, u32[]{:S(2)}) collective-permute-start(bf16[128,1792]{1,0:T(8,128)(2,1)} %get-tuple-element.43.refs_0_.x_ref), channel_id=1, source_target_pairs={{0,2},{1,3},{2,0},{3,1},{4,6},{5,7},{6,4},{7,5},{8,10},{9,11},{10,... | collective-permute-start | bytes 1376264 | tf_op jit(solution)/shard_map/ppermute | solution.py:322
  10.0 1.6 collective-permute-start.1
  11.7 3.3 %reshape.14 = bf16[8,2,4,64,112]{4,3,2,1,0:T(8,128)(2,1)} reshape(bf16[8,2,4,7168]{3,2,1,0:T(4,128)(2,1)} %param.20) | data formatting | bytes 1835008 | tf_op jit(solution)/shard_map/reshape | solution.py:615
  15.0 1.3 copy.16
  17.8 11.1 %collective-permute-done.2.refs_5_ = bf16[288,1792]{1,0:T(8,128)(2,1)S(1)} collective-permute-done((bf16[288,1792]{1,0:T(8,128)(2,1)}, bf16[288,1792]{1,0:T(8,128)(2,1)S(1)}, u32[]{:S(2)}, u32[]{:S(2)}) %collective-permute-start.2) | collective-permute-done | bytes 1032224 | tf_op jit(solution)/shard_map/ppermute | solution.py:322
  28.9 1.5 collective-permute-done.3.refs_6_
  30.4 1.6 collective-permute-start.4
  32.0 1.6 collective-permute-start.5
  34.7 6.8 %collective-permute-done.4.refs_3_ = bf16[128,1792]{1,0:T(8,128)(2,1)S(1)} collective-permute-done((bf16[128,1792]{1,0:T(8,128)(2,1)S(1)}, bf16[128,1792]{1,0:T(8,128)(2,1)S(1)}, u32[]{:S(2)}, u32[]{:S(2)}) %collective-permute-start.4) | collective-permute-done | bytes 458784 | tf_op jit(solution)/shard_map/ppermute | solution.py:322
  41.5 2.8 %collective-permute-done.5.refs_7_ = bf16[144,1792]{1,0:T(8,128)(2,1)S(1)} collective-permute-done((bf16[144,1792]{1,0:T(8,128)(2,1)S(1)}, bf16[144,1792]{1,0:T(8,128)(2,1)S(1)}, u32[]{:S(2)}, u32[]{:S(2)}) %collective-permute-start.5) | collective-permute-done | bytes 516128 | tf_op jit(solution)/shard_map/ppermute | solution.py:322
  45.9 1.4 collective-permute-done.10.refs_12_
  48.1 5.3 %shard_map.146 = (bf16[512,1792]{1,0:T(8,128)(2,1)S(1)}, bf16[1792,1408]{1,0:T(8,128)(2,1)S(1)}, bf16[1792,512]{1,0:T(8,128)(2,1)S(1)}, bf16[256,1792]{1,0:T(8,1...) custom-call(bf16[128,1792]{1,0:T(8,128)(2,1)S(1)} %copy-done.2, ...), custom_call_target="tpu_custom_call" | custom-call | flops 1 | bytes 1 | tf_op jit(solution)/shard_map/pallas_call | solution.py:469
  55.2 8.7 %shard_map.147 = (bf16[512,512]{1,0:T(8,128)(2,1)S(1)}, bf16[512,512]{1,0:T(8,128)(2,1)S(1)}, bf16[512,512]{1,0:T(8,128)(2,1)S(1)}, bf16[128,1792]{1,0:T(8,128)(2,1)S(1)}, bf16[128,1792]{1,0:T(8,128)(2,1)S(1)}) custom-call(bf16[512,1792]{1,0:T(8,128)(2,1)S(1)} %get-tuple-element.55.x_all, bf16[1792,1408]{1,0:T(8,128)(2,1)S(1)} %get-tuple-element.56.w_all, ...), custom_call_target="tpu_custom_call" | custom-call | flops 1 | bytes 1 | tf_op jit(solution)/shard_map/pallas_call | solution.py:498
  63.9 1.7 %collective-permute-start.14 = (bf16[128,1792]{1,0:T(8,128)(2,1)S(1)}, bf16[128,1792]{1,0:T(8,128)(2,1)S(1)}, u32[]{:S(2)}, u32[]{:S(2)}) collective-permute-start(bf16[128,1792]{1,0:T(8,128)(2,1)S(1)} %get-tuple-element.66), channel_id=1, source_target_pairs={{0,1},{1,0},{2,3},{3,2},{4,5},{5,4},{6,7},{7,6},{8,9},{9,8},{10,11... | collective-permute-start | bytes 1376264 | tf_op jit(solution)/shard_map/ppermute | solution.py:322
  66.4 2.7 %collective-permute-start.13 = (bf16[128,1792]{1,0:T(8,128)(2,1)S(1)}, bf16[128,1792]{1,0:T(8,128)(2,1)S(1)}, u32[]{:S(2)}, u32[]{:S(2)}) collective-permute-start(bf16[128,1792]{1,0:T(8,128)(2,1)S(1)} %add_convert_fusion.2), channel_id=1, source_target_pairs={{0,2},{1,3},{2,0},{3,1},{4,6},{5,7},{6,4},{7,5},{8,10},{9,11},{10,... | collective-permute-start | bytes 1376264 | tf_op jit(solution)/shard_map/ppermute | solution.py:322
  69.1 3.7 %shard_map.148.own_ref = f32[128,1792]{1,0:T(8,128)S(1)} custom-call(bf16[512,512]{1,0:T(8,128)(2,1)S(1)} %get-tuple-element.58.q_ref, bf16[512,512]{1,0:T(8,128)(2,1)S(1)} %get-tuple-element.59.k_ref, bf16[512,512]{1,0:T(8,128)(2,1)S(1)} %get-tuple-element.60.v_ref, bf16[1792,512]{1,0:T(8,128)(2,1)S(1)} %get-tuple-element.57.out_w, ...), custom_call_target="tpu_custom_call" | custom-call | flops 1 | bytes 1 | tf_op jit(solution)/shard_map/pallas_call | solution.py:519
  72.8 12.5 %collective-permute-done.14.one_ref = bf16[128,1792]{1,0:T(8,128)(2,1)S(1)} collective-permute-done((bf16[128,1792]{1,0:T(8,128)(2,1)S(1)}, bf16[128,1792]{1,0:T(8,128)(2,1)S(1)}, u32[]{:S(2)}, u32[]{:S(2)}) %collective-permute-start.14) | collective-permute-done | bytes 458784 | tf_op jit(solution)/shard_map/ppermute | solution.py:322
  86.3 2.5 %collective-permute-done.13.two_ref = bf16[128,1792]{1,0:T(8,128)(2,1)S(1)} collective-permute-done((bf16[128,1792]{1,0:T(8,128)(2,1)S(1)}, bf16[128,1792]{1,0:T(8,128)(2,1)S(1)}, u32[]{:S(2)}, u32[]{:S(2)}) %collective-permute-start.13) | collective-permute-done | bytes 458784 | tf_op jit(solution)/shard_map/ppermute | solution.py:322
  89.4 2.9 %collective-permute-start.18 = (bf16[128,1792]{1,0:T(8,128)(2,1)S(1)}, bf16[128,1792]{1,0:T(8,128)(2,1)S(1)}, u32[]{:S(2)}, u32[]{:S(2)}) collective-permute-start(bf16[128,1792]{1,0:T(8,128)(2,1)S(1)} %get-tuple-element.70.refs_2_), channel_id=1, source_target_pairs={{0,1},{1,0},{2,3},{3,2},{4,5},{5,4},{6,7},{7,6},{8,9},{9,8},{10,11... | collective-permute-start | bytes 1376264 | tf_op jit(solution)/shard_map/ppermute | solution.py:322
  92.3 1.4 collective-permute-start.19
  94.5 14.2 %collective-permute-done.17.refs_0_ = bf16[128,1792]{1,0:T(8,128)(2,1)S(1)} collective-permute-done((bf16[128,1792]{1,0:T(8,128)(2,1)S(1)}, bf16[128,1792]{1,0:T(8,128)(2,1)S(1)}, u32[]{:S(2)}, u32[]{:S(2)}) %collective-permute-start.17) | collective-permute-done | bytes 458784 | tf_op jit(solution)/shard_map/ppermute | solution.py:322
  111.4 3.4 %collective-permute-done.24.refs_11_ = bf16[3,112,1024]{2,1,0:T(8,128)(2,1)S(1)} collective-permute-done((bf16[3,112,1024]{2,1,0:T(8,128)(2,1)S(1)}, bf16[3,112,1024]{2,1,0:T(8,128)(2,1)S(1)}, u32[]{:S(2)}, u32[]{:S(2)}) %collective-permute-start.24) | collective-permute-done | bytes 688160 | tf_op jit(solution)/shard_map/ppermute | solution.py:322
  115.8 5.3 %shard_map.150 = (bf16[3,1792,1024]{2,1,0:T(8,128)(2,1)S(1)}, bf16[128,1792]{1,0:T(8,128)(2,1)S(1)}, bf16[128,1792]{1,0:T(8,128)(2,1)S(1)}, f32[128,1792]{1,0:T(8,128)S(1)}) custom-call(bf16[128,1792]{1,0:T(8,128)(2,1)S(1)} %collective-permute-done.17.refs_0_, bf16[128,1792]{1,0:T(8,128)(2,1)S(1)} %collective-permute-done.18.refs_1_, ...), custom_call_target="tpu_custom_call" | custom-call | flops 1 | bytes 1 | tf_op jit(solution)/shard_map/pallas_call | solution.py:553
  121.1 3.2 %collective-permute-done.26.x_ref = bf16[128,1792]{1,0:T(8,128)(2,1)S(1)} collective-permute-done((bf16[128,1792]{1,0:T(8,128)(2,1)S(1)}, bf16[128,1792]{1,0:T(8,128)(2,1)S(1)}, u32[]{:S(2)}, u32[]{:S(2)}) %collective-permute-start.26) | collective-permute-done | bytes 458784 | tf_op jit(solution)/shard_map/ppermute | solution.py:322
  124.3 2.1 %shard_map.151 = bf16[128,1792]{1,0:T(8,128)(2,1)S(1)} custom-call(bf16[128,1792]{1,0:T(8,128)(2,1)S(1)} %collective-permute-done.26.x_ref, bf16[3,1792,1024]{2,1,0:T(8,128)(2,1)S(1)} %get-tuple-element.77.all_w), custom_call_target="tpu_custom_call" | custom-call | flops 1 | bytes 1 | tf_op jit(solution)/shard_map/pallas_call | solution.py:570
  126.8 11.9 %collective-permute-done.27 = bf16[128,1792]{1,0:T(8,128)(2,1)S(1)} collective-permute-done((bf16[128,1792]{1,0:T(8,128)(2,1)S(1)}, bf16[128,1792]{1,0:T(8,128)(2,1)S(1)}, u32[]{:S(2)}, u32[]{:S(2)}) %collective-permute-start.27) | collective-permute-done | bytes 458784 | tf_op jit(solution)/shard_map/ppermute | solution.py:322
  139.3 1.3 collective-permute-start.29
  140.6 17.7 %collective-permute-done.28 = bf16[128,1792]{1,0:T(8,128)(2,1)S(1)} collective-permute-done((bf16[128,1792]{1,0:T(8,128)(2,1)S(1)}, bf16[128,1792]{1,0:T(8,128)(2,1)S(1)}, u32[]{:S(2)}, u32[]{:S(2)}) %collective-permute-start.28) | collective-permute-done | bytes 458784 | tf_op jit(solution)/shard_map/ppermute | solution.py:322
  158.3 3.0 %collective-permute-done.29 = bf16[128,1792]{1,0:T(8,128)(2,1)S(1)} collective-permute-done((bf16[128,1792]{1,0:T(8,128)(2,1)S(1)}, bf16[128,1792]{1,0:T(8,128)(2,1)S(1)}, u32[]{:S(2)}, u32[]{:S(2)}) %collective-permute-start.29) | collective-permute-done | bytes 458784 | tf_op jit(solution)/shard_map/ppermute | solution.py:322
  (71 shorter events, 15.7 us)
Async XLA Ops:
  2.9 26.0 %collective-permute-start.2 = (bf16[288,1792]{1,0:T(8,128)(2,1)}, bf16[288,1792]{1,0:T(8,128)(2,1)S(1)}, u32[]{:S(2)}, u32[]{:S(2)}) collective-permute-start(bf16[288,1792]{1,0:T(8,128)(2,1)} %get-tuple-element.44.refs_4_), channel_id=1, source_target_pairs={{0,8},{4,12},{8,0},{12,4},{16,24},{20,28},{24,16},{28,20},{1,9},{5... | collective-permute-start | bytes 3096584 | tf_op jit(solution)/shard_map/ppermute | solution.py:322
  5.9 24.5 %collective-permute-start.3 = (bf16[288,1792]{1,0:T(8,128)(2,1)}, bf16[288,1792]{1,0:T(8,128)(2,1)S(1)}, u32[]{:S(2)}, u32[]{:S(2)}) collective-permute-start(bf16[288,1792]{1,0:T(8,128)(2,1)} %get-tuple-element.44.refs_4_), channel_id=1, source_target_pairs={{0,16},{4,20},{8,24},{12,28},{16,0},{20,4},{24,8},{28,12},{1,17},{... | collective-permute-start | bytes 3096584 | tf_op jit(solution)/shard_map/ppermute | solution.py:322
  7.4 23.0 %collective-permute-start = (bf16[128,1792]{1,0:T(8,128)(2,1)}, bf16[128,1792]{1,0:T(8,128)(2,1)S(1)}, u32[]{:S(2)}, u32[]{:S(2)}) collective-permute-start(bf16[128,1792]{1,0:T(8,128)(2,1)} %get-tuple-element.43.refs_0_.x_ref), channel_id=1, source_target_pairs={{0,2},{1,3},{2,0},{3,1},{4,6},{5,7},{6,4},{7,5},{8,10},{9,11},{10,... | collective-permute-start | bytes 1376264 | tf_op jit(solution)/shard_map/ppermute | solution.py:322
  10.0 20.4 %collective-permute-start.1 = (bf16[128,1792]{1,0:T(8,128)(2,1)}, bf16[128,1792]{1,0:T(8,128)(2,1)S(1)}, u32[]{:S(2)}, u32[]{:S(2)}) collective-permute-start(bf16[128,1792]{1,0:T(8,128)(2,1)} %get-tuple-element.43.refs_0_.x_ref), channel_id=1, source_target_pairs={{0,1},{1,0},{2,3},{3,2},{4,5},{5,4},{6,7},{7,6},{8,9},{9,8},{10,11... | collective-permute-start | bytes 1376264 | tf_op jit(solution)/shard_map/ppermute | solution.py:322
  17.8 30.3 %copy-start.2 = (bf16[128,1792]{1,0:T(8,128)(2,1)S(1)}, bf16[128,1792]{1,0:T(8,128)(2,1)}, u32[]{:S(2)}) copy-start(bf16[128,1792]{1,0:T(8,128)(2,1)} %get-tuple-element.43.refs_0_.x_ref) | copy-start | bytes 1376260
  17.8 30.3 %copy-start.4 = (f32[3,2,448]{2,1,0:T(2,128)S(1)}, f32[3,2,448]{2,1,0:T(2,128)}, u32[]{:S(2)}) copy-start(f32[3,2,448]{2,1,0:T(2,128)} %taps_ref.1) | copy-start | bytes 32260
  30.4 11.2 %collective-permute-start.4 = (bf16[128,1792]{1,0:T(8,128)(2,1)S(1)}, bf16[128,1792]{1,0:T(8,128)(2,1)S(1)}, u32[]{:S(2)}, u32[]{:S(2)}) collective-permute-start(bf16[128,1792]{1,0:T(8,128)(2,1)S(1)} %collective-permute-done.refs_2_), channel_id=1, source_target_pairs={{0,1},{1,0},{2,3},{3,2},{4,5},{5,4},{6,7},{7,6},{8,9},{9,8},{10,11... | collective-permute-start | bytes 1376264 | tf_op jit(solution)/shard_map/ppermute | solution.py:322
  32.0 12.3 %collective-permute-start.5 = (bf16[144,1792]{1,0:T(8,128)(2,1)S(1)}, bf16[144,1792]{1,0:T(8,128)(2,1)S(1)}, u32[]{:S(2)}, u32[]{:S(2)}) collective-permute-start(bf16[144,1792]{1,0:T(8,128)(2,1)S(1)} %slice.12), channel_id=1, source_target_pairs={{0,16},{4,20},{8,24},{12,28},{16,0},{20,4},{24,8},{28,12},{1,17},{... | collective-permute-start | bytes 1548296 | tf_op jit(solution)/shard_map/ppermute | solution.py:322
  33.6 11.8 %collective-permute-start.6 = (bf16[144,1792]{1,0:T(8,128)(2,1)S(1)}, bf16[144,1792]{1,0:T(8,128)(2,1)S(1)}, u32[]{:S(2)}, u32[]{:S(2)}) collective-permute-start(bf16[144,1792]{1,0:T(8,128)(2,1)S(1)} %slice.13), channel_id=1, source_target_pairs={{0,8},{4,12},{8,0},{12,4},{16,24},{20,28},{24,16},{28,20},{1,9},{5... | collective-permute-start | bytes 1548296 | tf_op jit(solution)/shard_map/ppermute | solution.py:322
  34.2 11.7 %collective-permute-start.7 = (bf16[288,1792]{1,0:T(8,128)(2,1)S(1)}, bf16[288,1792]{1,0:T(8,128)(2,1)S(1)}, u32[]{:S(2)}, u32[]{:S(2)}) collective-permute-start(bf16[288,1792]{1,0:T(8,128)(2,1)S(1)} %copy-done.3), channel_id=1, source_target_pairs={{0,4},{4,0},{8,12},{12,8},{16,20},{20,16},{24,28},{28,24},{1,5},{5... | collective-permute-start | bytes 3096584 | tf_op jit(solution)/shard_map/ppermute | solution.py:322
  34.2 13.8 %collective-permute-start.8 = (bf16[288,1792]{1,0:T(8,128)(2,1)S(1)}, bf16[288,1792]{1,0:T(8,128)(2,1)S(1)}, u32[]{:S(2)}, u32[]{:S(2)}) collective-permute-start(bf16[288,1792]{1,0:T(8,128)(2,1)S(1)} %collective-permute-done.2.refs_5_), channel_id=1, source_target_pairs={{0,4},{4,0},{8,12},{12,8},{16,20},{20,16},{24,28},{28,24},{1,5},{5... | collective-permute-start | bytes 3096584 | tf_op jit(solution)/shard_map/ppermute | solution.py:322
  41.5 6.5 %collective-permute-start.9 = (bf16[288,1792]{1,0:T(8,128)(2,1)S(1)}, bf16[288,1792]{1,0:T(8,128)(2,1)S(1)}, u32[]{:S(2)}, u32[]{:S(2)}) collective-permute-start(bf16[288,1792]{1,0:T(8,128)(2,1)S(1)} %collective-permute-done.3.refs_6_), channel_id=1, source_target_pairs={{0,4},{4,0},{8,12},{12,8},{16,20},{20,16},{24,28},{28,24},{1,5},{5... | collective-permute-start | bytes 3096584 | tf_op jit(solution)/shard_map/ppermute | solution.py:322
  45.4 1.9 %collective-permute-start.10 = (bf16[144,1792]{1,0:T(8,128)(2,1)S(1)}, bf16[144,1792]{1,0:T(8,128)(2,1)S(1)}, u32[]{:S(2)}, u32[]{:S(2)}) collective-permute-start(bf16[144,1792]{1,0:T(8,128)(2,1)S(1)} %collective-permute-done.5.refs_7_), channel_id=1, source_target_pairs={{0,4},{4,0},{8,12},{12,8},{16,20},{20,16},{24,28},{28,24},{1,5},{5... | collective-permute-start | bytes 1548296 | tf_op jit(solution)/shard_map/ppermute | solution.py:322
  45.4 2.6 %collective-permute-start.11 = (bf16[144,1792]{1,0:T(8,128)(2,1)S(1)}, bf16[144,1792]{1,0:T(8,128)(2,1)S(1)}, u32[]{:S(2)}, u32[]{:S(2)}) collective-permute-start(bf16[144,1792]{1,0:T(8,128)(2,1)S(1)} %collective-permute-done.6.refs_8_), channel_id=1, source_target_pairs={{0,4},{4,0},{8,12},{12,8},{16,20},{20,16},{24,28},{28,24},{1,5},{5... | collective-permute-start | bytes 1548296 | tf_op jit(solution)/shard_map/ppermute | solution.py:322
  53.5 12.8 %collective-permute-start.12 = (bf16[128,1792]{1,0:T(8,128)(2,1)S(1)}, bf16[128,1792]{1,0:T(8,128)(2,1)S(1)}, u32[]{:S(2)}, u32[]{:S(2)}) collective-permute-start(bf16[128,1792]{1,0:T(8,128)(2,1)S(1)} %get-tuple-element.65), channel_id=1, source_target_pairs={{0,1},{1,0},{2,3},{3,2},{4,5},{5,4},{6,7},{7,6},{8,9},{9,8},{10,11... | collective-permute-start | bytes 1376264 | tf_op jit(solution)/shard_map/ppermute | solution.py:322
  54.0 31.9 %collective-permute-start.15 = (bf16[3,224,1024]{2,1,0:T(8,128)(2,1)S(1)}, bf16[3,224,1024]{2,1,0:T(8,128)(2,1)S(1)}, u32[]{:S(2)}, u32[]{:S(2)}) collective-permute-start(bf16[3,224,1024]{2,1,0:T(8,128)(2,1)S(1)} %pad_maximum_fusion.refs_3_), channel_id=1, source_target_pairs={{0,8},{4,12},{8,0},{12,4},{16,24},{20,28},{24,16},{28,20},{1,9},{5... | collective-permute-start | bytes 4128776 | tf_op jit(solution)/shard_map/ppermute | solution.py:322
  54.7 31.7 %collective-permute-start.16 = (bf16[3,224,1024]{2,1,0:T(8,128)(2,1)S(1)}, bf16[3,224,1024]{2,1,0:T(8,128)(2,1)S(1)}, u32[]{:S(2)}, u32[]{:S(2)}) collective-permute-start(bf16[3,224,1024]{2,1,0:T(8,128)(2,1)S(1)} %pad_maximum_fusion.refs_3_), channel_id=1, source_target_pairs={{0,16},{4,20},{8,24},{12,28},{16,0},{20,4},{24,8},{28,12},{1,17},{... | collective-permute-start | bytes 4128776 | tf_op jit(solution)/shard_map/ppermute | solution.py:322
  63.9 21.4 %collective-permute-start.14 = (bf16[128,1792]{1,0:T(8,128)(2,1)S(1)}, bf16[128,1792]{1,0:T(8,128)(2,1)S(1)}, u32[]{:S(2)}, u32[]{:S(2)}) collective-permute-start(bf16[128,1792]{1,0:T(8,128)(2,1)S(1)} %get-tuple-element.66), channel_id=1, source_target_pairs={{0,1},{1,0},{2,3},{3,2},{4,5},{5,4},{6,7},{7,6},{8,9},{9,8},{10,11... | collective-permute-start | bytes 1376264 | tf_op jit(solution)/shard_map/ppermute | solution.py:322
  66.4 22.4 %collective-permute-start.13 = (bf16[128,1792]{1,0:T(8,128)(2,1)S(1)}, bf16[128,1792]{1,0:T(8,128)(2,1)S(1)}, u32[]{:S(2)}, u32[]{:S(2)}) collective-permute-start(bf16[128,1792]{1,0:T(8,128)(2,1)S(1)} %add_convert_fusion.2), channel_id=1, source_target_pairs={{0,2},{1,3},{2,0},{3,1},{4,6},{5,7},{6,4},{7,5},{8,10},{9,11},{10,... | collective-permute-start | bytes 1376264 | tf_op jit(solution)/shard_map/ppermute | solution.py:322
  89.2 19.6 %collective-permute-start.17 = (bf16[128,1792]{1,0:T(8,128)(2,1)S(1)}, bf16[128,1792]{1,0:T(8,128)(2,1)S(1)}, u32[]{:S(2)}, u32[]{:S(2)}) collective-permute-start(bf16[128,1792]{1,0:T(8,128)(2,1)S(1)} %get-tuple-element.70.refs_2_), channel_id=1, source_target_pairs={{0,2},{1,3},{2,0},{3,1},{4,6},{5,7},{6,4},{7,5},{8,10},{9,11},{10,... | collective-permute-start | bytes 1376264 | tf_op jit(solution)/shard_map/ppermute | solution.py:322
  89.4 19.4 %collective-permute-start.18 = (bf16[128,1792]{1,0:T(8,128)(2,1)S(1)}, bf16[128,1792]{1,0:T(8,128)(2,1)S(1)}, u32[]{:S(2)}, u32[]{:S(2)}) collective-permute-start(bf16[128,1792]{1,0:T(8,128)(2,1)S(1)} %get-tuple-element.70.refs_2_), channel_id=1, source_target_pairs={{0,1},{1,0},{2,3},{3,2},{4,5},{5,4},{6,7},{7,6},{8,9},{9,8},{10,11... | collective-permute-start | bytes 1376264 | tf_op jit(solution)/shard_map/ppermute | solution.py:322
  92.3 19.1 %collective-permute-start.21 = (bf16[3,224,1024]{2,1,0:T(8,128)(2,1)S(1)}, bf16[3,224,1024]{2,1,0:T(8,128)(2,1)S(1)}, u32[]{:S(2)}, u32[]{:S(2)}) collective-permute-start(bf16[3,224,1024]{2,1,0:T(8,128)(2,1)S(1)} %pad_maximum_fusion.refs_3_), channel_id=1, source_target_pairs={{0,4},{4,0},{8,12},{12,8},{16,20},{20,16},{24,28},{28,24},{1,5},{5... | collective-permute-start | bytes 4128776 | tf_op jit(solution)/shard_map/ppermute | solution.py:322
  92.3 17.9 %collective-permute-start.19 = (bf16[3,112,1024]{2,1,0:T(8,128)(2,1)S(1)}, bf16[3,112,1024]{2,1,0:T(8,128)(2,1)S(1)}, u32[]{:S(2)}, u32[]{:S(2)}) collective-permute-start(bf16[3,112,1024]{2,1,0:T(8,128)(2,1)S(1)} %slice.14), channel_id=1, source_target_pairs={{0,16},{4,20},{8,24},{12,28},{16,0},{20,4},{24,8},{28,12},{1,17},{... | collective-permute-start | bytes 2064392 | tf_op jit(solution)/shard_map/ppermute | solution.py:322
  93.7 17.6 %collective-permute-start.20 = (bf16[3,112,1024]{2,1,0:T(8,128)(2,1)S(1)}, bf16[3,112,1024]{2,1,0:T(8,128)(2,1)S(1)}, u32[]{:S(2)}, u32[]{:S(2)}) collective-permute-start(bf16[3,112,1024]{2,1,0:T(8,128)(2,1)S(1)} %slice.15), channel_id=1, source_target_pairs={{0,8},{4,12},{8,0},{12,4},{16,24},{20,28},{24,16},{28,20},{1,9},{5... | collective-permute-start | bytes 2064392 | tf_op jit(solution)/shard_map/ppermute | solution.py:322
  108.7 7.1 %collective-permute-start.22 = (bf16[3,224,1024]{2,1,0:T(8,128)(2,1)S(1)}, bf16[3,224,1024]{2,1,0:T(8,128)(2,1)S(1)}, u32[]{:S(2)}, u32[]{:S(2)}) collective-permute-start(bf16[3,224,1024]{2,1,0:T(8,128)(2,1)S(1)} %collective-permute-done.15.refs_4_), channel_id=1, source_target_pairs={{0,4},{4,0},{8,12},{12,8},{16,20},{20,16},{24,28},{28,24},{1,5},{5... | collective-permute-start | bytes 4128776 | tf_op jit(solution)/shard_map/ppermute | solution.py:322
  108.8 7.0 %collective-permute-start.23 = (bf16[3,224,1024]{2,1,0:T(8,128)(2,1)S(1)}, bf16[3,224,1024]{2,1,0:T(8,128)(2,1)S(1)}, u32[]{:S(2)}, u32[]{:S(2)}) collective-permute-start(bf16[3,224,1024]{2,1,0:T(8,128)(2,1)S(1)} %collective-permute-done.16.refs_5_), channel_id=1, source_target_pairs={{0,4},{4,0},{8,12},{12,8},{16,20},{20,16},{24,28},{28,24},{1,5},{5... | collective-permute-start | bytes 4128776 | tf_op jit(solution)/shard_map/ppermute | solution.py:322
  110.2 4.6 %collective-permute-start.24 = (bf16[3,112,1024]{2,1,0:T(8,128)(2,1)S(1)}, bf16[3,112,1024]{2,1,0:T(8,128)(2,1)S(1)}, u32[]{:S(2)}, u32[]{:S(2)}) collective-permute-start(bf16[3,112,1024]{2,1,0:T(8,128)(2,1)S(1)} %collective-permute-done.19.refs_6_), channel_id=1, source_target_pairs={{0,4},{4,0},{8,12},{12,8},{16,20},{20,16},{24,28},{28,24},{1,5},{5... | collective-permute-start | bytes 2064392 | tf_op jit(solution)/shard_map/ppermute | solution.py:322
  111.4 4.4 %collective-permute-start.25 = (bf16[3,112,1024]{2,1,0:T(8,128)(2,1)S(1)}, bf16[3,112,1024]{2,1,0:T(8,128)(2,1)S(1)}, u32[]{:S(2)}, u32[]{:S(2)}) collective-permute-start(bf16[3,112,1024]{2,1,0:T(8,128)(2,1)S(1)} %collective-permute-done.20.refs_7_), channel_id=1, source_target_pairs={{0,4},{4,0},{8,12},{12,8},{16,20},{20,16},{24,28},{28,24},{1,5},{5... | collective-permute-start | bytes 2064392 | tf_op jit(solution)/shard_map/ppermute | solution.py:322
  111.4 12.9 %collective-permute-start.26 = (bf16[128,1792]{1,0:T(8,128)(2,1)S(1)}, bf16[128,1792]{1,0:T(8,128)(2,1)S(1)}, u32[]{:S(2)}, u32[]{:S(2)}) collective-permute-start(bf16[128,1792]{1,0:T(8,128)(2,1)S(1)} %collective-permute-done.17.refs_0_), channel_id=1, source_target_pairs={{0,1},{1,0},{2,3},{3,2},{4,5},{5,4},{6,7},{7,6},{8,9},{9,8},{10,11... | collective-permute-start | bytes 1376264 | tf_op jit(solution)/shard_map/ppermute | solution.py:322
  126.4 12.2 %collective-permute-start.27 = (bf16[128,1792]{1,0:T(8,128)(2,1)S(1)}, bf16[128,1792]{1,0:T(8,128)(2,1)S(1)}, u32[]{:S(2)}, u32[]{:S(2)}) collective-permute-start(bf16[128,1792]{1,0:T(8,128)(2,1)S(1)} %shard_map.151), channel_id=1, source_target_pairs={{0,1},{1,0},{2,3},{3,2},{4,5},{5,4},{6,7},{7,6},{8,9},{9,8},{10,11... | collective-permute-start | bytes 1376264 | tf_op jit(solution)/shard_map/ppermute | solution.py:322
  138.8 19.6 %collective-permute-start.28 = (bf16[128,1792]{1,0:T(8,128)(2,1)S(1)}, bf16[128,1792]{1,0:T(8,128)(2,1)S(1)}, u32[]{:S(2)}, u32[]{:S(2)}) collective-permute-start(bf16[128,1792]{1,0:T(8,128)(2,1)S(1)} %get-tuple-element.79), channel_id=1, source_target_pairs={{0,1},{1,0},{2,3},{3,2},{4,5},{5,4},{6,7},{7,6},{8,9},{9,8},{10,11... | collective-permute-start | bytes 1376264 | tf_op jit(solution)/shard_map/ppermute | solution.py:322
  139.3 22.0 %collective-permute-start.29 = (bf16[128,1792]{1,0:T(8,128)(2,1)S(1)}, bf16[128,1792]{1,0:T(8,128)(2,1)S(1)}, u32[]{:S(2)}, u32[]{:S(2)}) collective-permute-start(bf16[128,1792]{1,0:T(8,128)(2,1)S(1)} %add_convert_fusion.1), channel_id=1, source_target_pairs={{0,2},{1,3},{2,0},{3,1},{4,6},{5,7},{6,4},{7,5},{8,10},{9,11},{10,... | collective-permute-start | bytes 1376264 | tf_op jit(solution)/shard_map/ppermute | solution.py:322
  (9 other events, 117.1 us)

commit v5 on v4

--- a/solution.py
+++ b/solution.py
@@ -561,20 +561,62 @@
     )(*blocks, *(piece for piece, _, _ in pieces))
 
 
-def feed_last_kernel(x_ref, all_w, out_ref):
-    out_ref[...] = feed(x_ref[...], all_w).astype(out_ref.dtype)
-
-
-def feed_last_call(block, all_w):
-    count, (_, width, hidden) = block.shape[0], all_w.shape
+def feed_last_kernel(x_ref, all_w, near_ref, far_ref):
+    down = feed(x_ref[...], all_w).astype(near_ref.dtype)
+    near_ref[...] = down[: near_ref.shape[0]]
+    far_ref[...] = down[near_ref.shape[0] :]
+
+
+def feed_last_call(block, all_w, near):
+    count, width = block.shape
     return pl.pallas_call(
         feed_last_kernel,
-        out_shape=jax.ShapeDtypeStruct((count, width), jnp.bfloat16),
+        out_shape=[
+            jax.ShapeDtypeStruct((rows, width), jnp.bfloat16) for rows in (near, count - near)
+        ],
+        in_specs=[VMEM] * 2,
+        out_specs=[VMEM] * 2,
+        compiler_params=params(20),
+        cost_estimate=LIGHT,
+    )(block, all_w)
+
+
+def sum_kernel(part_ref, passed_ref, out_ref):
+    near = passed_ref.shape[0]
+    both = part_ref[:near].astype(jnp.float32) + passed_ref[...].astype(jnp.float32)
+    out_ref[:near] = both.astype(out_ref.dtype)
+    out_ref[near:] = part_ref[near:]
+
+
+def sum_call(part, passed):
+    return pl.pallas_call(
+        sum_kernel,
+        out_shape=jax.ShapeDtypeStruct(part.shape, jnp.bfloat16),
         in_specs=[VMEM] * 2,
         out_specs=VMEM,
-        compiler_params=params(20),
-        cost_estimate=LIGHT,
-    )(block, all_w)
+        compiler_params=params(12),
+        cost_estimate=LIGHT,
+    )(part, passed)
+
+
+def last_kernel(residual_ref, own_ref, two_ref, one_ref, far_ref, out_ref):
+    near = out_ref.shape[0] - far_ref.shape[0]
+    total = own_ref[...] + one_ref[...].astype(jnp.float32) + two_ref[...].astype(jnp.float32)
+    residual = residual_ref[...].astype(jnp.float32)
+    far = total[near:] + far_ref[...].astype(jnp.float32)
+    out_ref[:near] = (residual[:near] + total[:near]).astype(out_ref.dtype)
+    out_ref[near:] = (residual[near:] + far).astype(out_ref.dtype)
+
+
+def last_call(residual, own, two, one, far):
+    return pl.pallas_call(
+        last_kernel,
+        out_shape=jax.ShapeDtypeStruct(residual.shape, jnp.bfloat16),
+        in_specs=[VMEM] * 5,
+        out_specs=VMEM,
+        compiler_params=params(12),
+        cost_estimate=LIGHT,
+    )(residual, own, two, one, far)
 
 
 def tuned(
@@ -655,13 +697,13 @@
     feed_w, part_two, part_one, part_own = feed_first_call(
         [token_two, token_one, normed_mlp], feed_pieces, [bf16, bf16, f32]
     )
-    part_three = feed_last_call(token_three, feed_w)
-    passed = swap(part_three, "col", 1)
-    part_two = (part_two.astype(f32) + passed.astype(f32)).astype(bf16)
-    part_two, part_one = lax.optimization_barrier((part_two, part_one))
-    got_two, got_one = swap(part_two, "col", 2), swap(part_one, "col", 1)
-    added = part_own + got_one.astype(f32) + got_two.astype(f32)
-    return (residual.astype(f32) + added).astype(bf16)
+    near, far = feed_last_call(token_three, feed_w, count * 5 // 8)
+    passed, got_far = swap(near, "col", 1), swap(far, "col", 3)
+    part_two = sum_call(part_two, passed)
+    got_two = swap(part_two, "col", 2)
+    _, got_far, part_one = lax.optimization_barrier((part_two, got_far, part_one))
+    got_one = swap(part_one, "col", 1)
+    return last_call(residual, part_own, got_two, got_one, got_far)
 
 
 def on_device(*args):

time: 162 us -> 161 us (level)
  waiting for transfers between devices: 98.6 us -> 95.6 us
    ppermute x30 -> x31, waiting for transfers between devices: 98.6 us -> 95.6 us  [swap(): return lax.ppermute(value, axis, xor_pairs(lax.axis_size(axis), mask))]
    ppermute x30 -> x31, starting transfers between devices: 27.5 us -> 27.3 us  [swap(): return lax.ppermute(value, axis, xor_pairs(lax.axis_size(axis), mask))]
  transfers between devices with their start and end apart: 30 -> 31, of which waited for: 22 -> 23; matrix products, arithmetic and copies ran while one was open for 3% -> 5% of each run, Pallas kernels for 11% -> 11%
where the time goes in v5:
time: 161 us; the launch traced here: 160 us
  waiting for transfers between devices  95.6 us (59%)
  Pallas kernels  29.5 us (18%)
  starting transfers between devices  27.3 us (17%)
  local copies, waits for them, and re-layouts  7.43 us (5%)
    ppermute x31, waiting for transfers between devices, swap(): return lax.ppermute(value, axis, xor_pairs(lax.axis_size(axis), mask))  95.6 us
    ppermute x31, starting transfers between devices, swap(): return lax.ppermute(value, axis, xor_pairs(lax.axis_size(axis), mask))  27.3 us
    pallas_call x1, Pallas kernels, rest_call(): pl.pallas_call(functools.partial(rest_kernel, masks), out_shape=[jax.Shap...  8.68 us
    reshape x2, local copies, waits for them, and re-layouts, tuned(): cache = window_key_value.reshape(requests, 2, heads, window, HD)  5.55 us
    pallas_call x1, Pallas kernels, first_call(): pl.pallas_call(functools.partial(first_kernel, places, n_x, n_w), out_sha...  5.35 us
    pallas_call x1, Pallas kernels, feed_first_call(): pl.pallas_call(functools.partial(feed_first_kernel, places, n_x, n_w), ou...  5.28 us
    pallas_call x1, Pallas kernels, own_call(): pl.pallas_call(functools.partial(own_kernel, rank), out_shape=jax.ShapeDt...  3.7 us
  transfers between devices with their start and end apart: 31, of which 23 were waited for; matrix products, arithmetic and copies ran while one was open for 5% of the time, Pallas kernels for 11%

profile of v5, /device:TPU:0, one launch (start us, length us, event | category | flops | bytes accessed | tf_op | source)
XLA Modules:
  0.0 160.4 jit_solution(3302599855112427727)
XLA Ops:
  0.0 2.9 %shard_map.145 = (bf16[128,1792]{1,0:T(8,128)(2,1)}, bf16[288,1792]{1,0:T(8,128)(2,1)}) custom-call(bf16[128,1792]{1,0:T(8,128)(2,1)} %x_ref.1, bf16[3,224,448]{2,1,0:T(8,128)(2,1)} %bitcast.14, bf16[448,224]{1,0:T(8,128)(2,1)} %refs_2_.1, f32[1792]{0:T(1024)} %refs_3_.1, bf16[32,1792]{1,0:T(8,128)(2,1)} %bitcast.18, bf16[32,1792]{1,0:T(8,128)(2,1)} %bitcast.19), custom_call_target="tpu_custom_call" | custom-call | flops 1 | bytes 1 | tf_op jit(solution)/shard_map/pallas_call | solution.py:276
  2.9 3.0 %collective-permute-start.2 = (bf16[288,1792]{1,0:T(8,128)(2,1)}, bf16[288,1792]{1,0:T(8,128)(2,1)S(1)}, u32[]{:S(2)}, u32[]{:S(2)}) collective-permute-start(bf16[288,1792]{1,0:T(8,128)(2,1)} %get-tuple-element.46.refs_4_), channel_id=1, source_target_pairs={{0,8},{4,12},{8,0},{12,4},{16,24},{20,28},{24,16},{28,20},{1,9},{5... | collective-permute-start | bytes 3096584 | tf_op jit(solution)/shard_map/ppermute | solution.py:322
  5.9 1.5 collective-permute-start.3
  7.4 2.6 %collective-permute-start = (bf16[128,1792]{1,0:T(8,128)(2,1)}, bf16[128,1792]{1,0:T(8,128)(2,1)S(1)}, u32[]{:S(2)}, u32[]{:S(2)}) collective-permute-start(bf16[128,1792]{1,0:T(8,128)(2,1)} %get-tuple-element.45.refs_0_.x_ref), channel_id=1, source_target_pairs={{0,2},{1,3},{2,0},{3,1},{4,6},{5,7},{6,4},{7,5},{8,10},{9,11},{10,... | collective-permute-start | bytes 1376264 | tf_op jit(solution)/shard_map/ppermute | solution.py:322
  10.0 1.6 collective-permute-start.1
  11.6 3.3 %reshape.14 = bf16[8,2,4,64,112]{4,3,2,1,0:T(8,128)(2,1)} reshape(bf16[8,2,4,7168]{3,2,1,0:T(4,128)(2,1)} %param.20) | data formatting | bytes 1835008 | tf_op jit(solution)/shard_map/reshape | solution.py:657
  14.8 2.3 %copy.16 = bf16[8,2,4,64,112]{4,3,0,2,1:T(8,128)(2,1)} copy(bf16[8,2,4,64,112]{4,3,2,1,0:T(8,128)(2,1)} %reshape.14) | data formatting | bytes 1835008 | tf_op jit(solution)/shard_map/reshape | solution.py:657
  17.3 1.5 pad.4.refs_17_.cache_ref.refs_2_
  19.1 9.8 %collective-permute-done.2.refs_5_ = bf16[288,1792]{1,0:T(8,128)(2,1)S(1)} collective-permute-done((bf16[288,1792]{1,0:T(8,128)(2,1)}, bf16[288,1792]{1,0:T(8,128)(2,1)S(1)}, u32[]{:S(2)}, u32[]{:S(2)}) %collective-permute-start.2) | collective-permute-done | bytes 1032224 | tf_op jit(solution)/shard_map/ppermute | solution.py:322
  28.9 1.5 collective-permute-done.3.refs_6_
  30.4 1.6 collective-permute-start.4
  32.0 1.6 collective-permute-start.5
  34.7 6.8 %collective-permute-done.4.refs_3_ = bf16[128,1792]{1,0:T(8,128)(2,1)S(1)} collective-permute-done((bf16[128,1792]{1,0:T(8,128)(2,1)S(1)}, bf16[128,1792]{1,0:T(8,128)(2,1)S(1)}, u32[]{:S(2)}, u32[]{:S(2)}) %collective-permute-start.4) | collective-permute-done | bytes 458784 | tf_op jit(solution)/shard_map/ppermute | solution.py:322
  41.5 2.8 %collective-permute-done.5.refs_7_ = bf16[144,1792]{1,0:T(8,128)(2,1)S(1)} collective-permute-done((bf16[144,1792]{1,0:T(8,128)(2,1)S(1)}, bf16[144,1792]{1,0:T(8,128)(2,1)S(1)}, u32[]{:S(2)}, u32[]{:S(2)}) %collective-permute-start.5) | collective-permute-done | bytes 516128 | tf_op jit(solution)/shard_map/ppermute | solution.py:322
  45.9 1.4 collective-permute-done.10.refs_12_
  48.1 5.3 %shard_map.146 = (bf16[512,1792]{1,0:T(8,128)(2,1)S(1)}, bf16[1792,1408]{1,0:T(8,128)(2,1)S(1)}, bf16[1792,512]{1,0:T(8,128)(2,1)S(1)}, bf16[256,1792]{1,0:T(8,1...) custom-call(bf16[128,1792]{1,0:T(8,128)(2,1)S(1)} %copy-done.2, ...), custom_call_target="tpu_custom_call" | custom-call | flops 1 | bytes 1 | tf_op jit(solution)/shard_map/pallas_call | solution.py:469
  55.2 8.7 %shard_map.147 = (bf16[512,512]{1,0:T(8,128)(2,1)S(1)}, bf16[512,512]{1,0:T(8,128)(2,1)S(1)}, bf16[512,512]{1,0:T(8,128)(2,1)S(1)}, bf16[128,1792]{1,0:T(8,128)(2,1)S(1)}, bf16[128,1792]{1,0:T(8,128)(2,1)S(1)}) custom-call(bf16[512,1792]{1,0:T(8,128)(2,1)S(1)} %get-tuple-element.57.x_all, bf16[1792,1408]{1,0:T(8,128)(2,1)S(1)} %get-tuple-element.58.w_all, ...), custom_call_target="tpu_custom_call" | custom-call | flops 1 | bytes 1 | tf_op jit(solution)/shard_map/pallas_call | solution.py:498
  63.9 1.7 %collective-permute-start.14 = (bf16[128,1792]{1,0:T(8,128)(2,1)S(1)}, bf16[128,1792]{1,0:T(8,128)(2,1)S(1)}, u32[]{:S(2)}, u32[]{:S(2)}) collective-permute-start(bf16[128,1792]{1,0:T(8,128)(2,1)S(1)} %get-tuple-element.68), channel_id=1, source_target_pairs={{0,1},{1,0},{2,3},{3,2},{4,5},{5,4},{6,7},{7,6},{8,9},{9,8},{10,11... | collective-permute-start | bytes 1376264 | tf_op jit(solution)/shard_map/ppermute | solution.py:322
  66.3 2.7 %collective-permute-start.13 = (bf16[128,1792]{1,0:T(8,128)(2,1)S(1)}, bf16[128,1792]{1,0:T(8,128)(2,1)S(1)}, u32[]{:S(2)}, u32[]{:S(2)}) collective-permute-start(bf16[128,1792]{1,0:T(8,128)(2,1)S(1)} %add_convert_fusion), channel_id=1, source_target_pairs={{0,2},{1,3},{2,0},{3,1},{4,6},{5,7},{6,4},{7,5},{8,10},{9,11},{10,... | collective-permute-start | bytes 1376264 | tf_op jit(solution)/shard_map/ppermute | solution.py:322
  69.1 3.7 %shard_map.148.own_ref = f32[128,1792]{1,0:T(8,128)S(1)} custom-call(bf16[512,512]{1,0:T(8,128)(2,1)S(1)} %get-tuple-element.60.q_ref, bf16[512,512]{1,0:T(8,128)(2,1)S(1)} %get-tuple-element.61.k_ref, bf16[512,512]{1,0:T(8,128)(2,1)S(1)} %get-tuple-element.62.v_ref, bf16[1792,512]{1,0:T(8,128)(2,1)S(1)} %get-tuple-element.59.out_w, ...), custom_call_target="tpu_custom_call" | custom-call | flops 1 | bytes 1 | tf_op jit(solution)/shard_map/pallas_call | solution.py:519
  72.8 12.5 %collective-permute-done.14.one_ref = bf16[128,1792]{1,0:T(8,128)(2,1)S(1)} collective-permute-done((bf16[128,1792]{1,0:T(8,128)(2,1)S(1)}, bf16[128,1792]{1,0:T(8,128)(2,1)S(1)}, u32[]{:S(2)}, u32[]{:S(2)}) %collective-permute-start.14) | collective-permute-done | bytes 458784 | tf_op jit(solution)/shard_map/ppermute | solution.py:322
  86.3 2.5 %collective-permute-done.13.two_ref = bf16[128,1792]{1,0:T(8,128)(2,1)S(1)} collective-permute-done((bf16[128,1792]{1,0:T(8,128)(2,1)S(1)}, bf16[128,1792]{1,0:T(8,128)(2,1)S(1)}, u32[]{:S(2)}, u32[]{:S(2)}) %collective-permute-start.13) | collective-permute-done | bytes 458784 | tf_op jit(solution)/shard_map/ppermute | solution.py:322
  89.3 2.9 %collective-permute-start.18 = (bf16[128,1792]{1,0:T(8,128)(2,1)S(1)}, bf16[128,1792]{1,0:T(8,128)(2,1)S(1)}, u32[]{:S(2)}, u32[]{:S(2)}) collective-permute-start(bf16[128,1792]{1,0:T(8,128)(2,1)S(1)} %get-tuple-element.72.refs_2_), channel_id=1, source_target_pairs={{0,1},{1,0},{2,3},{3,2},{4,5},{5,4},{6,7},{7,6},{8,9},{9,8},{10,11... | collective-permute-start | bytes 1376264 | tf_op jit(solution)/shard_map/ppermute | solution.py:322
  92.3 1.4 collective-permute-start.19
  94.5 14.2 %collective-permute-done.17.refs_0_ = bf16[128,1792]{1,0:T(8,128)(2,1)S(1)} collective-permute-done((bf16[128,1792]{1,0:T(8,128)(2,1)S(1)}, bf16[128,1792]{1,0:T(8,128)(2,1)S(1)}, u32[]{:S(2)}, u32[]{:S(2)}) %collective-permute-start.17) | collective-permute-done | bytes 458784 | tf_op jit(solution)/shard_map/ppermute | solution.py:322
  111.4 3.4 %collective-permute-done.24.refs_11_ = bf16[3,112,1024]{2,1,0:T(8,128)(2,1)S(1)} collective-permute-done((bf16[3,112,1024]{2,1,0:T(8,128)(2,1)S(1)}, bf16[3,112,1024]{2,1,0:T(8,128)(2,1)S(1)}, u32[]{:S(2)}, u32[]{:S(2)}) %collective-permute-start.24) | collective-permute-done | bytes 688160 | tf_op jit(solution)/shard_map/ppermute | solution.py:322
  115.7 5.3 %shard_map.150 = (bf16[3,1792,1024]{2,1,0:T(8,128)(2,1)S(1)}, bf16[128,1792]{1,0:T(8,128)(2,1)S(1)}, bf16[128,1792]{1,0:T(8,128)(2,1)S(1)}, f32[128,1792]{1,0:T(8,128)S(1)}) custom-call(bf16[128,1792]{1,0:T(8,128)(2,1)S(1)} %collective-permute-done.17.refs_0_, bf16[128,1792]{1,0:T(8,128)(2,1)S(1)} %collective-permute-done.18.refs_1_, ...), custom_call_target="tpu_custom_call" | custom-call | flops 1 | bytes 1 | tf_op jit(solution)/shard_map/pallas_call | solution.py:553
  121.0 3.3 %collective-permute-done.26.x_ref = bf16[128,1792]{1,0:T(8,128)(2,1)S(1)} collective-permute-done((bf16[128,1792]{1,0:T(8,128)(2,1)S(1)}, bf16[128,1792]{1,0:T(8,128)(2,1)S(1)}, u32[]{:S(2)}, u32[]{:S(2)}) %collective-permute-start.26) | collective-permute-done | bytes 458784 | tf_op jit(solution)/shard_map/ppermute | solution.py:322
  124.3 2.1 %shard_map.151 = (bf16[80,1792]{1,0:T(8,128)(2,1)S(1)}, bf16[48,1792]{1,0:T(8,128)(2,1)S(1)}) custom-call(bf16[128,1792]{1,0:T(8,128)(2,1)S(1)} %collective-permute-done.26.x_ref, bf16[3,1792,1024]{2,1,0:T(8,128)(2,1)S(1)} %get-tuple-element.79.all_w), custom_call_target="tpu_custom_call" | custom-call | flops 1 | bytes 1 | tf_op jit(solution)/shard_map/pallas_call | solution.py:572
  126.8 1.6 collective-permute-start.29
  128.3 9.7 %collective-permute-done.27.passed_ref = bf16[80,1792]{1,0:T(8,128)(2,1)S(1)} collective-permute-done((bf16[80,1792]{1,0:T(8,128)(2,1)S(1)}, bf16[80,1792]{1,0:T(8,128)(2,1)S(1)}, u32[]{:S(2)}, u32[]{:S(2)}) %collective-permute-start.27) | collective-permute-done | bytes 286752 | tf_op jit(solution)/shard_map/ppermute | solution.py:322
  139.3 18.9 %collective-permute-done.28.two_ref = bf16[128,1792]{1,0:T(8,128)(2,1)S(1)} collective-permute-done((bf16[128,1792]{1,0:T(8,128)(2,1)S(1)}, bf16[128,1792]{1,0:T(8,128)(2,1)S(1)}, u32[]{:S(2)}, u32[]{:S(2)}) %collective-permute-start.28) | collective-permute-done | bytes 458784 | tf_op jit(solution)/shard_map/ppermute | solution.py:322
  (73 shorter events, 16.2 us)
Async XLA Ops:
  2.9 26.0 %collective-permute-start.2 = (bf16[288,1792]{1,0:T(8,128)(2,1)}, bf16[288,1792]{1,0:T(8,128)(2,1)S(1)}, u32[]{:S(2)}, u32[]{:S(2)}) collective-permute-start(bf16[288,1792]{1,0:T(8,128)(2,1)} %get-tuple-element.46.refs_4_), channel_id=1, source_target_pairs={{0,8},{4,12},{8,0},{12,4},{16,24},{20,28},{24,16},{28,20},{1,9},{5... | collective-permute-start | bytes 3096584 | tf_op jit(solution)/shard_map/ppermute | solution.py:322
  5.9 24.5 %collective-permute-start.3 = (bf16[288,1792]{1,0:T(8,128)(2,1)}, bf16[288,1792]{1,0:T(8,128)(2,1)S(1)}, u32[]{:S(2)}, u32[]{:S(2)}) collective-permute-start(bf16[288,1792]{1,0:T(8,128)(2,1)} %get-tuple-element.46.refs_4_), channel_id=1, source_target_pairs={{0,16},{4,20},{8,24},{12,28},{16,0},{20,4},{24,8},{28,12},{1,17},{... | collective-permute-start | bytes 3096584 | tf_op jit(solution)/shard_map/ppermute | solution.py:322
  7.4 23.0 %collective-permute-start = (bf16[128,1792]{1,0:T(8,128)(2,1)}, bf16[128,1792]{1,0:T(8,128)(2,1)S(1)}, u32[]{:S(2)}, u32[]{:S(2)}) collective-permute-start(bf16[128,1792]{1,0:T(8,128)(2,1)} %get-tuple-element.45.refs_0_.x_ref), channel_id=1, source_target_pairs={{0,2},{1,3},{2,0},{3,1},{4,6},{5,7},{6,4},{7,5},{8,10},{9,11},{10,... | collective-permute-start | bytes 1376264 | tf_op jit(solution)/shard_map/ppermute | solution.py:322
  10.0 20.4 %collective-permute-start.1 = (bf16[128,1792]{1,0:T(8,128)(2,1)}, bf16[128,1792]{1,0:T(8,128)(2,1)S(1)}, u32[]{:S(2)}, u32[]{:S(2)}) collective-permute-start(bf16[128,1792]{1,0:T(8,128)(2,1)} %get-tuple-element.45.refs_0_.x_ref), channel_id=1, source_target_pairs={{0,1},{1,0},{2,3},{3,2},{4,5},{5,4},{6,7},{7,6},{8,9},{9,8},{10,11... | collective-permute-start | bytes 1376264 | tf_op jit(solution)/shard_map/ppermute | solution.py:322
  19.0 29.0 %copy-start.2 = (bf16[128,1792]{1,0:T(8,128)(2,1)S(1)}, bf16[128,1792]{1,0:T(8,128)(2,1)}, u32[]{:S(2)}) copy-start(bf16[128,1792]{1,0:T(8,128)(2,1)} %get-tuple-element.45.refs_0_.x_ref) | copy-start | bytes 1376260
  30.4 11.2 %collective-permute-start.4 = (bf16[128,1792]{1,0:T(8,128)(2,1)S(1)}, bf16[128,1792]{1,0:T(8,128)(2,1)S(1)}, u32[]{:S(2)}, u32[]{:S(2)}) collective-permute-start(bf16[128,1792]{1,0:T(8,128)(2,1)S(1)} %collective-permute-done.refs_2_), channel_id=1, source_target_pairs={{0,1},{1,0},{2,3},{3,2},{4,5},{5,4},{6,7},{7,6},{8,9},{9,8},{10,11... | collective-permute-start | bytes 1376264 | tf_op jit(solution)/shard_map/ppermute | solution.py:322
  32.0 12.3 %collective-permute-start.5 = (bf16[144,1792]{1,0:T(8,128)(2,1)S(1)}, bf16[144,1792]{1,0:T(8,128)(2,1)S(1)}, u32[]{:S(2)}, u32[]{:S(2)}) collective-permute-start(bf16[144,1792]{1,0:T(8,128)(2,1)S(1)} %slice.12), channel_id=1, source_target_pairs={{0,16},{4,20},{8,24},{12,28},{16,0},{20,4},{24,8},{28,12},{1,17},{... | collective-permute-start | bytes 1548296 | tf_op jit(solution)/shard_map/ppermute | solution.py:322
  33.6 11.8 %collective-permute-start.6 = (bf16[144,1792]{1,0:T(8,128)(2,1)S(1)}, bf16[144,1792]{1,0:T(8,128)(2,1)S(1)}, u32[]{:S(2)}, u32[]{:S(2)}) collective-permute-start(bf16[144,1792]{1,0:T(8,128)(2,1)S(1)} %slice.13), channel_id=1, source_target_pairs={{0,8},{4,12},{8,0},{12,4},{16,24},{20,28},{24,16},{28,20},{1,9},{5... | collective-permute-start | bytes 1548296 | tf_op jit(solution)/shard_map/ppermute | solution.py:322
  34.2 11.7 %collective-permute-start.7 = (bf16[288,1792]{1,0:T(8,128)(2,1)S(1)}, bf16[288,1792]{1,0:T(8,128)(2,1)S(1)}, u32[]{:S(2)}, u32[]{:S(2)}) collective-permute-start(bf16[288,1792]{1,0:T(8,128)(2,1)S(1)} %copy-done.3), channel_id=1, source_target_pairs={{0,4},{4,0},{8,12},{12,8},{16,20},{20,16},{24,28},{28,24},{1,5},{5... | collective-permute-start | bytes 3096584 | tf_op jit(solution)/shard_map/ppermute | solution.py:322
  34.2 11.7 %collective-permute-start.8 = (bf16[288,1792]{1,0:T(8,128)(2,1)S(1)}, bf16[288,1792]{1,0:T(8,128)(2,1)S(1)}, u32[]{:S(2)}, u32[]{:S(2)}) collective-permute-start(bf16[288,1792]{1,0:T(8,128)(2,1)S(1)} %collective-permute-done.2.refs_5_), channel_id=1, source_target_pairs={{0,4},{4,0},{8,12},{12,8},{16,20},{20,16},{24,28},{28,24},{1,5},{5... | collective-permute-start | bytes 3096584 | tf_op jit(solution)/shard_map/ppermute | solution.py:322
  41.5 4.4 %collective-permute-start.9 = (bf16[288,1792]{1,0:T(8,128)(2,1)S(1)}, bf16[288,1792]{1,0:T(8,128)(2,1)S(1)}, u32[]{:S(2)}, u32[]{:S(2)}) collective-permute-start(bf16[288,1792]{1,0:T(8,128)(2,1)S(1)} %collective-permute-done.3.refs_6_), channel_id=1, source_target_pairs={{0,4},{4,0},{8,12},{12,8},{16,20},{20,16},{24,28},{28,24},{1,5},{5... | collective-permute-start | bytes 3096584 | tf_op jit(solution)/shard_map/ppermute | solution.py:322
  45.4 1.9 %collective-permute-start.10 = (bf16[144,1792]{1,0:T(8,128)(2,1)S(1)}, bf16[144,1792]{1,0:T(8,128)(2,1)S(1)}, u32[]{:S(2)}, u32[]{:S(2)}) collective-permute-start(bf16[144,1792]{1,0:T(8,128)(2,1)S(1)} %collective-permute-done.5.refs_7_), channel_id=1, source_target_pairs={{0,4},{4,0},{8,12},{12,8},{16,20},{20,16},{24,28},{28,24},{1,5},{5... | collective-permute-start | bytes 1548296 | tf_op jit(solution)/shard_map/ppermute | solution.py:322
  45.4 2.6 %collective-permute-start.11 = (bf16[144,1792]{1,0:T(8,128)(2,1)S(1)}, bf16[144,1792]{1,0:T(8,128)(2,1)S(1)}, u32[]{:S(2)}, u32[]{:S(2)}) collective-permute-start(bf16[144,1792]{1,0:T(8,128)(2,1)S(1)} %collective-permute-done.6.refs_8_), channel_id=1, source_target_pairs={{0,4},{4,0},{8,12},{12,8},{16,20},{20,16},{24,28},{28,24},{1,5},{5... | collective-permute-start | bytes 1548296 | tf_op jit(solution)/shard_map/ppermute | solution.py:322
  53.4 12.8 %collective-permute-start.12 = (bf16[128,1792]{1,0:T(8,128)(2,1)S(1)}, bf16[128,1792]{1,0:T(8,128)(2,1)S(1)}, u32[]{:S(2)}, u32[]{:S(2)}) collective-permute-start(bf16[128,1792]{1,0:T(8,128)(2,1)S(1)} %get-tuple-element.67), channel_id=1, source_target_pairs={{0,1},{1,0},{2,3},{3,2},{4,5},{5,4},{6,7},{7,6},{8,9},{9,8},{10,11... | collective-permute-start | bytes 1376264 | tf_op jit(solution)/shard_map/ppermute | solution.py:322
  53.9 31.9 %collective-permute-start.15 = (bf16[3,224,1024]{2,1,0:T(8,128)(2,1)S(1)}, bf16[3,224,1024]{2,1,0:T(8,128)(2,1)S(1)}, u32[]{:S(2)}, u32[]{:S(2)}) collective-permute-start(bf16[3,224,1024]{2,1,0:T(8,128)(2,1)S(1)} %pad_maximum_fusion.refs_3_), channel_id=1, source_target_pairs={{0,8},{4,12},{8,0},{12,4},{16,24},{20,28},{24,16},{28,20},{1,9},{5... | collective-permute-start | bytes 4128776 | tf_op jit(solution)/shard_map/ppermute | solution.py:322
  54.6 31.6 %collective-permute-start.16 = (bf16[3,224,1024]{2,1,0:T(8,128)(2,1)S(1)}, bf16[3,224,1024]{2,1,0:T(8,128)(2,1)S(1)}, u32[]{:S(2)}, u32[]{:S(2)}) collective-permute-start(bf16[3,224,1024]{2,1,0:T(8,128)(2,1)S(1)} %pad_maximum_fusion.refs_3_), channel_id=1, source_target_pairs={{0,16},{4,20},{8,24},{12,28},{16,0},{20,4},{24,8},{28,12},{1,17},{... | collective-permute-start | bytes 4128776 | tf_op jit(solution)/shard_map/ppermute | solution.py:322
  63.9 21.4 %collective-permute-start.14 = (bf16[128,1792]{1,0:T(8,128)(2,1)S(1)}, bf16[128,1792]{1,0:T(8,128)(2,1)S(1)}, u32[]{:S(2)}, u32[]{:S(2)}) collective-permute-start(bf16[128,1792]{1,0:T(8,128)(2,1)S(1)} %get-tuple-element.68), channel_id=1, source_target_pairs={{0,1},{1,0},{2,3},{3,2},{4,5},{5,4},{6,7},{7,6},{8,9},{9,8},{10,11... | collective-permute-start | bytes 1376264 | tf_op jit(solution)/shard_map/ppermute | solution.py:322
  66.3 22.4 %collective-permute-start.13 = (bf16[128,1792]{1,0:T(8,128)(2,1)S(1)}, bf16[128,1792]{1,0:T(8,128)(2,1)S(1)}, u32[]{:S(2)}, u32[]{:S(2)}) collective-permute-start(bf16[128,1792]{1,0:T(8,128)(2,1)S(1)} %add_convert_fusion), channel_id=1, source_target_pairs={{0,2},{1,3},{2,0},{3,1},{4,6},{5,7},{6,4},{7,5},{8,10},{9,11},{10,... | collective-permute-start | bytes 1376264 | tf_op jit(solution)/shard_map/ppermute | solution.py:322
  89.1 19.5 %collective-permute-start.17 = (bf16[128,1792]{1,0:T(8,128)(2,1)S(1)}, bf16[128,1792]{1,0:T(8,128)(2,1)S(1)}, u32[]{:S(2)}, u32[]{:S(2)}) collective-permute-start(bf16[128,1792]{1,0:T(8,128)(2,1)S(1)} %get-tuple-element.72.refs_2_), channel_id=1, source_target_pairs={{0,2},{1,3},{2,0},{3,1},{4,6},{5,7},{6,4},{7,5},{8,10},{9,11},{10,... | collective-permute-start | bytes 1376264 | tf_op jit(solution)/shard_map/ppermute | solution.py:322
  89.3 19.4 %collective-permute-start.18 = (bf16[128,1792]{1,0:T(8,128)(2,1)S(1)}, bf16[128,1792]{1,0:T(8,128)(2,1)S(1)}, u32[]{:S(2)}, u32[]{:S(2)}) collective-permute-start(bf16[128,1792]{1,0:T(8,128)(2,1)S(1)} %get-tuple-element.72.refs_2_), channel_id=1, source_target_pairs={{0,1},{1,0},{2,3},{3,2},{4,5},{5,4},{6,7},{7,6},{8,9},{9,8},{10,11... | collective-permute-start | bytes 1376264 | tf_op jit(solution)/shard_map/ppermute | solution.py:322
  92.2 19.1 %collective-permute-start.21 = (bf16[3,224,1024]{2,1,0:T(8,128)(2,1)S(1)}, bf16[3,224,1024]{2,1,0:T(8,128)(2,1)S(1)}, u32[]{:S(2)}, u32[]{:S(2)}) collective-permute-start(bf16[3,224,1024]{2,1,0:T(8,128)(2,1)S(1)} %pad_maximum_fusion.refs_3_), channel_id=1, source_target_pairs={{0,4},{4,0},{8,12},{12,8},{16,20},{20,16},{24,28},{28,24},{1,5},{5... | collective-permute-start | bytes 4128776 | tf_op jit(solution)/shard_map/ppermute | solution.py:322
  92.3 17.9 %collective-permute-start.19 = (bf16[3,112,1024]{2,1,0:T(8,128)(2,1)S(1)}, bf16[3,112,1024]{2,1,0:T(8,128)(2,1)S(1)}, u32[]{:S(2)}, u32[]{:S(2)}) collective-permute-start(bf16[3,112,1024]{2,1,0:T(8,128)(2,1)S(1)} %slice.14), channel_id=1, source_target_pairs={{0,16},{4,20},{8,24},{12,28},{16,0},{20,4},{24,8},{28,12},{1,17},{... | collective-permute-start | bytes 2064392 | tf_op jit(solution)/shard_map/ppermute | solution.py:322
  93.7 17.6 %collective-permute-start.20 = (bf16[3,112,1024]{2,1,0:T(8,128)(2,1)S(1)}, bf16[3,112,1024]{2,1,0:T(8,128)(2,1)S(1)}, u32[]{:S(2)}, u32[]{:S(2)}) collective-permute-start(bf16[3,112,1024]{2,1,0:T(8,128)(2,1)S(1)} %slice.15), channel_id=1, source_target_pairs={{0,8},{4,12},{8,0},{12,4},{16,24},{20,28},{24,16},{28,20},{1,9},{5... | collective-permute-start | bytes 2064392 | tf_op jit(solution)/shard_map/ppermute | solution.py:322
  108.6 7.1 %collective-permute-start.22 = (bf16[3,224,1024]{2,1,0:T(8,128)(2,1)S(1)}, bf16[3,224,1024]{2,1,0:T(8,128)(2,1)S(1)}, u32[]{:S(2)}, u32[]{:S(2)}) collective-permute-start(bf16[3,224,1024]{2,1,0:T(8,128)(2,1)S(1)} %collective-permute-done.15.refs_4_), channel_id=1, source_target_pairs={{0,4},{4,0},{8,12},{12,8},{16,20},{20,16},{24,28},{28,24},{1,5},{5... | collective-permute-start | bytes 4128776 | tf_op jit(solution)/shard_map/ppermute | solution.py:322
  108.7 7.0 %collective-permute-start.23 = (bf16[3,224,1024]{2,1,0:T(8,128)(2,1)S(1)}, bf16[3,224,1024]{2,1,0:T(8,128)(2,1)S(1)}, u32[]{:S(2)}, u32[]{:S(2)}) collective-permute-start(bf16[3,224,1024]{2,1,0:T(8,128)(2,1)S(1)} %collective-permute-done.16.refs_5_), channel_id=1, source_target_pairs={{0,4},{4,0},{8,12},{12,8},{16,20},{20,16},{24,28},{28,24},{1,5},{5... | collective-permute-start | bytes 4128776 | tf_op jit(solution)/shard_map/ppermute | solution.py:322
  110.2 4.5 %collective-permute-start.24 = (bf16[3,112,1024]{2,1,0:T(8,128)(2,1)S(1)}, bf16[3,112,1024]{2,1,0:T(8,128)(2,1)S(1)}, u32[]{:S(2)}, u32[]{:S(2)}) collective-permute-start(bf16[3,112,1024]{2,1,0:T(8,128)(2,1)S(1)} %collective-permute-done.19.refs_6_), channel_id=1, source_target_pairs={{0,4},{4,0},{8,12},{12,8},{16,20},{20,16},{24,28},{28,24},{1,5},{5... | collective-permute-start | bytes 2064392 | tf_op jit(solution)/shard_map/ppermute | solution.py:322
  111.3 4.4 %collective-permute-start.25 = (bf16[3,112,1024]{2,1,0:T(8,128)(2,1)S(1)}, bf16[3,112,1024]{2,1,0:T(8,128)(2,1)S(1)}, u32[]{:S(2)}, u32[]{:S(2)}) collective-permute-start(bf16[3,112,1024]{2,1,0:T(8,128)(2,1)S(1)} %collective-permute-done.20.refs_7_), channel_id=1, source_target_pairs={{0,4},{4,0},{8,12},{12,8},{16,20},{20,16},{24,28},{28,24},{1,5},{5... | collective-permute-start | bytes 2064392 | tf_op jit(solution)/shard_map/ppermute | solution.py:322
  111.3 12.9 %collective-permute-start.26 = (bf16[128,1792]{1,0:T(8,128)(2,1)S(1)}, bf16[128,1792]{1,0:T(8,128)(2,1)S(1)}, u32[]{:S(2)}, u32[]{:S(2)}) collective-permute-start(bf16[128,1792]{1,0:T(8,128)(2,1)S(1)} %collective-permute-done.17.refs_0_), channel_id=1, source_target_pairs={{0,1},{1,0},{2,3},{3,2},{4,5},{5,4},{6,7},{7,6},{8,9},{9,8},{10,11... | collective-permute-start | bytes 1376264 | tf_op jit(solution)/shard_map/ppermute | solution.py:322
  126.4 11.6 %collective-permute-start.27 = (bf16[80,1792]{1,0:T(8,128)(2,1)S(1)}, bf16[80,1792]{1,0:T(8,128)(2,1)S(1)}, u32[]{:S(2)}, u32[]{:S(2)}) collective-permute-start(bf16[80,1792]{1,0:T(8,128)(2,1)S(1)} %get-tuple-element.80), channel_id=1, source_target_pairs={{0,1},{1,0},{2,3},{3,2},{4,5},{5,4},{6,7},{7,6},{8,9},{9,8},{10,11... | collective-permute-start | bytes 860168 | tf_op jit(solution)/shard_map/ppermute | solution.py:322
  126.8 12.6 %collective-permute-start.29 = (bf16[48,1792]{1,0:T(8,128)(2,1)S(1)}, bf16[48,1792]{1,0:T(8,128)(2,1)S(1)}, u32[]{:S(2)}, u32[]{:S(2)}) collective-permute-start(bf16[48,1792]{1,0:T(8,128)(2,1)S(1)} %get-tuple-element.81), channel_id=1, source_target_pairs={{0,3},{1,2},{2,1},{3,0},{4,7},{5,6},{6,5},{7,4},{8,11},{9,10},{10,... | collective-permute-start | bytes 516104 | tf_op jit(solution)/shard_map/ppermute | solution.py:322
  138.1 20.1 %collective-permute-start.28 = (bf16[128,1792]{1,0:T(8,128)(2,1)S(1)}, bf16[128,1792]{1,0:T(8,128)(2,1)S(1)}, u32[]{:S(2)}, u32[]{:S(2)}) collective-permute-start(bf16[128,1792]{1,0:T(8,128)(2,1)S(1)} %shard_map.152), channel_id=1, source_target_pairs={{0,2},{1,3},{2,0},{3,1},{4,6},{5,7},{6,4},{7,5},{8,10},{9,11},{10,... | collective-permute-start | bytes 1376264 | tf_op jit(solution)/shard_map/ppermute | solution.py:322
  139.3 20.0 %collective-permute-start.30 = (bf16[128,1792]{1,0:T(8,128)(2,1)S(1)}, bf16[128,1792]{1,0:T(8,128)(2,1)S(1)}, u32[]{:S(2)}, u32[]{:S(2)}) collective-permute-start(bf16[128,1792]{1,0:T(8,128)(2,1)S(1)} %get-tuple-element.83), channel_id=1, source_target_pairs={{0,1},{1,0},{2,3},{3,2},{4,5},{5,4},{6,7},{7,6},{8,9},{9,8},{10,11... | collective-permute-start | bytes 1376264 | tf_op jit(solution)/shard_map/ppermute | solution.py:322
  (10 other events, 149.1 us)

commit v6 on v5

--- a/solution.py
+++ b/solution.py
@@ -260,9 +260,11 @@
         load.start()
     x_ref, qkv_ref, out_ref, gain_ref, down_ref, up_ref = targets
     rows, part, ranks = qkv_ref.shape[1], qkv_ref.shape[2], down_ref.shape[0]
-    for load in loads:
-        load.wait()
+    loads[0].wait()
+    loads[3].wait()
     normed_ref[...] = normed(x_ref[...].astype(jnp.float32), gain_ref[...][None, :])
+    for at in (1, 2, 4, 5):
+        loads[at].wait()
     for place, which in enumerate((1, 0, 2)):
         packed_ref[:rows, place * part : (place + 1) * part] = qkv_ref[which]
     out_rows = jnp.transpose(out_ref[...].astype(jnp.float32)).astype(jnp.bfloat16)

time: 161 us -> 160 us (level)
  no operation moved by 1% of the time
where the time goes in v6:
time: 160 us
  waiting for transfers between devices  95.6 us (60%)
  Pallas kernels  29.3 us (18%)
  starting transfers between devices  27.3 us (17%)
  local copies, waits for them, and re-layouts  7.43 us (5%)
    ppermute x31, waiting for transfers between devices, swap(): return lax.ppermute(value, axis, xor_pairs(lax.axis_size(axis), mask))  95.6 us
    ppermute x31, starting transfers between devices, swap(): return lax.ppermute(value, axis, xor_pairs(lax.axis_size(axis), mask))  27.3 us
    pallas_call x1, Pallas kernels, rest_call(): pl.pallas_call(functools.partial(rest_kernel, masks), out_shape=[jax.Shap...  8.68 us
    reshape x2, local copies, waits for them, and re-layouts, tuned(): cache = window_key_value.reshape(requests, 2, heads, window, HD)  5.55 us
    pallas_call x1, Pallas kernels, first_call(): pl.pallas_call(functools.partial(first_kernel, places, n_x, n_w), out_sha...  5.35 us
    pallas_call x1, Pallas kernels, feed_first_call(): pl.pallas_call(functools.partial(feed_first_kernel, places, n_x, n_w), ou...  5.28 us
    pallas_call x1, Pallas kernels, own_call(): pl.pallas_call(functools.partial(own_kernel, rank), out_shape=jax.ShapeDt...  3.7 us
  transfers between devices with their start and end apart: 31, of which 23 were waited for; matrix products, arithmetic and copies ran while one was open for 5% of the time, Pallas kernels for 11%

profile of v6, /device:TPU:0, one launch (start us, length us, event | category | flops | bytes accessed | tf_op | source)
XLA Modules:
  0.0 160.2 jit_solution(13703213083880216225)
XLA Ops:
  0.0 2.7 %shard_map.145 = (bf16[128,1792]{1,0:T(8,128)(2,1)}, bf16[288,1792]{1,0:T(8,128)(2,1)}) custom-call(bf16[128,1792]{1,0:T(8,128)(2,1)} %x_ref.1, bf16[3,224,448]{2,1,0:T(8,128)(2,1)} %bitcast.14, bf16[448,224]{1,0:T(8,128)(2,1)} %refs_2_.1, f32[1792]{0:T(1024)} %refs_3_.1, bf16[32,1792]{1,0:T(8,128)(2,1)} %bitcast.18, bf16[32,1792]{1,0:T(8,128)(2,1)} %bitcast.19), custom_call_target="tpu_custom_call" | custom-call | flops 1 | bytes 1 | tf_op jit(solution)/shard_map/pallas_call | solution.py:278
  2.7 3.0 %collective-permute-start.2 = (bf16[288,1792]{1,0:T(8,128)(2,1)}, bf16[288,1792]{1,0:T(8,128)(2,1)S(1)}, u32[]{:S(2)}, u32[]{:S(2)}) collective-permute-start(bf16[288,1792]{1,0:T(8,128)(2,1)} %get-tuple-element.46.refs_4_), channel_id=1, source_target_pairs={{0,8},{4,12},{8,0},{12,4},{16,24},{20,28},{24,16},{28,20},{1,9},{5... | collective-permute-start | bytes 3096584 | tf_op jit(solution)/shard_map/ppermute | solution.py:324
  5.7 1.5 collective-permute-start.3
  7.2 2.6 %collective-permute-start = (bf16[128,1792]{1,0:T(8,128)(2,1)}, bf16[128,1792]{1,0:T(8,128)(2,1)S(1)}, u32[]{:S(2)}, u32[]{:S(2)}) collective-permute-start(bf16[128,1792]{1,0:T(8,128)(2,1)} %get-tuple-element.45.refs_0_.x_ref), channel_id=1, source_target_pairs={{0,2},{1,3},{2,0},{3,1},{4,6},{5,7},{6,4},{7,5},{8,10},{9,11},{10,... | collective-permute-start | bytes 1376264 | tf_op jit(solution)/shard_map/ppermute | solution.py:324
  9.8 1.6 collective-permute-start.1
  11.4 3.3 %reshape.14 = bf16[8,2,4,64,112]{4,3,2,1,0:T(8,128)(2,1)} reshape(bf16[8,2,4,7168]{3,2,1,0:T(4,128)(2,1)} %param.20) | data formatting | bytes 1835008 | tf_op jit(solution)/shard_map/reshape | solution.py:659
  14.7 2.3 %copy.16 = bf16[8,2,4,64,112]{4,3,0,2,1:T(8,128)(2,1)} copy(bf16[8,2,4,64,112]{4,3,2,1,0:T(8,128)(2,1)} %reshape.14) | data formatting | bytes 1835008 | tf_op jit(solution)/shard_map/reshape | solution.py:659
  17.1 1.5 pad.4.refs_17_.cache_ref.refs_2_
  18.9 9.8 %collective-permute-done.2.refs_5_ = bf16[288,1792]{1,0:T(8,128)(2,1)S(1)} collective-permute-done((bf16[288,1792]{1,0:T(8,128)(2,1)}, bf16[288,1792]{1,0:T(8,128)(2,1)S(1)}, u32[]{:S(2)}, u32[]{:S(2)}) %collective-permute-start.2) | collective-permute-done | bytes 1032224 | tf_op jit(solution)/shard_map/ppermute | solution.py:324
  28.7 1.5 collective-permute-done.3.refs_6_
  30.2 1.6 collective-permute-start.4
  31.8 1.6 collective-permute-start.5
  34.6 6.8 %collective-permute-done.4.refs_3_ = bf16[128,1792]{1,0:T(8,128)(2,1)S(1)} collective-permute-done((bf16[128,1792]{1,0:T(8,128)(2,1)S(1)}, bf16[128,1792]{1,0:T(8,128)(2,1)S(1)}, u32[]{:S(2)}, u32[]{:S(2)}) %collective-permute-start.4) | collective-permute-done | bytes 458784 | tf_op jit(solution)/shard_map/ppermute | solution.py:324
  41.4 2.8 %collective-permute-done.5.refs_7_ = bf16[144,1792]{1,0:T(8,128)(2,1)S(1)} collective-permute-done((bf16[144,1792]{1,0:T(8,128)(2,1)S(1)}, bf16[144,1792]{1,0:T(8,128)(2,1)S(1)}, u32[]{:S(2)}, u32[]{:S(2)}) %collective-permute-start.5) | collective-permute-done | bytes 516128 | tf_op jit(solution)/shard_map/ppermute | solution.py:324
  45.8 1.4 collective-permute-done.10.refs_12_
  47.9 5.3 %shard_map.146 = (bf16[512,1792]{1,0:T(8,128)(2,1)S(1)}, bf16[1792,1408]{1,0:T(8,128)(2,1)S(1)}, bf16[1792,512]{1,0:T(8,128)(2,1)S(1)}, bf16[256,1792]{1,0:T(8,1...) custom-call(bf16[128,1792]{1,0:T(8,128)(2,1)S(1)} %copy-done.2, ...), custom_call_target="tpu_custom_call" | custom-call | flops 1 | bytes 1 | tf_op jit(solution)/shard_map/pallas_call | solution.py:471
  55.0 8.7 %shard_map.147 = (bf16[512,512]{1,0:T(8,128)(2,1)S(1)}, bf16[512,512]{1,0:T(8,128)(2,1)S(1)}, bf16[512,512]{1,0:T(8,128)(2,1)S(1)}, bf16[128,1792]{1,0:T(8,128)(2,1)S(1)}, bf16[128,1792]{1,0:T(8,128)(2,1)S(1)}) custom-call(bf16[512,1792]{1,0:T(8,128)(2,1)S(1)} %get-tuple-element.57.x_all, bf16[1792,1408]{1,0:T(8,128)(2,1)S(1)} %get-tuple-element.58.w_all, ...), custom_call_target="tpu_custom_call" | custom-call | flops 1 | bytes 1 | tf_op jit(solution)/shard_map/pallas_call | solution.py:500
  63.7 1.7 %collective-permute-start.14 = (bf16[128,1792]{1,0:T(8,128)(2,1)S(1)}, bf16[128,1792]{1,0:T(8,128)(2,1)S(1)}, u32[]{:S(2)}, u32[]{:S(2)}) collective-permute-start(bf16[128,1792]{1,0:T(8,128)(2,1)S(1)} %get-tuple-element.68), channel_id=1, source_target_pairs={{0,1},{1,0},{2,3},{3,2},{4,5},{5,4},{6,7},{7,6},{8,9},{9,8},{10,11... | collective-permute-start | bytes 1376264 | tf_op jit(solution)/shard_map/ppermute | solution.py:324
  66.2 2.7 %collective-permute-start.13 = (bf16[128,1792]{1,0:T(8,128)(2,1)S(1)}, bf16[128,1792]{1,0:T(8,128)(2,1)S(1)}, u32[]{:S(2)}, u32[]{:S(2)}) collective-permute-start(bf16[128,1792]{1,0:T(8,128)(2,1)S(1)} %add_convert_fusion), channel_id=1, source_target_pairs={{0,2},{1,3},{2,0},{3,1},{4,6},{5,7},{6,4},{7,5},{8,10},{9,11},{10,... | collective-permute-start | bytes 1376264 | tf_op jit(solution)/shard_map/ppermute | solution.py:324
  68.9 3.7 %shard_map.148.own_ref = f32[128,1792]{1,0:T(8,128)S(1)} custom-call(bf16[512,512]{1,0:T(8,128)(2,1)S(1)} %get-tuple-element.60.q_ref, bf16[512,512]{1,0:T(8,128)(2,1)S(1)} %get-tuple-element.61.k_ref, bf16[512,512]{1,0:T(8,128)(2,1)S(1)} %get-tuple-element.62.v_ref, bf16[1792,512]{1,0:T(8,128)(2,1)S(1)} %get-tuple-element.59.out_w, ...), custom_call_target="tpu_custom_call" | custom-call | flops 1 | bytes 1 | tf_op jit(solution)/shard_map/pallas_call | solution.py:521
  72.6 12.5 %collective-permute-done.14.one_ref = bf16[128,1792]{1,0:T(8,128)(2,1)S(1)} collective-permute-done((bf16[128,1792]{1,0:T(8,128)(2,1)S(1)}, bf16[128,1792]{1,0:T(8,128)(2,1)S(1)}, u32[]{:S(2)}, u32[]{:S(2)}) %collective-permute-start.14) | collective-permute-done | bytes 458784 | tf_op jit(solution)/shard_map/ppermute | solution.py:324
  86.1 2.5 %collective-permute-done.13.two_ref = bf16[128,1792]{1,0:T(8,128)(2,1)S(1)} collective-permute-done((bf16[128,1792]{1,0:T(8,128)(2,1)S(1)}, bf16[128,1792]{1,0:T(8,128)(2,1)S(1)}, u32[]{:S(2)}, u32[]{:S(2)}) %collective-permute-start.13) | collective-permute-done | bytes 458784 | tf_op jit(solution)/shard_map/ppermute | solution.py:324
  89.2 2.9 %collective-permute-start.18 = (bf16[128,1792]{1,0:T(8,128)(2,1)S(1)}, bf16[128,1792]{1,0:T(8,128)(2,1)S(1)}, u32[]{:S(2)}, u32[]{:S(2)}) collective-permute-start(bf16[128,1792]{1,0:T(8,128)(2,1)S(1)} %get-tuple-element.72.refs_2_), channel_id=1, source_target_pairs={{0,1},{1,0},{2,3},{3,2},{4,5},{5,4},{6,7},{7,6},{8,9},{9,8},{10,11... | collective-permute-start | bytes 1376264 | tf_op jit(solution)/shard_map/ppermute | solution.py:324
  92.1 1.3 collective-permute-start.19
  94.3 14.2 %collective-permute-done.17.refs_0_ = bf16[128,1792]{1,0:T(8,128)(2,1)S(1)} collective-permute-done((bf16[128,1792]{1,0:T(8,128)(2,1)S(1)}, bf16[128,1792]{1,0:T(8,128)(2,1)S(1)}, u32[]{:S(2)}, u32[]{:S(2)}) %collective-permute-start.17) | collective-permute-done | bytes 458784 | tf_op jit(solution)/shard_map/ppermute | solution.py:324
  111.2 3.4 %collective-permute-done.24.refs_11_ = bf16[3,112,1024]{2,1,0:T(8,128)(2,1)S(1)} collective-permute-done((bf16[3,112,1024]{2,1,0:T(8,128)(2,1)S(1)}, bf16[3,112,1024]{2,1,0:T(8,128)(2,1)S(1)}, u32[]{:S(2)}, u32[]{:S(2)}) %collective-permute-start.24) | collective-permute-done | bytes 688160 | tf_op jit(solution)/shard_map/ppermute | solution.py:324
  115.5 5.3 %shard_map.150 = (bf16[3,1792,1024]{2,1,0:T(8,128)(2,1)S(1)}, bf16[128,1792]{1,0:T(8,128)(2,1)S(1)}, bf16[128,1792]{1,0:T(8,128)(2,1)S(1)}, f32[128,1792]{1,0:T(8,128)S(1)}) custom-call(bf16[128,1792]{1,0:T(8,128)(2,1)S(1)} %collective-permute-done.17.refs_0_, bf16[128,1792]{1,0:T(8,128)(2,1)S(1)} %collective-permute-done.18.refs_1_, ...), custom_call_target="tpu_custom_call" | custom-call | flops 1 | bytes 1 | tf_op jit(solution)/shard_map/pallas_call | solution.py:555
  120.8 3.2 %collective-permute-done.26.x_ref = bf16[128,1792]{1,0:T(8,128)(2,1)S(1)} collective-permute-done((bf16[128,1792]{1,0:T(8,128)(2,1)S(1)}, bf16[128,1792]{1,0:T(8,128)(2,1)S(1)}, u32[]{:S(2)}, u32[]{:S(2)}) %collective-permute-start.26) | collective-permute-done | bytes 458784 | tf_op jit(solution)/shard_map/ppermute | solution.py:324
  124.1 2.1 %shard_map.151 = (bf16[80,1792]{1,0:T(8,128)(2,1)S(1)}, bf16[48,1792]{1,0:T(8,128)(2,1)S(1)}) custom-call(bf16[128,1792]{1,0:T(8,128)(2,1)S(1)} %collective-permute-done.26.x_ref, bf16[3,1792,1024]{2,1,0:T(8,128)(2,1)S(1)} %get-tuple-element.79.all_w), custom_call_target="tpu_custom_call" | custom-call | flops 1 | bytes 1 | tf_op jit(solution)/shard_map/pallas_call | solution.py:574
  126.6 1.6 collective-permute-start.29
  128.1 9.6 %collective-permute-done.27.passed_ref = bf16[80,1792]{1,0:T(8,128)(2,1)S(1)} collective-permute-done((bf16[80,1792]{1,0:T(8,128)(2,1)S(1)}, bf16[80,1792]{1,0:T(8,128)(2,1)S(1)}, u32[]{:S(2)}, u32[]{:S(2)}) %collective-permute-start.27) | collective-permute-done | bytes 286752 | tf_op jit(solution)/shard_map/ppermute | solution.py:324
  139.2 18.9 %collective-permute-done.28.two_ref = bf16[128,1792]{1,0:T(8,128)(2,1)S(1)} collective-permute-done((bf16[128,1792]{1,0:T(8,128)(2,1)S(1)}, bf16[128,1792]{1,0:T(8,128)(2,1)S(1)}, u32[]{:S(2)}, u32[]{:S(2)}) %collective-permute-start.28) | collective-permute-done | bytes 458784 | tf_op jit(solution)/shard_map/ppermute | solution.py:324
  (73 shorter events, 16.3 us)
Async XLA Ops:
  2.7 26.0 %collective-permute-start.2 = (bf16[288,1792]{1,0:T(8,128)(2,1)}, bf16[288,1792]{1,0:T(8,128)(2,1)S(1)}, u32[]{:S(2)}, u32[]{:S(2)}) collective-permute-start(bf16[288,1792]{1,0:T(8,128)(2,1)} %get-tuple-element.46.refs_4_), channel_id=1, source_target_pairs={{0,8},{4,12},{8,0},{12,4},{16,24},{20,28},{24,16},{28,20},{1,9},{5... | collective-permute-start | bytes 3096584 | tf_op jit(solution)/shard_map/ppermute | solution.py:324
  5.7 24.5 %collective-permute-start.3 = (bf16[288,1792]{1,0:T(8,128)(2,1)}, bf16[288,1792]{1,0:T(8,128)(2,1)S(1)}, u32[]{:S(2)}, u32[]{:S(2)}) collective-permute-start(bf16[288,1792]{1,0:T(8,128)(2,1)} %get-tuple-element.46.refs_4_), channel_id=1, source_target_pairs={{0,16},{4,20},{8,24},{12,28},{16,0},{20,4},{24,8},{28,12},{1,17},{... | collective-permute-start | bytes 3096584 | tf_op jit(solution)/shard_map/ppermute | solution.py:324
  7.2 23.0 %collective-permute-start = (bf16[128,1792]{1,0:T(8,128)(2,1)}, bf16[128,1792]{1,0:T(8,128)(2,1)S(1)}, u32[]{:S(2)}, u32[]{:S(2)}) collective-permute-start(bf16[128,1792]{1,0:T(8,128)(2,1)} %get-tuple-element.45.refs_0_.x_ref), channel_id=1, source_target_pairs={{0,2},{1,3},{2,0},{3,1},{4,6},{5,7},{6,4},{7,5},{8,10},{9,11},{10,... | collective-permute-start | bytes 1376264 | tf_op jit(solution)/shard_map/ppermute | solution.py:324
  9.8 20.4 %collective-permute-start.1 = (bf16[128,1792]{1,0:T(8,128)(2,1)}, bf16[128,1792]{1,0:T(8,128)(2,1)S(1)}, u32[]{:S(2)}, u32[]{:S(2)}) collective-permute-start(bf16[128,1792]{1,0:T(8,128)(2,1)} %get-tuple-element.45.refs_0_.x_ref), channel_id=1, source_target_pairs={{0,1},{1,0},{2,3},{3,2},{4,5},{5,4},{6,7},{7,6},{8,9},{9,8},{10,11... | collective-permute-start | bytes 1376264 | tf_op jit(solution)/shard_map/ppermute | solution.py:324
  18.8 29.0 %copy-start.2 = (bf16[128,1792]{1,0:T(8,128)(2,1)S(1)}, bf16[128,1792]{1,0:T(8,128)(2,1)}, u32[]{:S(2)}) copy-start(bf16[128,1792]{1,0:T(8,128)(2,1)} %get-tuple-element.45.refs_0_.x_ref) | copy-start | bytes 1376260
  30.2 11.2 %collective-permute-start.4 = (bf16[128,1792]{1,0:T(8,128)(2,1)S(1)}, bf16[128,1792]{1,0:T(8,128)(2,1)S(1)}, u32[]{:S(2)}, u32[]{:S(2)}) collective-permute-start(bf16[128,1792]{1,0:T(8,128)(2,1)S(1)} %collective-permute-done.refs_2_), channel_id=1, source_target_pairs={{0,1},{1,0},{2,3},{3,2},{4,5},{5,4},{6,7},{7,6},{8,9},{9,8},{10,11... | collective-permute-start | bytes 1376264 | tf_op jit(solution)/shard_map/ppermute | solution.py:324
  31.8 12.3 %collective-permute-start.5 = (bf16[144,1792]{1,0:T(8,128)(2,1)S(1)}, bf16[144,1792]{1,0:T(8,128)(2,1)S(1)}, u32[]{:S(2)}, u32[]{:S(2)}) collective-permute-start(bf16[144,1792]{1,0:T(8,128)(2,1)S(1)} %slice.12), channel_id=1, source_target_pairs={{0,16},{4,20},{8,24},{12,28},{16,0},{20,4},{24,8},{28,12},{1,17},{... | collective-permute-start | bytes 1548296 | tf_op jit(solution)/shard_map/ppermute | solution.py:324
  33.4 11.8 %collective-permute-start.6 = (bf16[144,1792]{1,0:T(8,128)(2,1)S(1)}, bf16[144,1792]{1,0:T(8,128)(2,1)S(1)}, u32[]{:S(2)}, u32[]{:S(2)}) collective-permute-start(bf16[144,1792]{1,0:T(8,128)(2,1)S(1)} %slice.13), channel_id=1, source_target_pairs={{0,8},{4,12},{8,0},{12,4},{16,24},{20,28},{24,16},{28,20},{1,9},{5... | collective-permute-start | bytes 1548296 | tf_op jit(solution)/shard_map/ppermute | solution.py:324
  34.0 11.7 %collective-permute-start.7 = (bf16[288,1792]{1,0:T(8,128)(2,1)S(1)}, bf16[288,1792]{1,0:T(8,128)(2,1)S(1)}, u32[]{:S(2)}, u32[]{:S(2)}) collective-permute-start(bf16[288,1792]{1,0:T(8,128)(2,1)S(1)} %copy-done.3), channel_id=1, source_target_pairs={{0,4},{4,0},{8,12},{12,8},{16,20},{20,16},{24,28},{28,24},{1,5},{5... | collective-permute-start | bytes 3096584 | tf_op jit(solution)/shard_map/ppermute | solution.py:324
  34.0 11.7 %collective-permute-start.8 = (bf16[288,1792]{1,0:T(8,128)(2,1)S(1)}, bf16[288,1792]{1,0:T(8,128)(2,1)S(1)}, u32[]{:S(2)}, u32[]{:S(2)}) collective-permute-start(bf16[288,1792]{1,0:T(8,128)(2,1)S(1)} %collective-permute-done.2.refs_5_), channel_id=1, source_target_pairs={{0,4},{4,0},{8,12},{12,8},{16,20},{20,16},{24,28},{28,24},{1,5},{5... | collective-permute-start | bytes 3096584 | tf_op jit(solution)/shard_map/ppermute | solution.py:324
  41.4 4.4 %collective-permute-start.9 = (bf16[288,1792]{1,0:T(8,128)(2,1)S(1)}, bf16[288,1792]{1,0:T(8,128)(2,1)S(1)}, u32[]{:S(2)}, u32[]{:S(2)}) collective-permute-start(bf16[288,1792]{1,0:T(8,128)(2,1)S(1)} %collective-permute-done.3.refs_6_), channel_id=1, source_target_pairs={{0,4},{4,0},{8,12},{12,8},{16,20},{20,16},{24,28},{28,24},{1,5},{5... | collective-permute-start | bytes 3096584 | tf_op jit(solution)/shard_map/ppermute | solution.py:324
  45.2 1.9 %collective-permute-start.10 = (bf16[144,1792]{1,0:T(8,128)(2,1)S(1)}, bf16[144,1792]{1,0:T(8,128)(2,1)S(1)}, u32[]{:S(2)}, u32[]{:S(2)}) collective-permute-start(bf16[144,1792]{1,0:T(8,128)(2,1)S(1)} %collective-permute-done.5.refs_7_), channel_id=1, source_target_pairs={{0,4},{4,0},{8,12},{12,8},{16,20},{20,16},{24,28},{28,24},{1,5},{5... | collective-permute-start | bytes 1548296 | tf_op jit(solution)/shard_map/ppermute | solution.py:324
  45.2 2.6 %collective-permute-start.11 = (bf16[144,1792]{1,0:T(8,128)(2,1)S(1)}, bf16[144,1792]{1,0:T(8,128)(2,1)S(1)}, u32[]{:S(2)}, u32[]{:S(2)}) collective-permute-start(bf16[144,1792]{1,0:T(8,128)(2,1)S(1)} %collective-permute-done.6.refs_8_), channel_id=1, source_target_pairs={{0,4},{4,0},{8,12},{12,8},{16,20},{20,16},{24,28},{28,24},{1,5},{5... | collective-permute-start | bytes 1548296 | tf_op jit(solution)/shard_map/ppermute | solution.py:324
  53.3 12.8 %collective-permute-start.12 = (bf16[128,1792]{1,0:T(8,128)(2,1)S(1)}, bf16[128,1792]{1,0:T(8,128)(2,1)S(1)}, u32[]{:S(2)}, u32[]{:S(2)}) collective-permute-start(bf16[128,1792]{1,0:T(8,128)(2,1)S(1)} %get-tuple-element.67), channel_id=1, source_target_pairs={{0,1},{1,0},{2,3},{3,2},{4,5},{5,4},{6,7},{7,6},{8,9},{9,8},{10,11... | collective-permute-start | bytes 1376264 | tf_op jit(solution)/shard_map/ppermute | solution.py:324
  53.8 31.9 %collective-permute-start.15 = (bf16[3,224,1024]{2,1,0:T(8,128)(2,1)S(1)}, bf16[3,224,1024]{2,1,0:T(8,128)(2,1)S(1)}, u32[]{:S(2)}, u32[]{:S(2)}) collective-permute-start(bf16[3,224,1024]{2,1,0:T(8,128)(2,1)S(1)} %pad_maximum_fusion.refs_3_), channel_id=1, source_target_pairs={{0,8},{4,12},{8,0},{12,4},{16,24},{20,28},{24,16},{28,20},{1,9},{5... | collective-permute-start | bytes 4128776 | tf_op jit(solution)/shard_map/ppermute | solution.py:324
  54.4 31.7 %collective-permute-start.16 = (bf16[3,224,1024]{2,1,0:T(8,128)(2,1)S(1)}, bf16[3,224,1024]{2,1,0:T(8,128)(2,1)S(1)}, u32[]{:S(2)}, u32[]{:S(2)}) collective-permute-start(bf16[3,224,1024]{2,1,0:T(8,128)(2,1)S(1)} %pad_maximum_fusion.refs_3_), channel_id=1, source_target_pairs={{0,16},{4,20},{8,24},{12,28},{16,0},{20,4},{24,8},{28,12},{1,17},{... | collective-permute-start | bytes 4128776 | tf_op jit(solution)/shard_map/ppermute | solution.py:324
  63.7 21.4 %collective-permute-start.14 = (bf16[128,1792]{1,0:T(8,128)(2,1)S(1)}, bf16[128,1792]{1,0:T(8,128)(2,1)S(1)}, u32[]{:S(2)}, u32[]{:S(2)}) collective-permute-start(bf16[128,1792]{1,0:T(8,128)(2,1)S(1)} %get-tuple-element.68), channel_id=1, source_target_pairs={{0,1},{1,0},{2,3},{3,2},{4,5},{5,4},{6,7},{7,6},{8,9},{9,8},{10,11... | collective-permute-start | bytes 1376264 | tf_op jit(solution)/shard_map/ppermute | solution.py:324
  66.2 22.4 %collective-permute-start.13 = (bf16[128,1792]{1,0:T(8,128)(2,1)S(1)}, bf16[128,1792]{1,0:T(8,128)(2,1)S(1)}, u32[]{:S(2)}, u32[]{:S(2)}) collective-permute-start(bf16[128,1792]{1,0:T(8,128)(2,1)S(1)} %add_convert_fusion), channel_id=1, source_target_pairs={{0,2},{1,3},{2,0},{3,1},{4,6},{5,7},{6,4},{7,5},{8,10},{9,11},{10,... | collective-permute-start | bytes 1376264 | tf_op jit(solution)/shard_map/ppermute | solution.py:324
  89.0 19.5 %collective-permute-start.17 = (bf16[128,1792]{1,0:T(8,128)(2,1)S(1)}, bf16[128,1792]{1,0:T(8,128)(2,1)S(1)}, u32[]{:S(2)}, u32[]{:S(2)}) collective-permute-start(bf16[128,1792]{1,0:T(8,128)(2,1)S(1)} %get-tuple-element.72.refs_2_), channel_id=1, source_target_pairs={{0,2},{1,3},{2,0},{3,1},{4,6},{5,7},{6,4},{7,5},{8,10},{9,11},{10,... | collective-permute-start | bytes 1376264 | tf_op jit(solution)/shard_map/ppermute | solution.py:324
  89.2 19.4 %collective-permute-start.18 = (bf16[128,1792]{1,0:T(8,128)(2,1)S(1)}, bf16[128,1792]{1,0:T(8,128)(2,1)S(1)}, u32[]{:S(2)}, u32[]{:S(2)}) collective-permute-start(bf16[128,1792]{1,0:T(8,128)(2,1)S(1)} %get-tuple-element.72.refs_2_), channel_id=1, source_target_pairs={{0,1},{1,0},{2,3},{3,2},{4,5},{5,4},{6,7},{7,6},{8,9},{9,8},{10,11... | collective-permute-start | bytes 1376264 | tf_op jit(solution)/shard_map/ppermute | solution.py:324
  92.1 19.1 %collective-permute-start.21 = (bf16[3,224,1024]{2,1,0:T(8,128)(2,1)S(1)}, bf16[3,224,1024]{2,1,0:T(8,128)(2,1)S(1)}, u32[]{:S(2)}, u32[]{:S(2)}) collective-permute-start(bf16[3,224,1024]{2,1,0:T(8,128)(2,1)S(1)} %pad_maximum_fusion.refs_3_), channel_id=1, source_target_pairs={{0,4},{4,0},{8,12},{12,8},{16,20},{20,16},{24,28},{28,24},{1,5},{5... | collective-permute-start | bytes 4128776 | tf_op jit(solution)/shard_map/ppermute | solution.py:324
  92.1 17.9 %collective-permute-start.19 = (bf16[3,112,1024]{2,1,0:T(8,128)(2,1)S(1)}, bf16[3,112,1024]{2,1,0:T(8,128)(2,1)S(1)}, u32[]{:S(2)}, u32[]{:S(2)}) collective-permute-start(bf16[3,112,1024]{2,1,0:T(8,128)(2,1)S(1)} %slice.14), channel_id=1, source_target_pairs={{0,16},{4,20},{8,24},{12,28},{16,0},{20,4},{24,8},{28,12},{1,17},{... | collective-permute-start | bytes 2064392 | tf_op jit(solution)/shard_map/ppermute | solution.py:324
  93.5 17.6 %collective-permute-start.20 = (bf16[3,112,1024]{2,1,0:T(8,128)(2,1)S(1)}, bf16[3,112,1024]{2,1,0:T(8,128)(2,1)S(1)}, u32[]{:S(2)}, u32[]{:S(2)}) collective-permute-start(bf16[3,112,1024]{2,1,0:T(8,128)(2,1)S(1)} %slice.15), channel_id=1, source_target_pairs={{0,8},{4,12},{8,0},{12,4},{16,24},{20,28},{24,16},{28,20},{1,9},{5... | collective-permute-start | bytes 2064392 | tf_op jit(solution)/shard_map/ppermute | solution.py:324
  108.5 7.1 %collective-permute-start.22 = (bf16[3,224,1024]{2,1,0:T(8,128)(2,1)S(1)}, bf16[3,224,1024]{2,1,0:T(8,128)(2,1)S(1)}, u32[]{:S(2)}, u32[]{:S(2)}) collective-permute-start(bf16[3,224,1024]{2,1,0:T(8,128)(2,1)S(1)} %collective-permute-done.15.refs_4_), channel_id=1, source_target_pairs={{0,4},{4,0},{8,12},{12,8},{16,20},{20,16},{24,28},{28,24},{1,5},{5... | collective-permute-start | bytes 4128776 | tf_op jit(solution)/shard_map/ppermute | solution.py:324
  108.5 7.0 %collective-permute-start.23 = (bf16[3,224,1024]{2,1,0:T(8,128)(2,1)S(1)}, bf16[3,224,1024]{2,1,0:T(8,128)(2,1)S(1)}, u32[]{:S(2)}, u32[]{:S(2)}) collective-permute-start(bf16[3,224,1024]{2,1,0:T(8,128)(2,1)S(1)} %collective-permute-done.16.refs_5_), channel_id=1, source_target_pairs={{0,4},{4,0},{8,12},{12,8},{16,20},{20,16},{24,28},{28,24},{1,5},{5... | collective-permute-start | bytes 4128776 | tf_op jit(solution)/shard_map/ppermute | solution.py:324
  110.0 4.5 %collective-permute-start.24 = (bf16[3,112,1024]{2,1,0:T(8,128)(2,1)S(1)}, bf16[3,112,1024]{2,1,0:T(8,128)(2,1)S(1)}, u32[]{:S(2)}, u32[]{:S(2)}) collective-permute-start(bf16[3,112,1024]{2,1,0:T(8,128)(2,1)S(1)} %collective-permute-done.19.refs_6_), channel_id=1, source_target_pairs={{0,4},{4,0},{8,12},{12,8},{16,20},{20,16},{24,28},{28,24},{1,5},{5... | collective-permute-start | bytes 2064392 | tf_op jit(solution)/shard_map/ppermute | solution.py:324
  111.1 4.4 %collective-permute-start.25 = (bf16[3,112,1024]{2,1,0:T(8,128)(2,1)S(1)}, bf16[3,112,1024]{2,1,0:T(8,128)(2,1)S(1)}, u32[]{:S(2)}, u32[]{:S(2)}) collective-permute-start(bf16[3,112,1024]{2,1,0:T(8,128)(2,1)S(1)} %collective-permute-done.20.refs_7_), channel_id=1, source_target_pairs={{0,4},{4,0},{8,12},{12,8},{16,20},{20,16},{24,28},{28,24},{1,5},{5... | collective-permute-start | bytes 2064392 | tf_op jit(solution)/shard_map/ppermute | solution.py:324
  111.1 12.9 %collective-permute-start.26 = (bf16[128,1792]{1,0:T(8,128)(2,1)S(1)}, bf16[128,1792]{1,0:T(8,128)(2,1)S(1)}, u32[]{:S(2)}, u32[]{:S(2)}) collective-permute-start(bf16[128,1792]{1,0:T(8,128)(2,1)S(1)} %collective-permute-done.17.refs_0_), channel_id=1, source_target_pairs={{0,1},{1,0},{2,3},{3,2},{4,5},{5,4},{6,7},{7,6},{8,9},{9,8},{10,11... | collective-permute-start | bytes 1376264 | tf_op jit(solution)/shard_map/ppermute | solution.py:324
  126.2 11.6 %collective-permute-start.27 = (bf16[80,1792]{1,0:T(8,128)(2,1)S(1)}, bf16[80,1792]{1,0:T(8,128)(2,1)S(1)}, u32[]{:S(2)}, u32[]{:S(2)}) collective-permute-start(bf16[80,1792]{1,0:T(8,128)(2,1)S(1)} %get-tuple-element.80), channel_id=1, source_target_pairs={{0,1},{1,0},{2,3},{3,2},{4,5},{5,4},{6,7},{7,6},{8,9},{9,8},{10,11... | collective-permute-start | bytes 860168 | tf_op jit(solution)/shard_map/ppermute | solution.py:324
  126.6 12.6 %collective-permute-start.29 = (bf16[48,1792]{1,0:T(8,128)(2,1)S(1)}, bf16[48,1792]{1,0:T(8,128)(2,1)S(1)}, u32[]{:S(2)}, u32[]{:S(2)}) collective-permute-start(bf16[48,1792]{1,0:T(8,128)(2,1)S(1)} %get-tuple-element.81), channel_id=1, source_target_pairs={{0,3},{1,2},{2,1},{3,0},{4,7},{5,6},{6,5},{7,4},{8,11},{9,10},{10,... | collective-permute-start | bytes 516104 | tf_op jit(solution)/shard_map/ppermute | solution.py:324
  137.9 20.2 %collective-permute-start.28 = (bf16[128,1792]{1,0:T(8,128)(2,1)S(1)}, bf16[128,1792]{1,0:T(8,128)(2,1)S(1)}, u32[]{:S(2)}, u32[]{:S(2)}) collective-permute-start(bf16[128,1792]{1,0:T(8,128)(2,1)S(1)} %shard_map.152), channel_id=1, source_target_pairs={{0,2},{1,3},{2,0},{3,1},{4,6},{5,7},{6,4},{7,5},{8,10},{9,11},{10,... | collective-permute-start | bytes 1376264 | tf_op jit(solution)/shard_map/ppermute | solution.py:324
  139.2 20.0 %collective-permute-start.30 = (bf16[128,1792]{1,0:T(8,128)(2,1)S(1)}, bf16[128,1792]{1,0:T(8,128)(2,1)S(1)}, u32[]{:S(2)}, u32[]{:S(2)}) collective-permute-start(bf16[128,1792]{1,0:T(8,128)(2,1)S(1)} %get-tuple-element.83), channel_id=1, source_target_pairs={{0,1},{1,0},{2,3},{3,2},{4,5},{5,4},{6,7},{7,6},{8,9},{9,8},{10,11... | collective-permute-start | bytes 1376264 | tf_op jit(solution)/shard_map/ppermute | solution.py:324
  (10 other events, 148.9 us)

commit v7 on v4

--- a/solution.py
+++ b/solution.py
@@ -260,9 +260,11 @@
         load.start()
     x_ref, qkv_ref, out_ref, gain_ref, down_ref, up_ref = targets
     rows, part, ranks = qkv_ref.shape[1], qkv_ref.shape[2], down_ref.shape[0]
-    for load in loads:
-        load.wait()
+    loads[0].wait()
+    loads[3].wait()
     normed_ref[...] = normed(x_ref[...].astype(jnp.float32), gain_ref[...][None, :])
+    for at in (1, 2, 4, 5):
+        loads[at].wait()
     for place, which in enumerate((1, 0, 2)):
         packed_ref[:rows, place * part : (place + 1) * part] = qkv_ref[which]
     out_rows = jnp.transpose(out_ref[...].astype(jnp.float32)).astype(jnp.bfloat16)
@@ -565,16 +567,47 @@
     out_ref[...] = feed(x_ref[...], all_w).astype(out_ref.dtype)
 
 
-def feed_last_call(block, all_w):
-    count, (_, width, hidden) = block.shape[0], all_w.shape
+def feed_last_call(rows, all_w):
     return pl.pallas_call(
         feed_last_kernel,
-        out_shape=jax.ShapeDtypeStruct((count, width), jnp.bfloat16),
+        out_shape=jax.ShapeDtypeStruct(rows.shape, jnp.bfloat16),
         in_specs=[VMEM] * 2,
         out_specs=VMEM,
         compiler_params=params(20),
         cost_estimate=LIGHT,
-    )(block, all_w)
+    )(rows, all_w)
+
+
+def sum_kernel(part_ref, near_ref, far_ref, out_ref):
+    passed = jnp.concatenate([near_ref[...], far_ref[...]], axis=0).astype(jnp.float32)
+    out_ref[...] = (part_ref[...].astype(jnp.float32) + passed).astype(out_ref.dtype)
+
+
+def sum_call(part, near, far):
+    return pl.pallas_call(
+        sum_kernel,
+        out_shape=jax.ShapeDtypeStruct(part.shape, jnp.bfloat16),
+        in_specs=[VMEM] * 3,
+        out_specs=VMEM,
+        compiler_params=params(12),
+        cost_estimate=LIGHT,
+    )(part, near, far)
+
+
+def last_kernel(residual_ref, own_ref, two_ref, one_ref, out_ref):
+    total = own_ref[...] + one_ref[...].astype(jnp.float32) + two_ref[...].astype(jnp.float32)
+    out_ref[...] = (residual_ref[...].astype(jnp.float32) + total).astype(out_ref.dtype)
+
+
+def last_call(residual, own, two, one):
+    return pl.pallas_call(
+        last_kernel,
+        out_shape=jax.ShapeDtypeStruct(residual.shape, jnp.bfloat16),
+        in_specs=[VMEM] * 4,
+        out_specs=VMEM,
+        compiler_params=params(12),
+        cost_estimate=LIGHT,
+    )(residual, own, two, one)
 
 
 def tuned(
@@ -650,18 +683,17 @@
     token_two, token_one = swap(normed_mlp, "col", 2), swap(normed_mlp, "col", 1)
     feed_thirds = tuple(swap(piece, "row", 1) for piece in feed_seconds[:2])
     token_two, token_one = lax.optimization_barrier((token_two, token_one))
-    token_three = swap(token_two, "col", 1)
+    split = count * 5 // 8
+    three = [swap(rows, "col", 1) for rows in (token_two[:split], token_two[split:])]
     feed_pieces = named_pieces(feed_own, feed_firsts, feed_seconds, feed_thirds)
     feed_w, part_two, part_one, part_own = feed_first_call(
         [token_two, token_one, normed_mlp], feed_pieces, [bf16, bf16, f32]
     )
-    part_three = feed_last_call(token_three, feed_w)
-    passed = swap(part_three, "col", 1)
-    part_two = (part_two.astype(f32) + passed.astype(f32)).astype(bf16)
+    near, far = (feed_last_call(rows, feed_w) for rows in three)
+    part_two = sum_call(part_two, swap(near, "col", 1), swap(far, "col", 1))
     part_two, part_one = lax.optimization_barrier((part_two, part_one))
     got_two, got_one = swap(part_two, "col", 2), swap(part_one, "col", 1)
-    added = part_own + got_one.astype(f32) + got_two.astype(f32)
-    return (residual.astype(f32) + added).astype(bf16)
+    return last_call(residual, part_own, got_two, got_one)
 
 
 def on_device(*args):

time: 162 us -> 160 us (0.988)
  waiting for transfers between devices: 98.6 us -> 87.6 us
  starting transfers between devices: 27.5 us -> 32.2 us
  Pallas kernels: 28.4 us -> 32.2 us
    ppermute x30 -> x32, waiting for transfers between devices: 98.6 us -> 87.6 us  [swap(): return lax.ppermute(value, axis, xor_pairs(lax.axis_size(axis), mask))]
    ppermute x30 -> x32, starting transfers between devices: 27.5 us -> 32.2 us  [swap(): return lax.ppermute(value, axis, xor_pairs(lax.axis_size(axis), mask))]
    pallas_call x1 -> x4, Pallas kernels: 2.13 us -> 5.92 us  [the longest x2 4.85 us: feed_last_call(): pl.pallas_call(feed_last_kernel, out_shape=jax.ShapeDtypeStruct(rows.shap...]
  transfers between devices with their start and end apart: 30 -> 32, of which waited for: 22 -> 21; matrix products, arithmetic and copies ran while one was open for 3% -> 5% of each run, Pallas kernels for 11% -> 14%
where the time goes in v7:
time: 160 us
  waiting for transfers between devices  87.6 us (55%)
  Pallas kernels  32.2 us (20%)
  starting transfers between devices  32.2 us (20%)
  local copies, waits for them, and re-layouts  7.47 us (5%)
    ppermute x32, waiting for transfers between devices, swap(): return lax.ppermute(value, axis, xor_pairs(lax.axis_size(axis), mask))  87.6 us
    ppermute x32, starting transfers between devices, swap(): return lax.ppermute(value, axis, xor_pairs(lax.axis_size(axis), mask))  32.2 us
    pallas_call x1, Pallas kernels, rest_call(): pl.pallas_call(functools.partial(rest_kernel, masks), out_shape=[jax.Shap...  8.68 us
    reshape x2, local copies, waits for them, and re-layouts, tuned(): cache = window_key_value.reshape(requests, 2, heads, window, HD)  5.55 us
    pallas_call x1, Pallas kernels, feed_first_call(): pl.pallas_call(functools.partial(feed_first_kernel, places, n_x, n_w), ou...  5.49 us
    pallas_call x1, Pallas kernels, first_call(): pl.pallas_call(functools.partial(first_kernel, places, n_x, n_w), out_sha...  5.35 us
    pallas_call x2, Pallas kernels, feed_last_call(): pl.pallas_call(feed_last_kernel, out_shape=jax.ShapeDtypeStruct(rows.shap...  4.85 us
    pallas_call x1, Pallas kernels, own_call(): pl.pallas_call(functools.partial(own_kernel, rank), out_shape=jax.ShapeDt...  3.72 us
  transfers between devices with their start and end apart: 32, of which 21 were waited for; matrix products, arithmetic and copies ran while one was open for 5% of the time, Pallas kernels for 14%

profile of v7, /device:TPU:0, one launch (start us, length us, event | category | flops | bytes accessed | tf_op | source)
XLA Modules:
  0.0 160.1 jit_solution(13950921837661694701)
XLA Ops:
  0.0 2.7 %shard_map.145 = (bf16[128,1792]{1,0:T(8,128)(2,1)}, bf16[288,1792]{1,0:T(8,128)(2,1)}) custom-call(bf16[128,1792]{1,0:T(8,128)(2,1)} %x_ref.1, bf16[3,224,448]{2,1,0:T(8,128)(2,1)} %bitcast.14, bf16[448,224]{1,0:T(8,128)(2,1)} %refs_2_.1, f32[1792]{0:T(1024)} %refs_3_.1, bf16[32,1792]{1,0:T(8,128)(2,1)} %bitcast.18, bf16[32,1792]{1,0:T(8,128)(2,1)} %bitcast.19), custom_call_target="tpu_custom_call" | custom-call | flops 1 | bytes 1 | tf_op jit(solution)/shard_map/pallas_call | solution.py:278
  2.7 3.0 %collective-permute-start.2 = (bf16[288,1792]{1,0:T(8,128)(2,1)}, bf16[288,1792]{1,0:T(8,128)(2,1)S(1)}, u32[]{:S(2)}, u32[]{:S(2)}) collective-permute-start(bf16[288,1792]{1,0:T(8,128)(2,1)} %get-tuple-element.44.refs_4_), channel_id=1, source_target_pairs={{0,8},{4,12},{8,0},{12,4},{16,24},{20,28},{24,16},{28,20},{1,9},{5... | collective-permute-start | bytes 3096584 | tf_op jit(solution)/shard_map/ppermute | solution.py:324
  5.7 1.5 collective-permute-start.3
  7.2 2.6 %collective-permute-start = (bf16[128,1792]{1,0:T(8,128)(2,1)}, bf16[128,1792]{1,0:T(8,128)(2,1)S(1)}, u32[]{:S(2)}, u32[]{:S(2)}) collective-permute-start(bf16[128,1792]{1,0:T(8,128)(2,1)} %get-tuple-element.43.refs_0_.x_ref), channel_id=1, source_target_pairs={{0,2},{1,3},{2,0},{3,1},{4,6},{5,7},{6,4},{7,5},{8,10},{9,11},{10,... | collective-permute-start | bytes 1376264 | tf_op jit(solution)/shard_map/ppermute | solution.py:324
  9.8 1.6 collective-permute-start.1
  11.4 3.3 %reshape.14 = bf16[8,2,4,64,112]{4,3,2,1,0:T(8,128)(2,1)} reshape(bf16[8,2,4,7168]{3,2,1,0:T(4,128)(2,1)} %param.20) | data formatting | bytes 1835008 | tf_op jit(solution)/shard_map/reshape | solution.py:648
  14.7 2.3 %copy.16 = bf16[8,2,4,64,112]{4,3,0,2,1:T(8,128)(2,1)} copy(bf16[8,2,4,64,112]{4,3,2,1,0:T(8,128)(2,1)} %reshape.14) | data formatting | bytes 1835008 | tf_op jit(solution)/shard_map/reshape | solution.py:648
  17.1 1.5 pad.4.refs_17_.cache_ref.refs_2_
  18.9 9.8 %collective-permute-done.2.refs_5_ = bf16[288,1792]{1,0:T(8,128)(2,1)S(1)} collective-permute-done((bf16[288,1792]{1,0:T(8,128)(2,1)}, bf16[288,1792]{1,0:T(8,128)(2,1)S(1)}, u32[]{:S(2)}, u32[]{:S(2)}) %collective-permute-start.2) | collective-permute-done | bytes 1032224 | tf_op jit(solution)/shard_map/ppermute | solution.py:324
  28.7 1.5 collective-permute-done.3.refs_6_
  30.2 1.6 collective-permute-start.4
  31.8 1.6 collective-permute-start.5
  34.6 6.8 %collective-permute-done.4.refs_3_ = bf16[128,1792]{1,0:T(8,128)(2,1)S(1)} collective-permute-done((bf16[128,1792]{1,0:T(8,128)(2,1)S(1)}, bf16[128,1792]{1,0:T(8,128)(2,1)S(1)}, u32[]{:S(2)}, u32[]{:S(2)}) %collective-permute-start.4) | collective-permute-done | bytes 458784 | tf_op jit(solution)/shard_map/ppermute | solution.py:324
  41.4 2.8 %collective-permute-done.5.refs_7_ = bf16[144,1792]{1,0:T(8,128)(2,1)S(1)} collective-permute-done((bf16[144,1792]{1,0:T(8,128)(2,1)S(1)}, bf16[144,1792]{1,0:T(8,128)(2,1)S(1)}, u32[]{:S(2)}, u32[]{:S(2)}) %collective-permute-start.5) | collective-permute-done | bytes 516128 | tf_op jit(solution)/shard_map/ppermute | solution.py:324
  45.8 1.4 collective-permute-done.10.refs_12_
  47.9 5.3 %shard_map.146 = (bf16[512,1792]{1,0:T(8,128)(2,1)S(1)}, bf16[1792,1408]{1,0:T(8,128)(2,1)S(1)}, bf16[1792,512]{1,0:T(8,128)(2,1)S(1)}, bf16[256,1792]{1,0:T(8,1...) custom-call(bf16[128,1792]{1,0:T(8,128)(2,1)S(1)} %copy-done.2, ...), custom_call_target="tpu_custom_call" | custom-call | flops 1 | bytes 1 | tf_op jit(solution)/shard_map/pallas_call | solution.py:471
  55.0 8.7 %shard_map.147 = (bf16[512,512]{1,0:T(8,128)(2,1)S(1)}, bf16[512,512]{1,0:T(8,128)(2,1)S(1)}, bf16[512,512]{1,0:T(8,128)(2,1)S(1)}, bf16[128,1792]{1,0:T(8,128)(2,1)S(1)}, bf16[128,1792]{1,0:T(8,128)(2,1)S(1)}) custom-call(bf16[512,1792]{1,0:T(8,128)(2,1)S(1)} %get-tuple-element.55.x_all, bf16[1792,1408]{1,0:T(8,128)(2,1)S(1)} %get-tuple-element.56.w_all, ...), custom_call_target="tpu_custom_call" | custom-call | flops 1 | bytes 1 | tf_op jit(solution)/shard_map/pallas_call | solution.py:500
  63.7 1.7 %collective-permute-start.14 = (bf16[128,1792]{1,0:T(8,128)(2,1)S(1)}, bf16[128,1792]{1,0:T(8,128)(2,1)S(1)}, u32[]{:S(2)}, u32[]{:S(2)}) collective-permute-start(bf16[128,1792]{1,0:T(8,128)(2,1)S(1)} %get-tuple-element.66), channel_id=1, source_target_pairs={{0,1},{1,0},{2,3},{3,2},{4,5},{5,4},{6,7},{7,6},{8,9},{9,8},{10,11... | collective-permute-start | bytes 1376264 | tf_op jit(solution)/shard_map/ppermute | solution.py:324
  66.2 2.7 %collective-permute-start.13 = (bf16[128,1792]{1,0:T(8,128)(2,1)S(1)}, bf16[128,1792]{1,0:T(8,128)(2,1)S(1)}, u32[]{:S(2)}, u32[]{:S(2)}) collective-permute-start(bf16[128,1792]{1,0:T(8,128)(2,1)S(1)} %add_convert_fusion), channel_id=1, source_target_pairs={{0,2},{1,3},{2,0},{3,1},{4,6},{5,7},{6,4},{7,5},{8,10},{9,11},{10,... | collective-permute-start | bytes 1376264 | tf_op jit(solution)/shard_map/ppermute | solution.py:324
  68.9 3.7 %shard_map.148.own_ref = f32[128,1792]{1,0:T(8,128)S(1)} custom-call(bf16[512,512]{1,0:T(8,128)(2,1)S(1)} %get-tuple-element.58.q_ref, bf16[512,512]{1,0:T(8,128)(2,1)S(1)} %get-tuple-element.59.k_ref, bf16[512,512]{1,0:T(8,128)(2,1)S(1)} %get-tuple-element.60.v_ref, bf16[1792,512]{1,0:T(8,128)(2,1)S(1)} %get-tuple-element.57.out_w, ...), custom_call_target="tpu_custom_call" | custom-call | flops 1 | bytes 1 | tf_op jit(solution)/shard_map/pallas_call | solution.py:521
  72.6 12.5 %collective-permute-done.14.one_ref = bf16[128,1792]{1,0:T(8,128)(2,1)S(1)} collective-permute-done((bf16[128,1792]{1,0:T(8,128)(2,1)S(1)}, bf16[128,1792]{1,0:T(8,128)(2,1)S(1)}, u32[]{:S(2)}, u32[]{:S(2)}) %collective-permute-start.14) | collective-permute-done | bytes 458784 | tf_op jit(solution)/shard_map/ppermute | solution.py:324
  86.1 2.4 %collective-permute-done.13.two_ref = bf16[128,1792]{1,0:T(8,128)(2,1)S(1)} collective-permute-done((bf16[128,1792]{1,0:T(8,128)(2,1)S(1)}, bf16[128,1792]{1,0:T(8,128)(2,1)S(1)}, u32[]{:S(2)}, u32[]{:S(2)}) %collective-permute-start.13) | collective-permute-done | bytes 458784 | tf_op jit(solution)/shard_map/ppermute | solution.py:324
  89.1 2.9 %collective-permute-start.18 = (bf16[128,1792]{1,0:T(8,128)(2,1)S(1)}, bf16[128,1792]{1,0:T(8,128)(2,1)S(1)}, u32[]{:S(2)}, u32[]{:S(2)}) collective-permute-start(bf16[128,1792]{1,0:T(8,128)(2,1)S(1)} %get-tuple-element.70.refs_2_), channel_id=1, source_target_pairs={{0,1},{1,0},{2,3},{3,2},{4,5},{5,4},{6,7},{7,6},{8,9},{9,8},{10,11... | collective-permute-start | bytes 1376264 | tf_op jit(solution)/shard_map/ppermute | solution.py:324
  92.1 1.3 collective-permute-start.19
  94.3 14.2 %collective-permute-done.17.refs_0_ = bf16[128,1792]{1,0:T(8,128)(2,1)S(1)} collective-permute-done((bf16[128,1792]{1,0:T(8,128)(2,1)S(1)}, bf16[128,1792]{1,0:T(8,128)(2,1)S(1)}, u32[]{:S(2)}, u32[]{:S(2)}) %collective-permute-start.17) | collective-permute-done | bytes 458784 | tf_op jit(solution)/shard_map/ppermute | solution.py:324
  111.2 3.3 %collective-permute-done.24.refs_11_ = bf16[3,112,1024]{2,1,0:T(8,128)(2,1)S(1)} collective-permute-done((bf16[3,112,1024]{2,1,0:T(8,128)(2,1)S(1)}, bf16[3,112,1024]{2,1,0:T(8,128)(2,1)S(1)}, u32[]{:S(2)}, u32[]{:S(2)}) %collective-permute-start.24) | collective-permute-done | bytes 688160 | tf_op jit(solution)/shard_map/ppermute | solution.py:324
  115.5 5.5 %shard_map.150 = (bf16[3,1792,1024]{2,1,0:T(8,128)(2,1)S(1)}, bf16[128,1792]{1,0:T(8,128)(2,1)S(1)}, bf16[128,1792]{1,0:T(8,128)(2,1)S(1)}, f32[128,1792]{1,0:T(8,128)S(1)}) custom-call(bf16[128,1792]{1,0:T(8,128)(2,1)S(1)} %collective-permute-done.17.refs_0_, bf16[128,1792]{1,0:T(8,128)(2,1)S(1)} %collective-permute-done.18.refs_1_, ...), custom_call_target="tpu_custom_call" | custom-call | flops 1 | bytes 1 | tf_op jit(solution)/shard_map/pallas_call | solution.py:555
  121.0 2.5 %shard_map.151 = bf16[80,1792]{1,0:T(8,128)(2,1)S(1)} custom-call(bf16[80,1792]{1,0:T(8,128)(2,1)S(1)} %collective-permute-done.26.x_ref, bf16[3,1792,1024]{2,1,0:T(8,128)(2,1)S(1)} %get-tuple-element.77.all_w), custom_call_target="tpu_custom_call" | custom-call | flops 1 | bytes 1 | tf_op jit(solution)/shard_map/pallas_call | solution.py:571
  124.7 2.4 %shard_map.152 = bf16[48,1792]{1,0:T(8,128)(2,1)S(1)} custom-call(bf16[48,1792]{1,0:T(8,128)(2,1)S(1)} %collective-permute-done.28.x_ref, bf16[3,1792,1024]{2,1,0:T(8,128)(2,1)S(1)} %get-tuple-element.77.all_w), custom_call_target="tpu_custom_call" | custom-call | flops 1 | bytes 1 | tf_op jit(solution)/shard_map/pallas_call | solution.py:571
  128.1 8.1 %collective-permute-done.29.far_ref = bf16[48,1792]{1,0:T(8,128)(2,1)S(1)} collective-permute-done((bf16[48,1792]{1,0:T(8,128)(2,1)S(1)}, bf16[48,1792]{1,0:T(8,128)(2,1)S(1)}, u32[]{:S(2)}, u32[]{:S(2)}) %collective-permute-start.29) | collective-permute-done | bytes 172064 | tf_op jit(solution)/shard_map/ppermute | solution.py:324
  136.3 2.9 %collective-permute-start.30 = (bf16[128,1792]{1,0:T(8,128)(2,1)S(1)}, bf16[128,1792]{1,0:T(8,128)(2,1)S(1)}, u32[]{:S(2)}, u32[]{:S(2)}) collective-permute-start(bf16[128,1792]{1,0:T(8,128)(2,1)S(1)} %shard_map.153), channel_id=1, source_target_pairs={{0,2},{1,3},{2,0},{3,1},{4,6},{5,7},{6,4},{7,5},{8,10},{9,11},{10,... | collective-permute-start | bytes 1376264 | tf_op jit(solution)/shard_map/ppermute | solution.py:324
  140.4 18.5 %collective-permute-done.30.two_ref = bf16[128,1792]{1,0:T(8,128)(2,1)S(1)} collective-permute-done((bf16[128,1792]{1,0:T(8,128)(2,1)S(1)}, bf16[128,1792]{1,0:T(8,128)(2,1)S(1)}, u32[]{:S(2)}, u32[]{:S(2)}) %collective-permute-start.30) | collective-permute-done | bytes 458784 | tf_op jit(solution)/shard_map/ppermute | solution.py:324
  (78 shorter events, 17.3 us)
Async XLA Ops:
  2.7 26.0 %collective-permute-start.2 = (bf16[288,1792]{1,0:T(8,128)(2,1)}, bf16[288,1792]{1,0:T(8,128)(2,1)S(1)}, u32[]{:S(2)}, u32[]{:S(2)}) collective-permute-start(bf16[288,1792]{1,0:T(8,128)(2,1)} %get-tuple-element.44.refs_4_), channel_id=1, source_target_pairs={{0,8},{4,12},{8,0},{12,4},{16,24},{20,28},{24,16},{28,20},{1,9},{5... | collective-permute-start | bytes 3096584 | tf_op jit(solution)/shard_map/ppermute | solution.py:324
  5.7 24.5 %collective-permute-start.3 = (bf16[288,1792]{1,0:T(8,128)(2,1)}, bf16[288,1792]{1,0:T(8,128)(2,1)S(1)}, u32[]{:S(2)}, u32[]{:S(2)}) collective-permute-start(bf16[288,1792]{1,0:T(8,128)(2,1)} %get-tuple-element.44.refs_4_), channel_id=1, source_target_pairs={{0,16},{4,20},{8,24},{12,28},{16,0},{20,4},{24,8},{28,12},{1,17},{... | collective-permute-start | bytes 3096584 | tf_op jit(solution)/shard_map/ppermute | solution.py:324
  7.2 23.0 %collective-permute-start = (bf16[128,1792]{1,0:T(8,128)(2,1)}, bf16[128,1792]{1,0:T(8,128)(2,1)S(1)}, u32[]{:S(2)}, u32[]{:S(2)}) collective-permute-start(bf16[128,1792]{1,0:T(8,128)(2,1)} %get-tuple-element.43.refs_0_.x_ref), channel_id=1, source_target_pairs={{0,2},{1,3},{2,0},{3,1},{4,6},{5,7},{6,4},{7,5},{8,10},{9,11},{10,... | collective-permute-start | bytes 1376264 | tf_op jit(solution)/shard_map/ppermute | solution.py:324
  9.8 20.4 %collective-permute-start.1 = (bf16[128,1792]{1,0:T(8,128)(2,1)}, bf16[128,1792]{1,0:T(8,128)(2,1)S(1)}, u32[]{:S(2)}, u32[]{:S(2)}) collective-permute-start(bf16[128,1792]{1,0:T(8,128)(2,1)} %get-tuple-element.43.refs_0_.x_ref), channel_id=1, source_target_pairs={{0,1},{1,0},{2,3},{3,2},{4,5},{5,4},{6,7},{7,6},{8,9},{9,8},{10,11... | collective-permute-start | bytes 1376264 | tf_op jit(solution)/shard_map/ppermute | solution.py:324
  30.2 11.2 %collective-permute-start.4 = (bf16[128,1792]{1,0:T(8,128)(2,1)S(1)}, bf16[128,1792]{1,0:T(8,128)(2,1)S(1)}, u32[]{:S(2)}, u32[]{:S(2)}) collective-permute-start(bf16[128,1792]{1,0:T(8,128)(2,1)S(1)} %collective-permute-done.refs_2_), channel_id=1, source_target_pairs={{0,1},{1,0},{2,3},{3,2},{4,5},{5,4},{6,7},{7,6},{8,9},{9,8},{10,11... | collective-permute-start | bytes 1376264 | tf_op jit(solution)/shard_map/ppermute | solution.py:324
  31.8 12.3 %collective-permute-start.5 = (bf16[144,1792]{1,0:T(8,128)(2,1)S(1)}, bf16[144,1792]{1,0:T(8,128)(2,1)S(1)}, u32[]{:S(2)}, u32[]{:S(2)}) collective-permute-start(bf16[144,1792]{1,0:T(8,128)(2,1)S(1)} %slice.18), channel_id=1, source_target_pairs={{0,16},{4,20},{8,24},{12,28},{16,0},{20,4},{24,8},{28,12},{1,17},{... | collective-permute-start | bytes 1548296 | tf_op jit(solution)/shard_map/ppermute | solution.py:324
  33.4 11.8 %collective-permute-start.6 = (bf16[144,1792]{1,0:T(8,128)(2,1)S(1)}, bf16[144,1792]{1,0:T(8,128)(2,1)S(1)}, u32[]{:S(2)}, u32[]{:S(2)}) collective-permute-start(bf16[144,1792]{1,0:T(8,128)(2,1)S(1)} %slice.19), channel_id=1, source_target_pairs={{0,8},{4,12},{8,0},{12,4},{16,24},{20,28},{24,16},{28,20},{1,9},{5... | collective-permute-start | bytes 1548296 | tf_op jit(solution)/shard_map/ppermute | solution.py:324
  34.0 11.7 %collective-permute-start.7 = (bf16[288,1792]{1,0:T(8,128)(2,1)S(1)}, bf16[288,1792]{1,0:T(8,128)(2,1)S(1)}, u32[]{:S(2)}, u32[]{:S(2)}) collective-permute-start(bf16[288,1792]{1,0:T(8,128)(2,1)S(1)} %copy-done.3), channel_id=1, source_target_pairs={{0,4},{4,0},{8,12},{12,8},{16,20},{20,16},{24,28},{28,24},{1,5},{5... | collective-permute-start | bytes 3096584 | tf_op jit(solution)/shard_map/ppermute | solution.py:324
  34.0 11.7 %collective-permute-start.8 = (bf16[288,1792]{1,0:T(8,128)(2,1)S(1)}, bf16[288,1792]{1,0:T(8,128)(2,1)S(1)}, u32[]{:S(2)}, u32[]{:S(2)}) collective-permute-start(bf16[288,1792]{1,0:T(8,128)(2,1)S(1)} %collective-permute-done.2.refs_5_), channel_id=1, source_target_pairs={{0,4},{4,0},{8,12},{12,8},{16,20},{20,16},{24,28},{28,24},{1,5},{5... | collective-permute-start | bytes 3096584 | tf_op jit(solution)/shard_map/ppermute | solution.py:324
  41.4 4.4 %collective-permute-start.9 = (bf16[288,1792]{1,0:T(8,128)(2,1)S(1)}, bf16[288,1792]{1,0:T(8,128)(2,1)S(1)}, u32[]{:S(2)}, u32[]{:S(2)}) collective-permute-start(bf16[288,1792]{1,0:T(8,128)(2,1)S(1)} %collective-permute-done.3.refs_6_), channel_id=1, source_target_pairs={{0,4},{4,0},{8,12},{12,8},{16,20},{20,16},{24,28},{28,24},{1,5},{5... | collective-permute-start | bytes 3096584 | tf_op jit(solution)/shard_map/ppermute | solution.py:324
  45.2 1.9 %collective-permute-start.10 = (bf16[144,1792]{1,0:T(8,128)(2,1)S(1)}, bf16[144,1792]{1,0:T(8,128)(2,1)S(1)}, u32[]{:S(2)}, u32[]{:S(2)}) collective-permute-start(bf16[144,1792]{1,0:T(8,128)(2,1)S(1)} %collective-permute-done.5.refs_7_), channel_id=1, source_target_pairs={{0,4},{4,0},{8,12},{12,8},{16,20},{20,16},{24,28},{28,24},{1,5},{5... | collective-permute-start | bytes 1548296 | tf_op jit(solution)/shard_map/ppermute | solution.py:324
  45.2 2.6 %collective-permute-start.11 = (bf16[144,1792]{1,0:T(8,128)(2,1)S(1)}, bf16[144,1792]{1,0:T(8,128)(2,1)S(1)}, u32[]{:S(2)}, u32[]{:S(2)}) collective-permute-start(bf16[144,1792]{1,0:T(8,128)(2,1)S(1)} %collective-permute-done.6.refs_8_), channel_id=1, source_target_pairs={{0,4},{4,0},{8,12},{12,8},{16,20},{20,16},{24,28},{28,24},{1,5},{5... | collective-permute-start | bytes 1548296 | tf_op jit(solution)/shard_map/ppermute | solution.py:324
  53.3 12.8 %collective-permute-start.12 = (bf16[128,1792]{1,0:T(8,128)(2,1)S(1)}, bf16[128,1792]{1,0:T(8,128)(2,1)S(1)}, u32[]{:S(2)}, u32[]{:S(2)}) collective-permute-start(bf16[128,1792]{1,0:T(8,128)(2,1)S(1)} %get-tuple-element.65), channel_id=1, source_target_pairs={{0,1},{1,0},{2,3},{3,2},{4,5},{5,4},{6,7},{7,6},{8,9},{9,8},{10,11... | collective-permute-start | bytes 1376264 | tf_op jit(solution)/shard_map/ppermute | solution.py:324
  53.8 31.9 %collective-permute-start.15 = (bf16[3,224,1024]{2,1,0:T(8,128)(2,1)S(1)}, bf16[3,224,1024]{2,1,0:T(8,128)(2,1)S(1)}, u32[]{:S(2)}, u32[]{:S(2)}) collective-permute-start(bf16[3,224,1024]{2,1,0:T(8,128)(2,1)S(1)} %pad_maximum_fusion.refs_3_), channel_id=1, source_target_pairs={{0,8},{4,12},{8,0},{12,4},{16,24},{20,28},{24,16},{28,20},{1,9},{5... | collective-permute-start | bytes 4128776 | tf_op jit(solution)/shard_map/ppermute | solution.py:324
  54.4 31.7 %collective-permute-start.16 = (bf16[3,224,1024]{2,1,0:T(8,128)(2,1)S(1)}, bf16[3,224,1024]{2,1,0:T(8,128)(2,1)S(1)}, u32[]{:S(2)}, u32[]{:S(2)}) collective-permute-start(bf16[3,224,1024]{2,1,0:T(8,128)(2,1)S(1)} %pad_maximum_fusion.refs_3_), channel_id=1, source_target_pairs={{0,16},{4,20},{8,24},{12,28},{16,0},{20,4},{24,8},{28,12},{1,17},{... | collective-permute-start | bytes 4128776 | tf_op jit(solution)/shard_map/ppermute | solution.py:324
  63.7 21.4 %collective-permute-start.14 = (bf16[128,1792]{1,0:T(8,128)(2,1)S(1)}, bf16[128,1792]{1,0:T(8,128)(2,1)S(1)}, u32[]{:S(2)}, u32[]{:S(2)}) collective-permute-start(bf16[128,1792]{1,0:T(8,128)(2,1)S(1)} %get-tuple-element.66), channel_id=1, source_target_pairs={{0,1},{1,0},{2,3},{3,2},{4,5},{5,4},{6,7},{7,6},{8,9},{9,8},{10,11... | collective-permute-start | bytes 1376264 | tf_op jit(solution)/shard_map/ppermute | solution.py:324
  66.2 22.4 %collective-permute-start.13 = (bf16[128,1792]{1,0:T(8,128)(2,1)S(1)}, bf16[128,1792]{1,0:T(8,128)(2,1)S(1)}, u32[]{:S(2)}, u32[]{:S(2)}) collective-permute-start(bf16[128,1792]{1,0:T(8,128)(2,1)S(1)} %add_convert_fusion), channel_id=1, source_target_pairs={{0,2},{1,3},{2,0},{3,1},{4,6},{5,7},{6,4},{7,5},{8,10},{9,11},{10,... | collective-permute-start | bytes 1376264 | tf_op jit(solution)/shard_map/ppermute | solution.py:324
  88.9 19.6 %collective-permute-start.17 = (bf16[128,1792]{1,0:T(8,128)(2,1)S(1)}, bf16[128,1792]{1,0:T(8,128)(2,1)S(1)}, u32[]{:S(2)}, u32[]{:S(2)}) collective-permute-start(bf16[128,1792]{1,0:T(8,128)(2,1)S(1)} %get-tuple-element.70.refs_2_), channel_id=1, source_target_pairs={{0,2},{1,3},{2,0},{3,1},{4,6},{5,7},{6,4},{7,5},{8,10},{9,11},{10,... | collective-permute-start | bytes 1376264 | tf_op jit(solution)/shard_map/ppermute | solution.py:324
  89.1 19.4 %collective-permute-start.18 = (bf16[128,1792]{1,0:T(8,128)(2,1)S(1)}, bf16[128,1792]{1,0:T(8,128)(2,1)S(1)}, u32[]{:S(2)}, u32[]{:S(2)}) collective-permute-start(bf16[128,1792]{1,0:T(8,128)(2,1)S(1)} %get-tuple-element.70.refs_2_), channel_id=1, source_target_pairs={{0,1},{1,0},{2,3},{3,2},{4,5},{5,4},{6,7},{7,6},{8,9},{9,8},{10,11... | collective-permute-start | bytes 1376264 | tf_op jit(solution)/shard_map/ppermute | solution.py:324
  92.0 19.1 %collective-permute-start.21 = (bf16[3,224,1024]{2,1,0:T(8,128)(2,1)S(1)}, bf16[3,224,1024]{2,1,0:T(8,128)(2,1)S(1)}, u32[]{:S(2)}, u32[]{:S(2)}) collective-permute-start(bf16[3,224,1024]{2,1,0:T(8,128)(2,1)S(1)} %pad_maximum_fusion.refs_3_), channel_id=1, source_target_pairs={{0,4},{4,0},{8,12},{12,8},{16,20},{20,16},{24,28},{28,24},{1,5},{5... | collective-permute-start | bytes 4128776 | tf_op jit(solution)/shard_map/ppermute | solution.py:324
  92.1 17.9 %collective-permute-start.19 = (bf16[3,112,1024]{2,1,0:T(8,128)(2,1)S(1)}, bf16[3,112,1024]{2,1,0:T(8,128)(2,1)S(1)}, u32[]{:S(2)}, u32[]{:S(2)}) collective-permute-start(bf16[3,112,1024]{2,1,0:T(8,128)(2,1)S(1)} %slice.20), channel_id=1, source_target_pairs={{0,16},{4,20},{8,24},{12,28},{16,0},{20,4},{24,8},{28,12},{1,17},{... | collective-permute-start | bytes 2064392 | tf_op jit(solution)/shard_map/ppermute | solution.py:324
  93.5 17.6 %collective-permute-start.20 = (bf16[3,112,1024]{2,1,0:T(8,128)(2,1)S(1)}, bf16[3,112,1024]{2,1,0:T(8,128)(2,1)S(1)}, u32[]{:S(2)}, u32[]{:S(2)}) collective-permute-start(bf16[3,112,1024]{2,1,0:T(8,128)(2,1)S(1)} %slice.21), channel_id=1, source_target_pairs={{0,8},{4,12},{8,0},{12,4},{16,24},{20,28},{24,16},{28,20},{1,9},{5... | collective-permute-start | bytes 2064392 | tf_op jit(solution)/shard_map/ppermute | solution.py:324
  108.5 7.1 %collective-permute-start.22 = (bf16[3,224,1024]{2,1,0:T(8,128)(2,1)S(1)}, bf16[3,224,1024]{2,1,0:T(8,128)(2,1)S(1)}, u32[]{:S(2)}, u32[]{:S(2)}) collective-permute-start(bf16[3,224,1024]{2,1,0:T(8,128)(2,1)S(1)} %collective-permute-done.15.refs_4_), channel_id=1, source_target_pairs={{0,4},{4,0},{8,12},{12,8},{16,20},{20,16},{24,28},{28,24},{1,5},{5... | collective-permute-start | bytes 4128776 | tf_op jit(solution)/shard_map/ppermute | solution.py:324
  108.5 7.0 %collective-permute-start.23 = (bf16[3,224,1024]{2,1,0:T(8,128)(2,1)S(1)}, bf16[3,224,1024]{2,1,0:T(8,128)(2,1)S(1)}, u32[]{:S(2)}, u32[]{:S(2)}) collective-permute-start(bf16[3,224,1024]{2,1,0:T(8,128)(2,1)S(1)} %collective-permute-done.16.refs_5_), channel_id=1, source_target_pairs={{0,4},{4,0},{8,12},{12,8},{16,20},{20,16},{24,28},{28,24},{1,5},{5... | collective-permute-start | bytes 4128776 | tf_op jit(solution)/shard_map/ppermute | solution.py:324
  110.0 4.6 %collective-permute-start.24 = (bf16[3,112,1024]{2,1,0:T(8,128)(2,1)S(1)}, bf16[3,112,1024]{2,1,0:T(8,128)(2,1)S(1)}, u32[]{:S(2)}, u32[]{:S(2)}) collective-permute-start(bf16[3,112,1024]{2,1,0:T(8,128)(2,1)S(1)} %collective-permute-done.19.refs_6_), channel_id=1, source_target_pairs={{0,4},{4,0},{8,12},{12,8},{16,20},{20,16},{24,28},{28,24},{1,5},{5... | collective-permute-start | bytes 2064392 | tf_op jit(solution)/shard_map/ppermute | solution.py:324
  111.1 4.4 %collective-permute-start.25 = (bf16[3,112,1024]{2,1,0:T(8,128)(2,1)S(1)}, bf16[3,112,1024]{2,1,0:T(8,128)(2,1)S(1)}, u32[]{:S(2)}, u32[]{:S(2)}) collective-permute-start(bf16[3,112,1024]{2,1,0:T(8,128)(2,1)S(1)} %collective-permute-done.20.refs_7_), channel_id=1, source_target_pairs={{0,4},{4,0},{8,12},{12,8},{16,20},{20,16},{24,28},{28,24},{1,5},{5... | collective-permute-start | bytes 2064392 | tf_op jit(solution)/shard_map/ppermute | solution.py:324
  111.1 9.9 %collective-permute-start.26 = (bf16[80,1792]{1,0:T(8,128)(2,1)S(1)}, bf16[80,1792]{1,0:T(8,128)(2,1)S(1)}, u32[]{:S(2)}, u32[]{:S(2)}) collective-permute-start(bf16[80,1792]{1,0:T(8,128)(2,1)S(1)} %slice.22), channel_id=1, source_target_pairs={{0,1},{1,0},{2,3},{3,2},{4,5},{5,4},{6,7},{7,6},{8,9},{9,8},{10,11... | collective-permute-start | bytes 860168 | tf_op jit(solution)/shard_map/ppermute | solution.py:324
  114.6 10.1 %collective-permute-start.28 = (bf16[48,1792]{1,0:T(8,128)(2,1)S(1)}, bf16[48,1792]{1,0:T(8,128)(2,1)S(1)}, u32[]{:S(2)}, u32[]{:S(2)}) collective-permute-start(bf16[48,1792]{1,0:T(8,128)(2,1)S(1)} %slice.23), channel_id=1, source_target_pairs={{0,1},{1,0},{2,3},{3,2},{4,5},{5,4},{6,7},{7,6},{8,9},{9,8},{10,11... | collective-permute-start | bytes 516104 | tf_op jit(solution)/shard_map/ppermute | solution.py:324
  123.5 12.6 %collective-permute-start.27 = (bf16[80,1792]{1,0:T(8,128)(2,1)S(1)}, bf16[80,1792]{1,0:T(8,128)(2,1)S(1)}, u32[]{:S(2)}, u32[]{:S(2)}) collective-permute-start(bf16[80,1792]{1,0:T(8,128)(2,1)S(1)} %shard_map.151), channel_id=1, source_target_pairs={{0,1},{1,0},{2,3},{3,2},{4,5},{5,4},{6,7},{7,6},{8,9},{9,8},{10,11... | collective-permute-start | bytes 860168 | tf_op jit(solution)/shard_map/ppermute | solution.py:324
  127.1 9.1 %collective-permute-start.29 = (bf16[48,1792]{1,0:T(8,128)(2,1)S(1)}, bf16[48,1792]{1,0:T(8,128)(2,1)S(1)}, u32[]{:S(2)}, u32[]{:S(2)}) collective-permute-start(bf16[48,1792]{1,0:T(8,128)(2,1)S(1)} %shard_map.152), channel_id=1, source_target_pairs={{0,1},{1,0},{2,3},{3,2},{4,5},{5,4},{6,7},{7,6},{8,9},{9,8},{10,11... | collective-permute-start | bytes 516104 | tf_op jit(solution)/shard_map/ppermute | solution.py:324
  136.3 22.6 %collective-permute-start.30 = (bf16[128,1792]{1,0:T(8,128)(2,1)S(1)}, bf16[128,1792]{1,0:T(8,128)(2,1)S(1)}, u32[]{:S(2)}, u32[]{:S(2)}) collective-permute-start(bf16[128,1792]{1,0:T(8,128)(2,1)S(1)} %shard_map.153), channel_id=1, source_target_pairs={{0,2},{1,3},{2,0},{3,1},{4,6},{5,7},{6,4},{7,5},{8,10},{9,11},{10,... | collective-permute-start | bytes 1376264 | tf_op jit(solution)/shard_map/ppermute | solution.py:324
  139.1 20.0 %collective-permute-start.31 = (bf16[128,1792]{1,0:T(8,128)(2,1)S(1)}, bf16[128,1792]{1,0:T(8,128)(2,1)S(1)}, u32[]{:S(2)}, u32[]{:S(2)}) collective-permute-start(bf16[128,1792]{1,0:T(8,128)(2,1)S(1)} %get-tuple-element.80), channel_id=1, source_target_pairs={{0,1},{1,0},{2,3},{3,2},{4,5},{5,4},{6,7},{7,6},{8,9},{9,8},{10,11... | collective-permute-start | bytes 1376264 | tf_op jit(solution)/shard_map/ppermute | solution.py:324
  (11 other events, 178.0 us)

commit v8 on v7

--- a/solution.py
+++ b/solution.py
@@ -683,7 +683,7 @@
     token_two, token_one = swap(normed_mlp, "col", 2), swap(normed_mlp, "col", 1)
     feed_thirds = tuple(swap(piece, "row", 1) for piece in feed_seconds[:2])
     token_two, token_one = lax.optimization_barrier((token_two, token_one))
-    split = count * 5 // 8
+    split = count // 2
     three = [swap(rows, "col", 1) for rows in (token_two[:split], token_two[split:])]
     feed_pieces = named_pieces(feed_own, feed_firsts, feed_seconds, feed_thirds)
     feed_w, part_two, part_one, part_own = feed_first_call(

time: 160 us -> 160 us (level)
  transfers between devices with their start and end apart: 32 -> 32, of which waited for: 21 -> 22; matrix products, arithmetic and copies ran while one was open for 5% -> 5% of each run, Pallas kernels for 14% -> 14%
where the time goes in v8:
time: 160 us
  waiting for transfers between devices  87.5 us (55%)
  starting transfers between devices  32.3 us (20%)
  Pallas kernels  32 us (20%)
  local copies, waits for them, and re-layouts  7.47 us (5%)
    ppermute x32, waiting for transfers between devices, swap(): return lax.ppermute(value, axis, xor_pairs(lax.axis_size(axis), mask))  87.5 us
    ppermute x32, starting transfers between devices, swap(): return lax.ppermute(value, axis, xor_pairs(lax.axis_size(axis), mask))  32.3 us
    pallas_call x1, Pallas kernels, rest_call(): pl.pallas_call(functools.partial(rest_kernel, masks), out_shape=[jax.Shap...  8.68 us
    reshape x2, local copies, waits for them, and re-layouts, tuned(): cache = window_key_value.reshape(requests, 2, heads, window, HD)  5.56 us
    pallas_call x1, Pallas kernels, first_call(): pl.pallas_call(functools.partial(first_kernel, places, n_x, n_w), out_sha...  5.34 us
    pallas_call x1, Pallas kernels, feed_first_call(): pl.pallas_call(functools.partial(feed_first_kernel, places, n_x, n_w), ou...  5.29 us
    pallas_call x2, Pallas kernels, feed_last_call(): pl.pallas_call(feed_last_kernel, out_shape=jax.ShapeDtypeStruct(rows.shap...  4.83 us
    pallas_call x1, Pallas kernels, own_call(): pl.pallas_call(functools.partial(own_kernel, rank), out_shape=jax.ShapeDt...  3.7 us
  transfers between devices with their start and end apart: 32, of which 22 were waited for; matrix products, arithmetic and copies ran while one was open for 5% of the time, Pallas kernels for 14%

profile of v8, /device:TPU:0, one launch (start us, length us, event | category | flops | bytes accessed | tf_op | source)
XLA Modules:
  0.0 159.9 jit_solution(15194727373171720428)
XLA Ops:
  0.0 2.7 %shard_map.145 = (bf16[128,1792]{1,0:T(8,128)(2,1)}, bf16[288,1792]{1,0:T(8,128)(2,1)}) custom-call(bf16[128,1792]{1,0:T(8,128)(2,1)} %x_ref.1, bf16[3,224,448]{2,1,0:T(8,128)(2,1)} %bitcast.14, bf16[448,224]{1,0:T(8,128)(2,1)} %refs_2_.1, f32[1792]{0:T(1024)} %refs_3_.1, bf16[32,1792]{1,0:T(8,128)(2,1)} %bitcast.18, bf16[32,1792]{1,0:T(8,128)(2,1)} %bitcast.19), custom_call_target="tpu_custom_call" | custom-call | flops 1 | bytes 1 | tf_op jit(solution)/shard_map/pallas_call | solution.py:278
  2.7 3.0 %collective-permute-start.2 = (bf16[288,1792]{1,0:T(8,128)(2,1)}, bf16[288,1792]{1,0:T(8,128)(2,1)S(1)}, u32[]{:S(2)}, u32[]{:S(2)}) collective-permute-start(bf16[288,1792]{1,0:T(8,128)(2,1)} %get-tuple-element.44.refs_4_), channel_id=1, source_target_pairs={{0,8},{4,12},{8,0},{12,4},{16,24},{20,28},{24,16},{28,20},{1,9},{5... | collective-permute-start | bytes 3096584 | tf_op jit(solution)/shard_map/ppermute | solution.py:324
  5.7 1.5 collective-permute-start.3
  7.2 2.6 %collective-permute-start = (bf16[128,1792]{1,0:T(8,128)(2,1)}, bf16[128,1792]{1,0:T(8,128)(2,1)S(1)}, u32[]{:S(2)}, u32[]{:S(2)}) collective-permute-start(bf16[128,1792]{1,0:T(8,128)(2,1)} %get-tuple-element.43.refs_0_.x_ref), channel_id=1, source_target_pairs={{0,2},{1,3},{2,0},{3,1},{4,6},{5,7},{6,4},{7,5},{8,10},{9,11},{10,... | collective-permute-start | bytes 1376264 | tf_op jit(solution)/shard_map/ppermute | solution.py:324
  9.8 1.6 collective-permute-start.1
  11.4 3.2 %reshape.14 = bf16[8,2,4,64,112]{4,3,2,1,0:T(8,128)(2,1)} reshape(bf16[8,2,4,7168]{3,2,1,0:T(4,128)(2,1)} %param.20) | data formatting | bytes 1835008 | tf_op jit(solution)/shard_map/reshape | solution.py:648
  14.6 2.3 %copy.16 = bf16[8,2,4,64,112]{4,3,0,2,1:T(8,128)(2,1)} copy(bf16[8,2,4,64,112]{4,3,2,1,0:T(8,128)(2,1)} %reshape.14) | data formatting | bytes 1835008 | tf_op jit(solution)/shard_map/reshape | solution.py:648
  17.1 1.5 pad.4.refs_17_.cache_ref.refs_2_
  18.9 9.8 %collective-permute-done.2.refs_5_ = bf16[288,1792]{1,0:T(8,128)(2,1)S(1)} collective-permute-done((bf16[288,1792]{1,0:T(8,128)(2,1)}, bf16[288,1792]{1,0:T(8,128)(2,1)S(1)}, u32[]{:S(2)}, u32[]{:S(2)}) %collective-permute-start.2) | collective-permute-done | bytes 1032224 | tf_op jit(solution)/shard_map/ppermute | solution.py:324
  28.7 1.5 collective-permute-done.3.refs_6_
  30.2 1.6 collective-permute-start.4
  31.8 1.6 collective-permute-start.5
  34.5 6.8 %collective-permute-done.4.refs_3_ = bf16[128,1792]{1,0:T(8,128)(2,1)S(1)} collective-permute-done((bf16[128,1792]{1,0:T(8,128)(2,1)S(1)}, bf16[128,1792]{1,0:T(8,128)(2,1)S(1)}, u32[]{:S(2)}, u32[]{:S(2)}) %collective-permute-start.4) | collective-permute-done | bytes 458784 | tf_op jit(solution)/shard_map/ppermute | solution.py:324
  41.4 2.8 %collective-permute-done.5.refs_7_ = bf16[144,1792]{1,0:T(8,128)(2,1)S(1)} collective-permute-done((bf16[144,1792]{1,0:T(8,128)(2,1)S(1)}, bf16[144,1792]{1,0:T(8,128)(2,1)S(1)}, u32[]{:S(2)}, u32[]{:S(2)}) %collective-permute-start.5) | collective-permute-done | bytes 516128 | tf_op jit(solution)/shard_map/ppermute | solution.py:324
  45.8 1.4 collective-permute-done.10.refs_12_
  47.9 5.3 %shard_map.146 = (bf16[512,1792]{1,0:T(8,128)(2,1)S(1)}, bf16[1792,1408]{1,0:T(8,128)(2,1)S(1)}, bf16[1792,512]{1,0:T(8,128)(2,1)S(1)}, bf16[256,1792]{1,0:T(8,1...) custom-call(bf16[128,1792]{1,0:T(8,128)(2,1)S(1)} %copy-done.2, ...), custom_call_target="tpu_custom_call" | custom-call | flops 1 | bytes 1 | tf_op jit(solution)/shard_map/pallas_call | solution.py:471
  55.0 8.7 %shard_map.147 = (bf16[512,512]{1,0:T(8,128)(2,1)S(1)}, bf16[512,512]{1,0:T(8,128)(2,1)S(1)}, bf16[512,512]{1,0:T(8,128)(2,1)S(1)}, bf16[128,1792]{1,0:T(8,128)(2,1)S(1)}, bf16[128,1792]{1,0:T(8,128)(2,1)S(1)}) custom-call(bf16[512,1792]{1,0:T(8,128)(2,1)S(1)} %get-tuple-element.55.x_all, bf16[1792,1408]{1,0:T(8,128)(2,1)S(1)} %get-tuple-element.56.w_all, ...), custom_call_target="tpu_custom_call" | custom-call | flops 1 | bytes 1 | tf_op jit(solution)/shard_map/pallas_call | solution.py:500
  63.7 1.7 %collective-permute-start.14 = (bf16[128,1792]{1,0:T(8,128)(2,1)S(1)}, bf16[128,1792]{1,0:T(8,128)(2,1)S(1)}, u32[]{:S(2)}, u32[]{:S(2)}) collective-permute-start(bf16[128,1792]{1,0:T(8,128)(2,1)S(1)} %get-tuple-element.66), channel_id=1, source_target_pairs={{0,1},{1,0},{2,3},{3,2},{4,5},{5,4},{6,7},{7,6},{8,9},{9,8},{10,11... | collective-permute-start | bytes 1376264 | tf_op jit(solution)/shard_map/ppermute | solution.py:324
  66.1 2.7 %collective-permute-start.13 = (bf16[128,1792]{1,0:T(8,128)(2,1)S(1)}, bf16[128,1792]{1,0:T(8,128)(2,1)S(1)}, u32[]{:S(2)}, u32[]{:S(2)}) collective-permute-start(bf16[128,1792]{1,0:T(8,128)(2,1)S(1)} %add_convert_fusion), channel_id=1, source_target_pairs={{0,2},{1,3},{2,0},{3,1},{4,6},{5,7},{6,4},{7,5},{8,10},{9,11},{10,... | collective-permute-start | bytes 1376264 | tf_op jit(solution)/shard_map/ppermute | solution.py:324
  68.9 3.7 %shard_map.148.own_ref = f32[128,1792]{1,0:T(8,128)S(1)} custom-call(bf16[512,512]{1,0:T(8,128)(2,1)S(1)} %get-tuple-element.58.q_ref, bf16[512,512]{1,0:T(8,128)(2,1)S(1)} %get-tuple-element.59.k_ref, bf16[512,512]{1,0:T(8,128)(2,1)S(1)} %get-tuple-element.60.v_ref, bf16[1792,512]{1,0:T(8,128)(2,1)S(1)} %get-tuple-element.57.out_w, ...), custom_call_target="tpu_custom_call" | custom-call | flops 1 | bytes 1 | tf_op jit(solution)/shard_map/pallas_call | solution.py:521
  72.6 12.5 %collective-permute-done.14.one_ref = bf16[128,1792]{1,0:T(8,128)(2,1)S(1)} collective-permute-done((bf16[128,1792]{1,0:T(8,128)(2,1)S(1)}, bf16[128,1792]{1,0:T(8,128)(2,1)S(1)}, u32[]{:S(2)}, u32[]{:S(2)}) %collective-permute-start.14) | collective-permute-done | bytes 458784 | tf_op jit(solution)/shard_map/ppermute | solution.py:324
  86.1 2.5 %collective-permute-done.13.two_ref = bf16[128,1792]{1,0:T(8,128)(2,1)S(1)} collective-permute-done((bf16[128,1792]{1,0:T(8,128)(2,1)S(1)}, bf16[128,1792]{1,0:T(8,128)(2,1)S(1)}, u32[]{:S(2)}, u32[]{:S(2)}) %collective-permute-start.13) | collective-permute-done | bytes 458784 | tf_op jit(solution)/shard_map/ppermute | solution.py:324
  89.2 2.9 %collective-permute-start.18 = (bf16[128,1792]{1,0:T(8,128)(2,1)S(1)}, bf16[128,1792]{1,0:T(8,128)(2,1)S(1)}, u32[]{:S(2)}, u32[]{:S(2)}) collective-permute-start(bf16[128,1792]{1,0:T(8,128)(2,1)S(1)} %get-tuple-element.70.refs_2_), channel_id=1, source_target_pairs={{0,1},{1,0},{2,3},{3,2},{4,5},{5,4},{6,7},{7,6},{8,9},{9,8},{10,11... | collective-permute-start | bytes 1376264 | tf_op jit(solution)/shard_map/ppermute | solution.py:324
  94.3 14.2 %collective-permute-done.17.refs_0_ = bf16[128,1792]{1,0:T(8,128)(2,1)S(1)} collective-permute-done((bf16[128,1792]{1,0:T(8,128)(2,1)S(1)}, bf16[128,1792]{1,0:T(8,128)(2,1)S(1)}, u32[]{:S(2)}, u32[]{:S(2)}) %collective-permute-start.17) | collective-permute-done | bytes 458784 | tf_op jit(solution)/shard_map/ppermute | solution.py:324
  111.3 3.3 %collective-permute-done.24.refs_11_ = bf16[3,112,1024]{2,1,0:T(8,128)(2,1)S(1)} collective-permute-done((bf16[3,112,1024]{2,1,0:T(8,128)(2,1)S(1)}, bf16[3,112,1024]{2,1,0:T(8,128)(2,1)S(1)}, u32[]{:S(2)}, u32[]{:S(2)}) %collective-permute-start.24) | collective-permute-done | bytes 688160 | tf_op jit(solution)/shard_map/ppermute | solution.py:324
  115.5 5.3 %shard_map.150 = (bf16[3,1792,1024]{2,1,0:T(8,128)(2,1)S(1)}, bf16[128,1792]{1,0:T(8,128)(2,1)S(1)}, bf16[128,1792]{1,0:T(8,128)(2,1)S(1)}, f32[128,1792]{1,0:T(8,128)S(1)}) custom-call(bf16[128,1792]{1,0:T(8,128)(2,1)S(1)} %collective-permute-done.17.refs_0_, bf16[128,1792]{1,0:T(8,128)(2,1)S(1)} %collective-permute-done.18.refs_1_, ...), custom_call_target="tpu_custom_call" | custom-call | flops 1 | bytes 1 | tf_op jit(solution)/shard_map/pallas_call | solution.py:555
  120.9 2.4 %shard_map.151 = bf16[64,1792]{1,0:T(8,128)(2,1)S(1)} custom-call(bf16[64,1792]{1,0:T(8,128)(2,1)S(1)} %collective-permute-done.26.x_ref, bf16[3,1792,1024]{2,1,0:T(8,128)(2,1)S(1)} %get-tuple-element.77.all_w), custom_call_target="tpu_custom_call" | custom-call | flops 1 | bytes 1 | tf_op jit(solution)/shard_map/pallas_call | solution.py:571
  124.4 2.4 %shard_map.152 = bf16[64,1792]{1,0:T(8,128)(2,1)S(1)} custom-call(bf16[64,1792]{1,0:T(8,128)(2,1)S(1)} %collective-permute-done.28.x_ref, bf16[3,1792,1024]{2,1,0:T(8,128)(2,1)S(1)} %get-tuple-element.77.all_w), custom_call_target="tpu_custom_call" | custom-call | flops 1 | bytes 1 | tf_op jit(solution)/shard_map/pallas_call | solution.py:571
  127.9 3.9 %collective-permute-done.27.near_ref = bf16[64,1792]{1,0:T(8,128)(2,1)S(1)} collective-permute-done((bf16[64,1792]{1,0:T(8,128)(2,1)S(1)}, bf16[64,1792]{1,0:T(8,128)(2,1)S(1)}, u32[]{:S(2)}, u32[]{:S(2)}) %collective-permute-start.27) | collective-permute-done | bytes 229408 | tf_op jit(solution)/shard_map/ppermute | solution.py:324
  131.8 4.1 %collective-permute-done.29.far_ref = bf16[64,1792]{1,0:T(8,128)(2,1)S(1)} collective-permute-done((bf16[64,1792]{1,0:T(8,128)(2,1)S(1)}, bf16[64,1792]{1,0:T(8,128)(2,1)S(1)}, u32[]{:S(2)}, u32[]{:S(2)}) %collective-permute-start.29) | collective-permute-done | bytes 229408 | tf_op jit(solution)/shard_map/ppermute | solution.py:324
  136.0 2.9 %collective-permute-start.30 = (bf16[128,1792]{1,0:T(8,128)(2,1)S(1)}, bf16[128,1792]{1,0:T(8,128)(2,1)S(1)}, u32[]{:S(2)}, u32[]{:S(2)}) collective-permute-start(bf16[128,1792]{1,0:T(8,128)(2,1)S(1)} %shard_map.153), channel_id=1, source_target_pairs={{0,2},{1,3},{2,0},{3,1},{4,6},{5,7},{6,4},{7,5},{8,10},{9,11},{10,... | collective-permute-start | bytes 1376264 | tf_op jit(solution)/shard_map/ppermute | solution.py:324
  140.2 18.5 %collective-permute-done.30.two_ref = bf16[128,1792]{1,0:T(8,128)(2,1)S(1)} collective-permute-done((bf16[128,1792]{1,0:T(8,128)(2,1)S(1)}, bf16[128,1792]{1,0:T(8,128)(2,1)S(1)}, u32[]{:S(2)}, u32[]{:S(2)}) %collective-permute-start.30) | collective-permute-done | bytes 458784 | tf_op jit(solution)/shard_map/ppermute | solution.py:324
  (77 shorter events, 18.7 us)
Async XLA Ops:
  2.7 26.0 %collective-permute-start.2 = (bf16[288,1792]{1,0:T(8,128)(2,1)}, bf16[288,1792]{1,0:T(8,128)(2,1)S(1)}, u32[]{:S(2)}, u32[]{:S(2)}) collective-permute-start(bf16[288,1792]{1,0:T(8,128)(2,1)} %get-tuple-element.44.refs_4_), channel_id=1, source_target_pairs={{0,8},{4,12},{8,0},{12,4},{16,24},{20,28},{24,16},{28,20},{1,9},{5... | collective-permute-start | bytes 3096584 | tf_op jit(solution)/shard_map/ppermute | solution.py:324
  5.7 24.5 %collective-permute-start.3 = (bf16[288,1792]{1,0:T(8,128)(2,1)}, bf16[288,1792]{1,0:T(8,128)(2,1)S(1)}, u32[]{:S(2)}, u32[]{:S(2)}) collective-permute-start(bf16[288,1792]{1,0:T(8,128)(2,1)} %get-tuple-element.44.refs_4_), channel_id=1, source_target_pairs={{0,16},{4,20},{8,24},{12,28},{16,0},{20,4},{24,8},{28,12},{1,17},{... | collective-permute-start | bytes 3096584 | tf_op jit(solution)/shard_map/ppermute | solution.py:324
  7.2 23.0 %collective-permute-start = (bf16[128,1792]{1,0:T(8,128)(2,1)}, bf16[128,1792]{1,0:T(8,128)(2,1)S(1)}, u32[]{:S(2)}, u32[]{:S(2)}) collective-permute-start(bf16[128,1792]{1,0:T(8,128)(2,1)} %get-tuple-element.43.refs_0_.x_ref), channel_id=1, source_target_pairs={{0,2},{1,3},{2,0},{3,1},{4,6},{5,7},{6,4},{7,5},{8,10},{9,11},{10,... | collective-permute-start | bytes 1376264 | tf_op jit(solution)/shard_map/ppermute | solution.py:324
  9.8 20.4 %collective-permute-start.1 = (bf16[128,1792]{1,0:T(8,128)(2,1)}, bf16[128,1792]{1,0:T(8,128)(2,1)S(1)}, u32[]{:S(2)}, u32[]{:S(2)}) collective-permute-start(bf16[128,1792]{1,0:T(8,128)(2,1)} %get-tuple-element.43.refs_0_.x_ref), channel_id=1, source_target_pairs={{0,1},{1,0},{2,3},{3,2},{4,5},{5,4},{6,7},{7,6},{8,9},{9,8},{10,11... | collective-permute-start | bytes 1376264 | tf_op jit(solution)/shard_map/ppermute | solution.py:324
  30.2 11.2 %collective-permute-start.4 = (bf16[128,1792]{1,0:T(8,128)(2,1)S(1)}, bf16[128,1792]{1,0:T(8,128)(2,1)S(1)}, u32[]{:S(2)}, u32[]{:S(2)}) collective-permute-start(bf16[128,1792]{1,0:T(8,128)(2,1)S(1)} %collective-permute-done.refs_2_), channel_id=1, source_target_pairs={{0,1},{1,0},{2,3},{3,2},{4,5},{5,4},{6,7},{7,6},{8,9},{9,8},{10,11... | collective-permute-start | bytes 1376264 | tf_op jit(solution)/shard_map/ppermute | solution.py:324
  31.8 12.3 %collective-permute-start.5 = (bf16[144,1792]{1,0:T(8,128)(2,1)S(1)}, bf16[144,1792]{1,0:T(8,128)(2,1)S(1)}, u32[]{:S(2)}, u32[]{:S(2)}) collective-permute-start(bf16[144,1792]{1,0:T(8,128)(2,1)S(1)} %slice.18), channel_id=1, source_target_pairs={{0,16},{4,20},{8,24},{12,28},{16,0},{20,4},{24,8},{28,12},{1,17},{... | collective-permute-start | bytes 1548296 | tf_op jit(solution)/shard_map/ppermute | solution.py:324
  33.4 11.8 %collective-permute-start.6 = (bf16[144,1792]{1,0:T(8,128)(2,1)S(1)}, bf16[144,1792]{1,0:T(8,128)(2,1)S(1)}, u32[]{:S(2)}, u32[]{:S(2)}) collective-permute-start(bf16[144,1792]{1,0:T(8,128)(2,1)S(1)} %slice.19), channel_id=1, source_target_pairs={{0,8},{4,12},{8,0},{12,4},{16,24},{20,28},{24,16},{28,20},{1,9},{5... | collective-permute-start | bytes 1548296 | tf_op jit(solution)/shard_map/ppermute | solution.py:324
  34.0 11.7 %collective-permute-start.7 = (bf16[288,1792]{1,0:T(8,128)(2,1)S(1)}, bf16[288,1792]{1,0:T(8,128)(2,1)S(1)}, u32[]{:S(2)}, u32[]{:S(2)}) collective-permute-start(bf16[288,1792]{1,0:T(8,128)(2,1)S(1)} %copy-done.3), channel_id=1, source_target_pairs={{0,4},{4,0},{8,12},{12,8},{16,20},{20,16},{24,28},{28,24},{1,5},{5... | collective-permute-start | bytes 3096584 | tf_op jit(solution)/shard_map/ppermute | solution.py:324
  34.0 11.7 %collective-permute-start.8 = (bf16[288,1792]{1,0:T(8,128)(2,1)S(1)}, bf16[288,1792]{1,0:T(8,128)(2,1)S(1)}, u32[]{:S(2)}, u32[]{:S(2)}) collective-permute-start(bf16[288,1792]{1,0:T(8,128)(2,1)S(1)} %collective-permute-done.2.refs_5_), channel_id=1, source_target_pairs={{0,4},{4,0},{8,12},{12,8},{16,20},{20,16},{24,28},{28,24},{1,5},{5... | collective-permute-start | bytes 3096584 | tf_op jit(solution)/shard_map/ppermute | solution.py:324
  41.4 4.4 %collective-permute-start.9 = (bf16[288,1792]{1,0:T(8,128)(2,1)S(1)}, bf16[288,1792]{1,0:T(8,128)(2,1)S(1)}, u32[]{:S(2)}, u32[]{:S(2)}) collective-permute-start(bf16[288,1792]{1,0:T(8,128)(2,1)S(1)} %collective-permute-done.3.refs_6_), channel_id=1, source_target_pairs={{0,4},{4,0},{8,12},{12,8},{16,20},{20,16},{24,28},{28,24},{1,5},{5... | collective-permute-start | bytes 3096584 | tf_op jit(solution)/shard_map/ppermute | solution.py:324
  45.2 1.9 %collective-permute-start.10 = (bf16[144,1792]{1,0:T(8,128)(2,1)S(1)}, bf16[144,1792]{1,0:T(8,128)(2,1)S(1)}, u32[]{:S(2)}, u32[]{:S(2)}) collective-permute-start(bf16[144,1792]{1,0:T(8,128)(2,1)S(1)} %collective-permute-done.5.refs_7_), channel_id=1, source_target_pairs={{0,4},{4,0},{8,12},{12,8},{16,20},{20,16},{24,28},{28,24},{1,5},{5... | collective-permute-start | bytes 1548296 | tf_op jit(solution)/shard_map/ppermute | solution.py:324
  45.2 2.6 %collective-permute-start.11 = (bf16[144,1792]{1,0:T(8,128)(2,1)S(1)}, bf16[144,1792]{1,0:T(8,128)(2,1)S(1)}, u32[]{:S(2)}, u32[]{:S(2)}) collective-permute-start(bf16[144,1792]{1,0:T(8,128)(2,1)S(1)} %collective-permute-done.6.refs_8_), channel_id=1, source_target_pairs={{0,4},{4,0},{8,12},{12,8},{16,20},{20,16},{24,28},{28,24},{1,5},{5... | collective-permute-start | bytes 1548296 | tf_op jit(solution)/shard_map/ppermute | solution.py:324
  53.2 12.8 %collective-permute-start.12 = (bf16[128,1792]{1,0:T(8,128)(2,1)S(1)}, bf16[128,1792]{1,0:T(8,128)(2,1)S(1)}, u32[]{:S(2)}, u32[]{:S(2)}) collective-permute-start(bf16[128,1792]{1,0:T(8,128)(2,1)S(1)} %get-tuple-element.65), channel_id=1, source_target_pairs={{0,1},{1,0},{2,3},{3,2},{4,5},{5,4},{6,7},{7,6},{8,9},{9,8},{10,11... | collective-permute-start | bytes 1376264 | tf_op jit(solution)/shard_map/ppermute | solution.py:324
  53.8 31.9 %collective-permute-start.15 = (bf16[3,224,1024]{2,1,0:T(8,128)(2,1)S(1)}, bf16[3,224,1024]{2,1,0:T(8,128)(2,1)S(1)}, u32[]{:S(2)}, u32[]{:S(2)}) collective-permute-start(bf16[3,224,1024]{2,1,0:T(8,128)(2,1)S(1)} %pad_maximum_fusion.refs_3_), channel_id=1, source_target_pairs={{0,8},{4,12},{8,0},{12,4},{16,24},{20,28},{24,16},{28,20},{1,9},{5... | collective-permute-start | bytes 4128776 | tf_op jit(solution)/shard_map/ppermute | solution.py:324
  54.4 31.7 %collective-permute-start.16 = (bf16[3,224,1024]{2,1,0:T(8,128)(2,1)S(1)}, bf16[3,224,1024]{2,1,0:T(8,128)(2,1)S(1)}, u32[]{:S(2)}, u32[]{:S(2)}) collective-permute-start(bf16[3,224,1024]{2,1,0:T(8,128)(2,1)S(1)} %pad_maximum_fusion.refs_3_), channel_id=1, source_target_pairs={{0,16},{4,20},{8,24},{12,28},{16,0},{20,4},{24,8},{28,12},{1,17},{... | collective-permute-start | bytes 4128776 | tf_op jit(solution)/shard_map/ppermute | solution.py:324
  63.7 21.4 %collective-permute-start.14 = (bf16[128,1792]{1,0:T(8,128)(2,1)S(1)}, bf16[128,1792]{1,0:T(8,128)(2,1)S(1)}, u32[]{:S(2)}, u32[]{:S(2)}) collective-permute-start(bf16[128,1792]{1,0:T(8,128)(2,1)S(1)} %get-tuple-element.66), channel_id=1, source_target_pairs={{0,1},{1,0},{2,3},{3,2},{4,5},{5,4},{6,7},{7,6},{8,9},{9,8},{10,11... | collective-permute-start | bytes 1376264 | tf_op jit(solution)/shard_map/ppermute | solution.py:324
  66.1 22.4 %collective-permute-start.13 = (bf16[128,1792]{1,0:T(8,128)(2,1)S(1)}, bf16[128,1792]{1,0:T(8,128)(2,1)S(1)}, u32[]{:S(2)}, u32[]{:S(2)}) collective-permute-start(bf16[128,1792]{1,0:T(8,128)(2,1)S(1)} %add_convert_fusion), channel_id=1, source_target_pairs={{0,2},{1,3},{2,0},{3,1},{4,6},{5,7},{6,4},{7,5},{8,10},{9,11},{10,... | collective-permute-start | bytes 1376264 | tf_op jit(solution)/shard_map/ppermute | solution.py:324
  88.9 19.5 %collective-permute-start.17 = (bf16[128,1792]{1,0:T(8,128)(2,1)S(1)}, bf16[128,1792]{1,0:T(8,128)(2,1)S(1)}, u32[]{:S(2)}, u32[]{:S(2)}) collective-permute-start(bf16[128,1792]{1,0:T(8,128)(2,1)S(1)} %get-tuple-element.70.refs_2_), channel_id=1, source_target_pairs={{0,2},{1,3},{2,0},{3,1},{4,6},{5,7},{6,4},{7,5},{8,10},{9,11},{10,... | collective-permute-start | bytes 1376264 | tf_op jit(solution)/shard_map/ppermute | solution.py:324
  89.2 19.4 %collective-permute-start.18 = (bf16[128,1792]{1,0:T(8,128)(2,1)S(1)}, bf16[128,1792]{1,0:T(8,128)(2,1)S(1)}, u32[]{:S(2)}, u32[]{:S(2)}) collective-permute-start(bf16[128,1792]{1,0:T(8,128)(2,1)S(1)} %get-tuple-element.70.refs_2_), channel_id=1, source_target_pairs={{0,1},{1,0},{2,3},{3,2},{4,5},{5,4},{6,7},{7,6},{8,9},{9,8},{10,11... | collective-permute-start | bytes 1376264 | tf_op jit(solution)/shard_map/ppermute | solution.py:324
  92.1 19.1 %collective-permute-start.21 = (bf16[3,224,1024]{2,1,0:T(8,128)(2,1)S(1)}, bf16[3,224,1024]{2,1,0:T(8,128)(2,1)S(1)}, u32[]{:S(2)}, u32[]{:S(2)}) collective-permute-start(bf16[3,224,1024]{2,1,0:T(8,128)(2,1)S(1)} %pad_maximum_fusion.refs_3_), channel_id=1, source_target_pairs={{0,4},{4,0},{8,12},{12,8},{16,20},{20,16},{24,28},{28,24},{1,5},{5... | collective-permute-start | bytes 4128776 | tf_op jit(solution)/shard_map/ppermute | solution.py:324
  92.1 17.9 %collective-permute-start.19 = (bf16[3,112,1024]{2,1,0:T(8,128)(2,1)S(1)}, bf16[3,112,1024]{2,1,0:T(8,128)(2,1)S(1)}, u32[]{:S(2)}, u32[]{:S(2)}) collective-permute-start(bf16[3,112,1024]{2,1,0:T(8,128)(2,1)S(1)} %slice.20), channel_id=1, source_target_pairs={{0,16},{4,20},{8,24},{12,28},{16,0},{20,4},{24,8},{28,12},{1,17},{... | collective-permute-start | bytes 2064392 | tf_op jit(solution)/shard_map/ppermute | solution.py:324
  93.5 17.6 %collective-permute-start.20 = (bf16[3,112,1024]{2,1,0:T(8,128)(2,1)S(1)}, bf16[3,112,1024]{2,1,0:T(8,128)(2,1)S(1)}, u32[]{:S(2)}, u32[]{:S(2)}) collective-permute-start(bf16[3,112,1024]{2,1,0:T(8,128)(2,1)S(1)} %slice.21), channel_id=1, source_target_pairs={{0,8},{4,12},{8,0},{12,4},{16,24},{20,28},{24,16},{28,20},{1,9},{5... | collective-permute-start | bytes 2064392 | tf_op jit(solution)/shard_map/ppermute | solution.py:324
  108.5 7.1 %collective-permute-start.22 = (bf16[3,224,1024]{2,1,0:T(8,128)(2,1)S(1)}, bf16[3,224,1024]{2,1,0:T(8,128)(2,1)S(1)}, u32[]{:S(2)}, u32[]{:S(2)}) collective-permute-start(bf16[3,224,1024]{2,1,0:T(8,128)(2,1)S(1)} %collective-permute-done.15.refs_4_), channel_id=1, source_target_pairs={{0,4},{4,0},{8,12},{12,8},{16,20},{20,16},{24,28},{28,24},{1,5},{5... | collective-permute-start | bytes 4128776 | tf_op jit(solution)/shard_map/ppermute | solution.py:324
  108.6 7.0 %collective-permute-start.23 = (bf16[3,224,1024]{2,1,0:T(8,128)(2,1)S(1)}, bf16[3,224,1024]{2,1,0:T(8,128)(2,1)S(1)}, u32[]{:S(2)}, u32[]{:S(2)}) collective-permute-start(bf16[3,224,1024]{2,1,0:T(8,128)(2,1)S(1)} %collective-permute-done.16.refs_5_), channel_id=1, source_target_pairs={{0,4},{4,0},{8,12},{12,8},{16,20},{20,16},{24,28},{28,24},{1,5},{5... | collective-permute-start | bytes 4128776 | tf_op jit(solution)/shard_map/ppermute | solution.py:324
  110.0 4.5 %collective-permute-start.24 = (bf16[3,112,1024]{2,1,0:T(8,128)(2,1)S(1)}, bf16[3,112,1024]{2,1,0:T(8,128)(2,1)S(1)}, u32[]{:S(2)}, u32[]{:S(2)}) collective-permute-start(bf16[3,112,1024]{2,1,0:T(8,128)(2,1)S(1)} %collective-permute-done.19.refs_6_), channel_id=1, source_target_pairs={{0,4},{4,0},{8,12},{12,8},{16,20},{20,16},{24,28},{28,24},{1,5},{5... | collective-permute-start | bytes 2064392 | tf_op jit(solution)/shard_map/ppermute | solution.py:324
  111.1 4.4 %collective-permute-start.25 = (bf16[3,112,1024]{2,1,0:T(8,128)(2,1)S(1)}, bf16[3,112,1024]{2,1,0:T(8,128)(2,1)S(1)}, u32[]{:S(2)}, u32[]{:S(2)}) collective-permute-start(bf16[3,112,1024]{2,1,0:T(8,128)(2,1)S(1)} %collective-permute-done.20.refs_7_), channel_id=1, source_target_pairs={{0,4},{4,0},{8,12},{12,8},{16,20},{20,16},{24,28},{28,24},{1,5},{5... | collective-permute-start | bytes 2064392 | tf_op jit(solution)/shard_map/ppermute | solution.py:324
  111.2 9.7 %collective-permute-start.26 = (bf16[64,1792]{1,0:T(8,128)(2,1)S(1)}, bf16[64,1792]{1,0:T(8,128)(2,1)S(1)}, u32[]{:S(2)}, u32[]{:S(2)}) collective-permute-start(bf16[64,1792]{1,0:T(8,128)(2,1)S(1)} %get-tuple-element.82), channel_id=1, source_target_pairs={{0,1},{1,0},{2,3},{3,2},{4,5},{5,4},{6,7},{7,6},{8,9},{9,8},{10,11... | collective-permute-start | bytes 688136 | tf_op jit(solution)/shard_map/ppermute | solution.py:324
  114.6 9.8 %collective-permute-start.28 = (bf16[64,1792]{1,0:T(8,128)(2,1)S(1)}, bf16[64,1792]{1,0:T(8,128)(2,1)S(1)}, u32[]{:S(2)}, u32[]{:S(2)}) collective-permute-start(bf16[64,1792]{1,0:T(8,128)(2,1)S(1)} %get-tuple-element.81), channel_id=1, source_target_pairs={{0,1},{1,0},{2,3},{3,2},{4,5},{5,4},{6,7},{7,6},{8,9},{9,8},{10,11... | collective-permute-start | bytes 688136 | tf_op jit(solution)/shard_map/ppermute | solution.py:324
  123.3 8.5 %collective-permute-start.27 = (bf16[64,1792]{1,0:T(8,128)(2,1)S(1)}, bf16[64,1792]{1,0:T(8,128)(2,1)S(1)}, u32[]{:S(2)}, u32[]{:S(2)}) collective-permute-start(bf16[64,1792]{1,0:T(8,128)(2,1)S(1)} %shard_map.151), channel_id=1, source_target_pairs={{0,1},{1,0},{2,3},{3,2},{4,5},{5,4},{6,7},{7,6},{8,9},{9,8},{10,11... | collective-permute-start | bytes 688136 | tf_op jit(solution)/shard_map/ppermute | solution.py:324
  126.8 9.1 %collective-permute-start.29 = (bf16[64,1792]{1,0:T(8,128)(2,1)S(1)}, bf16[64,1792]{1,0:T(8,128)(2,1)S(1)}, u32[]{:S(2)}, u32[]{:S(2)}) collective-permute-start(bf16[64,1792]{1,0:T(8,128)(2,1)S(1)} %shard_map.152), channel_id=1, source_target_pairs={{0,1},{1,0},{2,3},{3,2},{4,5},{5,4},{6,7},{7,6},{8,9},{9,8},{10,11... | collective-permute-start | bytes 688136 | tf_op jit(solution)/shard_map/ppermute | solution.py:324
  136.0 22.6 %collective-permute-start.30 = (bf16[128,1792]{1,0:T(8,128)(2,1)S(1)}, bf16[128,1792]{1,0:T(8,128)(2,1)S(1)}, u32[]{:S(2)}, u32[]{:S(2)}) collective-permute-start(bf16[128,1792]{1,0:T(8,128)(2,1)S(1)} %shard_map.153), channel_id=1, source_target_pairs={{0,2},{1,3},{2,0},{3,1},{4,6},{5,7},{6,4},{7,5},{8,10},{9,11},{10,... | collective-permute-start | bytes 1376264 | tf_op jit(solution)/shard_map/ppermute | solution.py:324
  138.9 20.0 %collective-permute-start.31 = (bf16[128,1792]{1,0:T(8,128)(2,1)S(1)}, bf16[128,1792]{1,0:T(8,128)(2,1)S(1)}, u32[]{:S(2)}, u32[]{:S(2)}) collective-permute-start(bf16[128,1792]{1,0:T(8,128)(2,1)S(1)} %get-tuple-element.80), channel_id=1, source_target_pairs={{0,1},{1,0},{2,3},{3,2},{4,5},{5,4},{6,7},{7,6},{8,9},{9,8},{10,11... | collective-permute-start | bytes 1376264 | tf_op jit(solution)/shard_map/ppermute | solution.py:324
  (11 other events, 178.0 us)
